TPU v7x, 256 devices: a whole 4x4x8 slice. The times are simulated.
256 devices in a mesh: win: 32 (over y, x, core), tile: 8 (over z).
Axes of the slice: x: 4, y: 4, z: 8, core: 2. Of those that a mesh axis runs over, the one named last changes fastest.
Arguments:
- increment: float32 [32, 3, 137, 64, 128], P('win', None, None, 'tile'), may hold values from -4 to 4
- forcing: float32 [32, 3, 137, 64, 128], P('win', None, None, 'tile'), may hold values from -6 to 6
- error_root: float32 [411, 411], replicated, may hold values from -0.09375 to 0.09375
- physics: float32 [32, 411, 411], P('win'), may hold values from -0.3125 to 0.3125
- coefficients: float32 [32, 4, 64, 128], P('win', None, 'tile'), may hold values from 0.04 to 0.24
- obs_index: int32 [3, 32, 4096], P(None, 'win', 'tile'), may hold values from 0 to 409, as said below
- obs_frac: float32 [2, 32, 4096], P(None, 'win', 'tile'), may hold values from 0 to 1
- obs_value: float32 [32, 4096], P('win', 'tile'), may hold values from -6 to 6
- obs_count: int32 [32, 8], P('win', 'tile'), may hold values from 128 to 512, as said below
Outputs:
- summed: float32 [32, 3, 137, 64, 128], P('win', None, None, 'tile')
- departure: float32 [32, 4096], P('win', 'tile')
Inputs may be any that keep to these rules, and one draw needn't show every extreme that they name: `obs_index`: x < 64, y <= 126, r mod 137 <= 135. Of each block of 512 slots at most 128 have x // 8 equal to one value; in every sub-window one value of x // 8 takes exactly 128 slots of every block. `obs_count`: every sub-window has one block with all 512 slots live.
All inputs are finite; a program needn't handle non-finite values.
Results may differ from a plain program's by a relative error of at most 0.0001.
Values sent between devices are 32-bit elements; how exact they have to be, the bound alone decides.
No kernel may reach another device: no remote copies, remote signals or barrier semaphores. Data moves between devices by JAX's collectives and lax.ppermute only.
A program may use at most 192 MiB of HBM per device.

v0:
```python
import jax
import jax.numpy as jnp
from jax import lax
from jax.sharding import PartitionSpec as P

STEPS = 6


def with_halo(cells, sides, width):
    for axis, dim in sides:
        count = lax.axis_size(axis)
        ends = count - 1
        head = lax.slice_in_dim(cells, 0, width, axis=dim)
        tail = lax.slice_in_dim(cells, cells.shape[dim] - width, cells.shape[dim], axis=dim)
        cells = jnp.concatenate(
            [
                lax.ppermute(tail, axis, [(i, (i + 1) % count) for i in range(ends)]),
                cells,
                lax.ppermute(head, axis, [((i + 1) % count, i) for i in range(ends)]),
            ],
            axis=dim,
        )
    return cells


def shifted(shard, axis, by):
    size = lax.axis_size(axis)
    pairs = [(i, i + by) for i in range(size) if 0 <= i + by < size]
    return lax.ppermute(shard, axis, pairs)


def entering(value, axis, join, neutral):
    count, mine = (lax.axis_size(axis), lax.axis_index(axis))
    pieces = lax.all_gather(value, axis)
    subtotal = jnp.full_like(value, 0) + jnp.asarray(neutral, value.dtype)

    def step(position, subtotal):
        longer = join(subtotal, pieces[position])
        return jnp.where(position < mine, longer, subtotal)

    return lax.fori_loop(0, count - 1, step, subtotal)


def tl_update(padded_state, stencil_rates, jacobian):
    center = padded_state[:, 1:-1]
    side_pad = jnp.pad(center, ((0, 0), (0, 0), (1, 1)))
    smooth = center + stencil_rates[0] * (padded_state[:, 2:] - center)
    smooth = smooth + stencil_rates[1] * (padded_state[:, :-2] - center)
    smooth = smooth + stencil_rates[2] * (side_pad[:, :, 2:] - center)
    smooth = smooth + stencil_rates[3] * (side_pad[:, :, :-2] - center)
    flat_state = smooth.reshape(smooth.shape[0], -1)
    column_mixed = flat_state + 0.2 * jnp.dot(
        jacobian, flat_state, precision=lax.Precision.HIGHEST, preferred_element_type=jnp.float32
    )
    return column_mixed.reshape(smooth.shape)


def corner_values(end_field, column_x, column_y, row_ids, tile_start, stack_axis):
    tile_rows = end_field.shape[1]
    col_count = end_field.shape[2]
    plane_size = tile_rows * col_count
    local_col = jnp.clip(column_x - tile_start, 0, tile_rows - 1)
    anchor = row_ids * plane_size + local_col * col_count + column_y
    flat_state = end_field.reshape(-1)
    return jnp.stack(
        [
            flat_state[anchor],
            flat_state[anchor + 1],
            flat_state[anchor + plane_size],
            flat_state[anchor + plane_size + 1],
        ],
        stack_axis,
    )


def add_fields(earlier, later):
    return earlier + later


def per_device(
    increment, forcing, error_root, physics, coefficients, obs_index, obs_frac, obs_value, obs_count
):
    row_count = increment.shape[1] * increment.shape[2]
    tile_rows = increment.shape[3]
    col_count = increment.shape[4]
    tile_start = lax.axis_index("tile") * tile_rows
    field_state = increment.reshape(row_count, tile_rows, col_count)
    stencil_rates = coefficients[0]
    jacobian = physics[0]
    current = field_state
    for step_index in range(STEPS):
        padded_now = with_halo(current, (("tile", 1),), 1)
        current = tl_update(padded_now, stencil_rates, jacobian)
    forced = jnp.dot(
        error_root,
        forcing.reshape(row_count, -1),
        precision=lax.Precision.HIGHEST,
        preferred_element_type=jnp.float32,
    )
    base_cells = field_state.reshape(row_count, -1) - forced
    end_flat = current.reshape(row_count, -1)
    previous = shifted(end_flat, "win", 1)
    residual = base_cells - previous
    earlier_sum = entering(residual, "win", add_fields, jnp.zeros_like(residual))
    summed = earlier_sum + residual
    own_places = obs_index[:, 0, :]
    slot_total = own_places.shape[1]
    all_places = lax.all_gather(own_places, "tile", axis=1, tiled=True)
    mine = all_places[0] // tile_rows == lax.axis_index("tile")
    values = corner_values(current, all_places[0], all_places[1], all_places[2], tile_start, 0)
    partial_terms = jnp.where(mine[None, :], values, jnp.zeros_like(values))
    corners = lax.psum_scatter(partial_terms, "tile", scatter_dimension=1, tiled=True)
    frac_y = obs_frac[0, 0]
    upward = obs_frac[1, 0]
    evolved = (1.0 - upward) * (1.0 - frac_y) * corners[0]
    evolved = evolved + (1.0 - upward) * frac_y * corners[1]
    evolved = evolved + upward * (1.0 - frac_y) * corners[2]
    evolved = evolved + upward * frac_y * corners[3]
    live_slots = jnp.arange(slot_total) < obs_count[0, 0]
    misfit = obs_value[0] - evolved
    departure = jnp.where(live_slots, misfit, jnp.zeros_like(misfit))
    return (summed.reshape(increment.shape), departure[None, :])


def solution(mesh):
    return jax.shard_map(
        per_device,
        mesh=mesh,
        in_specs=(
            P("win", None, None, "tile", None),
            P("win", None, None, "tile", None),
            P(),
            P("win", None, None),
            P("win", None, "tile", None),
            P(None, "win", "tile"),
            P(None, "win", "tile"),
            P("win", "tile"),
            P("win", "tile"),
        ),
        out_specs=(P("win", None, None, "tile", None), P("win", "tile")),
        check_vma=False,
    )
```

profile of v0, /device:TPU:1, one launch (start us, length us, event | category | flops | bytes accessed | tf_op | source)
XLA Modules:
  0.0 493.3 jit_solution(11003845697281208216)
XLA Ops:
  8.1 2.3 fusion.101
  11.7 5.0 %collective-permute-start.1 = (f32[411,1,128]{2,1,0:T(1,128)S(1)}, f32[411,1,128]{2,1,0:T(1,128)S(1)}, u32[]{:S(2)}, u32[]{:S(2)}) collective-permute-start(f32[411,1,128]{2,1,0:T(1,128)S(1)} %get-tuple-element.118), channel_id=1, source_target_pairs={{0,1},{1,2},{2,3},{3,4},{4,5},{5,6},{6,7},{8,9},{9,10},{10,11},{11... | collective-permute-start | bytes 631304 | tf_op jit(solution)/shard_map/ppermute | solution.py:17
  19.4 5.5 %fusion.3 = f32[411,8,128]{2,1,0:T(8,128)S(1)} fusion(f32[411,8,128]{2,1,0:T(8,128)} %bitcast.166, f32[411,1,128]{2,1,0:T(1,128)S(1)} %collective-permute-done.1, f32[411,1,128]{2,1,0:T(1,128)S(1)} %collective-permute-done, f32[8,128]{1,0:T(8,128)S(1)} %get-tuple-element.128, f32[8,128]{1,0:T(8,128)S(1)} %get-tuple-element.129, ...), kind=kLoop, calls=%fused_computation.27 | loop fusion | flops 5892096 | bytes 3804160 | tf_op jit(solution)/shard_map/add | solution.py:50
  26.2 3.0 bitcast_add_fusion.5
  31.1 5.2 %collective-permute-start.3 = (f32[411,1,128]{2,1,0:T(1,128)S(1)}, f32[411,1,128]{2,1,0:T(1,128)S(1)}, u32[]{:S(2)}, u32[]{:S(2)}) collective-permute-start(f32[411,1,128]{2,1,0:T(1,128)S(1)} %get-tuple-element.116), channel_id=1, source_target_pairs={{0,1},{1,2},{2,3},{3,4},{4,5},{5,6},{6,7},{8,9},{9,10},{10,11},{11... | collective-permute-start | bytes 631304 | tf_op jit(solution)/shard_map/ppermute | solution.py:17
  40.9 3.0 bitcast_add_fusion.4
  46.5 5.4 %collective-permute-start.5 = (f32[411,1,128]{2,1,0:T(1,128)}, f32[411,1,128]{2,1,0:T(1,128)}, u32[]{:S(2)}, u32[]{:S(2)}) collective-permute-start(f32[411,1,128]{2,1,0:T(1,128)} %get-tuple-element.114), channel_id=1, source_target_pairs={{0,1},{1,2},{2,3},{3,4},{4,5},{5,6},{6,7},{8,9},{9,10},{10,11},{11... | collective-permute-start | bytes 631304 | tf_op jit(solution)/shard_map/ppermute | solution.py:17
  51.9 22.8 %all-gather.1 = s32[3,1,4096]{2,1,0:T(1,128)S(1)} all-gather(s32[3,1,512]{2,1,0:T(1,128)S(1)} %copy-done.5), channel_id=3, replica_groups=mesh['win'=32,'tile'=8] {'tile'}, dimensions={2}, use_global_device_ids=true | all-gather | bytes 55296 | tf_op jit(solution)/shard_map/all_gather | solution.py:108
  74.9 2.4 fusion.15
  77.8 3.0 bitcast_add_fusion.3
  82.7 4.0 collective-permute-start.7
  91.3 3.0 bitcast_add_fusion.2
  96.3 4.6 collective-permute-start.9
  106.5 3.0 bitcast_add_fusion.1
  111.4 4.0 collective-permute-start.11
  120.0 4.2 bitcast_add_fusion
  124.2 14.5 %collective-permute-start.12 = (f32[411,1024]{1,0:T(8,128)}, f32[411,1024]{1,0:T(8,128)}, u32[]{:S(2)}, u32[]{:S(2)}) collective-permute-start(f32[411,1024]{1,0:T(8,128)} %bitcast_add_fusion), channel_id=1, source_target_pairs={{0,8},{8,16},{16,24},{24,32},{32,40},{40,48},{48,56},{56,64},{64,7... | collective-permute-start | bytes 5050376 | tf_op jit(solution)/shard_map/ppermute | solution.py:29
  140.5 23.0 %gather_fusion.1 = f32[4096]{0:T(1024)S(1)} fusion(f32[420864]{0:T(1024)S(1)} %reshape_reshape.7, s32[4096]{0:T(1024)S(1)} %broadcast_clamp_fusion.2), kind=kCustom, calls=%fused_computation.1 | custom fusion | bytes 49152 | tf_op jit(solution)/shard_map/gather | solution.py:68
  163.5 23.0 %gather_fusion.2 = f32[4096]{0:T(1024)S(1)} fusion(f32[420864]{0:T(1024)S(1)} %reshape_reshape.7, s32[4096]{0:T(1024)S(1)} %broadcast_clamp_fusion.1), kind=kCustom, calls=%fused_computation.2 | custom fusion | bytes 49152 | tf_op jit(solution)/shard_map/gather | solution.py:69
  186.5 23.0 %gather_fusion.3 = f32[4096]{0:T(1024)S(1)} fusion(f32[420864]{0:T(1024)S(1)} %reshape_reshape.7, s32[4096]{0:T(1024)S(1)} %broadcast_clamp_fusion), kind=kCustom, calls=%fused_computation.3 | custom fusion | bytes 49152 | tf_op jit(solution)/shard_map/gather | solution.py:70
  209.6 23.0 %gather_fusion = f32[4096]{0:T(1024)S(1)} fusion(f32[420864]{0:T(1024)S(1)} %reshape_reshape.7, s32[4096]{0:T(1024)S(1)} %broadcast_clamp_fusion.3), kind=kCustom, calls=%fused_computation | custom fusion | bytes 49152 | tf_op jit(solution)/shard_map/gather | solution.py:67
  234.8 6.1 %subtract_subtract_fusion = f32[411,1024]{1,0:T(8,128)} fusion(f32[411,1024]{1,0:T(8,128)} %collective-permute-done.12, f32[411,1024]{1,0:T(8,128)S(1)} %bitcast.199, f32[411,411]{1,0:T(8,128)S(1)} %copy-done, f32[411,1024]{1,0:T(8,128)} %bitcast.200), kind=kOutput, calls=%fused_computation.23 | convolution fusion | flops 2076542976 | bytes 7409508 | tf_op jit(solution)/shard_map/dot_general | solution.py:94
  241.6 35.0 %reduce-scatter.4.cloned.1.call-done = f32[512,4]{1,0:T(8,128)} async-done(((f32[4096,4]{1,0:T(8,128)}), f32[512,4]{1,0:T(8,128)}) %reduce-scatter.4.cloned.1.call-update) | async-done | bytes 8208
  276.6 2.2 fusion.102
  280.8 137.5 %all-gather.5.cloned.1.call-done = f32[32,411,1024]{2,1,0:T(8,128)} async-done(((f32[1,411,1024]{2,1,0:T(8,128)}), f32[32,411,1024]{2,1,0:T(8,128)}) %all-gather.5.cloned.1.call-update) | async-done | bytes 53870608 | tf_op jit(solution)/shard_map/all_gather | solution.py:34
  418.3 64.0 %while.14 = (s32[]{:T(128)}, f32[411,1024]{1,0:T(8,128)S(1)}, s32[]{:T(128)}, f32[32,411,1024]{2,1,0:T(8,128)}, s32[]{:T(128)}, /*index=5*/s32[]{:T(128)}) while((s32[]{:T(128)}, f32[411,1024]{1,0:T(8,128)S(1)}, s32[]{:T(128)}, f32[32,411,1024]{2,1,0:T(8,128)}, s32[]{:T(128)}, /*index=5*/s32[]{:T(128)}) %tuple.51), condition=%wide.region_1.2_spmd.clone, body=%wide.region_0.1_spmd.clone.sunk | while | flops 1262596 | bytes 5050461 | solution.py:41
  420.3 2.0 add_select_fusion.2
  424.5 2.0 add_select_fusion.2
  426.5 2.0 add_select_fusion.2
  428.6 2.0 add_select_fusion.2
  430.7 2.0 add_select_fusion.2
  434.8 2.0 add_select_fusion.2
  (119 shorter events, 95.7 us)
Async XLA Ops:
  8.0 226.8 %copy-start = (f32[411,411]{1,0:T(8,128)S(1)}, f32[411,411]{1,0:T(8,128)}, u32[]{:S(2)}) copy-start(f32[411,411]{1,0:T(8,128)} %param.13) | copy-start | bytes 2027056
  8.0 268.5 %reduce-scatter.4.cloned.1.call-start = ((), (), s32[]{:S(2)}) async-start(), calls=%async_computation.2 | async-start | bytes 2359296
  10.4 7.6 %collective-permute-start = (f32[411,1,128]{2,1,0:T(1,128)S(1)}, f32[411,1,128]{2,1,0:T(1,128)S(1)}, u32[]{:S(2)}, u32[]{:S(2)}) collective-permute-start(f32[411,1,128]{2,1,0:T(1,128)S(1)} %get-tuple-element.117), channel_id=1, source_target_pairs={{1,0},{2,1},{3,2},{4,3},{5,4},{6,5},{7,6},{9,8},{10,9},{11,10},{12... | collective-permute-start | bytes 631304 | tf_op jit(solution)/shard_map/ppermute | solution.py:19
  11.7 7.8 %collective-permute-start.1 = (f32[411,1,128]{2,1,0:T(1,128)S(1)}, f32[411,1,128]{2,1,0:T(1,128)S(1)}, u32[]{:S(2)}, u32[]{:S(2)}) collective-permute-start(f32[411,1,128]{2,1,0:T(1,128)S(1)} %get-tuple-element.118), channel_id=1, source_target_pairs={{0,1},{1,2},{2,3},{3,4},{4,5},{5,6},{6,7},{8,9},{9,10},{10,11},{11... | collective-permute-start | bytes 631304 | tf_op jit(solution)/shard_map/ppermute | solution.py:17
  25.0 1.2 copy-start.1
  29.8 7.7 %collective-permute-start.2 = (f32[411,1,128]{2,1,0:T(1,128)S(1)}, f32[411,1,128]{2,1,0:T(1,128)S(1)}, u32[]{:S(2)}, u32[]{:S(2)}) collective-permute-start(f32[411,1,128]{2,1,0:T(1,128)S(1)} %get-tuple-element.115), channel_id=1, source_target_pairs={{1,0},{2,1},{3,2},{4,3},{5,4},{6,5},{7,6},{9,8},{10,9},{11,10},{12... | collective-permute-start | bytes 631304 | tf_op jit(solution)/shard_map/ppermute | solution.py:19
  31.1 7.9 %collective-permute-start.3 = (f32[411,1,128]{2,1,0:T(1,128)S(1)}, f32[411,1,128]{2,1,0:T(1,128)S(1)}, u32[]{:S(2)}, u32[]{:S(2)}) collective-permute-start(f32[411,1,128]{2,1,0:T(1,128)S(1)} %get-tuple-element.116), channel_id=1, source_target_pairs={{0,1},{1,2},{2,3},{3,4},{4,5},{5,6},{6,7},{8,9},{9,10},{10,11},{11... | collective-permute-start | bytes 631304 | tf_op jit(solution)/shard_map/ppermute | solution.py:17
  43.8 8.1 %copy-start.5 = (s32[3,1,512]{2,1,0:T(1,128)S(1)}, s32[3,1,512]{2,1,0:T(1,128)}, u32[]{:S(2)}) copy-start(s32[3,1,512]{2,1,0:T(1,128)} %param.16) | copy-start | bytes 18436
  45.2 29.7 %collective-permute-start.4 = (f32[411,1,128]{2,1,0:T(1,128)}, f32[411,1,128]{2,1,0:T(1,128)}, u32[]{:S(2)}, u32[]{:S(2)}) collective-permute-start(f32[411,1,128]{2,1,0:T(1,128)} %get-tuple-element.113), channel_id=1, source_target_pairs={{1,0},{2,1},{3,2},{4,3},{5,4},{6,5},{7,6},{9,8},{10,9},{11,10},{12... | collective-permute-start | bytes 631304 | tf_op jit(solution)/shard_map/ppermute | solution.py:19
  46.5 28.4 %collective-permute-start.5 = (f32[411,1,128]{2,1,0:T(1,128)}, f32[411,1,128]{2,1,0:T(1,128)}, u32[]{:S(2)}, u32[]{:S(2)}) collective-permute-start(f32[411,1,128]{2,1,0:T(1,128)} %get-tuple-element.114), channel_id=1, source_target_pairs={{0,1},{1,2},{2,3},{3,4},{4,5},{5,6},{6,7},{8,9},{9,10},{10,11},{11... | collective-permute-start | bytes 631304 | tf_op jit(solution)/shard_map/ppermute | solution.py:17
  81.4 6.6 %collective-permute-start.6 = (f32[411,1,128]{2,1,0:T(1,128)S(1)}, f32[411,1,128]{2,1,0:T(1,128)S(1)}, u32[]{:S(2)}, u32[]{:S(2)}) collective-permute-start(f32[411,1,128]{2,1,0:T(1,128)S(1)} %get-tuple-element.111), channel_id=1, source_target_pairs={{1,0},{2,1},{3,2},{4,3},{5,4},{6,5},{7,6},{9,8},{10,9},{11,10},{12... | collective-permute-start | bytes 631304 | tf_op jit(solution)/shard_map/ppermute | solution.py:19
  82.7 6.7 %collective-permute-start.7 = (f32[411,1,128]{2,1,0:T(1,128)S(1)}, f32[411,1,128]{2,1,0:T(1,128)S(1)}, u32[]{:S(2)}, u32[]{:S(2)}) collective-permute-start(f32[411,1,128]{2,1,0:T(1,128)S(1)} %get-tuple-element.112), channel_id=1, source_target_pairs={{0,1},{1,2},{2,3},{3,4},{4,5},{5,6},{6,7},{8,9},{9,10},{10,11},{11... | collective-permute-start | bytes 631304 | tf_op jit(solution)/shard_map/ppermute | solution.py:17
  94.3 6.7 %copy-start.2 = (f32[1,3,137,8,128]{4,3,2,1,0:T(8,128)S(1)}, f32[1,3,137,8,128]{4,3,2,1,0:T(8,128)}, u32[]{:S(2)}) copy-start(f32[1,3,137,8,128]{4,3,2,1,0:T(8,128)} %param.11) | copy-start | bytes 5050372
  95.0 9.7 %collective-permute-start.8 = (f32[411,1,128]{2,1,0:T(1,128)S(1)}, f32[411,1,128]{2,1,0:T(1,128)S(1)}, u32[]{:S(2)}, u32[]{:S(2)}) collective-permute-start(f32[411,1,128]{2,1,0:T(1,128)S(1)} %get-tuple-element.109), channel_id=1, source_target_pairs={{1,0},{2,1},{3,2},{4,3},{5,4},{6,5},{7,6},{9,8},{10,9},{11,10},{12... | collective-permute-start | bytes 631304 | tf_op jit(solution)/shard_map/ppermute | solution.py:19
  96.3 8.4 %collective-permute-start.9 = (f32[411,1,128]{2,1,0:T(1,128)S(1)}, f32[411,1,128]{2,1,0:T(1,128)S(1)}, u32[]{:S(2)}, u32[]{:S(2)}) collective-permute-start(f32[411,1,128]{2,1,0:T(1,128)S(1)} %get-tuple-element.110), channel_id=1, source_target_pairs={{0,1},{1,2},{2,3},{3,4},{4,5},{5,6},{6,7},{8,9},{9,10},{10,11},{11... | collective-permute-start | bytes 631304 | tf_op jit(solution)/shard_map/ppermute | solution.py:17
  101.1 1.7 copy-start.4
  110.1 6.6 %collective-permute-start.10 = (f32[411,1,128]{2,1,0:T(1,128)S(1)}, f32[411,1,128]{2,1,0:T(1,128)S(1)}, u32[]{:S(2)}, u32[]{:S(2)}) collective-permute-start(f32[411,1,128]{2,1,0:T(1,128)S(1)} %get-tuple-element.107), channel_id=1, source_target_pairs={{1,0},{2,1},{3,2},{4,3},{5,4},{6,5},{7,6},{9,8},{10,9},{11,10},{12... | collective-permute-start | bytes 631304 | tf_op jit(solution)/shard_map/ppermute | solution.py:19
  111.4 6.7 %collective-permute-start.11 = (f32[411,1,128]{2,1,0:T(1,128)S(1)}, f32[411,1,128]{2,1,0:T(1,128)S(1)}, u32[]{:S(2)}, u32[]{:S(2)}) collective-permute-start(f32[411,1,128]{2,1,0:T(1,128)S(1)} %get-tuple-element.108), channel_id=1, source_target_pairs={{0,1},{1,2},{2,3},{3,4},{4,5},{5,6},{6,7},{8,9},{9,10},{10,11},{11... | collective-permute-start | bytes 631304 | tf_op jit(solution)/shard_map/ppermute | solution.py:17
  124.2 110.5 %collective-permute-start.12 = (f32[411,1024]{1,0:T(8,128)}, f32[411,1024]{1,0:T(8,128)}, u32[]{:S(2)}, u32[]{:S(2)}) collective-permute-start(f32[411,1024]{1,0:T(8,128)} %bitcast_add_fusion), channel_id=1, source_target_pairs={{0,8},{8,16},{16,24},{24,32},{32,40},{40,48},{48,56},{56,64},{64,7... | collective-permute-start | bytes 5050376 | tf_op jit(solution)/shard_map/ppermute | solution.py:29
  232.7 2.1 copy-start.3
  234.7 183.6 %all-gather.5.cloned.1.call-start = ((), (), s32[]{:S(2)}) async-start(), calls=%async_computation.1 | async-start | bytes 56229888 | tf_op jit(solution)/shard_map/all_gather | solution.py:34
  240.9 39.3 %copy-start.6 = (f32[2,1,512]{2,1,0:T(1,128)S(1)}, f32[2,1,512]{2,1,0:T(1,128)}, u32[]{:S(2)}) copy-start(f32[2,1,512]{2,1,0:T(1,128)} %param.17) | copy-start | bytes 12292
  240.9 39.3 %copy-start.7 = (f32[1,512]{1,0:T(1,128)S(1)}, f32[1,512]{1,0:T(1,128)}, u32[]{:S(2)}) copy-start(f32[1,512]{1,0:T(1,128)} %param.18) | copy-start | bytes 6148
Sparse Core Ops, SparseCore 0:
  234.8 41.6 reduce-scatter.3
Sparse Core Ops, SparseCore 1:
  241.0 177.2 all-gather.4
where the time goes:
time: 503 us; the launch traced here: 493 us
  waiting for transfers between devices  182 us (36%)
  local copies, waits for them, and re-layouts  116 us (23%)
  other arithmetic  79.2 us (16%)
  starting transfers between devices  50.6 us (10%)
  matrix products  25.2 us (5%)
  blocking collectives  22.8 us (5%)
  between operations  17 us (3%)
    all_gather x1, waiting for transfers between devices, entering(): pieces = lax.all_gather(value, axis)  137 us
    select_n x31, other arithmetic, step(): return jnp.where(position < mine, longer, subtotal)  63.2 us
    unnamed x3, waiting for transfers between devices  35 us
    ppermute x6, starting transfers between devices, with_halo(): lax.ppermute(tail, axis, [(i, (i + 1) % count) for i in range(ends)])  28.2 us
    gather x1, local copies, waits for them, and re-layouts, corner_values(): flat_state[anchor + 1]  23 us
    gather x1, local copies, waits for them, and re-layouts, corner_values(): flat_state[anchor + plane_size]  23 us
    gather x1, local copies, waits for them, and re-layouts, corner_values(): flat_state[anchor + plane_size + 1]  23 us
    gather x1, local copies, waits for them, and re-layouts, corner_values(): flat_state[anchor]  23 us
  transfers between devices with their start and end apart: 15, of which 10 were waited for; matrix products, arithmetic and copies ran while one was open for 23% of the time, Pallas kernels for 0%

commit v1 on v0

v1 whole, which is shorter than its diff:
```python
import jax
import jax.numpy as jnp
from jax import lax
from jax.experimental import pallas as pl
from jax.experimental.pallas import tpu as pltpu
from jax.sharding import Mesh, PartitionSpec as P

STEPS = 6
ROWS = 411
PAD = 416
COLS = 8
LANES = 128
GRID_Y = 4
GRID_X = 4
CORES = 2
PARTS = 16
PART = 104
TILES = 8
SLOTS = 512
CAP = 128
FIELDS = 8

F32 = jnp.float32
BF16 = jnp.bfloat16
HIGHEST = lax.Precision.HIGHEST
MIB = 1 << 20


def call(body, outs, ins, mib, scratch=(), flops=0, moved=0, smem=(), unread=()):
    specs = [
        pl.BlockSpec(memory_space=pltpu.SMEM if at in smem else pl.ANY if at in unread else pltpu.VMEM)
        for at in range(len(ins))
    ]
    many = isinstance(outs, (list, tuple))
    out_specs = [pl.BlockSpec(memory_space=pltpu.VMEM)] * len(outs) if many else pl.BlockSpec(memory_space=pltpu.VMEM)
    return pl.pallas_call(
        body,
        out_shape=outs,
        in_specs=specs,
        out_specs=out_specs,
        scratch_shapes=list(scratch),
        compiler_params=pltpu.CompilerParams(vmem_limit_bytes=mib * MIB),
        cost_estimate=pl.CostEstimate(flops=flops, bytes_accessed=moved, transcendentals=0),
    )(*ins)


def shape(*dims, dtype=F32):
    return jax.ShapeDtypeStruct(dims, dtype)


def two_parts(value):
    high = value.astype(BF16)
    low = (value - high.astype(F32)).astype(BF16)
    return high, low


def product(left_high, left_low, right):
    high, low = two_parts(right)
    total = jnp.dot(left_high, high, preferred_element_type=F32)
    total = total + jnp.dot(left_high, low, preferred_element_type=F32)
    return total + jnp.dot(left_low, high, preferred_element_type=F32)


def pack_kernel(inc_ref, rate_ref, west_ref, east_ref, sent_ref):
    block = pl.program_id(0)
    flat = inc_ref.reshape(PART * COLS, LANES)
    for c in range(COLS):
        column = flat[pl.ds(c, PART, stride=COLS), :]
        if c < STEPS:
            west_ref[c] = column
        if c >= COLS - STEPS:
            east_ref[c - COLS + STEPS] = column

    sent_ref[...] = jnp.zeros((8, LANES), F32)

    @pl.when(block == pl.num_programs(0) - 1)
    def _():
        last = ROWS % PART
        for c in range(COLS):
            rates = jnp.concatenate([rate_ref[i, c : c + 1, :] for i in range(4)] + [jnp.zeros((1, LANES), F32)], 0)
            if c < STEPS:
                west_ref[c, last:, :] = rates
            if c >= COLS - STEPS:
                east_ref[c - COLS + STEPS, last:, :] = rates


def pack(state, rates):
    halo = shape(STEPS, PAD, LANES)
    field = PAD * COLS * LANES * 4
    return pl.pallas_call(
        pack_kernel,
        grid=(PAD // PART,),
        out_shape=[halo, halo, shape(8, LANES)],
        in_specs=[
            pl.BlockSpec((PART, COLS, LANES), lambda i: (i, 0, 0)),
            pl.BlockSpec((4, COLS, LANES), lambda i: (0, 0, 0)),
        ],
        out_specs=[pl.BlockSpec((STEPS, PART, LANES), lambda i: (0, i, 0))] * 2
        + [pl.BlockSpec((8, LANES), lambda i: (0, 0))],
        compiler_params=pltpu.CompilerParams(vmem_limit_bytes=8 * MIB),
        cost_estimate=pl.CostEstimate(flops=0, bytes_accessed=3 * field, transcendentals=0),
    )(state, rates)


def prepare_kernel(inc_ref, forcing_ref, root_ref, physics_ref, base_ref, high_ref, low_ref, square, drive):
    square[...] = jnp.zeros((PAD, PAD), F32)
    square[:ROWS, :ROWS] = root_ref[...]
    root_high, root_low = two_parts(square[...])
    flat = forcing_ref.reshape(ROWS * COLS, LANES)
    start = inc_ref.reshape(ROWS * COLS, LANES)
    drive[ROWS - 3 :, :] = jnp.zeros((PAD - ROWS + 3, 2 * LANES), F32)
    for c in range(0, COLS, 2):
        drive[:ROWS, :LANES] = flat[pl.ds(c, ROWS, stride=COLS), :]
        drive[:ROWS, LANES:] = flat[pl.ds(c + 1, ROWS, stride=COLS), :]
        forced = product(root_high, root_low, drive[...])
        for k in range(2):
            column = forced[:, k * LANES : (k + 1) * LANES]
            base_ref[c + k, :ROWS, :] = start[pl.ds(c + k, ROWS, stride=COLS), :] - column[:ROWS]
            base_ref[c + k, ROWS:, :] = column[ROWS:]
    square[:ROWS, :ROWS] = 0.2 * physics_ref[...]
    once = square[...]
    twice = 2.0 * once + jnp.dot(once, once, precision=HIGHEST, preferred_element_type=F32)
    four = 2.0 * twice + jnp.dot(twice, twice, precision=HIGHEST, preferred_element_type=F32)
    six = twice + four + jnp.dot(twice, four, precision=HIGHEST, preferred_element_type=F32)
    high, low = two_parts(six)
    high_ref[...] = high
    low_ref[...] = low


def transport_kernel(inc_ref, rate_ref, west_ref, east_ref, order_ref, out_ref, table, own, odd, even):
    lane = lax.broadcasted_iota(jnp.int32, (1, LANES), 1)
    wide = COLS + 2 * STEPS
    for j in range(1, wide - 1):
        if j < STEPS:
            rates = [west_ref[j, ROWS + i : ROWS + i + 1, :] for i in range(4)]
        elif j < STEPS + COLS:
            rates = [rate_ref[i, j - STEPS : j - STEPS + 1, :] for i in range(4)]
        else:
            rates = [east_ref[j - STEPS - COLS, ROWS + i : ROWS + i + 1, :] for i in range(4)]
        center = 1.0 - (rates[0] + rates[1] + rates[2] + rates[3])
        north = jnp.where(lane == LANES - 1, 0.0, rates[2])
        south = jnp.where(lane == 0, 0.0, rates[3])
        for i, value in enumerate((center, rates[0], rates[1], north, south)):
            table[5 * j + i] = jnp.broadcast_to(value, (8, LANES))
    flat = inc_ref.reshape(ROWS * COLS, LANES)
    for c in range(COLS):
        own[c, :ROWS, :] = flat[pl.ds(c, ROWS, stride=COLS), :]
        own[c, ROWS:, :] = jnp.zeros((PAD - ROWS, LANES), F32)

    def block(index, carry):
        here = pl.ds(pl.multiple_of(index * PART, 8), PART)

        def load(step, j):
            if step > 0:
                value = (odd if step % 2 else even)[j]
            elif j < STEPS:
                value = west_ref[j, here, :]
            elif j < STEPS + COLS:
                value = own[j - STEPS, here, :]
            else:
                value = east_ref[j - STEPS - COLS, here, :]
            return value.reshape(PART // 8, 8, LANES)

        for step in range(1, STEPS + 1):
            for j in range(step, wide - step):
                v = load(step - 1, j)
                total = table[5 * j] * v
                total = total + table[5 * j + 1] * load(step - 1, j + 1)
                total = total + table[5 * j + 2] * load(step - 1, j - 1)
                total = total + table[5 * j + 3] * pltpu.roll(v, LANES - 1, 2)
                total = total + table[5 * j + 4] * pltpu.roll(v, 1, 2)
                total = total.reshape(PART, LANES)
                if step == STEPS:
                    out_ref[j - STEPS, here, :] = total
                else:
                    (odd if step % 2 else even)[j] = total
        return carry

    lax.fori_loop(0, PAD // PART, block, 0)


def mix_kernel(core_ref, state_ref, high_ref, low_ref, base_ref, order_ref, end_ref, keep_ref, send_ref):
    core = core_ref[0]
    for kind, out_ref in ((1, send_ref), (0, keep_ref)):
        start = 4 * (core ^ kind)
        for i in (0, 2):
            c = start + i
            state = jnp.concatenate([state_ref[c], state_ref[c + 1]], 1)
            end = state + product(high_ref[...], low_ref[...], state)
            for k in range(2):
                column = end[:, k * LANES : (k + 1) * LANES]
                end_ref[c + k] = column
                rest = base_ref[c + k] - column
                for q in range(4):
                    out_ref[4 * (i + k) + q] = rest[q * PART : (q + 1) * PART]


def scan_kernel(in_ref, order_ref, out_ref):
    def block(index, carry):
        here = pl.ds(pl.multiple_of(index * 8, 8), 8)
        total = jnp.zeros((8, LANES), F32)
        for k in range(PARTS):
            out_ref[k, here, :] = total
            total = total + in_ref[k, here, :]
        return carry

    lax.fori_loop(0, PART // 8, block, 0)


def share_kernel(core_ref, before_ref, keep_ref, order_ref, out_ref):
    first = (core_ref[0] == 0).astype(F32)
    out_ref[...] = before_ref[...] + first * keep_ref[...]


def finish_kernel(core_ref, base_ref, before_ref, partner_ref, other_ref, out_ref):
    core = core_ref[0]
    flat = out_ref.reshape(ROWS * COLS, LANES)
    second = (core == 1).astype(F32)
    for c in range(COLS):
        mine = core == c // 4
        i = c % 4
        for q in range(4):
            size = min(PART, ROWS - q * PART)
            own = before_ref[4 * i + q, :size] + second * partner_ref[4 * i + q, :size]
            earlier = jnp.where(mine, own, other_ref[4 * i + q, :size])
            flat[pl.ds(q * PART * COLS + c, size, stride=COLS), :] = (
                base_ref[c, q * PART : q * PART + size, :] + earlier
            )


def slot_places(column_x, me):
    tile = column_x >> 3
    relative = (tile - me + TILES) & (TILES - 1)
    bucket = lax.broadcasted_iota(jnp.int32, (TILES, SLOTS), 0)
    chosen = (bucket == relative).astype(F32)
    earlier = lax.broadcasted_iota(jnp.int32, (SLOTS, SLOTS), 0) < lax.broadcasted_iota(jnp.int32, (SLOTS, SLOTS), 1)
    rank = jnp.dot(chosen.astype(BF16), earlier.astype(F32).astype(BF16), preferred_element_type=F32)
    place = jnp.sum(chosen * rank, axis=0, keepdims=True)
    return chosen, place


def sort_kernel(me_ref, index_ref, frac_ref, sent_ref, out_ref, chosen_ref, spread_ref):
    column_x = index_ref[0:1, :]
    chosen, place = slot_places(column_x, me_ref[0])
    spread = lax.broadcasted_iota(jnp.int32, (CAP, SLOTS), 0) == place.astype(jnp.int32)
    spread = spread.astype(F32)
    chosen_ref[...] = chosen
    spread_ref[...] = spread
    values = jnp.concatenate(
        [
            (column_x & (COLS - 1)).astype(F32),
            index_ref[1:2, :].astype(F32),
            index_ref[2:3, :].astype(F32),
            frac_ref[0:1, :],
            frac_ref[1:2, :],
            jnp.zeros((FIELDS - 5, SLOTS), F32),
        ],
        0,
    )
    for j in range(TILES):
        masked = values * chosen[j : j + 1, :]
        out_ref[j] = lax.dot_general(
            masked, spread, (((1,), (1,)), ((), ())), precision=HIGHEST, preferred_element_type=F32
        )


def observe_kernel(obs_ref, end_ref, order_ref, out_ref, end_high, end_low):
    for c in range(COLS):
        high, low = two_parts(end_ref[c])
        end_high[:, c * LANES : (c + 1) * LANES] = high
        end_low[:, c * LANES : (c + 1) * LANES] = low
    lanes = 2 * CAP
    for j in range(0, TILES, 2):
        fields = [jnp.concatenate([obs_ref[j, i : i + 1], obs_ref[j + 1, i : i + 1]], 1) for i in range(5)]
        column, line, row = [(f + 0.5).astype(jnp.int32) for f in fields[:3]]
        across, upward = fields[3:]
        y = lax.broadcasted_iota(jnp.int32, (LANES, lanes), 0)
        here, after = y == line, y == line + 1
        highs, lows = [], []
        for c in range(COLS):
            mine = column == c
            near = jnp.where(mine, 1.0 - across, 0.0)
            far = jnp.where(mine, across, 0.0)
            weight = jnp.where(here, near, jnp.where(after, far, 0.0))
            high, low = two_parts(weight)
            highs.append(high)
            lows.append(low)
        high, low = jnp.concatenate(highs, 0), jnp.concatenate(lows, 0)
        taken = jnp.dot(end_high[...], high, preferred_element_type=F32)
        taken = taken + jnp.dot(end_high[...], low, preferred_element_type=F32)
        taken = taken + jnp.dot(end_low[...], high, preferred_element_type=F32)
        r = lax.broadcasted_iota(jnp.int32, (PAD, lanes), 0)
        weight = jnp.where(r == row, 1.0 - upward, jnp.where(r == row + 1, upward, 0.0))
        value = jnp.sum(weight * taken, axis=0, keepdims=True)
        out_ref[j : j + 1, :] = value[:, :CAP]
        out_ref[j + 1 : j + 2, :] = value[:, CAP:]


def depart_kernel(count_ref, back_ref, chosen_ref, spread_ref, value_ref, out_ref):
    spread = jnp.dot(back_ref[...], spread_ref[...], precision=HIGHEST, preferred_element_type=F32)
    evolved = jnp.sum(spread * chosen_ref[...], axis=0, keepdims=True)
    live = lax.broadcasted_iota(jnp.int32, (1, SLOTS), 1) < count_ref[0, 0]
    out_ref[...] = jnp.where(live, value_ref[...] - evolved, 0.0)


def hop(blocks, bit, sign):
    moving = [j for j in range(TILES) if j & bit]
    parcel = jnp.concatenate([blocks[j] for j in moving], 0)
    parcel = lax.ppermute(parcel, "tile", [(i, (i + sign * bit) % TILES) for i in range(TILES)])
    size = blocks[0].shape[0]
    result = list(blocks)
    for at, j in enumerate(moving):
        result[j] = parcel[at * size : (at + 1) * size]
    return result


def per_device(
    increment, forcing, error_root, physics, coefficients, obs_index, obs_frac, obs_value, obs_count
):
    state = increment.reshape(ROWS, COLS, LANES)
    drive = forcing.reshape(ROWS, COLS, LANES)
    rates = coefficients.reshape(4, COLS, LANES)
    core = jnp.reshape(lax.axis_index("core"), (1,)).astype(jnp.int32)
    me = jnp.reshape(lax.axis_index("tile"), (1,)).astype(jnp.int32)
    field = PAD * COLS * LANES * 4

    west, east, sent = pack(state, rates)
    from_east = lax.ppermute(west, "tile", [(i + 1, i) for i in range(TILES - 1)])
    from_west = lax.ppermute(east, "tile", [(i, i + 1) for i in range(TILES - 1)])

    places = obs_index.reshape(3, SLOTS)
    sorted_obs, chosen, spread = call(
        sort_kernel,
        [shape(TILES, FIELDS, CAP), shape(TILES, SLOTS), shape(CAP, SLOTS)],
        (me, places, obs_frac.reshape(2, SLOTS), sent),
        16,
        flops=10**8,
        moved=10**6,
        smem=(0,),
    )
    blocks = hop([sorted_obs[j] for j in range(TILES)], 4, 1)

    base, high, low = call(
        prepare_kernel,
        [shape(COLS, PAD, LANES), shape(PAD, PAD, dtype=BF16), shape(PAD, PAD, dtype=BF16)],
        (state, drive, error_root, physics.reshape(ROWS, ROWS)),
        16,
        scratch=[pltpu.VMEM((PAD, PAD), F32), pltpu.VMEM((PAD, 2 * LANES), F32)],
        flops=8 * 10**9,
        moved=5 * field,
    )

    wide = COLS + 2 * STEPS
    moved = call(
        transport_kernel,
        shape(COLS, PAD, LANES),
        (state, rates, from_west, from_east, blocks[7]),
        16,
        scratch=[
            pltpu.VMEM((5 * wide, 8, LANES), F32),
            pltpu.VMEM((COLS, PAD, LANES), F32),
            pltpu.VMEM((wide, PART, LANES), F32),
            pltpu.VMEM((wide, PART, LANES), F32),
        ],
        flops=4 * 10**9,
        moved=5 * field,
    )
    blocks = hop(blocks, 2, 1)
    parts = shape(PARTS, PART, LANES)
    end, keep, send = call(
        mix_kernel,
        [shape(COLS, PAD, LANES), parts, parts],
        (core, moved, high, low, base, blocks[7]),
        16,
        flops=2 * 10**9,
        moved=5 * field,
        smem=(0,),
    )
    swap = [(0, 1), (1, 0)]
    partner = lax.ppermute(send, "core", swap)
    blocks = hop(blocks, 1, 1)
    pair = keep + partner
    gathered = lax.all_to_all(pair, ("y", "x"), 0, 0, tiled=True)
    found = call(
        observe_kernel,
        shape(TILES, CAP),
        (jnp.stack(blocks, 0), end, pair),
        16,
        scratch=[pltpu.VMEM((PAD, COLS * LANES), BF16), pltpu.VMEM((PAD, COLS * LANES), BF16)],
        flops=3 * 10**9,
        moved=field,
        unread=(2,),
    )
    back = hop([found[j : j + 1] for j in range(TILES)], 4, -1)
    totals = call(scan_kernel, parts, (gathered, found), 8, flops=10**7, moved=field)
    before = lax.all_to_all(totals, ("y", "x"), 0, 0, tiled=True)
    back = hop(hop(back, 2, -1), 1, -1)
    departure = call(
        depart_kernel,
        shape(1, SLOTS),
        (obs_count, jnp.concatenate(back, 0), chosen, spread, obs_value),
        8,
        flops=10**7,
        moved=10**6,
        smem=(0,),
    )
    for_partner = call(
        share_kernel, parts, (core, before, keep, departure), 8, flops=10**7, moved=2 * field, smem=(0,)
    )
    other = lax.ppermute(for_partner, "core", swap)
    summed = call(
        finish_kernel,
        shape(ROWS, COLS, LANES),
        (core, base, before, partner, other),
        16,
        flops=10**7,
        moved=4 * field,
        smem=(0,),
    )
    return summed.reshape(increment.shape), departure


def solution(mesh):
    split = Mesh(mesh.devices.reshape(GRID_Y, GRID_X, CORES, TILES), ("y", "x", "core", "tile"))
    win = ("y", "x", "core")
    return jax.shard_map(
        per_device,
        mesh=split,
        in_specs=(
            P(win, None, None, "tile", None),
            P(win, None, None, "tile", None),
            P(),
            P(win, None, None),
            P(win, None, "tile", None),
            P(None, win, "tile"),
            P(None, win, "tile"),
            P(win, "tile"),
            P(win, "tile"),
        ),
        out_specs=(P(win, None, None, "tile", None), P(win, "tile")),
        check_vma=False,
    )
```

time: 503 us -> 125 us (0.25); the launches traced: 493 us -> 124 us
  waiting for transfers between devices: 182 us -> 37.2 us
  local copies, waits for them, and re-layouts: 116 us -> 11.6 us
  other arithmetic: 79.2 us -> 1.03 us
  Pallas kernels: 0 us -> 31.8 us
  matrix products: 25.2 us -> 0 us
  blocking collectives: 22.8 us -> 0 us
  between operations: 17 us -> 1.56 us
  starting transfers between devices: 50.6 us -> 40.7 us
    all_gather x1 -> x0, waiting for transfers between devices: 137 us -> none  [entering(): pieces = lax.all_gather(value, axis)]
    gather x4 -> x0, local copies, waits for them, and re-layouts: 92.1 us -> none  [the longest x1 23 us: corner_values(): flat_state[anchor + 1]]
    select_n x35 -> x0, other arithmetic: 64 us -> none  [the longest x31 63.2 us: step(): return jnp.where(position < mine, longer, subtotal)]
    unnamed x3 -> x0, waiting for transfers between devices: 35 us -> none
    pallas_call x0 -> x10, Pallas kernels: none -> 31.8 us  [the longest x9 29.7 us: call(): pl.pallas_call(body, out_shape=outs, in_specs=specs, out_specs=out_specs,...]
    dot_general x7 -> x0, matrix products: 25.2 us -> none  [the longest x6 19.1 us: tl_update(): jnp.dot(jacobian, flat_state, precision=lax.Precision.HIGHEST, preferred_...]
    all_gather x1 -> x0, blocking collectives: 22.8 us -> none  [per_device(): all_places = lax.all_gather(own_places, 'tile', axis=1, tiled=True)]
    ppermute x13 -> x10, waiting for transfers between devices: 9.76 us -> 31.2 us  [the longest x6 27.2 us: hop(): lax.ppermute(parcel, 'tile', [(i, (i + sign * bit) % TILES) for i in rang...]
  transfers between devices with their start and end apart: 15 -> 12, of which waited for: 10 -> 8; matrix products, arithmetic and copies ran while one was open for 23% -> 1% of each run, Pallas kernels for 0% -> 9%
where the time goes in v1:
time: 125 us; the launch traced here: 124 us
  starting transfers between devices  40.7 us (33%)
  waiting for transfers between devices  37.2 us (30%)
  Pallas kernels  31.8 us (25%)
  local copies, waits for them, and re-layouts  11.6 us (9%)
  between operations  1.56 us (1%)
    pallas_call x9, Pallas kernels, call(): pl.pallas_call(body, out_shape=outs, in_specs=specs, out_specs=out_specs,...  29.7 us
    ppermute x6, waiting for transfers between devices, hop(): lax.ppermute(parcel, 'tile', [(i, (i + sign * bit) % TILES) for i in rang...  27.2 us
    ppermute x6, starting transfers between devices, hop(): lax.ppermute(parcel, 'tile', [(i, (i + sign * bit) % TILES) for i in rang...  19.3 us
    unnamed x45, local copies, waits for them, and re-layouts  11.5 us
    all_to_all x1, starting transfers between devices, per_device(): gathered = lax.all_to_all(pair, ('y', 'x'), 0, 0, tiled=True)  6.77 us
    all_to_all x1, starting transfers between devices, per_device(): before = lax.all_to_all(totals, ('y', 'x'), 0, 0, tiled=True)  4 us
    ppermute x1, starting transfers between devices, per_device(): lax.ppermute(east, 'tile', [(i, i + 1) for i in range(TILES - 1)])  3.7 us
    all_to_all x1, waiting for transfers between devices, per_device(): before = lax.all_to_all(totals, ('y', 'x'), 0, 0, tiled=True)  3.66 us
  transfers between devices with their start and end apart: 12, of which 8 were waited for; matrix products, arithmetic and copies ran while one was open for 1% of the time, Pallas kernels for 9%

profile of v1, /device:TPU:1, one launch (start us, length us, event | category | flops | bytes accessed | tf_op | source)
XLA Modules:
  0.0 123.9 jit_solution(12230229779056180069)
XLA Ops:
  2.0 1.4 %copy-done.2 = f32[1,3,137,8,128]{4,3,2,1,0:T(8,128)S(1)} copy-done((f32[1,3,137,8,128]{4,3,2,1,0:T(8,128)S(1)}, f32[1,3,137,8,128]{4,3,2,1,0:T(8,128)}, u32[]{:S(2)}) %copy-start.2) | copy-done | bytes 1683480
  4.2 2.1 %shard_map.105 = (f32[6,416,128]{2,1,0:T(8,128)}, f32[6,416,128]{2,1,0:T(8,128)}, f32[8,128]{1,0:T(8,128)S(1)}) custom-call(f32[411,8,128]{2,1,0:T(8,128)S(1)} %bitcast.57, f32[4,8,128]{2,1,0:T(8,128)S(1)} %bitcast.61), custom_call_target="tpu_custom_call" | custom-call | bytes 5111808 | tf_op jit(solution)/shard_map/pallas_call | solution.py:90
  6.3 1.9 %shard_map.106 = (f32[8,8,128]{2,1,0:T(8,128)S(1)}, f32[8,512]{1,0:T(8,128)S(1)}, f32[128,512]{1,0:T(8,128)S(1)}) custom-call(s32[1]{0:T(128)} %bitcast.4.me_ref, s32[3,512]{1,0:T(4,128)S(1)} %bitcast.63, f32[2,512]{1,0:T(2,128)S(1)} %bitcast.64, f32[8,128]{1,0:T(8,128)S(1)} %get-tuple-element.17.sent_ref), custom_call_target="tpu_custom_call" | custom-call | flops 100000000 | bytes 1000000 | tf_op jit(solution)/shard_map/pallas_call | solution.py:36
  8.9 7.8 %collective-permute-start.2 = (f32[32,128]{1,0:T(8,128)S(1)}, f32[32,128]{1,0:T(8,128)S(1)}, u32[]{:S(2)}, u32[]{:S(2)}) collective-permute-start(f32[32,128]{1,0:T(8,128)S(1)} %pad_maximum_fusion), channel_id=1, source_target_pairs={{0,4},{1,5},{2,6},{3,7},{4,0},{5,1},{6,2},{7,3},{8,12},{9,13},{10,... | collective-permute-start | bytes 49160 | tf_op jit(solution)/shard_map/ppermute | solution.py:309
  16.7 3.7 %collective-permute-start = (f32[6,416,128]{2,1,0:T(8,128)}, f32[6,416,128]{2,1,0:T(8,128)}, u32[]{:S(2)}, u32[]{:S(2)}) collective-permute-start(f32[6,416,128]{2,1,0:T(8,128)} %get-tuple-element.15), channel_id=1, source_target_pairs={{0,1},{1,2},{2,3},{3,4},{4,5},{5,6},{6,7},{8,9},{9,10},{10,11},{11... | collective-permute-start | bytes 3833864 | tf_op jit(solution)/shard_map/ppermute | solution.py:329
  20.4 1.3 %collective-permute-start.1 = (f32[6,416,128]{2,1,0:T(8,128)}, f32[6,416,128]{2,1,0:T(8,128)}, u32[]{:S(2)}, u32[]{:S(2)}) collective-permute-start(f32[6,416,128]{2,1,0:T(8,128)} %get-tuple-element.16), channel_id=1, source_target_pairs={{1,0},{2,1},{3,2},{4,3},{5,4},{6,5},{7,6},{9,8},{10,9},{11,10},{12... | collective-permute-start | bytes 3833864 | tf_op jit(solution)/shard_map/ppermute | solution.py:328
  21.7 1.2 copy.17
  23.0 1.6 %collective-permute-start.3 = (f32[32,128]{1,0:T(8,128)S(1)}, f32[32,128]{1,0:T(8,128)S(1)}, u32[]{:S(2)}, u32[]{:S(2)}) collective-permute-start(f32[32,128]{1,0:T(8,128)S(1)} %pad_maximum_fusion.1), channel_id=1, source_target_pairs={{0,2},{1,3},{2,4},{3,5},{4,6},{5,7},{6,0},{7,1},{8,10},{9,11},{10,... | collective-permute-start | bytes 49160 | tf_op jit(solution)/shard_map/ppermute | solution.py:309
  24.5 22.7 %collective-permute-done.3 = f32[32,128]{1,0:T(8,128)S(1)} collective-permute-done((f32[32,128]{1,0:T(8,128)S(1)}, f32[32,128]{1,0:T(8,128)S(1)}, u32[]{:S(2)}, u32[]{:S(2)}) %collective-permute-start.3) | collective-permute-done | bytes 16416 | tf_op jit(solution)/shard_map/ppermute | solution.py:309
  47.3 1.1 copy-done.11
  48.4 6.3 %shard_map.104 = (f32[8,416,128]{2,1,0:T(8,128)S(1)}, bf16[416,416]{1,0:T(8,128)(2,1)S(1)}, bf16[416,416]{1,0:T(8,128)(2,1)S(1)}) custom-call(f32[411,8,128]{2,1,0:T(8,128)S(1)} %bitcast.58, f32[411,8,128]{2,1,0:T(8,128)S(1)} %bitcast.65, f32[411,411]{1,0:T(8,128)S(1)} %copy-done.11, f32[411,411]{1,0:T(8,128)S(1)} %bitcast.60), custom_call_target="tpu_custom_call" | custom-call | flops 8000000000 | bytes 8519680 | tf_op jit(solution)/shard_map/pallas_call | solution.py:36
  56.4 12.4 %shard_map.107.state_ref = f32[8,416,128]{2,1,0:T(8,128)S(1)} custom-call(f32[411,8,128]{2,1,0:T(8,128)S(1)} %bitcast.59, f32[4,8,128]{2,1,0:T(8,128)S(1)} %bitcast.62, f32[6,416,128]{2,1,0:T(8,128)} %collective-permute-done.west_ref, f32[6,416,128]{2,1,0:T(8,128)} %collective-permute-done.1.east_ref, f32[8,128]{1,0:T(8,128)S(1)} %get-tuple-element.37.order_ref), custom_call_target="tpu_custom_call" | custom-call | flops 4000000000 | bytes 8519680 | tf_op jit(solution)/shard_map/pallas_call | solution.py:36
  68.8 1.6 %shard_map.108 = (f32[8,416,128]{2,1,0:T(8,128)S(1)}, f32[16,104,128]{2,1,0:T(8,128)S(1)}, f32[16,104,128]{2,1,0:T(8,128)S(1)}) custom-call(s32[1]{0:T(128)} %bitcast.core_ref, f32[8,416,128]{2,1,0:T(8,128)S(1)} %shard_map.107.state_ref, bf16[416,416]{1,0:T(8,128)(2,1)S(1)} %copy-done.15, bf16[416,416]{1,0:T(8,128)(2,1)S(1)} %copy-done.17, ...), custom_call_target="tpu_custom_call" | custom-call | flops 2000000000 | bytes 8519680 | tf_op jit(solution)/shard_map/pallas_call | solution.py:36
  70.4 1.2 copy-done.12
  71.6 2.3 %collective-permute-start.4 = (f32[16,104,128]{2,1,0:T(8,128)S(1)}, f32[16,104,128]{2,1,0:T(8,128)S(1)}, u32[]{:S(2)}, u32[]{:S(2)}) collective-permute-start(f32[16,104,128]{2,1,0:T(8,128)S(1)} %get-tuple-element.22), channel_id=1, source_target_pairs={{0,8},{8,0},{1,9},{9,1},{2,10},{10,2},{3,11},{11,3},{4,12},{12,4},... | collective-permute-start | bytes 2555912 | tf_op jit(solution)/shard_map/ppermute | solution.py:380
  74.0 2.0 %collective-permute-done.4.partner_ref = f32[16,104,128]{2,1,0:T(8,128)S(1)} collective-permute-done((f32[16,104,128]{2,1,0:T(8,128)S(1)}, f32[16,104,128]{2,1,0:T(8,128)S(1)}, u32[]{:S(2)}, u32[]{:S(2)}) %collective-permute-start.4) | collective-permute-done | bytes 852000 | tf_op jit(solution)/shard_map/ppermute | solution.py:380
  75.9 1.0 add.3.order_ref
  76.9 6.8 %all-to-all-start = ((f32[16,104,128]{2,1,0:T(8,128)}), f32[16,104,128]{2,1,0:T(8,128)S(1)}, u32[]{:S(2)}, u32[]{:S(2)}) async-start(f32[16,104,128]{2,1,0:T(8,128)} %add.3.order_ref), calls=%async_computation | async-start | bytes 1703936 | tf_op jit(solution)/shard_map/all_to_all | solution.py:383
  83.7 1.4 %copy-done.13 = f32[8,416,128]{2,1,0:T(8,128)S(1)} copy-done((f32[8,416,128]{2,1,0:T(8,128)S(1)}, f32[8,416,128]{2,1,0:T(8,128)}, u32[]{:S(2)}) %copy-start.13) | copy-done | bytes 1703960
  85.2 3.6 %shard_map.109.order_ref = f32[8,128]{1,0:T(8,128)S(1)} custom-call(f32[8,8,128]{2,1,0:T(8,128)S(1)} %constant_dynamic-update-slice_fusion.obs_ref, f32[8,416,128]{2,1,0:T(8,128)S(1)} %copy-done.13, f32[16,104,128]{2,1,0:T(8,128)} %add.3.order_ref), custom_call_target="tpu_custom_call" | custom-call | flops 3000000000 | bytes 1703936 | tf_op jit(solution)/shard_map/pallas_call | solution.py:36
  88.8 4.6 %collective-permute-start.6 = (f32[4,128]{1,0:T(4,128)S(1)}, f32[4,128]{1,0:T(4,128)S(1)}, u32[]{:S(2)}, u32[]{:S(2)}) collective-permute-start(f32[4,128]{1,0:T(4,128)S(1)} %slice.137), channel_id=1, source_target_pairs={{0,4},{1,5},{2,6},{3,7},{4,0},{5,1},{6,2},{7,3},{8,12},{9,13},{10,... | collective-permute-start | bytes 6152 | tf_op jit(solution)/shard_map/ppermute | solution.py:309
  93.4 2.2 %collective-permute-done.6 = f32[4,128]{1,0:T(4,128)S(1)} collective-permute-done((f32[4,128]{1,0:T(4,128)S(1)}, f32[4,128]{1,0:T(4,128)S(1)}, u32[]{:S(2)}, u32[]{:S(2)}) %collective-permute-start.6) | collective-permute-done | bytes 2080 | tf_op jit(solution)/shard_map/ppermute | solution.py:309
  95.6 2.4 %all-to-all-done.in_ref = f32[16,104,128]{2,1,0:T(8,128)S(1)} async-done(((f32[16,104,128]{2,1,0:T(8,128)}), f32[16,104,128]{2,1,0:T(8,128)S(1)}, u32[]{:S(2)}, u32[]{:S(2)}) %all-to-all-start) | async-done | bytes 852000 | tf_op jit(solution)/shard_map/all_to_all | solution.py:383
  97.9 1.1 shard_map.110
  99.0 4.0 %all-to-all-start.1 = ((f32[16,104,128]{2,1,0:T(8,128)}), f32[16,104,128]{2,1,0:T(8,128)S(1)}, u32[]{:S(2)}, u32[]{:S(2)}) async-start(f32[16,104,128]{2,1,0:T(8,128)} %shard_map.110), calls=%async_computation.1 | async-start | bytes 1703936 | tf_op jit(solution)/shard_map/all_to_all | solution.py:396
  103.1 1.7 %collective-permute-start.7 = (f32[4,128]{1,0:T(4,128)S(1)}, f32[4,128]{1,0:T(4,128)S(1)}, u32[]{:S(2)}, u32[]{:S(2)}) collective-permute-start(f32[4,128]{1,0:T(4,128)S(1)} %pad_maximum_fusion.3), channel_id=1, source_target_pairs={{0,6},{1,7},{2,0},{3,1},{4,2},{5,3},{6,4},{7,5},{8,14},{9,15},{10,... | collective-permute-start | bytes 6152 | tf_op jit(solution)/shard_map/ppermute | solution.py:309
  104.8 2.3 %collective-permute-done.7 = f32[4,128]{1,0:T(4,128)S(1)} collective-permute-done((f32[4,128]{1,0:T(4,128)S(1)}, f32[4,128]{1,0:T(4,128)S(1)}, u32[]{:S(2)}, u32[]{:S(2)}) %collective-permute-start.7) | collective-permute-done | bytes 2080 | tf_op jit(solution)/shard_map/ppermute | solution.py:309
  107.0 3.7 %collective-permute-start.8 = (f32[4,128]{1,0:T(4,128)S(1)}, f32[4,128]{1,0:T(4,128)S(1)}, u32[]{:S(2)}, u32[]{:S(2)}) collective-permute-start(f32[4,128]{1,0:T(4,128)S(1)} %pad_maximum_fusion.4), channel_id=1, source_target_pairs={{0,7},{1,0},{2,1},{3,2},{4,3},{5,4},{6,5},{7,6},{8,15},{9,8},{10,9... | collective-permute-start | bytes 6152 | tf_op jit(solution)/shard_map/ppermute | solution.py:309
  112.3 3.7 %all-to-all-done.1.before_ref = f32[16,104,128]{2,1,0:T(8,128)S(1)} async-done(((f32[16,104,128]{2,1,0:T(8,128)}), f32[16,104,128]{2,1,0:T(8,128)S(1)}, u32[]{:S(2)}, u32[]{:S(2)}) %all-to-all-start.1) | async-done | bytes 852000 | tf_op jit(solution)/shard_map/all_to_all | solution.py:396
  116.8 3.3 %collective-permute-start.9 = (f32[16,104,128]{2,1,0:T(8,128)S(1)}, f32[16,104,128]{2,1,0:T(8,128)S(1)}, u32[]{:S(2)}, u32[]{:S(2)}) collective-permute-start(f32[16,104,128]{2,1,0:T(8,128)S(1)} %shard_map.112), channel_id=1, source_target_pairs={{0,8},{8,0},{1,9},{9,1},{2,10},{10,2},{3,11},{11,3},{4,12},{12,4},... | collective-permute-start | bytes 2555912 | tf_op jit(solution)/shard_map/ppermute | solution.py:410
  120.1 2.0 %collective-permute-done.9.other_ref = f32[16,104,128]{2,1,0:T(8,128)S(1)} collective-permute-done((f32[16,104,128]{2,1,0:T(8,128)S(1)}, f32[16,104,128]{2,1,0:T(8,128)S(1)}, u32[]{:S(2)}, u32[]{:S(2)}) %collective-permute-start.9) | collective-permute-done | bytes 852000 | tf_op jit(solution)/shard_map/ppermute | solution.py:410
  122.1 1.8 %shard_map.113 = f32[411,8,128]{2,1,0:T(8,128)} custom-call(s32[1]{0:T(128)} %bitcast.core_ref, f32[8,416,128]{2,1,0:T(8,128)S(1)} %copy-done.1, f32[16,104,128]{2,1,0:T(8,128)S(1)} %all-to-all-done.1.before_ref, f32[16,104,128]{2,1,0:T(8,128)S(1)} %collective-permute-done.4.partner_ref, f32[16,104,128]{2,1,0:T(8,128)S(1)} %collective-permute-done.9.other_ref), custom_call_target="tpu_custom_call" | custom-call | flops 10000000 | bytes 6815744 | tf_op jit(solution)/shard_map/pallas_call | solution.py:36
  (66 shorter events, 6.3 us)
Async XLA Ops:
  2.0 1.4 %copy-start.2 = (f32[1,3,137,8,128]{4,3,2,1,0:T(8,128)S(1)}, f32[1,3,137,8,128]{4,3,2,1,0:T(8,128)}, u32[]{:S(2)}) copy-start(f32[1,3,137,8,128]{4,3,2,1,0:T(8,128)} %param.9) | copy-start | bytes 5050372
  3.5 0.7 copy-start.6
  4.2 43.0 %copy-start.3 = (f32[1,3,137,8,128]{4,3,2,1,0:T(8,128)S(1)}, f32[1,3,137,8,128]{4,3,2,1,0:T(8,128)}, u32[]{:S(2)}) copy-start(f32[1,3,137,8,128]{4,3,2,1,0:T(8,128)} %param.9) | copy-start | bytes 5050372
  4.2 43.1 %copy-start.10 = (f32[1,3,137,8,128]{4,3,2,1,0:T(8,128)S(1)}, f32[1,3,137,8,128]{4,3,2,1,0:T(8,128)}, u32[]{:S(2)}) copy-start(f32[1,3,137,8,128]{4,3,2,1,0:T(8,128)} %param.10) | copy-start | bytes 5050372
  8.2 0.7 copy-start.4
  8.9 14.0 %collective-permute-start.2 = (f32[32,128]{1,0:T(8,128)S(1)}, f32[32,128]{1,0:T(8,128)S(1)}, u32[]{:S(2)}, u32[]{:S(2)}) collective-permute-start(f32[32,128]{1,0:T(8,128)S(1)} %pad_maximum_fusion), channel_id=1, source_target_pairs={{0,4},{1,5},{2,6},{3,7},{4,0},{5,1},{6,2},{7,3},{8,12},{9,13},{10,... | collective-permute-start | bytes 49160 | tf_op jit(solution)/shard_map/ppermute | solution.py:309
  16.7 39.6 %collective-permute-start = (f32[6,416,128]{2,1,0:T(8,128)}, f32[6,416,128]{2,1,0:T(8,128)}, u32[]{:S(2)}, u32[]{:S(2)}) collective-permute-start(f32[6,416,128]{2,1,0:T(8,128)} %get-tuple-element.15), channel_id=1, source_target_pairs={{0,1},{1,2},{2,3},{3,4},{4,5},{5,6},{6,7},{8,9},{9,10},{10,11},{11... | collective-permute-start | bytes 3833864 | tf_op jit(solution)/shard_map/ppermute | solution.py:329
  20.4 35.9 %collective-permute-start.1 = (f32[6,416,128]{2,1,0:T(8,128)}, f32[6,416,128]{2,1,0:T(8,128)}, u32[]{:S(2)}, u32[]{:S(2)}) collective-permute-start(f32[6,416,128]{2,1,0:T(8,128)} %get-tuple-element.16), channel_id=1, source_target_pairs={{1,0},{2,1},{3,2},{4,3},{5,4},{6,5},{7,6},{9,8},{10,9},{11,10},{12... | collective-permute-start | bytes 3833864 | tf_op jit(solution)/shard_map/ppermute | solution.py:328
  23.0 24.3 %collective-permute-start.3 = (f32[32,128]{1,0:T(8,128)S(1)}, f32[32,128]{1,0:T(8,128)S(1)}, u32[]{:S(2)}, u32[]{:S(2)}) collective-permute-start(f32[32,128]{1,0:T(8,128)S(1)} %pad_maximum_fusion.1), channel_id=1, source_target_pairs={{0,2},{1,3},{2,4},{3,5},{4,6},{5,7},{6,0},{7,1},{8,10},{9,11},{10,... | collective-permute-start | bytes 49160 | tf_op jit(solution)/shard_map/ppermute | solution.py:309
  47.2 9.1 %collective-permute-start.5 = (f32[32,128]{1,0:T(8,128)S(1)}, f32[32,128]{1,0:T(8,128)S(1)}, u32[]{:S(2)}, u32[]{:S(2)}) collective-permute-start(f32[32,128]{1,0:T(8,128)S(1)} %pad_maximum_fusion.2), channel_id=1, source_target_pairs={{0,1},{1,2},{2,3},{3,4},{4,5},{5,6},{6,7},{7,0},{8,9},{9,10},{10,1... | collective-permute-start | bytes 49160 | tf_op jit(solution)/shard_map/ppermute | solution.py:309
  47.2 1.2 copy-start.11
  48.4 7.9 %copy-start.7 = (f32[1,4,8,128]{3,2,1,0:T(8,128)S(1)}, f32[1,4,8,128]{3,2,1,0:T(8,128)}, u32[]{:S(2)}) copy-start(f32[1,4,8,128]{3,2,1,0:T(8,128)} %param.13) | copy-start | bytes 49156
  54.7 0.8 copy-start.14
  55.5 0.8 copy-start.16
  56.3 12.5 %copy-start = (f32[8,416,128]{2,1,0:T(8,128)}, f32[8,416,128]{2,1,0:T(8,128)S(1)}, u32[]{:S(2)}) copy-start(f32[8,416,128]{2,1,0:T(8,128)S(1)} %get-tuple-element.14.base_ref) | copy-start | bytes 5111812
  56.3 12.4 %copy-start.15 = (bf16[416,416]{1,0:T(8,128)(2,1)S(1)}, bf16[416,416]{1,0:T(8,128)(2,1)}, u32[]{:S(2)}) copy-start(bf16[416,416]{1,0:T(8,128)(2,1)} %copy-done.14) | copy-start | bytes 1038340
  56.3 12.4 %copy-start.17 = (bf16[416,416]{1,0:T(8,128)(2,1)S(1)}, bf16[416,416]{1,0:T(8,128)(2,1)}, u32[]{:S(2)}) copy-start(bf16[416,416]{1,0:T(8,128)(2,1)} %copy-done.16) | copy-start | bytes 1038340
  70.4 1.2 copy-start.12
  71.6 4.3 %collective-permute-start.4 = (f32[16,104,128]{2,1,0:T(8,128)S(1)}, f32[16,104,128]{2,1,0:T(8,128)S(1)}, u32[]{:S(2)}, u32[]{:S(2)}) collective-permute-start(f32[16,104,128]{2,1,0:T(8,128)S(1)} %get-tuple-element.22), channel_id=1, source_target_pairs={{0,8},{8,0},{1,9},{9,1},{2,10},{10,2},{3,11},{11,3},{4,12},{12,4},... | collective-permute-start | bytes 2555912 | tf_op jit(solution)/shard_map/ppermute | solution.py:380
  76.9 21.0 %all-to-all-start = ((f32[16,104,128]{2,1,0:T(8,128)}), f32[16,104,128]{2,1,0:T(8,128)S(1)}, u32[]{:S(2)}, u32[]{:S(2)}) async-start(f32[16,104,128]{2,1,0:T(8,128)} %add.3.order_ref), calls=%async_computation | async-start | bytes 1703936 | tf_op jit(solution)/shard_map/all_to_all | solution.py:383
  83.7 1.5 %copy-start.13 = (f32[8,416,128]{2,1,0:T(8,128)S(1)}, f32[8,416,128]{2,1,0:T(8,128)}, u32[]{:S(2)}) copy-start(f32[8,416,128]{2,1,0:T(8,128)} %copy-done.12) | copy-start | bytes 5111812
  88.8 6.7 %collective-permute-start.6 = (f32[4,128]{1,0:T(4,128)S(1)}, f32[4,128]{1,0:T(4,128)S(1)}, u32[]{:S(2)}, u32[]{:S(2)}) collective-permute-start(f32[4,128]{1,0:T(4,128)S(1)} %slice.137), channel_id=1, source_target_pairs={{0,4},{1,5},{2,6},{3,7},{4,0},{5,1},{6,2},{7,3},{8,12},{9,13},{10,... | collective-permute-start | bytes 6152 | tf_op jit(solution)/shard_map/ppermute | solution.py:309
  95.6 15.9 %copy-start.5 = (f32[128,512]{1,0:T(8,128)S(1)}, f32[128,512]{1,0:T(8,128)}, u32[]{:S(2)}) copy-start(f32[128,512]{1,0:T(8,128)} %copy-done.4) | copy-start | bytes 786436
  95.6 15.9 %copy-start.9 = (f32[1,512]{1,0:T(1,128)S(1)}, f32[1,512]{1,0:T(1,128)}, u32[]{:S(2)}) copy-start(f32[1,512]{1,0:T(1,128)} %value_ref.1) | copy-start | bytes 6148
  99.0 16.9 %all-to-all-start.1 = ((f32[16,104,128]{2,1,0:T(8,128)}), f32[16,104,128]{2,1,0:T(8,128)S(1)}, u32[]{:S(2)}, u32[]{:S(2)}) async-start(f32[16,104,128]{2,1,0:T(8,128)} %shard_map.110), calls=%async_computation.1 | async-start | bytes 1703936 | tf_op jit(solution)/shard_map/all_to_all | solution.py:396
  103.1 4.0 %collective-permute-start.7 = (f32[4,128]{1,0:T(4,128)S(1)}, f32[4,128]{1,0:T(4,128)S(1)}, u32[]{:S(2)}, u32[]{:S(2)}) collective-permute-start(f32[4,128]{1,0:T(4,128)S(1)} %pad_maximum_fusion.3), channel_id=1, source_target_pairs={{0,6},{1,7},{2,0},{3,1},{4,2},{5,3},{6,4},{7,5},{8,14},{9,15},{10,... | collective-permute-start | bytes 6152 | tf_op jit(solution)/shard_map/ppermute | solution.py:309
  107.0 4.4 %collective-permute-start.8 = (f32[4,128]{1,0:T(4,128)S(1)}, f32[4,128]{1,0:T(4,128)S(1)}, u32[]{:S(2)}, u32[]{:S(2)}) collective-permute-start(f32[4,128]{1,0:T(4,128)S(1)} %pad_maximum_fusion.4), channel_id=1, source_target_pairs={{0,7},{1,0},{2,1},{3,2},{4,3},{5,4},{6,5},{7,6},{8,15},{9,8},{10,9... | collective-permute-start | bytes 6152 | tf_op jit(solution)/shard_map/ppermute | solution.py:309
  116.0 0.7 copy-start.8
  116.7 5.4 %copy-start.1 = (f32[8,416,128]{2,1,0:T(8,128)S(1)}, f32[8,416,128]{2,1,0:T(8,128)}, u32[]{:S(2)}) copy-start(f32[8,416,128]{2,1,0:T(8,128)} %copy-done) | copy-start | bytes 5111812
  116.8 5.3 %collective-permute-start.9 = (f32[16,104,128]{2,1,0:T(8,128)S(1)}, f32[16,104,128]{2,1,0:T(8,128)S(1)}, u32[]{:S(2)}, u32[]{:S(2)}) collective-permute-start(f32[16,104,128]{2,1,0:T(8,128)S(1)} %shard_map.112), channel_id=1, source_target_pairs={{0,8},{8,0},{1,9},{9,1},{2,10},{10,2},{3,11},{11,3},{4,12},{12,4},... | collective-permute-start | bytes 2555912 | tf_op jit(solution)/shard_map/ppermute | solution.py:410

commit v2 on v1

--- a/solution.py
+++ b/solution.py
@@ -16,6 +16,7 @@
 PARTS = 16
 PART = 104
 TILES = 8
+CHUNKS = ((0, 208), (208, 104), (312, 104))
 SLOTS = 512
 CAP = 128
 FIELDS = 8
@@ -26,18 +27,17 @@
 MIB = 1 << 20
 
 
-def call(body, outs, ins, mib, scratch=(), flops=0, moved=0, smem=(), unread=()):
+def call(body, outs, ins, mib, scratch=(), flops=0, moved=0, smem=(), far=(), far_out=False):
     specs = [
-        pl.BlockSpec(memory_space=pltpu.SMEM if at in smem else pl.ANY if at in unread else pltpu.VMEM)
+        pl.BlockSpec(memory_space=pltpu.SMEM if at in smem else pl.ANY if at in far else pltpu.VMEM)
         for at in range(len(ins))
     ]
-    many = isinstance(outs, (list, tuple))
-    out_specs = [pl.BlockSpec(memory_space=pltpu.VMEM)] * len(outs) if many else pl.BlockSpec(memory_space=pltpu.VMEM)
+    out_spec = pl.BlockSpec(memory_space=pl.ANY if far_out else pltpu.VMEM)
     return pl.pallas_call(
         body,
         out_shape=outs,
         in_specs=specs,
-        out_specs=out_specs,
+        out_specs=[out_spec] * len(outs) if isinstance(outs, (list, tuple)) else out_spec,
         scratch_shapes=list(scratch),
         compiler_params=pltpu.CompilerParams(vmem_limit_bytes=mib * MIB),
         cost_estimate=pl.CostEstimate(flops=flops, bytes_accessed=moved, transcendentals=0),
@@ -61,45 +61,60 @@
     return total + jnp.dot(left_low, high, preferred_element_type=F32)
 
 
-def pack_kernel(inc_ref, rate_ref, west_ref, east_ref, sent_ref):
-    block = pl.program_id(0)
-    flat = inc_ref.reshape(PART * COLS, LANES)
-    for c in range(COLS):
-        column = flat[pl.ds(c, PART, stride=COLS), :]
-        if c < STEPS:
-            west_ref[c] = column
-        if c >= COLS - STEPS:
-            east_ref[c - COLS + STEPS] = column
-
-    sent_ref[...] = jnp.zeros((8, LANES), F32)
-
-    @pl.when(block == pl.num_programs(0) - 1)
-    def _():
-        last = ROWS % PART
+def pack_kernel(inc_ref, rate_ref, *refs):
+    count = len(CHUNKS)
+    wests, easts = refs[:count], refs[count : 2 * count]
+    held, rates = refs[2 * count : 2 * count + 2]
+    west_bufs = refs[2 * count + 2 : 3 * count + 2]
+    east_bufs = refs[3 * count + 2 : 4 * count + 2]
+    in_sems, out_sems = refs[4 * count + 2 :]
+    incoming = []
+    for at, (start, size) in enumerate(CHUNKS):
+        size = min(size, ROWS - start)
+        rows = pl.ds(start, size)
+        incoming.append(pltpu.make_async_copy(inc_ref.at[rows], held.at[rows], in_sems.at[at]))
+    incoming.append(pltpu.make_async_copy(rate_ref, rates, in_sems.at[count]))
+    for copy in incoming:
+        copy.start()
+    held[ROWS:] = jnp.zeros((PAD - ROWS, COLS, LANES), F32)
+    flat = held.reshape(PAD * COLS, LANES)
+    outgoing = []
+    incoming[count].wait()
+    for at, (start, size) in enumerate(CHUNKS):
+        incoming[at].wait()
         for c in range(COLS):
-            rates = jnp.concatenate([rate_ref[i, c : c + 1, :] for i in range(4)] + [jnp.zeros((1, LANES), F32)], 0)
+            column = flat[pl.ds(start * COLS + c, size, stride=COLS), :]
+            if at == 0:
+                weights = [rates[i, c : c + 1, :] for i in range(4)]
+                column = jnp.concatenate([column] + weights + [jnp.zeros((4, LANES), F32)], 0)
             if c < STEPS:
-                west_ref[c, last:, :] = rates
+                west_bufs[at][c] = column
             if c >= COLS - STEPS:
-                east_ref[c - COLS + STEPS, last:, :] = rates
+                east_bufs[at][c - COLS + STEPS] = column
+        outgoing.append(pltpu.make_async_copy(west_bufs[at], wests[at], out_sems.at[2 * at]))
+        outgoing.append(pltpu.make_async_copy(east_bufs[at], easts[at], out_sems.at[2 * at + 1]))
+        outgoing[-2].start()
+        outgoing[-1].start()
+    for copy in outgoing:
+        copy.wait()
 
 
 def pack(state, rates):
-    halo = shape(STEPS, PAD, LANES)
-    field = PAD * COLS * LANES * 4
-    return pl.pallas_call(
+    dims = [(STEPS, size + (8 if at == 0 else 0), LANES) for at, (_, size) in enumerate(CHUNKS)]
+    count = len(CHUNKS)
+    outs = call(
         pack_kernel,
-        grid=(PAD // PART,),
-        out_shape=[halo, halo, shape(8, LANES)],
-        in_specs=[
-            pl.BlockSpec((PART, COLS, LANES), lambda i: (i, 0, 0)),
-            pl.BlockSpec((4, COLS, LANES), lambda i: (0, 0, 0)),
-        ],
-        out_specs=[pl.BlockSpec((STEPS, PART, LANES), lambda i: (0, i, 0))] * 2
-        + [pl.BlockSpec((8, LANES), lambda i: (0, 0))],
-        compiler_params=pltpu.CompilerParams(vmem_limit_bytes=8 * MIB),
-        cost_estimate=pl.CostEstimate(flops=0, bytes_accessed=3 * field, transcendentals=0),
-    )(state, rates)
+        [shape(*d) for d in dims] * 2,
+        (state, rates),
+        8,
+        scratch=[pltpu.VMEM((PAD, COLS, LANES), F32), pltpu.VMEM((4, COLS, LANES), F32)]
+        + [pltpu.VMEM(d, F32) for d in dims] * 2
+        + [pltpu.SemaphoreType.DMA((count + 1,)), pltpu.SemaphoreType.DMA((2 * count,))],
+        moved=3 * PAD * COLS * LANES * 4,
+        far=(0, 1),
+        far_out=True,
+    )
+    return outs[:count], outs[count:]
 
 
 def prepare_kernel(inc_ref, forcing_ref, root_ref, physics_ref, base_ref, high_ref, low_ref, square, drive):
@@ -127,25 +142,33 @@
     low_ref[...] = low
 
 
-def transport_kernel(inc_ref, rate_ref, west_ref, east_ref, order_ref, out_ref, table, own, odd, even):
+def transport_kernel(
+    start, size, inc_ref, rate_ref, west_ref, east_ref, west_rate_ref, east_rate_ref, order_ref, out_ref, passed_ref,
+    table, own, odd, even, sem
+):
+    valid = min(size, ROWS - start)
+    copy = pltpu.make_async_copy(inc_ref.at[pl.ds(start, valid)], own.at[pl.ds(0, valid)], sem)
+    copy.start()
+    passed_ref[...] = order_ref[...]
     lane = lax.broadcasted_iota(jnp.int32, (1, LANES), 1)
     wide = COLS + 2 * STEPS
+    at = CHUNKS[0][1]
     for j in range(1, wide - 1):
         if j < STEPS:
-            rates = [west_ref[j, ROWS + i : ROWS + i + 1, :] for i in range(4)]
+            rates = [west_rate_ref[j, at + i : at + i + 1, :] for i in range(4)]
         elif j < STEPS + COLS:
             rates = [rate_ref[i, j - STEPS : j - STEPS + 1, :] for i in range(4)]
         else:
-            rates = [east_ref[j - STEPS - COLS, ROWS + i : ROWS + i + 1, :] for i in range(4)]
+            rates = [east_rate_ref[j - STEPS - COLS, at + i : at + i + 1, :] for i in range(4)]
         center = 1.0 - (rates[0] + rates[1] + rates[2] + rates[3])
         north = jnp.where(lane == LANES - 1, 0.0, rates[2])
         south = jnp.where(lane == 0, 0.0, rates[3])
         for i, value in enumerate((center, rates[0], rates[1], north, south)):
             table[5 * j + i] = jnp.broadcast_to(value, (8, LANES))
-    flat = inc_ref.reshape(ROWS * COLS, LANES)
-    for c in range(COLS):
-        own[c, :ROWS, :] = flat[pl.ds(c, ROWS, stride=COLS), :]
-        own[c, ROWS:, :] = jnp.zeros((PAD - ROWS, LANES), F32)
+    if valid < size:
+        own[valid:] = jnp.zeros((size - valid, COLS, LANES), F32)
+    flat = own.reshape(size * COLS, LANES)
+    copy.wait()
 
     def block(index, carry):
         here = pl.ds(pl.multiple_of(index * PART, 8), PART)
@@ -156,7 +179,7 @@
             elif j < STEPS:
                 value = west_ref[j, here, :]
             elif j < STEPS + COLS:
-                value = own[j - STEPS, here, :]
+                value = flat[pl.ds(index * (PART * COLS) + j - STEPS, PART, stride=COLS), :]
             else:
                 value = east_ref[j - STEPS - COLS, here, :]
             return value.reshape(PART // 8, 8, LANES)
@@ -176,16 +199,25 @@
                     (odd if step % 2 else even)[j] = total
         return carry
 
-    lax.fori_loop(0, PAD // PART, block, 0)
-
-
-def mix_kernel(core_ref, state_ref, high_ref, low_ref, base_ref, order_ref, end_ref, keep_ref, send_ref):
+    if size == PART:
+        block(0, 0)
+    else:
+        lax.fori_loop(0, size // PART, block, 0)
+
+
+def mix_kernel(core_ref, upper_ref, middle_ref, lower_ref, high_ref, low_ref, base_ref, order_ref, end_ref, keep_ref, send_ref):
     core = core_ref[0]
     for kind, out_ref in ((1, send_ref), (0, keep_ref)):
         start = 4 * (core ^ kind)
         for i in (0, 2):
             c = start + i
-            state = jnp.concatenate([state_ref[c], state_ref[c + 1]], 1)
+            state = jnp.concatenate(
+                [
+                    jnp.concatenate([ref[c + k] for ref in (upper_ref, middle_ref, lower_ref)], 0)
+                    for k in range(2)
+                ],
+                1,
+            )
             end = state + product(high_ref[...], low_ref[...], state)
             for k in range(2):
                 column = end[:, k * LANES : (k + 1) * LANES]
@@ -228,20 +260,13 @@
             )
 
 
-def slot_places(column_x, me):
-    tile = column_x >> 3
-    relative = (tile - me + TILES) & (TILES - 1)
+def sort_kernel(index_ref, frac_ref, order_ref, out_ref, chosen_ref, spread_ref):
+    column_x = index_ref[0]
     bucket = lax.broadcasted_iota(jnp.int32, (TILES, SLOTS), 0)
-    chosen = (bucket == relative).astype(F32)
-    earlier = lax.broadcasted_iota(jnp.int32, (SLOTS, SLOTS), 0) < lax.broadcasted_iota(jnp.int32, (SLOTS, SLOTS), 1)
-    rank = jnp.dot(chosen.astype(BF16), earlier.astype(F32).astype(BF16), preferred_element_type=F32)
+    chosen = (bucket == (column_x >> 3)).astype(F32)
+    before = lax.broadcasted_iota(jnp.int32, (SLOTS, SLOTS), 0) < lax.broadcasted_iota(jnp.int32, (SLOTS, SLOTS), 1)
+    rank = jnp.dot(chosen.astype(BF16), before.astype(F32).astype(BF16), preferred_element_type=F32)
     place = jnp.sum(chosen * rank, axis=0, keepdims=True)
-    return chosen, place
-
-
-def sort_kernel(me_ref, index_ref, frac_ref, sent_ref, out_ref, chosen_ref, spread_ref):
-    column_x = index_ref[0:1, :]
-    chosen, place = slot_places(column_x, me_ref[0])
     spread = lax.broadcasted_iota(jnp.int32, (CAP, SLOTS), 0) == place.astype(jnp.int32)
     spread = spread.astype(F32)
     chosen_ref[...] = chosen
@@ -249,10 +274,10 @@
     values = jnp.concatenate(
         [
             (column_x & (COLS - 1)).astype(F32),
-            index_ref[1:2, :].astype(F32),
-            index_ref[2:3, :].astype(F32),
-            frac_ref[0:1, :],
-            frac_ref[1:2, :],
+            index_ref[1].astype(F32),
+            index_ref[2].astype(F32),
+            frac_ref[0],
+            frac_ref[1],
             jnp.zeros((FIELDS - 5, SLOTS), F32),
         ],
         0,
@@ -292,26 +317,16 @@
         r = lax.broadcasted_iota(jnp.int32, (PAD, lanes), 0)
         weight = jnp.where(r == row, 1.0 - upward, jnp.where(r == row + 1, upward, 0.0))
         value = jnp.sum(weight * taken, axis=0, keepdims=True)
-        out_ref[j : j + 1, :] = value[:, :CAP]
-        out_ref[j + 1 : j + 2, :] = value[:, CAP:]
+        out_ref[j] = jnp.broadcast_to(value[:, :CAP], (8, CAP))
+        out_ref[j + 1] = jnp.broadcast_to(value[:, CAP:], (8, CAP))
 
 
 def depart_kernel(count_ref, back_ref, chosen_ref, spread_ref, value_ref, out_ref):
-    spread = jnp.dot(back_ref[...], spread_ref[...], precision=HIGHEST, preferred_element_type=F32)
+    back = jnp.concatenate([back_ref[j, 0:1, :] for j in range(TILES)], 0)
+    spread = jnp.dot(back, spread_ref[...], precision=HIGHEST, preferred_element_type=F32)
     evolved = jnp.sum(spread * chosen_ref[...], axis=0, keepdims=True)
     live = lax.broadcasted_iota(jnp.int32, (1, SLOTS), 1) < count_ref[0, 0]
     out_ref[...] = jnp.where(live, value_ref[...] - evolved, 0.0)
-
-
-def hop(blocks, bit, sign):
-    moving = [j for j in range(TILES) if j & bit]
-    parcel = jnp.concatenate([blocks[j] for j in moving], 0)
-    parcel = lax.ppermute(parcel, "tile", [(i, (i + sign * bit) % TILES) for i in range(TILES)])
-    size = blocks[0].shape[0]
-    result = list(blocks)
-    for at, j in enumerate(moving):
-        result[j] = parcel[at * size : (at + 1) * size]
-    return result
 
 
 def per_device(
@@ -321,24 +336,15 @@
     drive = forcing.reshape(ROWS, COLS, LANES)
     rates = coefficients.reshape(4, COLS, LANES)
     core = jnp.reshape(lax.axis_index("core"), (1,)).astype(jnp.int32)
-    me = jnp.reshape(lax.axis_index("tile"), (1,)).astype(jnp.int32)
     field = PAD * COLS * LANES * 4
 
-    west, east, sent = pack(state, rates)
-    from_east = lax.ppermute(west, "tile", [(i + 1, i) for i in range(TILES - 1)])
-    from_west = lax.ppermute(east, "tile", [(i, i + 1) for i in range(TILES - 1)])
-
-    places = obs_index.reshape(3, SLOTS)
-    sorted_obs, chosen, spread = call(
-        sort_kernel,
-        [shape(TILES, FIELDS, CAP), shape(TILES, SLOTS), shape(CAP, SLOTS)],
-        (me, places, obs_frac.reshape(2, SLOTS), sent),
-        16,
-        flops=10**8,
-        moved=10**6,
-        smem=(0,),
-    )
-    blocks = hop([sorted_obs[j] for j in range(TILES)], 4, 1)
+    wests, easts = pack(state, rates)
+    to_west = [(i + 1, i) for i in range(TILES - 1)]
+    to_east = [(i, i + 1) for i in range(TILES - 1)]
+    halos = [
+        (lax.ppermute(east, "tile", to_east), lax.ppermute(west, "tile", to_west))
+        for west, east in zip(wests, easts)
+    ]
 
     base, high, low = call(
         prepare_kernel,
@@ -349,56 +355,69 @@
         flops=8 * 10**9,
         moved=5 * field,
     )
+    queries, chosen, spread = call(
+        sort_kernel,
+        [shape(TILES, FIELDS, CAP), shape(TILES, SLOTS), shape(CAP, SLOTS)],
+        (obs_index, obs_frac, halos[0][0]),
+        8,
+        flops=10**8,
+        moved=10**6,
+        far=(2,),
+    )
 
     wide = COLS + 2 * STEPS
-    moved = call(
-        transport_kernel,
-        shape(COLS, PAD, LANES),
-        (state, rates, from_west, from_east, blocks[7]),
-        16,
-        scratch=[
-            pltpu.VMEM((5 * wide, 8, LANES), F32),
-            pltpu.VMEM((COLS, PAD, LANES), F32),
-            pltpu.VMEM((wide, PART, LANES), F32),
-            pltpu.VMEM((wide, PART, LANES), F32),
-        ],
-        flops=4 * 10**9,
-        moved=5 * field,
-    )
-    blocks = hop(blocks, 2, 1)
+    moved = []
+    for at, (start, size) in enumerate(CHUNKS):
+        out, handed = call(
+            lambda *refs, start=start, size=size: transport_kernel(start, size, *refs),
+            [shape(COLS, size, LANES), shape(TILES, FIELDS, CAP)],
+            (state, rates, *halos[at], *halos[0], queries),
+            10,
+            scratch=[
+                pltpu.VMEM((5 * wide, 8, LANES), F32),
+                pltpu.VMEM((size, COLS, LANES), F32),
+                pltpu.VMEM((wide, PART, LANES), F32),
+                pltpu.VMEM((wide, PART, LANES), F32),
+                pltpu.SemaphoreType.DMA,
+            ],
+            flops=2 * 10**7 * size,
+            moved=3 * field * size // PAD,
+            far=(0,),
+        )
+        moved.append(out)
+        if at == len(CHUNKS) - 2:
+            arrived = lax.all_to_all(handed, "tile", 0, 0, tiled=True)
     parts = shape(PARTS, PART, LANES)
     end, keep, send = call(
         mix_kernel,
         [shape(COLS, PAD, LANES), parts, parts],
-        (core, moved, high, low, base, blocks[7]),
-        16,
+        (core, *moved, high, low, base, arrived),
+        14,
         flops=2 * 10**9,
         moved=5 * field,
         smem=(0,),
     )
     swap = [(0, 1), (1, 0)]
     partner = lax.ppermute(send, "core", swap)
-    blocks = hop(blocks, 1, 1)
     pair = keep + partner
     gathered = lax.all_to_all(pair, ("y", "x"), 0, 0, tiled=True)
     found = call(
         observe_kernel,
-        shape(TILES, CAP),
-        (jnp.stack(blocks, 0), end, pair),
+        shape(TILES, 8, CAP),
+        (arrived, end, pair),
         16,
         scratch=[pltpu.VMEM((PAD, COLS * LANES), BF16), pltpu.VMEM((PAD, COLS * LANES), BF16)],
         flops=3 * 10**9,
         moved=field,
-        unread=(2,),
-    )
-    back = hop([found[j : j + 1] for j in range(TILES)], 4, -1)
+        far=(2,),
+    )
+    back = lax.all_to_all(found, "tile", 0, 0, tiled=True)
     totals = call(scan_kernel, parts, (gathered, found), 8, flops=10**7, moved=field)
     before = lax.all_to_all(totals, ("y", "x"), 0, 0, tiled=True)
-    back = hop(hop(back, 2, -1), 1, -1)
     departure = call(
         depart_kernel,
         shape(1, SLOTS),
-        (obs_count, jnp.concatenate(back, 0), chosen, spread, obs_value),
+        (obs_count, back, chosen, spread, obs_value),
         8,
         flops=10**7,
         moved=10**6,

time: 125 us -> 138 us (1.10)
  starting transfers between devices: 40.7 us -> 52.7 us
  waiting for transfers between devices: 37.2 us -> 28.2 us
  local copies, waits for them, and re-layouts: 11.6 us -> 17.7 us
  Pallas kernels: 31.8 us -> 35.5 us
    ppermute x8 -> x6, waiting for transfers between devices: 27.2 us -> 0.02 us  [the longest x3 0.01 us: per_device(): lax.ppermute(east, 'tile', to_east)]
    all_to_all x0 -> x2, starting transfers between devices: none -> 16.9 us  [the longest x1 9.99 us: per_device(): arrived = lax.all_to_all(handed, 'tile', 0, 0, tiled=True)]
    all_to_all x1, waiting for transfers between devices: 3.66 us -> 10.7 us  [per_device(): before = lax.all_to_all(totals, ('y', 'x'), 0, 0, tiled=True)]
    all_to_all x1, waiting for transfers between devices: 2.37 us -> 8.54 us  [per_device(): gathered = lax.all_to_all(pair, ('y', 'x'), 0, 0, tiled=True)]
    unnamed x45 -> x55, local copies, waits for them, and re-layouts: 11.5 us -> 17.7 us
    ppermute x8 -> x6, starting transfers between devices: 24.3 us -> 18.5 us  [the longest x3 14.7 us: per_device(): lax.ppermute(east, 'tile', to_east)]
    all_to_all x0 -> x2, waiting for transfers between devices: none -> 4.94 us  [the longest x1 4.93 us: per_device(): back = lax.all_to_all(found, 'tile', 0, 0, tiled=True)]
    pallas_call x10 -> x12, Pallas kernels: 31.8 us -> 35.5 us  [call(): pl.pallas_call(body, out_shape=outs, in_specs=specs, out_specs=[out_spec]...]
  transfers between devices with their start and end apart: 12 -> 12, of which waited for: 8 -> 5; matrix products, arithmetic and copies ran while one was open for 1% -> 1% of each run, Pallas kernels for 9% -> 22%
where the time goes in v2:
time: 138 us; the launch traced here: 137 us
  starting transfers between devices  52.7 us (38%)
  Pallas kernels  35.5 us (26%)
  waiting for transfers between devices  28.2 us (20%)
  local copies, waits for them, and re-layouts  17.7 us (13%)
  between operations  1.55 us (1%)
    pallas_call x12, Pallas kernels, call(): pl.pallas_call(body, out_shape=outs, in_specs=specs, out_specs=[out_spec]...  35.5 us
    unnamed x55, local copies, waits for them, and re-layouts  17.7 us
    ppermute x3, starting transfers between devices, per_device(): lax.ppermute(east, 'tile', to_east)  14.7 us
    all_to_all x1, waiting for transfers between devices, per_device(): before = lax.all_to_all(totals, ('y', 'x'), 0, 0, tiled=True)  10.7 us
    all_to_all x1, starting transfers between devices, per_device(): arrived = lax.all_to_all(handed, 'tile', 0, 0, tiled=True)  9.99 us
    all_to_all x1, waiting for transfers between devices, per_device(): gathered = lax.all_to_all(pair, ('y', 'x'), 0, 0, tiled=True)  8.54 us
    all_to_all x1, starting transfers between devices, per_device(): back = lax.all_to_all(found, 'tile', 0, 0, tiled=True)  6.93 us
    all_to_all x1, starting transfers between devices, per_device(): gathered = lax.all_to_all(pair, ('y', 'x'), 0, 0, tiled=True)  6.76 us
  transfers between devices with their start and end apart: 12, of which 5 were waited for; matrix products, arithmetic and copies ran while one was open for 1% of the time, Pallas kernels for 22%

profile of v2, /device:TPU:1, one launch (start us, length us, event | category | flops | bytes accessed | tf_op | source)
XLA Modules:
  0.0 136.7 jit_solution(3765146061741746350)
XLA Ops:
  0.6 1.4 %copy-done.2 = f32[1,3,137,8,128]{4,3,2,1,0:T(8,128)S(1)} copy-done((f32[1,3,137,8,128]{4,3,2,1,0:T(8,128)S(1)}, f32[1,3,137,8,128]{4,3,2,1,0:T(8,128)}, u32[]{:S(2)}) %copy-start.2) | copy-done | bytes 1683480
  2.8 2.2 %shard_map.105 = (f32[6,216,128]{2,1,0:T(8,128)}, f32[6,104,128]{2,1,0:T(8,128)}, f32[6,104,128]{2,1,0:T(8,128)S(1)}, f32[6,216,128]{2,1,0:T(8,128)}, f32[6,104,128]{2,1,0:T(8,128)}, /*index=5*/f32[6,104,128]{2,1,0:T(8,128)}) custom-call(f32[411,8,128]{2,1,0:T(8,128)S(1)} %bitcast.8, f32[4,8,128]{2,1,0:T(8,128)S(1)} %bitcast.14), custom_call_target="tpu_custom_call" | custom-call | bytes 5111808 | tf_op jit(solution)/shard_map/pallas_call | solution.py:36
  5.0 5.2 %collective-permute-start = (f32[6,216,128]{2,1,0:T(8,128)}, f32[6,216,128]{2,1,0:T(8,128)}, u32[]{:S(2)}, u32[]{:S(2)}) collective-permute-start(f32[6,216,128]{2,1,0:T(8,128)} %get-tuple-element.22), channel_id=1, source_target_pairs={{0,1},{1,2},{2,3},{3,4},{4,5},{5,6},{6,7},{8,9},{9,10},{10,11},{11... | collective-permute-start | bytes 1990664 | tf_op jit(solution)/shard_map/ppermute | solution.py:345
  10.2 1.3 collective-permute-start.1
  11.5 4.7 %collective-permute-start.2 = (f32[6,104,128]{2,1,0:T(8,128)}, f32[6,104,128]{2,1,0:T(8,128)}, u32[]{:S(2)}, u32[]{:S(2)}) collective-permute-start(f32[6,104,128]{2,1,0:T(8,128)} %get-tuple-element.26), channel_id=1, source_target_pairs={{0,1},{1,2},{2,3},{3,4},{4,5},{5,6},{6,7},{8,9},{9,10},{10,11},{11... | collective-permute-start | bytes 958472 | tf_op jit(solution)/shard_map/ppermute | solution.py:345
  16.3 1.3 collective-permute-start.3
  17.5 4.7 %collective-permute-start.4 = (f32[6,104,128]{2,1,0:T(8,128)}, f32[6,104,128]{2,1,0:T(8,128)}, u32[]{:S(2)}, u32[]{:S(2)}) collective-permute-start(f32[6,104,128]{2,1,0:T(8,128)} %get-tuple-element.29), channel_id=1, source_target_pairs={{0,1},{1,2},{2,3},{3,4},{4,5},{5,6},{6,7},{8,9},{9,10},{10,11},{11... | collective-permute-start | bytes 958472 | tf_op jit(solution)/shard_map/ppermute | solution.py:345
  22.3 1.2 copy.13
  24.7 6.3 %shard_map.104 = (f32[8,416,128]{2,1,0:T(8,128)S(1)}, bf16[416,416]{1,0:T(8,128)(2,1)S(1)}, bf16[416,416]{1,0:T(8,128)(2,1)S(1)}) custom-call(f32[411,8,128]{2,1,0:T(8,128)S(1)} %bitcast.9, f32[411,8,128]{2,1,0:T(8,128)S(1)} %bitcast.18, f32[411,411]{1,0:T(8,128)S(1)} %copy-done.13, f32[411,411]{1,0:T(8,128)S(1)} %bitcast.13), custom_call_target="tpu_custom_call" | custom-call | flops 8000000000 | bytes 8519680 | tf_op jit(solution)/shard_map/pallas_call | solution.py:36
  32.5 1.3 collective-permute-start.5
  33.9 1.9 %shard_map.106 = (f32[8,8,128]{2,1,0:T(8,128)S(1)}, f32[8,512]{1,0:T(8,128)S(1)}, f32[128,512]{1,0:T(8,128)S(1)}) custom-call(s32[3,1,512]{2,1,0:T(1,128)S(1)} %copy-done.9, f32[2,1,512]{2,1,0:T(1,128)S(1)} %copy-done.10, f32[6,216,128]{2,1,0:T(8,128)} %collective-permute-done.order_ref.refs_2_.refs_4_), custom_call_target="tpu_custom_call" | custom-call | flops 100000000 | bytes 1000000 | tf_op jit(solution)/shard_map/pallas_call | solution.py:36
  36.5 4.0 %shard_map.108 = (f32[8,104,128]{2,1,0:T(8,128)S(1)}, f32[8,8,128]{2,1,0:T(8,128)}) custom-call(f32[411,8,128]{2,1,0:T(8,128)S(1)} %bitcast.10, f32[4,8,128]{2,1,0:T(8,128)S(1)} %bitcast.15, f32[6,104,128]{2,1,0:T(8,128)} %collective-permute-done.2.refs_2_, f32[6,104,128]{2,1,0:T(8,128)} %collective-permute-done.3.refs_3_, ...), custom_call_target="tpu_custom_call" | custom-call | flops 2080000000 | bytes 1277952 | tf_op jit(solution)/shard_map/pallas_call | solution.py:36
  41.3 10.0 %all-to-all-start = ((f32[8,8,128]{2,1,0:T(8,128)}), f32[8,8,128]{2,1,0:T(8,128)S(1)}, u32[]{:S(2)}, u32[]{:S(2)}) async-start(f32[8,8,128]{2,1,0:T(8,128)} %get-tuple-element.34), calls=%async_computation | async-start | bytes 65536 | tf_op jit(solution)/shard_map/all_to_all | solution.py:389
  51.3 6.7 %shard_map.107 = (f32[8,208,128]{2,1,0:T(8,128)S(1)}, f32[8,8,128]{2,1,0:T(8,128)}) custom-call(f32[411,8,128]{2,1,0:T(8,128)S(1)} %bitcast.11, f32[4,8,128]{2,1,0:T(8,128)S(1)} %bitcast.16, f32[6,216,128]{2,1,0:T(8,128)} %collective-permute-done.order_ref.refs_2_.refs_4_, f32[6,216,128]{2,1,0:T(8,128)} %collective-permute-done.1.refs_3_.refs_5_, ...), custom_call_target="tpu_custom_call" | custom-call | flops 4160000000 | bytes 2555904 | tf_op jit(solution)/shard_map/pallas_call | solution.py:36
  58.9 4.0 %shard_map.109 = (f32[8,104,128]{2,1,0:T(8,128)S(1)}, f32[8,8,128]{2,1,0:T(8,128)}) custom-call(f32[411,8,128]{2,1,0:T(8,128)S(1)} %bitcast.12, f32[4,8,128]{2,1,0:T(8,128)S(1)} %bitcast.17, f32[6,104,128]{2,1,0:T(8,128)} %collective-permute-done.4.refs_2_, f32[6,104,128]{2,1,0:T(8,128)} %collective-permute-done.5.refs_3_, ...), custom_call_target="tpu_custom_call" | custom-call | flops 2080000000 | bytes 1277952 | tf_op jit(solution)/shard_map/pallas_call | solution.py:36
  63.7 1.2 copy-done.18
  68.9 1.5 %shard_map.110 = (f32[8,416,128]{2,1,0:T(8,128)S(1)}, f32[16,104,128]{2,1,0:T(8,128)S(1)}, f32[16,104,128]{2,1,0:T(8,128)S(1)}) custom-call(s32[1]{0:T(128)} %bitcast.core_ref, f32[8,208,128]{2,1,0:T(8,128)S(1)} %copy-done.18, f32[8,104,128]{2,1,0:T(8,128)S(1)} %copy-done.24, f32[8,104,128]{2,1,0:T(8,128)S(1)} %copy-done.26, ...), custom_call_target="tpu_custom_call" | custom-call | flops 2000000000 | bytes 8519680 | tf_op jit(solution)/shard_map/pallas_call | solution.py:36
  70.4 1.2 copy-done.15
  71.6 2.6 %collective-permute-start.6 = (f32[16,104,128]{2,1,0:T(8,128)S(1)}, f32[16,104,128]{2,1,0:T(8,128)S(1)}, u32[]{:S(2)}, u32[]{:S(2)}) collective-permute-start(f32[16,104,128]{2,1,0:T(8,128)S(1)} %get-tuple-element.36), channel_id=1, source_target_pairs={{0,8},{8,0},{1,9},{9,1},{2,10},{10,2},{3,11},{11,3},{4,12},{12,4},... | collective-permute-start | bytes 2555912 | tf_op jit(solution)/shard_map/ppermute | solution.py:401
  74.2 2.0 %collective-permute-done.6.partner_ref = f32[16,104,128]{2,1,0:T(8,128)S(1)} collective-permute-done((f32[16,104,128]{2,1,0:T(8,128)S(1)}, f32[16,104,128]{2,1,0:T(8,128)S(1)}, u32[]{:S(2)}, u32[]{:S(2)}) %collective-permute-start.6) | collective-permute-done | bytes 852000 | tf_op jit(solution)/shard_map/ppermute | solution.py:401
  77.2 6.8 %all-to-all-start.1 = ((f32[16,104,128]{2,1,0:T(8,128)}), f32[16,104,128]{2,1,0:T(8,128)S(1)}, u32[]{:S(2)}, u32[]{:S(2)}) async-start(f32[16,104,128]{2,1,0:T(8,128)} %add.3.order_ref), calls=%async_computation.1 | async-start | bytes 1703936 | tf_op jit(solution)/shard_map/all_to_all | solution.py:403
  84.0 1.4 %copy-done.16 = f32[8,416,128]{2,1,0:T(8,128)S(1)} copy-done((f32[8,416,128]{2,1,0:T(8,128)S(1)}, f32[8,416,128]{2,1,0:T(8,128)}, u32[]{:S(2)}) %copy-start.16) | copy-done | bytes 1703960
  85.5 4.2 %shard_map.111.order_ref = f32[8,8,128]{2,1,0:T(8,128)} custom-call(f32[8,8,128]{2,1,0:T(8,128)S(1)} %all-to-all-done.order_ref.obs_ref, f32[8,416,128]{2,1,0:T(8,128)S(1)} %copy-done.16, f32[16,104,128]{2,1,0:T(8,128)} %add.3.order_ref), custom_call_target="tpu_custom_call" | custom-call | flops 3000000000 | bytes 1703936 | tf_op jit(solution)/shard_map/pallas_call | solution.py:36
  89.7 8.5 %all-to-all-done.1.in_ref = f32[16,104,128]{2,1,0:T(8,128)S(1)} async-done(((f32[16,104,128]{2,1,0:T(8,128)}), f32[16,104,128]{2,1,0:T(8,128)S(1)}, u32[]{:S(2)}, u32[]{:S(2)}) %all-to-all-start.1) | async-done | bytes 852000 | tf_op jit(solution)/shard_map/all_to_all | solution.py:403
  98.2 6.9 %all-to-all-start.3 = ((f32[8,8,128]{2,1,0:T(8,128)}), f32[8,8,128]{2,1,0:T(8,128)S(1)}, u32[]{:S(2)}, u32[]{:S(2)}) async-start(f32[8,8,128]{2,1,0:T(8,128)} %shard_map.111.order_ref), calls=%async_computation.3 | async-start | bytes 65536 | tf_op jit(solution)/shard_map/all_to_all | solution.py:414
  105.2 1.9 %shard_map.112 = f32[16,104,128]{2,1,0:T(8,128)} custom-call(f32[16,104,128]{2,1,0:T(8,128)S(1)} %all-to-all-done.1.in_ref, f32[8,8,128]{2,1,0:T(8,128)} %shard_map.111.order_ref), custom_call_target="tpu_custom_call" | custom-call | flops 10000000 | bytes 1703936 | tf_op jit(solution)/shard_map/pallas_call | solution.py:36
  107.1 4.9 %all-to-all-done.3.back_ref = f32[8,8,128]{2,1,0:T(8,128)S(1)} async-done(((f32[8,8,128]{2,1,0:T(8,128)}), f32[8,8,128]{2,1,0:T(8,128)S(1)}, u32[]{:S(2)}, u32[]{:S(2)}) %all-to-all-start.3) | async-done | bytes 32800 | tf_op jit(solution)/shard_map/all_to_all | solution.py:414
  112.0 3.8 %all-to-all-start.2 = ((f32[16,104,128]{2,1,0:T(8,128)}), f32[16,104,128]{2,1,0:T(8,128)S(1)}, u32[]{:S(2)}, u32[]{:S(2)}) async-start(f32[16,104,128]{2,1,0:T(8,128)} %shard_map.112), calls=%async_computation.2 | async-start | bytes 1703936 | tf_op jit(solution)/shard_map/all_to_all | solution.py:416
  117.3 10.7 %all-to-all-done.2.before_ref = f32[16,104,128]{2,1,0:T(8,128)S(1)} async-done(((f32[16,104,128]{2,1,0:T(8,128)}), f32[16,104,128]{2,1,0:T(8,128)S(1)}, u32[]{:S(2)}, u32[]{:S(2)}) %all-to-all-start.2) | async-done | bytes 852000 | tf_op jit(solution)/shard_map/all_to_all | solution.py:416
  128.8 4.0 %collective-permute-start.7 = (f32[16,104,128]{2,1,0:T(8,128)S(1)}, f32[16,104,128]{2,1,0:T(8,128)S(1)}, u32[]{:S(2)}, u32[]{:S(2)}) collective-permute-start(f32[16,104,128]{2,1,0:T(8,128)S(1)} %shard_map.114), channel_id=1, source_target_pairs={{0,8},{8,0},{1,9},{9,1},{2,10},{10,2},{3,11},{11,3},{4,12},{12,4},... | collective-permute-start | bytes 2555912 | tf_op jit(solution)/shard_map/ppermute | solution.py:429
  132.9 2.0 %collective-permute-done.7.other_ref = f32[16,104,128]{2,1,0:T(8,128)S(1)} collective-permute-done((f32[16,104,128]{2,1,0:T(8,128)S(1)}, f32[16,104,128]{2,1,0:T(8,128)S(1)}, u32[]{:S(2)}, u32[]{:S(2)}) %collective-permute-start.7) | collective-permute-done | bytes 852000 | tf_op jit(solution)/shard_map/ppermute | solution.py:429
  134.9 1.8 %shard_map.115 = f32[411,8,128]{2,1,0:T(8,128)} custom-call(s32[1]{0:T(128)} %bitcast.core_ref, f32[8,416,128]{2,1,0:T(8,128)S(1)} %copy-done.1, f32[16,104,128]{2,1,0:T(8,128)S(1)} %all-to-all-done.2.before_ref, f32[16,104,128]{2,1,0:T(8,128)S(1)} %collective-permute-done.6.partner_ref, f32[16,104,128]{2,1,0:T(8,128)S(1)} %collective-permute-done.7.other_ref), custom_call_target="tpu_custom_call" | custom-call | flops 10000000 | bytes 6815744 | tf_op jit(solution)/shard_map/pallas_call | solution.py:36
  (60 shorter events, 13.2 us)
Async XLA Ops:
  0.6 1.4 %copy-start.2 = (f32[1,3,137,8,128]{4,3,2,1,0:T(8,128)S(1)}, f32[1,3,137,8,128]{4,3,2,1,0:T(8,128)}, u32[]{:S(2)}) copy-start(f32[1,3,137,8,128]{4,3,2,1,0:T(8,128)} %param.9) | copy-start | bytes 5050372
  2.8 20.7 %copy-start.3 = (f32[1,3,137,8,128]{4,3,2,1,0:T(8,128)S(1)}, f32[1,3,137,8,128]{4,3,2,1,0:T(8,128)}, u32[]{:S(2)}) copy-start(f32[1,3,137,8,128]{4,3,2,1,0:T(8,128)} %param.9) | copy-start | bytes 5050372
  2.8 20.7 %copy-start.12 = (f32[1,3,137,8,128]{4,3,2,1,0:T(8,128)S(1)}, f32[1,3,137,8,128]{4,3,2,1,0:T(8,128)}, u32[]{:S(2)}) copy-start(f32[1,3,137,8,128]{4,3,2,1,0:T(8,128)} %param.10) | copy-start | bytes 5050372
  5.0 12.5 %copy-start.14 = (f32[6,104,128]{2,1,0:T(8,128)}, f32[6,104,128]{2,1,0:T(8,128)S(1)}, u32[]{:S(2)}) copy-start(f32[6,104,128]{2,1,0:T(8,128)S(1)} %get-tuple-element.30) | copy-start | bytes 958468
  5.0 27.5 %collective-permute-start = (f32[6,216,128]{2,1,0:T(8,128)}, f32[6,216,128]{2,1,0:T(8,128)}, u32[]{:S(2)}, u32[]{:S(2)}) collective-permute-start(f32[6,216,128]{2,1,0:T(8,128)} %get-tuple-element.22), channel_id=1, source_target_pairs={{0,1},{1,2},{2,3},{3,4},{4,5},{5,6},{6,7},{8,9},{9,10},{10,11},{11... | collective-permute-start | bytes 1990664 | tf_op jit(solution)/shard_map/ppermute | solution.py:345
  10.2 26.3 %collective-permute-start.1 = (f32[6,216,128]{2,1,0:T(8,128)}, f32[6,216,128]{2,1,0:T(8,128)}, u32[]{:S(2)}, u32[]{:S(2)}) collective-permute-start(f32[6,216,128]{2,1,0:T(8,128)} %get-tuple-element.23), channel_id=1, source_target_pairs={{1,0},{2,1},{3,2},{4,3},{5,4},{6,5},{7,6},{9,8},{10,9},{11,10},{12... | collective-permute-start | bytes 1990664 | tf_op jit(solution)/shard_map/ppermute | solution.py:345
  11.5 25.0 %collective-permute-start.2 = (f32[6,104,128]{2,1,0:T(8,128)}, f32[6,104,128]{2,1,0:T(8,128)}, u32[]{:S(2)}, u32[]{:S(2)}) collective-permute-start(f32[6,104,128]{2,1,0:T(8,128)} %get-tuple-element.26), channel_id=1, source_target_pairs={{0,1},{1,2},{2,3},{3,4},{4,5},{5,6},{6,7},{8,9},{9,10},{10,11},{11... | collective-permute-start | bytes 958472 | tf_op jit(solution)/shard_map/ppermute | solution.py:345
  16.3 20.2 %collective-permute-start.3 = (f32[6,104,128]{2,1,0:T(8,128)}, f32[6,104,128]{2,1,0:T(8,128)}, u32[]{:S(2)}, u32[]{:S(2)}) collective-permute-start(f32[6,104,128]{2,1,0:T(8,128)} %get-tuple-element.27), channel_id=1, source_target_pairs={{1,0},{2,1},{3,2},{4,3},{5,4},{6,5},{7,6},{9,8},{10,9},{11,10},{12... | collective-permute-start | bytes 958472 | tf_op jit(solution)/shard_map/ppermute | solution.py:345
  17.5 41.3 %collective-permute-start.4 = (f32[6,104,128]{2,1,0:T(8,128)}, f32[6,104,128]{2,1,0:T(8,128)}, u32[]{:S(2)}, u32[]{:S(2)}) collective-permute-start(f32[6,104,128]{2,1,0:T(8,128)} %get-tuple-element.29), channel_id=1, source_target_pairs={{0,1},{1,2},{2,3},{3,4},{4,5},{5,6},{6,7},{8,9},{9,10},{10,11},{11... | collective-permute-start | bytes 958472 | tf_op jit(solution)/shard_map/ppermute | solution.py:345
  23.5 1.2 copy-start.13
  24.7 9.2 %copy-start.9 = (s32[3,1,512]{2,1,0:T(1,128)S(1)}, s32[3,1,512]{2,1,0:T(1,128)}, u32[]{:S(2)}) copy-start(s32[3,1,512]{2,1,0:T(1,128)} %index_ref.1) | copy-start | bytes 18436
  24.7 9.2 %copy-start.10 = (f32[2,1,512]{2,1,0:T(1,128)S(1)}, f32[2,1,512]{2,1,0:T(1,128)}, u32[]{:S(2)}) copy-start(f32[2,1,512]{2,1,0:T(1,128)} %frac_ref.1) | copy-start | bytes 12292
  24.7 11.8 %copy-start.7 = (f32[1,4,8,128]{3,2,1,0:T(8,128)S(1)}, f32[1,4,8,128]{3,2,1,0:T(8,128)}, u32[]{:S(2)}) copy-start(f32[1,4,8,128]{3,2,1,0:T(8,128)} %param.13) | copy-start | bytes 49156
  32.5 31.1 %copy-start = (f32[8,416,128]{2,1,0:T(8,128)}, f32[8,416,128]{2,1,0:T(8,128)S(1)}, u32[]{:S(2)}) copy-start(f32[8,416,128]{2,1,0:T(8,128)S(1)} %get-tuple-element.21.base_ref) | copy-start | bytes 5111812
  32.5 26.4 %collective-permute-start.5 = (f32[6,104,128]{2,1,0:T(8,128)}, f32[6,104,128]{2,1,0:T(8,128)}, u32[]{:S(2)}, u32[]{:S(2)}) collective-permute-start(f32[6,104,128]{2,1,0:T(8,128)} %copy-done.14), channel_id=1, source_target_pairs={{1,0},{2,1},{3,2},{4,3},{5,4},{6,5},{7,6},{9,8},{10,9},{11,10},{12... | collective-permute-start | bytes 958472 | tf_op jit(solution)/shard_map/ppermute | solution.py:345
  41.3 22.4 %all-to-all-start = ((f32[8,8,128]{2,1,0:T(8,128)}), f32[8,8,128]{2,1,0:T(8,128)S(1)}, u32[]{:S(2)}, u32[]{:S(2)}) async-start(f32[8,8,128]{2,1,0:T(8,128)} %get-tuple-element.34), calls=%async_computation | async-start | bytes 65536 | tf_op jit(solution)/shard_map/all_to_all | solution.py:389
  58.0 0.9 copy-start.17
  63.7 1.2 copy-start.18
  64.8 1.0 copy-start.20
  65.8 1.0 copy-start.22
  66.8 1.0 copy-start.24
  67.9 1.0 copy-start.26
  70.4 1.2 copy-start.15
  71.6 4.6 %collective-permute-start.6 = (f32[16,104,128]{2,1,0:T(8,128)S(1)}, f32[16,104,128]{2,1,0:T(8,128)S(1)}, u32[]{:S(2)}, u32[]{:S(2)}) collective-permute-start(f32[16,104,128]{2,1,0:T(8,128)S(1)} %get-tuple-element.36), channel_id=1, source_target_pairs={{0,8},{8,0},{1,9},{9,1},{2,10},{10,2},{3,11},{11,3},{4,12},{12,4},... | collective-permute-start | bytes 2555912 | tf_op jit(solution)/shard_map/ppermute | solution.py:401
  77.2 21.0 %all-to-all-start.1 = ((f32[16,104,128]{2,1,0:T(8,128)}), f32[16,104,128]{2,1,0:T(8,128)S(1)}, u32[]{:S(2)}, u32[]{:S(2)}) async-start(f32[16,104,128]{2,1,0:T(8,128)} %add.3.order_ref), calls=%async_computation.1 | async-start | bytes 1703936 | tf_op jit(solution)/shard_map/all_to_all | solution.py:403
  84.0 1.5 %copy-start.16 = (f32[8,416,128]{2,1,0:T(8,128)S(1)}, f32[8,416,128]{2,1,0:T(8,128)}, u32[]{:S(2)}) copy-start(f32[8,416,128]{2,1,0:T(8,128)} %copy-done.15) | copy-start | bytes 5111812
  98.2 13.8 %all-to-all-start.3 = ((f32[8,8,128]{2,1,0:T(8,128)}), f32[8,8,128]{2,1,0:T(8,128)S(1)}, u32[]{:S(2)}, u32[]{:S(2)}) async-start(f32[8,8,128]{2,1,0:T(8,128)} %shard_map.111.order_ref), calls=%async_computation.3 | async-start | bytes 65536 | tf_op jit(solution)/shard_map/all_to_all | solution.py:414
  105.2 11.3 %copy-start.5 = (f32[128,512]{1,0:T(8,128)S(1)}, f32[128,512]{1,0:T(8,128)}, u32[]{:S(2)}) copy-start(f32[128,512]{1,0:T(8,128)} %copy-done.4) | copy-start | bytes 786436
  105.2 11.3 %copy-start.11 = (f32[1,512]{1,0:T(1,128)S(1)}, f32[1,512]{1,0:T(1,128)}, u32[]{:S(2)}) copy-start(f32[1,512]{1,0:T(1,128)} %value_ref.1) | copy-start | bytes 6148
  112.0 16.0 %all-to-all-start.2 = ((f32[16,104,128]{2,1,0:T(8,128)}), f32[16,104,128]{2,1,0:T(8,128)S(1)}, u32[]{:S(2)}, u32[]{:S(2)}) async-start(f32[16,104,128]{2,1,0:T(8,128)} %shard_map.112), calls=%async_computation.2 | async-start | bytes 1703936 | tf_op jit(solution)/shard_map/all_to_all | solution.py:416
  128.7 6.1 %copy-start.1 = (f32[8,416,128]{2,1,0:T(8,128)S(1)}, f32[8,416,128]{2,1,0:T(8,128)}, u32[]{:S(2)}) copy-start(f32[8,416,128]{2,1,0:T(8,128)} %copy-done) | copy-start | bytes 5111812
  128.8 6.0 %collective-permute-start.7 = (f32[16,104,128]{2,1,0:T(8,128)S(1)}, f32[16,104,128]{2,1,0:T(8,128)S(1)}, u32[]{:S(2)}, u32[]{:S(2)}) collective-permute-start(f32[16,104,128]{2,1,0:T(8,128)S(1)} %shard_map.114), channel_id=1, source_target_pairs={{0,8},{8,0},{1,9},{9,1},{2,10},{10,2},{3,11},{11,3},{4,12},{12,4},... | collective-permute-start | bytes 2555912 | tf_op jit(solution)/shard_map/ppermute | solution.py:429
  (7 other events, 5.2 us)

commit v3 on v2

v3 whole, which is shorter than its diff:
```python
import jax
import jax.numpy as jnp
from jax import lax
from jax.experimental import pallas as pl
from jax.experimental.pallas import tpu as pltpu
from jax.sharding import Mesh, PartitionSpec as P

STEPS = 6
ROWS = 411
PAD = 416
COLS = 8
LANES = 128
GRID_Y = 4
GRID_X = 4
CORES = 2
PARTS = 16
PART = 104
TILES = 8
CHUNKS = ((0, 208), (208, 208))
SLOTS = 512
CAP = 128
FIELDS = 8

F32 = jnp.float32
BF16 = jnp.bfloat16
HIGHEST = lax.Precision.HIGHEST
MIB = 1 << 20
WIDE = 56


def call(body, outs, ins, mib, scratch=(), flops=0, moved=0, smem=(), far=(), far_out=()):
    specs = [
        pl.BlockSpec(memory_space=pltpu.SMEM if at in smem else pltpu.HBM if at in far else pltpu.VMEM)
        for at in range(len(ins))
    ]
    many = isinstance(outs, (list, tuple))
    out_specs = [
        pl.BlockSpec(memory_space=pltpu.HBM if at in far_out else pltpu.VMEM)
        for at in range(len(outs) if many else 1)
    ]
    return pl.pallas_call(
        body,
        out_shape=outs,
        in_specs=specs,
        out_specs=out_specs if many else out_specs[0],
        scratch_shapes=list(scratch),
        compiler_params=pltpu.CompilerParams(vmem_limit_bytes=mib * MIB),
        cost_estimate=pl.CostEstimate(flops=flops, bytes_accessed=moved, transcendentals=0),
    )(*ins)


def shape(*dims, dtype=F32):
    return jax.ShapeDtypeStruct(dims, dtype)


def two_parts(value):
    high = value.astype(BF16)
    low = (value - high.astype(F32)).astype(BF16)
    return high, low


def product(left_high, left_low, right):
    high, low = two_parts(right)
    total = jnp.dot(left_high, high, preferred_element_type=F32)
    total = total + jnp.dot(left_high, low, preferred_element_type=F32)
    return total + jnp.dot(left_low, high, preferred_element_type=F32)


def pack_kernel(inc_ref, rate_ref, *refs):
    count = len(CHUNKS)
    wests, easts = refs[:count], refs[count : 2 * count]
    held, rates = refs[2 * count : 2 * count + 2]
    west_bufs = refs[2 * count + 2 : 3 * count + 2]
    east_bufs = refs[3 * count + 2 : 4 * count + 2]
    in_sems, out_sems = refs[4 * count + 2 :]
    incoming = [pltpu.make_async_copy(rate_ref, rates, in_sems.at[count])]
    for at, (start, size) in enumerate(CHUNKS):
        rows = pl.ds(start, min(size, ROWS - start))
        incoming.append(pltpu.make_async_copy(inc_ref.at[rows], held.at[rows], in_sems.at[at]))
    for copy in incoming:
        copy.start()
    held[ROWS:] = jnp.zeros((PAD - ROWS, COLS, LANES), F32)
    flat = held.reshape(PAD * COLS, LANES)
    outgoing = []
    incoming[0].wait()
    for at, (start, size) in enumerate(CHUNKS):
        incoming[at + 1].wait()
        for c in range(COLS):
            column = flat[pl.ds(start * COLS + c, size, stride=COLS), :]
            if at == 0:
                weights = [rates[i, c : c + 1, :] for i in range(4)]
                column = jnp.concatenate([column] + weights + [jnp.zeros((4, LANES), F32)], 0)
            if c < STEPS:
                west_bufs[at][c] = column
            if c >= COLS - STEPS:
                east_bufs[at][c - COLS + STEPS] = column
        outgoing.append(pltpu.make_async_copy(west_bufs[at], wests[at], out_sems.at[2 * at]))
        outgoing.append(pltpu.make_async_copy(east_bufs[at], easts[at], out_sems.at[2 * at + 1]))
        outgoing[-2].start()
        outgoing[-1].start()
    for copy in outgoing:
        copy.wait()


def pack(state, rates):
    dims = [(STEPS, size + (8 if at == 0 else 0), LANES) for at, (_, size) in enumerate(CHUNKS)]
    count = len(CHUNKS)
    outs = call(
        pack_kernel,
        [shape(*d) for d in dims] * 2,
        (state, rates),
        WIDE,
        scratch=[pltpu.VMEM((PAD, COLS, LANES), F32), pltpu.VMEM((4, COLS, LANES), F32)]
        + [pltpu.VMEM(d, F32) for d in dims] * 2
        + [pltpu.SemaphoreType.DMA((count + 1,)), pltpu.SemaphoreType.DMA((2 * count,))],
        moved=3 * PAD * COLS * LANES * 4,
        far=(0, 1),
        far_out=range(2 * count),
    )
    return outs[:count], outs[count:]


def prepare_kernel(
    inc_ref, forcing_ref, root_ref, physics_ref, base_ref, high_ref, low_ref,
    start, force, root, square, drive, base, high, low, sems
):
    incoming = [
        pltpu.make_async_copy(root_ref, root, sems.at[0]),
        pltpu.make_async_copy(forcing_ref, force, sems.at[1]),
        pltpu.make_async_copy(inc_ref, start, sems.at[2]),
    ]
    for copy in incoming:
        copy.start()
    square[...] = jnp.zeros((PAD, PAD), F32)
    square[:ROWS, :ROWS] = 0.2 * physics_ref[...]
    once = square[...]
    twice = 2.0 * once + product(*two_parts(once), once)
    twice_parts = two_parts(twice)
    four = 2.0 * twice + product(*twice_parts, twice)
    six = twice + four + product(*twice_parts, four)
    high[...], low[...] = two_parts(six)
    outgoing = [
        pltpu.make_async_copy(high, high_ref, sems.at[3]),
        pltpu.make_async_copy(low, low_ref, sems.at[4]),
    ]
    for copy in outgoing:
        copy.start()
    for copy in incoming:
        copy.wait()
    square[:ROWS, :ROWS] = root[...]
    root_high, root_low = two_parts(square[...])
    force_flat = force.reshape(ROWS * COLS, LANES)
    start_flat = start.reshape(ROWS * COLS, LANES)
    drive[ROWS - 3 :, :] = jnp.zeros((PAD - ROWS + 3, 2 * LANES), F32)
    for c in range(0, COLS, 2):
        drive[:ROWS, :LANES] = force_flat[pl.ds(c, ROWS, stride=COLS), :]
        drive[:ROWS, LANES:] = force_flat[pl.ds(c + 1, ROWS, stride=COLS), :]
        forced = product(root_high, root_low, drive[...])
        for k in range(2):
            column = forced[:, k * LANES : (k + 1) * LANES]
            base[c + k, :ROWS, :] = start_flat[pl.ds(c + k, ROWS, stride=COLS), :] - column[:ROWS]
            base[c + k, ROWS:, :] = column[ROWS:]
        pair = pl.ds(c, 2)
        outgoing.append(pltpu.make_async_copy(base.at[pair], base_ref.at[pair], sems.at[5 + c // 2]))
        outgoing[-1].start()
    for copy in outgoing:
        copy.wait()


def transport(at, refs, scratch, put, later=()):
    inc_ref, rate_ref, west_ref, east_ref, west_rate_ref, east_rate_ref = refs
    rate, west_rate, east_rate, table, own, west, east, odd, even, sems = scratch
    start, size = CHUNKS[at]
    blocks = size // PART
    first = CHUNKS[0][1]
    weights = [
        pltpu.make_async_copy(rate_ref, rate, sems.at[0]),
        pltpu.make_async_copy(west_rate_ref.at[:, pl.ds(first, 8)], west_rate, sems.at[1]),
        pltpu.make_async_copy(east_rate_ref.at[:, pl.ds(first, 8)], east_rate, sems.at[2]),
    ]
    fields = []
    for b in range(blocks):
        valid = min(PART, ROWS - start - b * PART)
        rows = pl.ds(b * PART, PART)
        fields.append(
            [
                pltpu.make_async_copy(
                    inc_ref.at[pl.ds(start + b * PART, valid)], own.at[b, pl.ds(0, valid)], sems.at[3 + 3 * b]
                ),
                pltpu.make_async_copy(west_ref.at[:, rows], west.at[b], sems.at[4 + 3 * b]),
                pltpu.make_async_copy(east_ref.at[:, rows], east.at[b], sems.at[5 + 3 * b]),
            ]
        )
    for copy in weights + [c for group in fields for c in group] + list(later):
        copy.start()
    for copy in weights:
        copy.wait()
    lane = lax.broadcasted_iota(jnp.int32, (1, LANES), 1)
    wide = COLS + 2 * STEPS
    for j in range(1, wide - 1):
        if j < STEPS:
            rates = [west_rate[j, i : i + 1, :] for i in range(4)]
        elif j < STEPS + COLS:
            rates = [rate[i, j - STEPS : j - STEPS + 1, :] for i in range(4)]
        else:
            rates = [east_rate[j - STEPS - COLS, i : i + 1, :] for i in range(4)]
        center = 1.0 - (rates[0] + rates[1] + rates[2] + rates[3])
        north = jnp.where(lane == LANES - 1, 0.0, rates[2])
        south = jnp.where(lane == 0, 0.0, rates[3])
        for i, value in enumerate((center, rates[0], rates[1], north, south)):
            table[5 * j + i] = jnp.broadcast_to(value, (8, LANES))
    flat = own.reshape(blocks * PART * COLS, LANES)
    for b in range(blocks):
        valid = min(PART, ROWS - start - b * PART)
        if valid < PART:
            own[b, valid:] = jnp.zeros((PART - valid, COLS, LANES), F32)
        for copy in fields[b]:
            copy.wait()

    def block(b, carry):
        def load(step, j):
            if step > 0:
                value = (odd if step % 2 else even)[j]
            elif j < STEPS:
                value = west[b, j]
            elif j < STEPS + COLS:
                value = flat[pl.ds(b * (PART * COLS) + j - STEPS, PART, stride=COLS), :]
            else:
                value = east[b, j - STEPS - COLS]
            return value.reshape(PART // 8, 8, LANES)

        for step in range(1, STEPS + 1):
            for j in range(step, wide - step):
                v = load(step - 1, j)
                total = table[5 * j] * v
                total = total + table[5 * j + 1] * load(step - 1, j + 1)
                total = total + table[5 * j + 2] * load(step - 1, j - 1)
                total = total + table[5 * j + 3] * pltpu.roll(v, LANES - 1, 2)
                total = total + table[5 * j + 4] * pltpu.roll(v, 1, 2)
                total = total.reshape(PART, LANES)
                if step == STEPS:
                    put(pl.ds(pl.multiple_of(b * PART, 8), PART), j - STEPS, total)
                else:
                    (odd if step % 2 else even)[j] = total
        return carry

    lax.fori_loop(0, blocks, block, 0)


def transport_scratch(at):
    blocks = CHUNKS[at][1] // PART
    wide = COLS + 2 * STEPS
    return [
        pltpu.VMEM((4, COLS, LANES), F32),
        pltpu.VMEM((STEPS, 8, LANES), F32),
        pltpu.VMEM((STEPS, 8, LANES), F32),
        pltpu.VMEM((5 * wide, 8, LANES), F32),
        pltpu.VMEM((blocks, PART, COLS, LANES), F32),
        pltpu.VMEM((blocks, STEPS, PART, LANES), F32),
        pltpu.VMEM((blocks, STEPS, PART, LANES), F32),
        pltpu.VMEM((wide, PART, LANES), F32),
        pltpu.VMEM((wide, PART, LANES), F32),
        pltpu.SemaphoreType.DMA((3 + 3 * blocks,)),
    ]


def upper_kernel(*refs):
    ins, out_ref, (out, sem), scratch = refs[:6], refs[6], refs[7:9], refs[9:]

    def put(rows, c, value):
        out[c, rows, :] = value

    transport(0, ins, scratch, put)
    copy = pltpu.make_async_copy(out, out_ref, sem)
    copy.start()
    copy.wait()


def lower_kernel(*refs):
    ins, (core_ref, upper_ref, high_ref, low_ref, base_ref) = refs[:6], refs[6:11]
    end_ref, keep_ref, send_ref, upper, lower, base, high, low, parts, sems = refs[12:22]
    incoming = [
        pltpu.make_async_copy(high_ref, high, sems.at[1]),
        pltpu.make_async_copy(low_ref, low, sems.at[2]),
        pltpu.make_async_copy(upper_ref, upper, sems.at[0]),
        pltpu.make_async_copy(base_ref, base, sems.at[3]),
    ]

    def put(rows, c, value):
        lower[c, rows, :] = value

    transport(1, ins, refs[22:], put, incoming)
    for copy in incoming:
        copy.wait()
    core = core_ref[0]
    outgoing = []
    for kind, out_ref in ((1, send_ref), (0, keep_ref)):
        start = 4 * (core ^ kind)
        for i in (0, 2):
            c = start + i
            column = jnp.concatenate(
                [jnp.concatenate([upper[c + k], lower[c + k]], 0) for k in range(2)], 1
            )
            end = column + product(high[...], low[...], column)
            for k in range(2):
                column = end[:, k * LANES : (k + 1) * LANES]
                rest = base[c + k] - column
                base[c + k] = column
                for q in range(4):
                    parts[kind, 4 * (i + k) + q] = rest[q * PART : (q + 1) * PART]
            pair, some = pl.ds(c, 2), pl.ds(4 * i, 8)
            outgoing.append(pltpu.make_async_copy(parts.at[kind, some], out_ref.at[some], sems.at[4 + kind * 2 + i // 2]))
            outgoing.append(pltpu.make_async_copy(base.at[pair], end_ref.at[pair], sems.at[8 + kind * 2 + i // 2]))
            outgoing[-2].start()
            outgoing[-1].start()
    for copy in outgoing:
        copy.wait()


def pair_kernel(keep_ref, partner_ref, order_ref, pair_ref):
    pair_ref[...] = keep_ref[...] + partner_ref[...]


def scan_kernel(in_ref, order_ref, out_ref):
    def block(index, carry):
        here = pl.ds(pl.multiple_of(index * 8, 8), 8)
        total = jnp.zeros((8, LANES), F32)
        for k in range(PARTS):
            out_ref[k, here, :] = total
            total = total + in_ref[k, here, :]
        return carry

    lax.fori_loop(0, PART // 8, block, 0)


def share_kernel(core_ref, before_ref, keep_ref, order_ref, out_ref):
    first = (core_ref[0] == 0).astype(F32)
    out_ref[...] = before_ref[...] + first * keep_ref[...]


def finish_kernel(core_ref, base_ref, before_ref, partner_ref, other_ref, out_ref):
    core = core_ref[0]
    flat = out_ref.reshape(ROWS * COLS, LANES)
    second = (core == 1).astype(F32)
    for c in range(COLS):
        mine = core == c // 4
        i = c % 4
        for q in range(4):
            size = min(PART, ROWS - q * PART)
            own = before_ref[4 * i + q, :size] + second * partner_ref[4 * i + q, :size]
            earlier = jnp.where(mine, own, other_ref[4 * i + q, :size])
            flat[pl.ds(q * PART * COLS + c, size, stride=COLS), :] = (
                base_ref[c, q * PART : q * PART + size, :] + earlier
            )


def sort_kernel(me_ref, index_ref, frac_ref, order_ref, out_ref, chosen_ref, spread_ref):
    column_x = index_ref[0]
    bucket = lax.broadcasted_iota(jnp.int32, (TILES, SLOTS), 0)
    further = ((column_x >> 3) - me_ref[0] + TILES) & (TILES - 1)
    chosen = (bucket == further).astype(F32)
    before = lax.broadcasted_iota(jnp.int32, (SLOTS, SLOTS), 0) < lax.broadcasted_iota(jnp.int32, (SLOTS, SLOTS), 1)
    rank = jnp.dot(chosen.astype(BF16), before.astype(F32).astype(BF16), preferred_element_type=F32)
    place = jnp.sum(chosen * rank, axis=0, keepdims=True)
    spread = lax.broadcasted_iota(jnp.int32, (CAP, SLOTS), 0) == place.astype(jnp.int32)
    spread = spread.astype(F32)
    chosen_ref[...] = chosen
    spread_ref[...] = spread
    values = jnp.concatenate(
        [
            (column_x & (COLS - 1)).astype(F32),
            index_ref[1].astype(F32),
            index_ref[2].astype(F32),
            frac_ref[0],
            frac_ref[1],
            jnp.zeros((FIELDS - 5, SLOTS), F32),
        ],
        0,
    )
    for j in range(TILES):
        masked = values * chosen[j : j + 1, :]
        out_ref[j] = lax.dot_general(
            masked, spread, (((1,), (1,)), ((), ())), precision=HIGHEST, preferred_element_type=F32
        )


def observe_kernel(obs_ref, end_ref, order_ref, out_ref, end_high, end_low):
    for c in range(COLS):
        high, low = two_parts(end_ref[c])
        end_high[:, c * LANES : (c + 1) * LANES] = high
        end_low[:, c * LANES : (c + 1) * LANES] = low
    lanes = 2 * CAP
    for j in range(0, TILES, 2):
        fields = [jnp.concatenate([obs_ref[j, i : i + 1], obs_ref[j + 1, i : i + 1]], 1) for i in range(5)]
        column, line, row = [(f + 0.5).astype(jnp.int32) for f in fields[:3]]
        across, upward = fields[3:]
        y = lax.broadcasted_iota(jnp.int32, (LANES, lanes), 0)
        here, after = y == line, y == line + 1
        highs, lows = [], []
        for c in range(COLS):
            mine = column == c
            near = jnp.where(mine, 1.0 - across, 0.0)
            far = jnp.where(mine, across, 0.0)
            weight = jnp.where(here, near, jnp.where(after, far, 0.0))
            high, low = two_parts(weight)
            highs.append(high)
            lows.append(low)
        high, low = jnp.concatenate(highs, 0), jnp.concatenate(lows, 0)
        taken = jnp.dot(end_high[...], high, preferred_element_type=F32)
        taken = taken + jnp.dot(end_high[...], low, preferred_element_type=F32)
        taken = taken + jnp.dot(end_low[...], high, preferred_element_type=F32)
        r = lax.broadcasted_iota(jnp.int32, (PAD, lanes), 0)
        weight = jnp.where(r == row, 1.0 - upward, jnp.where(r == row + 1, upward, 0.0))
        value = jnp.sum(weight * taken, axis=0, keepdims=True)
        out_ref[j : j + 1, :] = value[:, :CAP]
        out_ref[j + 1 : j + 2, :] = value[:, CAP:]


def depart_kernel(count_ref, back_ref, chosen_ref, spread_ref, value_ref, out_ref):
    spread = jnp.dot(back_ref[...], spread_ref[...], precision=HIGHEST, preferred_element_type=F32)
    evolved = jnp.sum(spread * chosen_ref[...], axis=0, keepdims=True)
    live = lax.broadcasted_iota(jnp.int32, (1, SLOTS), 1) < count_ref[0, 0]
    out_ref[...] = jnp.where(live, value_ref[...] - evolved, 0.0)


def hop(blocks, bit, sign):
    moving = [j for j in range(TILES) if j & bit]
    parcel = jnp.concatenate([blocks[j] for j in moving], 0)
    parcel = lax.ppermute(parcel, "tile", [(i, (i + sign * bit) % TILES) for i in range(TILES)])
    size = blocks[0].shape[0]
    result = list(blocks)
    for at, j in enumerate(moving):
        result[j] = parcel[at * size : (at + 1) * size]
    return result


def per_device(
    increment, forcing, error_root, physics, coefficients, obs_index, obs_frac, obs_value, obs_count
):
    state = increment.reshape(ROWS, COLS, LANES)
    drive = forcing.reshape(ROWS, COLS, LANES)
    rates = coefficients.reshape(4, COLS, LANES)
    core = jnp.reshape(lax.axis_index("core"), (1,)).astype(jnp.int32)
    me = jnp.reshape(lax.axis_index("tile"), (1,)).astype(jnp.int32)
    field = PAD * COLS * LANES * 4

    to_west = [(i + 1, i) for i in range(TILES - 1)]
    to_east = [(i, i + 1) for i in range(TILES - 1)]

    wests, easts = pack(state, rates)
    halo0, halo1 = [
        (lax.ppermute(east, "tile", to_east), lax.ppermute(west, "tile", to_west))
        for west, east in zip(wests, easts)
    ]
    base, high, low = call(
        prepare_kernel,
        [shape(COLS, PAD, LANES), shape(PAD, PAD, dtype=BF16), shape(PAD, PAD, dtype=BF16)],
        (state, drive, error_root, physics.reshape(ROWS, ROWS)),
        WIDE,
        scratch=[
            pltpu.VMEM((ROWS, COLS, LANES), F32),
            pltpu.VMEM((ROWS, COLS, LANES), F32),
            pltpu.VMEM((ROWS, ROWS), F32),
            pltpu.VMEM((PAD, PAD), F32),
            pltpu.VMEM((PAD, 2 * LANES), F32),
            pltpu.VMEM((COLS, PAD, LANES), F32),
            pltpu.VMEM((PAD, PAD), BF16),
            pltpu.VMEM((PAD, PAD), BF16),
            pltpu.SemaphoreType.DMA((9,)),
        ],
        flops=8 * 10**9,
        moved=5 * field,
        far=(0, 1, 2),
        far_out=(0, 1, 2),
    )
    upper = call(
        upper_kernel,
        shape(COLS, CHUNKS[0][1], LANES),
        (state, rates, *halo0, *halo0),
        WIDE,
        scratch=[pltpu.VMEM((COLS, CHUNKS[0][1], LANES), F32), pltpu.SemaphoreType.DMA] + transport_scratch(0),
        flops=4 * 10**9,
        moved=field,
        far=range(6),
        far_out=(0,),
    )
    queries, chosen, spread = call(
        sort_kernel,
        [shape(TILES, FIELDS, CAP), shape(TILES, SLOTS), shape(CAP, SLOTS)],
        (me, obs_index, obs_frac, upper),
        8,
        flops=10**8,
        moved=10**6,
        smem=(0,),
        far=(3,),
    )
    blocks = hop([queries[j] for j in range(TILES)], 4, 1)
    parts = shape(PARTS, PART, LANES)
    end, keep, send = call(
        lower_kernel,
        [shape(COLS, PAD, LANES), parts, parts],
        (state, rates, *halo1, *halo0, core, upper, high, low, base, blocks[7]),
        WIDE,
        scratch=[
            pltpu.VMEM((COLS, CHUNKS[0][1], LANES), F32),
            pltpu.VMEM((COLS, CHUNKS[1][1], LANES), F32),
            pltpu.VMEM((COLS, PAD, LANES), F32),
            pltpu.VMEM((PAD, PAD), BF16),
            pltpu.VMEM((PAD, PAD), BF16),
            pltpu.VMEM((2, PARTS, PART, LANES), F32),
            pltpu.SemaphoreType.DMA((12,)),
        ]
        + transport_scratch(1),
        flops=6 * 10**9,
        moved=5 * field,
        smem=(6,),
        far=(0, 1, 2, 3, 4, 5, 7, 8, 9, 10, 11),
        far_out=range(3),
    )
    swap = [(0, 1), (1, 0)]
    partner = lax.ppermute(send, "core", swap)
    blocks = hop(blocks, 2, 1)
    pair = call(pair_kernel, parts, (keep, partner, blocks[7]), 6, flops=10**6, moved=2 * field)
    gathered = lax.all_to_all(pair, ("y", "x"), 0, 0, tiled=True)
    blocks = hop(blocks, 1, 1)
    arrived = jnp.concatenate(blocks, 0).reshape(TILES, FIELDS, CAP)
    found = call(
        observe_kernel,
        shape(TILES, CAP),
        (arrived, end, pair),
        10,
        scratch=[pltpu.VMEM((PAD, COLS * LANES), BF16), pltpu.VMEM((PAD, COLS * LANES), BF16)],
        flops=3 * 10**9,
        moved=field,
        far=(2,),
    )
    totals = call(scan_kernel, parts, (gathered, found), 6, flops=10**7, moved=field)
    before = lax.all_to_all(totals, ("y", "x"), 0, 0, tiled=True)
    back = [found[j : j + 1] for j in range(TILES)]
    for bit in (4, 2, 1):
        back = hop(back, bit, -1)
    departure = call(
        depart_kernel,
        shape(1, SLOTS),
        (obs_count, jnp.concatenate(back, 0), chosen, spread, obs_value),
        4,
        flops=10**7,
        moved=10**6,
        smem=(0,),
    )
    for_partner = call(
        share_kernel, parts, (core, before, keep, departure), 6, flops=10**7, moved=2 * field, smem=(0,), far=(3,)
    )
    other = lax.ppermute(for_partner, "core", swap)
    summed = call(
        finish_kernel,
        shape(ROWS, COLS, LANES),
        (core, base, before, partner, other),
        10,
        flops=10**7,
        moved=4 * field,
        smem=(0,),
    )
    return summed.reshape(increment.shape), departure


def solution(mesh):
    split = Mesh(mesh.devices.reshape(GRID_Y, GRID_X, CORES, TILES), ("y", "x", "core", "tile"))
    win = ("y", "x", "core")
    return jax.shard_map(
        per_device,
        mesh=split,
        in_specs=(
            P(win, None, None, "tile", None),
            P(win, None, None, "tile", None),
            P(),
            P(win, None, None),
            P(win, None, "tile", None),
            P(None, win, "tile"),
            P(None, win, "tile"),
            P(win, "tile"),
            P(win, "tile"),
        ),
        out_specs=(P(win, None, None, "tile", None), P(win, "tile")),
        check_vma=False,
    )
```

time: 138 us -> 134 us (0.971)
  waiting for transfers between devices: 28.2 us -> 48.7 us
  starting transfers between devices: 52.7 us -> 38.1 us
  local copies, waits for them, and re-layouts: 17.7 us -> 7.98 us
  Pallas kernels: 35.5 us -> 37 us
    ppermute x0 -> x6, waiting for transfers between devices: none -> 19.8 us  [hop(): lax.ppermute(parcel, 'tile', [(i, (i + sign * bit) % TILES) for i in rang...]
    all_to_all x2 -> x0, starting transfers between devices: 16.9 us -> none  [the longest x1 9.99 us: per_device(): arrived = lax.all_to_all(handed, 'tile', 0, 0, tiled=True)]
    ppermute x3 -> x2, waiting for transfers between devices: 0.01 us -> 12.5 us  [per_device(): lax.ppermute(east, 'tile', to_east)]
    unnamed x55 -> x38, local copies, waits for them, and re-layouts: 17.7 us -> 7.91 us
    ppermute x0 -> x6, starting transfers between devices: none -> 9.39 us  [hop(): lax.ppermute(parcel, 'tile', [(i, (i + sign * bit) % TILES) for i in rang...]
    ppermute x3 -> x2, starting transfers between devices: 14.7 us -> 7.08 us  [per_device(): lax.ppermute(east, 'tile', to_east)]
    all_to_all x1, waiting for transfers between devices: 8.54 us -> 2.38 us  [per_device(): gathered = lax.all_to_all(pair, ('y', 'x'), 0, 0, tiled=True)]
    all_to_all x2 -> x0, waiting for transfers between devices: 4.94 us -> none  [the longest x1 4.93 us: per_device(): back = lax.all_to_all(found, 'tile', 0, 0, tiled=True)]
  transfers between devices with their start and end apart: 12 -> 14, of which waited for: 5 -> 11; matrix products, arithmetic and copies ran while one was open for 1% -> 1% of each run, Pallas kernels for 22% -> 8%
where the time goes in v3:
time: 134 us; the launch traced here: 133 us
  waiting for transfers between devices  48.7 us (36%)
  starting transfers between devices  38.1 us (28%)
  Pallas kernels  37 us (28%)
  local copies, waits for them, and re-layouts  7.98 us (6%)
  between operations  1.57 us (1%)
    pallas_call x11, Pallas kernels, call(): pl.pallas_call(body, out_shape=outs, in_specs=specs, out_specs=out_specs...  37 us
    ppermute x6, waiting for transfers between devices, hop(): lax.ppermute(parcel, 'tile', [(i, (i + sign * bit) % TILES) for i in rang...  19.8 us
    ppermute x2, waiting for transfers between devices, per_device(): lax.ppermute(east, 'tile', to_east)  12.5 us
    ppermute x6, starting transfers between devices, hop(): lax.ppermute(parcel, 'tile', [(i, (i + sign * bit) % TILES) for i in rang...  9.39 us
    unnamed x38, local copies, waits for them, and re-layouts  7.91 us
    ppermute x2, starting transfers between devices, per_device(): lax.ppermute(east, 'tile', to_east)  7.08 us
    all_to_all x1, starting transfers between devices, per_device(): gathered = lax.all_to_all(pair, ('y', 'x'), 0, 0, tiled=True)  6.75 us
    all_to_all x1, waiting for transfers between devices, per_device(): before = lax.all_to_all(totals, ('y', 'x'), 0, 0, tiled=True)  5.79 us
  transfers between devices with their start and end apart: 14, of which 11 were waited for; matrix products, arithmetic and copies ran while one was open for 1% of the time, Pallas kernels for 8%

profile of v3, /device:TPU:1, one launch (start us, length us, event | category | flops | bytes accessed | tf_op | source)
XLA Modules:
  0.0 133.4 jit_solution(4590315640747158764)
XLA Ops:
  0.6 2.8 %shard_map.105 = (f32[6,216,128]{2,1,0:T(8,128)}, f32[6,208,128]{2,1,0:T(8,128)}, f32[6,216,128]{2,1,0:T(8,128)}, f32[6,208,128]{2,1,0:T(8,128)}) custom-call(f32[411,8,128]{2,1,0:T(8,128)} %bitcast.27, f32[4,8,128]{2,1,0:T(8,128)} %bitcast.33), custom_call_target="tpu_custom_call" | custom-call | bytes 5111808 | tf_op jit(solution)/shard_map/pallas_call | solution.py:41
  3.5 4.4 %collective-permute-start.2 = (f32[6,216,128]{2,1,0:T(8,128)}, f32[6,216,128]{2,1,0:T(8,128)S(1)}, u32[]{:S(2)}, u32[]{:S(2)}) collective-permute-start(f32[6,216,128]{2,1,0:T(8,128)} %get-tuple-element.18), channel_id=1, source_target_pairs={{0,1},{1,2},{2,3},{3,4},{4,5},{5,6},{6,7},{8,9},{9,10},{10,11},{11... | collective-permute-start | bytes 1990664 | tf_op jit(solution)/shard_map/ppermute | solution.py:452
  7.9 1.3 collective-permute-start.3
  9.3 12.5 %collective-permute-done.2.refs_2_.refs_4_ = f32[6,216,128]{2,1,0:T(8,128)S(1)} collective-permute-done((f32[6,216,128]{2,1,0:T(8,128)}, f32[6,216,128]{2,1,0:T(8,128)S(1)}, u32[]{:S(2)}, u32[]{:S(2)}) %collective-permute-start.2) | collective-permute-done | bytes 663584 | tf_op jit(solution)/shard_map/ppermute | solution.py:452
  21.7 4.0 %collective-permute-done.3.refs_3_.refs_5_ = f32[6,216,128]{2,1,0:T(8,128)S(1)} collective-permute-done((f32[6,216,128]{2,1,0:T(8,128)}, f32[6,216,128]{2,1,0:T(8,128)S(1)}, u32[]{:S(2)}, u32[]{:S(2)}) %collective-permute-start.3) | collective-permute-done | bytes 663584 | tf_op jit(solution)/shard_map/ppermute | solution.py:452
  26.6 7.4 %shard_map.106.order_ref.refs_7_ = f32[8,208,128]{2,1,0:T(8,128)} custom-call(f32[411,8,128]{2,1,0:T(8,128)} %bitcast.28, f32[4,8,128]{2,1,0:T(8,128)} %bitcast.34, f32[6,216,128]{2,1,0:T(8,128)} %copy-done.10, f32[6,216,128]{2,1,0:T(8,128)} %copy-done.11, f32[6,216,128]{2,1,0:T(8,128)} %copy-done.10, f32[6,216,128]{2,1,0:T(8,128)} %copy-done.11), custom_call_target="tpu_custom_call" | custom-call | flops 4000000000 | bytes 1703936 | tf_op jit(solution)/shard_map/pallas_call | solution.py:41
  34.1 1.1 copy-done.3
  35.2 1.9 %shard_map.107 = (f32[8,8,128]{2,1,0:T(8,128)S(1)}, f32[8,512]{1,0:T(8,128)S(1)}, f32[128,512]{1,0:T(8,128)S(1)}) custom-call(s32[1]{0:T(128)} %bitcast.4.me_ref, s32[3,1,512]{2,1,0:T(1,128)S(1)} %copy-done.5, f32[2,1,512]{2,1,0:T(1,128)S(1)} %copy-done.6, f32[8,208,128]{2,1,0:T(8,128)S(1)} %copy-done.3), custom_call_target="tpu_custom_call" | custom-call | flops 100000000 | bytes 1000000 | tf_op jit(solution)/shard_map/pallas_call | solution.py:41
  37.1 5.7 %collective-permute-start.4 = (f32[32,128]{1,0:T(8,128)S(1)}, f32[32,128]{1,0:T(8,128)S(1)}, u32[]{:S(2)}, u32[]{:S(2)}) collective-permute-start(f32[32,128]{1,0:T(8,128)S(1)} %pad_maximum_fusion), channel_id=1, source_target_pairs={{0,4},{1,5},{2,6},{3,7},{4,0},{5,1},{6,2},{7,3},{8,12},{9,13},{10,... | collective-permute-start | bytes 49160 | tf_op jit(solution)/shard_map/ppermute | solution.py:429
  42.9 2.7 %collective-permute-start = (f32[6,208,128]{2,1,0:T(8,128)}, f32[6,208,128]{2,1,0:T(8,128)S(1)}, u32[]{:S(2)}, u32[]{:S(2)}) collective-permute-start(f32[6,208,128]{2,1,0:T(8,128)} %get-tuple-element.16), channel_id=1, source_target_pairs={{0,1},{1,2},{2,3},{3,4},{4,5},{5,6},{6,7},{8,9},{9,10},{10,11},{11... | collective-permute-start | bytes 1916936 | tf_op jit(solution)/shard_map/ppermute | solution.py:452
  45.6 1.3 collective-permute-start.1
  47.8 2.6 %collective-permute-start.6 = (f32[32,128]{1,0:T(8,128)S(1)}, f32[32,128]{1,0:T(8,128)S(1)}, u32[]{:S(2)}, u32[]{:S(2)}) collective-permute-start(f32[32,128]{1,0:T(8,128)S(1)} %pad_maximum_fusion.1), channel_id=1, source_target_pairs={{0,2},{1,3},{2,4},{3,5},{4,6},{5,7},{6,0},{7,1},{8,10},{9,11},{10,... | collective-permute-start | bytes 49160 | tf_op jit(solution)/shard_map/ppermute | solution.py:429
  50.4 6.5 %shard_map.104 = (f32[8,416,128]{2,1,0:T(8,128)}, bf16[416,416]{1,0:T(8,128)(2,1)}, bf16[416,416]{1,0:T(8,128)(2,1)}) custom-call(f32[411,8,128]{2,1,0:T(8,128)} %bitcast.29, f32[411,8,128]{2,1,0:T(8,128)} %bitcast.36, f32[411,411]{1,0:T(8,128)} %root_ref.1, f32[411,411]{1,0:T(8,128)} %bitcast.32), custom_call_target="tpu_custom_call" | custom-call | flops 8000000000 | bytes 8519680 | tf_op jit(solution)/shard_map/pallas_call | solution.py:41
  56.9 4.9 %collective-permute-done.6 = f32[32,128]{1,0:T(8,128)S(1)} collective-permute-done((f32[32,128]{1,0:T(8,128)S(1)}, f32[32,128]{1,0:T(8,128)S(1)}, u32[]{:S(2)}, u32[]{:S(2)}) %collective-permute-start.6) | collective-permute-done | bytes 16416 | tf_op jit(solution)/shard_map/ppermute | solution.py:429
  61.8 3.8 %collective-permute-done.7 = f32[32,128]{1,0:T(8,128)S(1)} collective-permute-done((f32[32,128]{1,0:T(8,128)S(1)}, f32[32,128]{1,0:T(8,128)S(1)}, u32[]{:S(2)}, u32[]{:S(2)}) %collective-permute-start.7) | collective-permute-done | bytes 16416 | tf_op jit(solution)/shard_map/ppermute | solution.py:429
  67.3 10.0 %shard_map.108 = (f32[8,416,128]{2,1,0:T(8,128)}, f32[16,104,128]{2,1,0:T(8,128)}, f32[16,104,128]{2,1,0:T(8,128)}) custom-call(f32[411,8,128]{2,1,0:T(8,128)} %bitcast.30, f32[4,8,128]{2,1,0:T(8,128)} %bitcast.35, f32[6,208,128]{2,1,0:T(8,128)} %copy-done.13, f32[6,208,128]{2,1,0:T(8,128)} %copy-done.14, f32[6,216,128]{2,1,0:T(8,128)} %copy-done.10, ...), custom_call_target="tpu_custom_call" | custom-call | flops 6000000000 | bytes 8519680 | tf_op jit(solution)/shard_map/pallas_call | solution.py:41
  77.2 5.0 %collective-permute-start.5 = (f32[16,104,128]{2,1,0:T(8,128)}, f32[16,104,128]{2,1,0:T(8,128)S(1)}, u32[]{:S(2)}, u32[]{:S(2)}) collective-permute-start(f32[16,104,128]{2,1,0:T(8,128)} %get-tuple-element.24), channel_id=1, source_target_pairs={{0,8},{8,0},{1,9},{9,1},{2,10},{10,2},{3,11},{11,3},{4,12},{12,4},... | collective-permute-start | bytes 2555912 | tf_op jit(solution)/shard_map/ppermute | solution.py:521
  82.2 2.2 %collective-permute-done.5.partner_ref = f32[16,104,128]{2,1,0:T(8,128)S(1)} collective-permute-done((f32[16,104,128]{2,1,0:T(8,128)}, f32[16,104,128]{2,1,0:T(8,128)S(1)}, u32[]{:S(2)}, u32[]{:S(2)}) %collective-permute-start.5) | collective-permute-done | bytes 852000 | tf_op jit(solution)/shard_map/ppermute | solution.py:521
  84.4 1.2 copy-done
  86.6 6.8 %all-to-all-start = ((f32[16,104,128]{2,1,0:T(8,128)}), f32[16,104,128]{2,1,0:T(8,128)S(1)}, u32[]{:S(2)}, u32[]{:S(2)}) async-start(f32[16,104,128]{2,1,0:T(8,128)} %shard_map.109.order_ref), calls=%async_computation | async-start | bytes 1703936 | tf_op jit(solution)/shard_map/all_to_all | solution.py:524
  93.3 1.4 %copy-done.8 = f32[8,416,128]{2,1,0:T(8,128)S(1)} copy-done((f32[8,416,128]{2,1,0:T(8,128)S(1)}, f32[8,416,128]{2,1,0:T(8,128)}, u32[]{:S(2)}) %copy-start.8) | copy-done | bytes 1703960
  94.8 3.6 %shard_map.110.order_ref = f32[8,128]{1,0:T(8,128)S(1)} custom-call(f32[8,8,128]{2,1,0:T(8,128)S(1)} %bitcast.26, f32[8,416,128]{2,1,0:T(8,128)S(1)} %copy-done.8, f32[16,104,128]{2,1,0:T(8,128)} %shard_map.109.order_ref), custom_call_target="tpu_custom_call" | custom-call | flops 3000000000 | bytes 1703936 | tf_op jit(solution)/shard_map/pallas_call | solution.py:41
  98.7 6.5 %collective-permute-done.8 = f32[4,128]{1,0:T(4,128)S(1)} collective-permute-done((f32[4,128]{1,0:T(4,128)S(1)}, f32[4,128]{1,0:T(4,128)S(1)}, u32[]{:S(2)}, u32[]{:S(2)}) %collective-permute-start.8) | collective-permute-done | bytes 2080 | tf_op jit(solution)/shard_map/ppermute | solution.py:429
  105.2 2.4 %all-to-all-done.in_ref = f32[16,104,128]{2,1,0:T(8,128)S(1)} async-done(((f32[16,104,128]{2,1,0:T(8,128)}), f32[16,104,128]{2,1,0:T(8,128)S(1)}, u32[]{:S(2)}, u32[]{:S(2)}) %all-to-all-start) | async-done | bytes 852000 | tf_op jit(solution)/shard_map/all_to_all | solution.py:524
  107.5 1.1 shard_map.111
  108.7 4.0 %all-to-all-start.1 = ((f32[16,104,128]{2,1,0:T(8,128)}), f32[16,104,128]{2,1,0:T(8,128)S(1)}, u32[]{:S(2)}, u32[]{:S(2)}) async-start(f32[16,104,128]{2,1,0:T(8,128)} %shard_map.111), calls=%async_computation.1 | async-start | bytes 1703936 | tf_op jit(solution)/shard_map/all_to_all | solution.py:538
  112.8 3.3 %collective-permute-done.9 = f32[4,128]{1,0:T(4,128)S(1)} collective-permute-done((f32[4,128]{1,0:T(4,128)S(1)}, f32[4,128]{1,0:T(4,128)S(1)}, u32[]{:S(2)}, u32[]{:S(2)}) %collective-permute-start.9) | collective-permute-done | bytes 2080 | tf_op jit(solution)/shard_map/ppermute | solution.py:429
  117.5 1.4 %collective-permute-done.10 = f32[4,128]{1,0:T(4,128)S(1)} collective-permute-done((f32[4,128]{1,0:T(4,128)S(1)}, f32[4,128]{1,0:T(4,128)S(1)}, u32[]{:S(2)}, u32[]{:S(2)}) %collective-permute-start.10) | collective-permute-done | bytes 2080 | tf_op jit(solution)/shard_map/ppermute | solution.py:429
  119.8 5.8 %all-to-all-done.1.before_ref = f32[16,104,128]{2,1,0:T(8,128)S(1)} async-done(((f32[16,104,128]{2,1,0:T(8,128)}), f32[16,104,128]{2,1,0:T(8,128)S(1)}, u32[]{:S(2)}, u32[]{:S(2)}) %all-to-all-start.1) | async-done | bytes 852000 | tf_op jit(solution)/shard_map/all_to_all | solution.py:538
  126.4 3.3 %collective-permute-start.11 = (f32[16,104,128]{2,1,0:T(8,128)S(1)}, f32[16,104,128]{2,1,0:T(8,128)S(1)}, u32[]{:S(2)}, u32[]{:S(2)}) collective-permute-start(f32[16,104,128]{2,1,0:T(8,128)S(1)} %shard_map.113), channel_id=1, source_target_pairs={{0,8},{8,0},{1,9},{9,1},{2,10},{10,2},{3,11},{11,3},{4,12},{12,4},... | collective-permute-start | bytes 2555912 | tf_op jit(solution)/shard_map/ppermute | solution.py:554
  129.7 2.0 %collective-permute-done.11.other_ref = f32[16,104,128]{2,1,0:T(8,128)S(1)} collective-permute-done((f32[16,104,128]{2,1,0:T(8,128)S(1)}, f32[16,104,128]{2,1,0:T(8,128)S(1)}, u32[]{:S(2)}, u32[]{:S(2)}) %collective-permute-start.11) | collective-permute-done | bytes 852000 | tf_op jit(solution)/shard_map/ppermute | solution.py:554
  131.7 1.7 %shard_map.114 = f32[411,8,128]{2,1,0:T(8,128)} custom-call(s32[1]{0:T(128)} %bitcast.refs_6_.core_ref, f32[8,416,128]{2,1,0:T(8,128)S(1)} %copy-done.2, f32[16,104,128]{2,1,0:T(8,128)S(1)} %all-to-all-done.1.before_ref, f32[16,104,128]{2,1,0:T(8,128)S(1)} %collective-permute-done.5.partner_ref, f32[16,104,128]{2,1,0:T(8,128)S(1)} %collective-permute-done.11.other_ref), custom_call_target="tpu_custom_call" | custom-call | flops 10000000 | bytes 6815744 | tf_op jit(solution)/shard_map/pallas_call | solution.py:41
  (63 shorter events, 7.3 us)
Async XLA Ops:
  3.5 18.3 %collective-permute-start.2 = (f32[6,216,128]{2,1,0:T(8,128)}, f32[6,216,128]{2,1,0:T(8,128)S(1)}, u32[]{:S(2)}, u32[]{:S(2)}) collective-permute-start(f32[6,216,128]{2,1,0:T(8,128)} %get-tuple-element.18), channel_id=1, source_target_pairs={{0,1},{1,2},{2,3},{3,4},{4,5},{5,6},{6,7},{8,9},{9,10},{10,11},{11... | collective-permute-start | bytes 1990664 | tf_op jit(solution)/shard_map/ppermute | solution.py:452
  7.9 17.9 %collective-permute-start.3 = (f32[6,216,128]{2,1,0:T(8,128)}, f32[6,216,128]{2,1,0:T(8,128)S(1)}, u32[]{:S(2)}, u32[]{:S(2)}) collective-permute-start(f32[6,216,128]{2,1,0:T(8,128)} %get-tuple-element.19), channel_id=1, source_target_pairs={{1,0},{2,1},{3,2},{4,3},{5,4},{6,5},{7,6},{9,8},{10,9},{11,10},{12... | collective-permute-start | bytes 1990664 | tf_op jit(solution)/shard_map/ppermute | solution.py:452
  9.2 24.8 %copy-start.5 = (s32[3,1,512]{2,1,0:T(1,128)S(1)}, s32[3,1,512]{2,1,0:T(1,128)}, u32[]{:S(2)}) copy-start(s32[3,1,512]{2,1,0:T(1,128)} %index_ref.1) | copy-start | bytes 18436
  9.2 24.8 %copy-start.6 = (f32[2,1,512]{2,1,0:T(1,128)S(1)}, f32[2,1,512]{2,1,0:T(1,128)}, u32[]{:S(2)}) copy-start(f32[2,1,512]{2,1,0:T(1,128)} %frac_ref.1) | copy-start | bytes 12292
  9.2 36.3 %copy-start.12 = (f32[6,208,128]{2,1,0:T(8,128)S(1)}, f32[6,208,128]{2,1,0:T(8,128)}, u32[]{:S(2)}) copy-start(f32[6,208,128]{2,1,0:T(8,128)} %get-tuple-element.17) | copy-start | bytes 1916932
  9.2 37.6 %copy-start.9 = (f32[1,411,411]{2,0,1:T(1,128)S(1)}, f32[1,411,411]{2,0,1:T(1,128)}, u32[]{:S(2)}) copy-start(f32[1,411,411]{2,0,1:T(1,128)} %param.12) | copy-start | bytes 2027056
  21.7 4.0 %copy-start.10 = (f32[6,216,128]{2,1,0:T(8,128)}, f32[6,216,128]{2,1,0:T(8,128)S(1)}, u32[]{:S(2)}) copy-start(f32[6,216,128]{2,1,0:T(8,128)S(1)} %collective-permute-done.2.refs_2_.refs_4_) | copy-start | bytes 1990660
  25.8 0.8 copy-start.11
  34.1 1.2 copy-start.3
  37.1 10.7 %collective-permute-start.4 = (f32[32,128]{1,0:T(8,128)S(1)}, f32[32,128]{1,0:T(8,128)S(1)}, u32[]{:S(2)}, u32[]{:S(2)}) collective-permute-start(f32[32,128]{1,0:T(8,128)S(1)} %pad_maximum_fusion), channel_id=1, source_target_pairs={{0,4},{1,5},{2,6},{3,7},{4,0},{5,1},{6,2},{7,3},{8,12},{9,13},{10,... | collective-permute-start | bytes 49160 | tf_op jit(solution)/shard_map/ppermute | solution.py:429
  42.9 23.3 %collective-permute-start = (f32[6,208,128]{2,1,0:T(8,128)}, f32[6,208,128]{2,1,0:T(8,128)S(1)}, u32[]{:S(2)}, u32[]{:S(2)}) collective-permute-start(f32[6,208,128]{2,1,0:T(8,128)} %get-tuple-element.16), channel_id=1, source_target_pairs={{0,1},{1,2},{2,3},{3,4},{4,5},{5,6},{6,7},{8,9},{9,10},{10,11},{11... | collective-permute-start | bytes 1916936 | tf_op jit(solution)/shard_map/ppermute | solution.py:452
  45.6 20.6 %collective-permute-start.1 = (f32[6,208,128]{2,1,0:T(8,128)S(1)}, f32[6,208,128]{2,1,0:T(8,128)S(1)}, u32[]{:S(2)}, u32[]{:S(2)}) collective-permute-start(f32[6,208,128]{2,1,0:T(8,128)S(1)} %copy-done.12), channel_id=1, source_target_pairs={{1,0},{2,1},{3,2},{4,3},{5,4},{6,5},{7,6},{9,8},{10,9},{11,10},{12... | collective-permute-start | bytes 1916936 | tf_op jit(solution)/shard_map/ppermute | solution.py:452
  47.8 13.9 %collective-permute-start.6 = (f32[32,128]{1,0:T(8,128)S(1)}, f32[32,128]{1,0:T(8,128)S(1)}, u32[]{:S(2)}, u32[]{:S(2)}) collective-permute-start(f32[32,128]{1,0:T(8,128)S(1)} %pad_maximum_fusion.1), channel_id=1, source_target_pairs={{0,2},{1,3},{2,4},{3,5},{4,6},{5,7},{6,0},{7,1},{8,10},{9,11},{10,... | collective-permute-start | bytes 49160 | tf_op jit(solution)/shard_map/ppermute | solution.py:429
  61.8 3.8 %collective-permute-start.7 = (f32[32,128]{1,0:T(8,128)S(1)}, f32[32,128]{1,0:T(8,128)S(1)}, u32[]{:S(2)}, u32[]{:S(2)}) collective-permute-start(f32[32,128]{1,0:T(8,128)S(1)} %pad_maximum_fusion.2), channel_id=1, source_target_pairs={{0,1},{1,2},{2,3},{3,4},{4,5},{5,6},{6,7},{7,0},{8,9},{9,10},{10,1... | collective-permute-start | bytes 49160 | tf_op jit(solution)/shard_map/ppermute | solution.py:429
  66.2 0.8 copy-start.13
  66.2 1.0 copy-start.14
  77.2 7.2 %collective-permute-start.5 = (f32[16,104,128]{2,1,0:T(8,128)}, f32[16,104,128]{2,1,0:T(8,128)S(1)}, u32[]{:S(2)}, u32[]{:S(2)}) collective-permute-start(f32[16,104,128]{2,1,0:T(8,128)} %get-tuple-element.24), channel_id=1, source_target_pairs={{0,8},{8,0},{1,9},{9,1},{2,10},{10,2},{3,11},{11,3},{4,12},{12,4},... | collective-permute-start | bytes 2555912 | tf_op jit(solution)/shard_map/ppermute | solution.py:521
  84.4 1.2 copy-start
  86.6 21.0 %all-to-all-start = ((f32[16,104,128]{2,1,0:T(8,128)}), f32[16,104,128]{2,1,0:T(8,128)S(1)}, u32[]{:S(2)}, u32[]{:S(2)}) async-start(f32[16,104,128]{2,1,0:T(8,128)} %shard_map.109.order_ref), calls=%async_computation | async-start | bytes 1703936 | tf_op jit(solution)/shard_map/all_to_all | solution.py:524
  93.3 1.5 %copy-start.8 = (f32[8,416,128]{2,1,0:T(8,128)S(1)}, f32[8,416,128]{2,1,0:T(8,128)}, u32[]{:S(2)}) copy-start(f32[8,416,128]{2,1,0:T(8,128)} %get-tuple-element.25.end_ref) | copy-start | bytes 5111812
  98.4 6.7 %collective-permute-start.8 = (f32[4,128]{1,0:T(4,128)S(1)}, f32[4,128]{1,0:T(4,128)S(1)}, u32[]{:S(2)}, u32[]{:S(2)}) collective-permute-start(f32[4,128]{1,0:T(4,128)S(1)} %slice.137), channel_id=1, source_target_pairs={{0,4},{1,5},{2,6},{3,7},{4,0},{5,1},{6,2},{7,3},{8,12},{9,13},{10,... | collective-permute-start | bytes 6152 | tf_op jit(solution)/shard_map/ppermute | solution.py:429
  105.1 13.8 %copy-start.7 = (f32[1,512]{1,0:T(1,128)S(1)}, f32[1,512]{1,0:T(1,128)}, u32[]{:S(2)}) copy-start(f32[1,512]{1,0:T(1,128)} %value_ref.1) | copy-start | bytes 6148
  105.2 20.4 %copy-start.1 = (f32[16,104,128]{2,1,0:T(8,128)S(1)}, f32[16,104,128]{2,1,0:T(8,128)}, u32[]{:S(2)}) copy-start(f32[16,104,128]{2,1,0:T(8,128)} %get-tuple-element.23.keep_ref) | copy-start | bytes 2555908
  108.7 16.9 %all-to-all-start.1 = ((f32[16,104,128]{2,1,0:T(8,128)}), f32[16,104,128]{2,1,0:T(8,128)S(1)}, u32[]{:S(2)}, u32[]{:S(2)}) async-start(f32[16,104,128]{2,1,0:T(8,128)} %shard_map.111), calls=%async_computation.1 | async-start | bytes 1703936 | tf_op jit(solution)/shard_map/all_to_all | solution.py:538
  112.7 3.4 %collective-permute-start.9 = (f32[4,128]{1,0:T(4,128)S(1)}, f32[4,128]{1,0:T(4,128)S(1)}, u32[]{:S(2)}, u32[]{:S(2)}) collective-permute-start(f32[4,128]{1,0:T(4,128)S(1)} %pad_maximum_fusion.3), channel_id=1, source_target_pairs={{0,6},{1,7},{2,0},{3,1},{4,2},{5,3},{6,4},{7,5},{8,14},{9,15},{10,... | collective-permute-start | bytes 6152 | tf_op jit(solution)/shard_map/ppermute | solution.py:429
  116.1 2.8 %collective-permute-start.10 = (f32[4,128]{1,0:T(4,128)S(1)}, f32[4,128]{1,0:T(4,128)S(1)}, u32[]{:S(2)}, u32[]{:S(2)}) collective-permute-start(f32[4,128]{1,0:T(4,128)S(1)} %pad_maximum_fusion.4), channel_id=1, source_target_pairs={{0,7},{1,0},{2,1},{3,2},{4,3},{5,4},{6,5},{7,6},{8,15},{9,8},{10,9... | collective-permute-start | bytes 6152 | tf_op jit(solution)/shard_map/ppermute | solution.py:429
  125.6 0.7 copy-start.4
  126.3 5.4 %copy-start.2 = (f32[8,416,128]{2,1,0:T(8,128)S(1)}, f32[8,416,128]{2,1,0:T(8,128)}, u32[]{:S(2)}) copy-start(f32[8,416,128]{2,1,0:T(8,128)} %get-tuple-element.15.refs_10_.base_ref) | copy-start | bytes 5111812
  126.4 5.3 %collective-permute-start.11 = (f32[16,104,128]{2,1,0:T(8,128)S(1)}, f32[16,104,128]{2,1,0:T(8,128)S(1)}, u32[]{:S(2)}, u32[]{:S(2)}) collective-permute-start(f32[16,104,128]{2,1,0:T(8,128)S(1)} %shard_map.113), channel_id=1, source_target_pairs={{0,8},{8,0},{1,9},{9,1},{2,10},{10,2},{3,11},{11,3},{4,12},{12,4},... | collective-permute-start | bytes 2555912 | tf_op jit(solution)/shard_map/ppermute | solution.py:554

commit v4 on v3

--- a/solution.py
+++ b/solution.py
@@ -16,7 +16,7 @@
 PARTS = 16
 PART = 104
 TILES = 8
-CHUNKS = ((0, 208), (208, 208))
+HALF = 208
 SLOTS = 512
 CAP = 128
 FIELDS = 8
@@ -28,9 +28,11 @@
 WIDE = 56
 
 
-def call(body, outs, ins, mib, scratch=(), flops=0, moved=0, smem=(), far=(), far_out=()):
+def call(body, outs, ins, mib, scratch=(), flops=0, moved=0, smem=(), far=(), far_out=(), unread=()):
     specs = [
-        pl.BlockSpec(memory_space=pltpu.SMEM if at in smem else pltpu.HBM if at in far else pltpu.VMEM)
+        pl.BlockSpec(
+            memory_space=pltpu.SMEM if at in smem else pltpu.HBM if at in far else pl.ANY if at in unread else pltpu.VMEM
+        )
         for at in range(len(ins))
     ]
     many = isinstance(outs, (list, tuple))
@@ -66,36 +68,32 @@
     return total + jnp.dot(left_low, high, preferred_element_type=F32)
 
 
-def pack_kernel(inc_ref, rate_ref, *refs):
-    count = len(CHUNKS)
-    wests, easts = refs[:count], refs[count : 2 * count]
-    held, rates = refs[2 * count : 2 * count + 2]
-    west_bufs = refs[2 * count + 2 : 3 * count + 2]
-    east_bufs = refs[3 * count + 2 : 4 * count + 2]
-    in_sems, out_sems = refs[4 * count + 2 :]
+def pack_kernel(inc_ref, rate_ref, west_ref, east_ref, held, rates, west, east, in_sems, out_sems):
+    count = PAD // PART
     incoming = [pltpu.make_async_copy(rate_ref, rates, in_sems.at[count])]
-    for at, (start, size) in enumerate(CHUNKS):
-        rows = pl.ds(start, min(size, ROWS - start))
-        incoming.append(pltpu.make_async_copy(inc_ref.at[rows], held.at[rows], in_sems.at[at]))
+    for b in range(count):
+        rows = pl.ds(b * PART, min(PART, ROWS - b * PART))
+        incoming.append(pltpu.make_async_copy(inc_ref.at[rows], held.at[rows], in_sems.at[b]))
     for copy in incoming:
         copy.start()
-    held[ROWS:] = jnp.zeros((PAD - ROWS, COLS, LANES), F32)
     flat = held.reshape(PAD * COLS, LANES)
     outgoing = []
     incoming[0].wait()
-    for at, (start, size) in enumerate(CHUNKS):
-        incoming[at + 1].wait()
+    for b in range(count):
+        incoming[b + 1].wait()
+        size = min(PART, ROWS - b * PART)
         for c in range(COLS):
-            column = flat[pl.ds(start * COLS + c, size, stride=COLS), :]
-            if at == 0:
+            column = flat[pl.ds(b * PART * COLS + c, size, stride=COLS), :]
+            if size < PART:
                 weights = [rates[i, c : c + 1, :] for i in range(4)]
-                column = jnp.concatenate([column] + weights + [jnp.zeros((4, LANES), F32)], 0)
+                column = jnp.concatenate([column] + weights + [jnp.zeros((1, LANES), F32)], 0)
             if c < STEPS:
-                west_bufs[at][c] = column
+                west[c, b * PART : (b + 1) * PART, :] = column
             if c >= COLS - STEPS:
-                east_bufs[at][c - COLS + STEPS] = column
-        outgoing.append(pltpu.make_async_copy(west_bufs[at], wests[at], out_sems.at[2 * at]))
-        outgoing.append(pltpu.make_async_copy(east_bufs[at], easts[at], out_sems.at[2 * at + 1]))
+                east[c - COLS + STEPS, b * PART : (b + 1) * PART, :] = column
+        rows = pl.ds(b * PART, PART)
+        outgoing.append(pltpu.make_async_copy(west.at[:, rows], west_ref.at[:, rows], out_sems.at[2 * b]))
+        outgoing.append(pltpu.make_async_copy(east.at[:, rows], east_ref.at[:, rows], out_sems.at[2 * b + 1]))
         outgoing[-2].start()
         outgoing[-1].start()
     for copy in outgoing:
@@ -103,25 +101,28 @@
 
 
 def pack(state, rates):
-    dims = [(STEPS, size + (8 if at == 0 else 0), LANES) for at, (_, size) in enumerate(CHUNKS)]
-    count = len(CHUNKS)
-    outs = call(
+    halo = shape(STEPS, PAD, LANES)
+    return call(
         pack_kernel,
-        [shape(*d) for d in dims] * 2,
+        [halo, halo],
         (state, rates),
         WIDE,
-        scratch=[pltpu.VMEM((PAD, COLS, LANES), F32), pltpu.VMEM((4, COLS, LANES), F32)]
-        + [pltpu.VMEM(d, F32) for d in dims] * 2
-        + [pltpu.SemaphoreType.DMA((count + 1,)), pltpu.SemaphoreType.DMA((2 * count,))],
+        scratch=[
+            pltpu.VMEM((PAD, COLS, LANES), F32),
+            pltpu.VMEM((4, COLS, LANES), F32),
+            pltpu.VMEM((STEPS, PAD, LANES), F32),
+            pltpu.VMEM((STEPS, PAD, LANES), F32),
+            pltpu.SemaphoreType.DMA((PAD // PART + 1,)),
+            pltpu.SemaphoreType.DMA((2 * PAD // PART,)),
+        ],
         moved=3 * PAD * COLS * LANES * 4,
         far=(0, 1),
-        far_out=range(2 * count),
-    )
-    return outs[:count], outs[count:]
+        far_out=(0, 1),
+    )
 
 
 def prepare_kernel(
-    inc_ref, forcing_ref, root_ref, physics_ref, base_ref, high_ref, low_ref,
+    inc_ref, forcing_ref, root_ref, physics_ref, order_ref, base_ref, high_ref, low_ref,
     start, force, root, square, drive, base, high, low, sems
 ):
     incoming = [
@@ -167,130 +168,94 @@
         copy.wait()
 
 
-def transport(at, refs, scratch, put, later=()):
-    inc_ref, rate_ref, west_ref, east_ref, west_rate_ref, east_rate_ref = refs
-    rate, west_rate, east_rate, table, own, west, east, odd, even, sems = scratch
-    start, size = CHUNKS[at]
-    blocks = size // PART
-    first = CHUNKS[0][1]
+def advance_kernel(
+    inc_ref, rate_ref, west_ref, east_ref, core_ref, high_ref, low_ref, base_ref,
+    end_ref, keep_ref, send_ref,
+    rate, west_rate, east_rate, table, band, own, west, east, odd, even, state, base, high, low, sems
+):
+    at = PAD - 8
     weights = [
         pltpu.make_async_copy(rate_ref, rate, sems.at[0]),
-        pltpu.make_async_copy(west_rate_ref.at[:, pl.ds(first, 8)], west_rate, sems.at[1]),
-        pltpu.make_async_copy(east_rate_ref.at[:, pl.ds(first, 8)], east_rate, sems.at[2]),
+        pltpu.make_async_copy(west_ref.at[:, pl.ds(at, 8)], west_rate, sems.at[1]),
+        pltpu.make_async_copy(east_ref.at[:, pl.ds(at, 8)], east_rate, sems.at[2]),
     ]
     fields = []
-    for b in range(blocks):
-        valid = min(PART, ROWS - start - b * PART)
-        rows = pl.ds(b * PART, PART)
-        fields.append(
-            [
-                pltpu.make_async_copy(
-                    inc_ref.at[pl.ds(start + b * PART, valid)], own.at[b, pl.ds(0, valid)], sems.at[3 + 3 * b]
-                ),
-                pltpu.make_async_copy(west_ref.at[:, rows], west.at[b], sems.at[4 + 3 * b]),
-                pltpu.make_async_copy(east_ref.at[:, rows], east.at[b], sems.at[5 + 3 * b]),
-            ]
-        )
-    for copy in weights + [c for group in fields for c in group] + list(later):
+    for b in range(2):
+        valid = min(HALF, ROWS - b * HALF)
+        rows = pl.ds(b * HALF, HALF)
+        mine = pl.ds(b * HALF, valid)
+        fields.append(pltpu.make_async_copy(inc_ref.at[mine], own.at[mine], sems.at[3 + 3 * b]))
+        fields.append(pltpu.make_async_copy(west_ref.at[:, rows], west.at[:, rows], sems.at[4 + 3 * b]))
+        fields.append(pltpu.make_async_copy(east_ref.at[:, rows], east.at[:, rows], sems.at[5 + 3 * b]))
+    later = [
+        pltpu.make_async_copy(high_ref, high, sems.at[9]),
+        pltpu.make_async_copy(low_ref, low, sems.at[10]),
+        pltpu.make_async_copy(base_ref, base, sems.at[11]),
+    ]
+    for copy in weights + fields + later:
         copy.start()
+    own[ROWS:] = jnp.zeros((PAD - ROWS, COLS, LANES), F32)
     for copy in weights:
         copy.wait()
-    lane = lax.broadcasted_iota(jnp.int32, (1, LANES), 1)
+    row = lax.broadcasted_iota(jnp.int32, (LANES, LANES), 0)
+    lane = lax.broadcasted_iota(jnp.int32, (LANES, LANES), 1)
     wide = COLS + 2 * STEPS
+    first = ROWS - at
     for j in range(1, wide - 1):
         if j < STEPS:
-            rates = [west_rate[j, i : i + 1, :] for i in range(4)]
+            rates = [west_rate[j, first + i : first + i + 1, :] for i in range(4)]
         elif j < STEPS + COLS:
             rates = [rate[i, j - STEPS : j - STEPS + 1, :] for i in range(4)]
         else:
-            rates = [east_rate[j - STEPS - COLS, i : i + 1, :] for i in range(4)]
+            rates = [east_rate[j - STEPS - COLS, first + i : first + i + 1, :] for i in range(4)]
         center = 1.0 - (rates[0] + rates[1] + rates[2] + rates[3])
-        north = jnp.where(lane == LANES - 1, 0.0, rates[2])
-        south = jnp.where(lane == 0, 0.0, rates[3])
-        for i, value in enumerate((center, rates[0], rates[1], north, south)):
-            table[5 * j + i] = jnp.broadcast_to(value, (8, LANES))
-    flat = own.reshape(blocks * PART * COLS, LANES)
-    for b in range(blocks):
-        valid = min(PART, ROWS - start - b * PART)
-        if valid < PART:
-            own[b, valid:] = jnp.zeros((PART - valid, COLS, LANES), F32)
-        for copy in fields[b]:
-            copy.wait()
+        table[2 * j] = jnp.broadcast_to(rates[0], (8, LANES))
+        table[2 * j + 1] = jnp.broadcast_to(rates[1], (8, LANES))
+        along = jnp.where(row == lane, center, 0.0)
+        along = jnp.where(row == lane + 1, rates[2], along)
+        along = jnp.where(row == lane - 1, rates[3], along)
+        along_high, along_low = two_parts(along)
+        band[j, :LANES, :LANES] = along_high
+        band[j, LANES:, :LANES] = along_high
+        band[j, :LANES, LANES:] = along_low
+        band[j, LANES:, LANES:] = jnp.zeros((LANES, LANES), BF16)
+    flat = own.reshape(PAD * COLS, LANES)
+
+    for copy in fields:
+        copy.wait()
 
     def block(b, carry):
+        rows = pl.ds(pl.multiple_of(b * HALF, 16), HALF)
+
         def load(step, j):
             if step > 0:
-                value = (odd if step % 2 else even)[j]
-            elif j < STEPS:
-                value = west[b, j]
-            elif j < STEPS + COLS:
-                value = flat[pl.ds(b * (PART * COLS) + j - STEPS, PART, stride=COLS), :]
-            else:
-                value = east[b, j - STEPS - COLS]
-            return value.reshape(PART // 8, 8, LANES)
+                return (odd if step % 2 else even)[j]
+            if j < STEPS:
+                return west[j, rows, :]
+            if j < STEPS + COLS:
+                return flat[pl.ds(b * (HALF * COLS) + j - STEPS, HALF, stride=COLS), :]
+            return east[j - STEPS - COLS, rows, :]
+
+        def tiles(value):
+            return value.reshape(HALF // 8, 8, LANES)
 
         for step in range(1, STEPS + 1):
             for j in range(step, wide - step):
-                v = load(step - 1, j)
-                total = table[5 * j] * v
-                total = total + table[5 * j + 1] * load(step - 1, j + 1)
-                total = total + table[5 * j + 2] * load(step - 1, j - 1)
-                total = total + table[5 * j + 3] * pltpu.roll(v, LANES - 1, 2)
-                total = total + table[5 * j + 4] * pltpu.roll(v, 1, 2)
-                total = total.reshape(PART, LANES)
+                parts = jnp.concatenate(two_parts(load(step - 1, j)), 1)
+                along = jnp.dot(parts, band[j], preferred_element_type=F32)
+                total = tiles(along[:, :LANES] + along[:, LANES:])
+                total = total + table[2 * j] * tiles(load(step - 1, j + 1))
+                total = total + table[2 * j + 1] * tiles(load(step - 1, j - 1))
+                total = total.reshape(HALF, LANES)
                 if step == STEPS:
-                    put(pl.ds(pl.multiple_of(b * PART, 8), PART), j - STEPS, total)
+                    state[j - STEPS, rows, :] = total
                 else:
                     (odd if step % 2 else even)[j] = total
         return carry
 
-    lax.fori_loop(0, blocks, block, 0)
-
-
-def transport_scratch(at):
-    blocks = CHUNKS[at][1] // PART
-    wide = COLS + 2 * STEPS
-    return [
-        pltpu.VMEM((4, COLS, LANES), F32),
-        pltpu.VMEM((STEPS, 8, LANES), F32),
-        pltpu.VMEM((STEPS, 8, LANES), F32),
-        pltpu.VMEM((5 * wide, 8, LANES), F32),
-        pltpu.VMEM((blocks, PART, COLS, LANES), F32),
-        pltpu.VMEM((blocks, STEPS, PART, LANES), F32),
-        pltpu.VMEM((blocks, STEPS, PART, LANES), F32),
-        pltpu.VMEM((wide, PART, LANES), F32),
-        pltpu.VMEM((wide, PART, LANES), F32),
-        pltpu.SemaphoreType.DMA((3 + 3 * blocks,)),
-    ]
-
-
-def upper_kernel(*refs):
-    ins, out_ref, (out, sem), scratch = refs[:6], refs[6], refs[7:9], refs[9:]
-
-    def put(rows, c, value):
-        out[c, rows, :] = value
-
-    transport(0, ins, scratch, put)
-    copy = pltpu.make_async_copy(out, out_ref, sem)
-    copy.start()
-    copy.wait()
-
-
-def lower_kernel(*refs):
-    ins, (core_ref, upper_ref, high_ref, low_ref, base_ref) = refs[:6], refs[6:11]
-    end_ref, keep_ref, send_ref, upper, lower, base, high, low, parts, sems = refs[12:22]
-    incoming = [
-        pltpu.make_async_copy(high_ref, high, sems.at[1]),
-        pltpu.make_async_copy(low_ref, low, sems.at[2]),
-        pltpu.make_async_copy(upper_ref, upper, sems.at[0]),
-        pltpu.make_async_copy(base_ref, base, sems.at[3]),
-    ]
-
-    def put(rows, c, value):
-        lower[c, rows, :] = value
-
-    transport(1, ins, refs[22:], put, incoming)
-    for copy in incoming:
+    lax.fori_loop(0, 2, block, 0)
+
+    for copy in later:
         copy.wait()
     core = core_ref[0]
     outgoing = []
@@ -298,20 +263,16 @@
         start = 4 * (core ^ kind)
         for i in (0, 2):
             c = start + i
-            column = jnp.concatenate(
-                [jnp.concatenate([upper[c + k], lower[c + k]], 0) for k in range(2)], 1
-            )
+            column = jnp.concatenate([state[c], state[c + 1]], 1)
             end = column + product(high[...], low[...], column)
             for k in range(2):
                 column = end[:, k * LANES : (k + 1) * LANES]
+                state[c + k] = column
                 rest = base[c + k] - column
-                base[c + k] = column
                 for q in range(4):
-                    parts[kind, 4 * (i + k) + q] = rest[q * PART : (q + 1) * PART]
-            pair, some = pl.ds(c, 2), pl.ds(4 * i, 8)
-            outgoing.append(pltpu.make_async_copy(parts.at[kind, some], out_ref.at[some], sems.at[4 + kind * 2 + i // 2]))
-            outgoing.append(pltpu.make_async_copy(base.at[pair], end_ref.at[pair], sems.at[8 + kind * 2 + i // 2]))
-            outgoing[-2].start()
+                    out_ref[4 * (i + k) + q] = rest[q * PART : (q + 1) * PART]
+            pair = pl.ds(c, 2)
+            outgoing.append(pltpu.make_async_copy(state.at[pair], end_ref.at[pair], sems.at[12 + kind * 2 + i // 2]))
             outgoing[-1].start()
     for copy in outgoing:
         copy.wait()
@@ -382,6 +343,10 @@
         out_ref[j] = lax.dot_general(
             masked, spread, (((1,), (1,)), ((), ())), precision=HIGHEST, preferred_element_type=F32
         )
+
+
+def hand_on_kernel(in_ref, west_ref, east_ref, out_ref):
+    out_ref[...] = in_ref[...]
 
 
 def observe_kernel(obs_ref, end_ref, order_ref, out_ref, end_high, end_low):
@@ -447,15 +412,13 @@
     to_west = [(i + 1, i) for i in range(TILES - 1)]
     to_east = [(i, i + 1) for i in range(TILES - 1)]
 
-    wests, easts = pack(state, rates)
-    halo0, halo1 = [
-        (lax.ppermute(east, "tile", to_east), lax.ppermute(west, "tile", to_west))
-        for west, east in zip(wests, easts)
-    ]
+    west, east = pack(state, rates)
+    from_west = lax.ppermute(east, "tile", to_east)
+    from_east = lax.ppermute(west, "tile", to_west)
     base, high, low = call(
         prepare_kernel,
         [shape(COLS, PAD, LANES), shape(PAD, PAD, dtype=BF16), shape(PAD, PAD, dtype=BF16)],
-        (state, drive, error_root, physics.reshape(ROWS, ROWS)),
+        (state, drive, error_root, physics.reshape(ROWS, ROWS), west),
         WIDE,
         scratch=[
             pltpu.VMEM((ROWS, COLS, LANES), F32),
@@ -468,59 +431,65 @@
             pltpu.VMEM((PAD, PAD), BF16),
             pltpu.SemaphoreType.DMA((9,)),
         ],
-        flops=8 * 10**9,
-        moved=5 * field,
+        flops=10**8,
+        moved=10**6,
         far=(0, 1, 2),
         far_out=(0, 1, 2),
-    )
-    upper = call(
-        upper_kernel,
-        shape(COLS, CHUNKS[0][1], LANES),
-        (state, rates, *halo0, *halo0),
-        WIDE,
-        scratch=[pltpu.VMEM((COLS, CHUNKS[0][1], LANES), F32), pltpu.SemaphoreType.DMA] + transport_scratch(0),
-        flops=4 * 10**9,
-        moved=field,
-        far=range(6),
-        far_out=(0,),
+        unread=(4,),
     )
     queries, chosen, spread = call(
         sort_kernel,
         [shape(TILES, FIELDS, CAP), shape(TILES, SLOTS), shape(CAP, SLOTS)],
-        (me, obs_index, obs_frac, upper),
+        (me, obs_index, obs_frac, base),
         8,
-        flops=10**8,
-        moved=10**6,
+        flops=10**7,
+        moved=10**5,
         smem=(0,),
-        far=(3,),
+        unread=(3,),
+    )
+    queries = call(
+        hand_on_kernel,
+        shape(TILES, FIELDS, CAP),
+        (queries, from_west, from_east),
+        4,
+        moved=10**5,
+        unread=(1, 2),
     )
     blocks = hop([queries[j] for j in range(TILES)], 4, 1)
     parts = shape(PARTS, PART, LANES)
+    wide = COLS + 2 * STEPS
     end, keep, send = call(
-        lower_kernel,
+        advance_kernel,
         [shape(COLS, PAD, LANES), parts, parts],
-        (state, rates, *halo1, *halo0, core, upper, high, low, base, blocks[7]),
-        WIDE,
+        (state, rates, from_west, from_east, core, high, low, base),
+        30,
         scratch=[
-            pltpu.VMEM((COLS, CHUNKS[0][1], LANES), F32),
-            pltpu.VMEM((COLS, CHUNKS[1][1], LANES), F32),
+            pltpu.VMEM((4, COLS, LANES), F32),
+            pltpu.VMEM((STEPS, 8, LANES), F32),
+            pltpu.VMEM((STEPS, 8, LANES), F32),
+            pltpu.VMEM((2 * wide, 8, LANES), F32),
+            pltpu.VMEM((wide, 2 * LANES, 2 * LANES), BF16),
+            pltpu.VMEM((PAD, COLS, LANES), F32),
+            pltpu.VMEM((STEPS, PAD, LANES), F32),
+            pltpu.VMEM((STEPS, PAD, LANES), F32),
+            pltpu.VMEM((wide, HALF, LANES), F32),
+            pltpu.VMEM((wide, HALF, LANES), F32),
+            pltpu.VMEM((COLS, PAD, LANES), F32),
             pltpu.VMEM((COLS, PAD, LANES), F32),
             pltpu.VMEM((PAD, PAD), BF16),
             pltpu.VMEM((PAD, PAD), BF16),
-            pltpu.VMEM((2, PARTS, PART, LANES), F32),
-            pltpu.SemaphoreType.DMA((12,)),
-        ]
-        + transport_scratch(1),
-        flops=6 * 10**9,
-        moved=5 * field,
-        smem=(6,),
-        far=(0, 1, 2, 3, 4, 5, 7, 8, 9, 10, 11),
-        far_out=range(3),
+            pltpu.SemaphoreType.DMA((16,)),
+        ],
+        flops=15 * 10**9,
+        moved=6 * field,
+        smem=(4,),
+        far=(0, 1, 2, 3, 5, 6, 7),
+        far_out=(0,),
     )
     swap = [(0, 1), (1, 0)]
     partner = lax.ppermute(send, "core", swap)
     blocks = hop(blocks, 2, 1)
-    pair = call(pair_kernel, parts, (keep, partner, blocks[7]), 6, flops=10**6, moved=2 * field)
+    pair = call(pair_kernel, parts, (keep, partner, blocks[7]), 6, flops=10**6, moved=2 * field, unread=(2,))
     gathered = lax.all_to_all(pair, ("y", "x"), 0, 0, tiled=True)
     blocks = hop(blocks, 1, 1)
     arrived = jnp.concatenate(blocks, 0).reshape(TILES, FIELDS, CAP)
@@ -532,9 +501,9 @@
         scratch=[pltpu.VMEM((PAD, COLS * LANES), BF16), pltpu.VMEM((PAD, COLS * LANES), BF16)],
         flops=3 * 10**9,
         moved=field,
-        far=(2,),
-    )
-    totals = call(scan_kernel, parts, (gathered, found), 6, flops=10**7, moved=field)
+        unread=(2,),
+    )
+    totals = call(scan_kernel, parts, (gathered, found), 6, flops=10**7, moved=field, unread=(1,))
     before = lax.all_to_all(totals, ("y", "x"), 0, 0, tiled=True)
     back = [found[j : j + 1] for j in range(TILES)]
     for bit in (4, 2, 1):
@@ -549,7 +518,7 @@
         smem=(0,),
     )
     for_partner = call(
-        share_kernel, parts, (core, before, keep, departure), 6, flops=10**7, moved=2 * field, smem=(0,), far=(3,)
+        share_kernel, parts, (core, before, keep, departure), 6, flops=10**7, moved=2 * field, smem=(0,), unread=(3,)
     )
     other = lax.ppermute(for_partner, "core", swap)
     summed = call(

time: 134 us -> 128 us (0.955)
  waiting for transfers between devices: 48.7 us -> 40.1 us
  local copies, waits for them, and re-layouts: 7.98 us -> 16.5 us
  Pallas kernels: 37 us -> 32.2 us
    unnamed x38 -> x50, local copies, waits for them, and re-layouts: 7.91 us -> 16.4 us
    ppermute x6, waiting for transfers between devices: 19.8 us -> 11.9 us  [hop(): lax.ppermute(parcel, 'tile', [(i, (i + sign * bit) % TILES) for i in rang...]
    pallas_call x11, Pallas kernels: 37 us -> 32.2 us  [call(): pl.pallas_call(body, out_shape=outs, in_specs=specs, out_specs=out_specs...]
    ppermute x6, starting transfers between devices: 9.39 us -> 13.9 us  [hop(): lax.ppermute(parcel, 'tile', [(i, (i + sign * bit) % TILES) for i in rang...]
    ppermute x4 -> x2, starting transfers between devices: 9.67 us -> 5.74 us  [the longest x1 4.45 us: per_device(): from_west = lax.ppermute(east, 'tile', to_east)]
    ppermute x1, starting transfers between devices: 4.97 us -> 3.53 us  [per_device(): partner = lax.ppermute(send, 'core', swap)]
    ppermute x4 -> x2, waiting for transfers between devices: 16.5 us -> 17 us  [the longest x1 14 us: per_device(): from_west = lax.ppermute(east, 'tile', to_east)]
  transfers between devices with their start and end apart: 14 -> 12, of which waited for: 11 -> 10; matrix products, arithmetic and copies ran while one was open for 1% -> 1% of each run, Pallas kernels for 8% -> 20%
where the time goes in v4:
time: 128 us
  waiting for transfers between devices  40.1 us (31%)
  starting transfers between devices  37.2 us (29%)
  Pallas kernels  32.2 us (25%)
  local copies, waits for them, and re-layouts  16.5 us (13%)
  between operations  1.53 us (1%)
    pallas_call x11, Pallas kernels, call(): pl.pallas_call(body, out_shape=outs, in_specs=specs, out_specs=out_specs...  32.2 us
    unnamed x50, local copies, waits for them, and re-layouts  16.4 us
    ppermute x1, waiting for transfers between devices, per_device(): from_west = lax.ppermute(east, 'tile', to_east)  14 us
    ppermute x6, starting transfers between devices, hop(): lax.ppermute(parcel, 'tile', [(i, (i + sign * bit) % TILES) for i in rang...  13.9 us
    ppermute x6, waiting for transfers between devices, hop(): lax.ppermute(parcel, 'tile', [(i, (i + sign * bit) % TILES) for i in rang...  11.9 us
    all_to_all x1, starting transfers between devices, per_device(): gathered = lax.all_to_all(pair, ('y', 'x'), 0, 0, tiled=True)  6.8 us
    all_to_all x1, waiting for transfers between devices, per_device(): before = lax.all_to_all(totals, ('y', 'x'), 0, 0, tiled=True)  4.84 us
    ppermute x1, starting transfers between devices, per_device(): from_west = lax.ppermute(east, 'tile', to_east)  4.45 us
  transfers between devices with their start and end apart: 12, of which 10 were waited for; matrix products, arithmetic and copies ran while one was open for 1% of the time, Pallas kernels for 20%

profile of v4, /device:TPU:1, one launch (start us, length us, event | category | flops | bytes accessed | tf_op | source)
XLA Modules:
  0.0 127.6 jit_solution(12327974537652673143)
XLA Ops:
  0.6 2.8 %shard_map.104 = (f32[6,416,128]{2,1,0:T(8,128)}, f32[6,416,128]{2,1,0:T(8,128)}) custom-call(f32[411,8,128]{2,1,0:T(8,128)} %bitcast.28, f32[4,8,128]{2,1,0:T(8,128)} %bitcast.31), custom_call_target="tpu_custom_call" | custom-call | bytes 5111808 | tf_op jit(solution)/shard_map/pallas_call | solution.py:43
  3.4 4.5 %collective-permute-start = (f32[6,416,128]{2,1,0:T(8,128)}, f32[6,416,128]{2,1,0:T(8,128)S(1)}, u32[]{:S(2)}, u32[]{:S(2)}) collective-permute-start(f32[6,416,128]{2,1,0:T(8,128)} %get-tuple-element.15), channel_id=1, source_target_pairs={{0,1},{1,2},{2,3},{3,4},{4,5},{5,6},{6,7},{8,9},{9,10},{10,11},{11... | collective-permute-start | bytes 3833864 | tf_op jit(solution)/shard_map/ppermute | solution.py:416
  7.9 1.3 %collective-permute-start.1 = (f32[6,416,128]{2,1,0:T(8,128)}, f32[6,416,128]{2,1,0:T(8,128)}, u32[]{:S(2)}, u32[]{:S(2)}) collective-permute-start(f32[6,416,128]{2,1,0:T(8,128)} %get-tuple-element.13.order_ref), channel_id=1, source_target_pairs={{1,0},{2,1},{3,2},{4,3},{5,4},{6,5},{7,6},{9,8},{10,9},{11,10},{12... | collective-permute-start | bytes 3833864 | tf_op jit(solution)/shard_map/ppermute | solution.py:417
  10.2 6.5 %shard_map.105 = (f32[8,416,128]{2,1,0:T(8,128)}, bf16[416,416]{1,0:T(8,128)(2,1)}, bf16[416,416]{1,0:T(8,128)(2,1)}) custom-call(f32[411,8,128]{2,1,0:T(8,128)} %bitcast.29, f32[411,8,128]{2,1,0:T(8,128)} %bitcast.35, f32[411,411]{1,0:T(8,128)} %root_ref.1, f32[411,411]{1,0:T(8,128)} %bitcast.34, f32[6,416,128]{2,1,0:T(8,128)} %get-tuple-element.13.order_ref), custom_call_target="tpu_custom_call" | custom-call | flops 100000000 | bytes 1000000 | tf_op jit(solution)/shard_map/pallas_call | solution.py:43
  16.7 1.4 %copy-done = f32[8,416,128]{2,1,0:T(8,128)S(1)} copy-done((f32[8,416,128]{2,1,0:T(8,128)S(1)}, f32[8,416,128]{2,1,0:T(8,128)}, u32[]{:S(2)}) %copy-start) | copy-done | bytes 1703960
  18.2 1.9 %shard_map.107 = (f32[8,8,128]{2,1,0:T(8,128)S(1)}, f32[8,512]{1,0:T(8,128)S(1)}, f32[128,512]{1,0:T(8,128)S(1)}) custom-call(s32[1]{0:T(128)} %bitcast.4.me_ref, s32[3,1,512]{2,1,0:T(1,128)S(1)} %copy-done.13, f32[2,1,512]{2,1,0:T(1,128)S(1)} %copy-done.14, f32[8,416,128]{2,1,0:T(8,128)S(1)} %copy-done), custom_call_target="tpu_custom_call" | custom-call | flops 10000000 | bytes 100000 | tf_op jit(solution)/shard_map/pallas_call | solution.py:43
  20.8 14.0 %collective-permute-done.west_ref = f32[6,416,128]{2,1,0:T(8,128)S(1)} collective-permute-done((f32[6,416,128]{2,1,0:T(8,128)}, f32[6,416,128]{2,1,0:T(8,128)S(1)}, u32[]{:S(2)}, u32[]{:S(2)}) %collective-permute-start) | collective-permute-done | bytes 1277984 | tf_op jit(solution)/shard_map/ppermute | solution.py:416
  35.9 3.0 %collective-permute-done.1.east_ref = f32[6,416,128]{2,1,0:T(8,128)} collective-permute-done((f32[6,416,128]{2,1,0:T(8,128)}, f32[6,416,128]{2,1,0:T(8,128)}, u32[]{:S(2)}, u32[]{:S(2)}) %collective-permute-start.1) | collective-permute-done | bytes 1277984 | tf_op jit(solution)/shard_map/ppermute | solution.py:417
  38.9 1.3 %copy-done.7 = f32[6,416,128]{2,1,0:T(8,128)S(1)} copy-done((f32[6,416,128]{2,1,0:T(8,128)S(1)}, f32[6,416,128]{2,1,0:T(8,128)}, u32[]{:S(2)}) %copy-start.7) | copy-done | bytes 1277976
  40.3 5.8 %collective-permute-start.3 = (f32[32,128]{1,0:T(8,128)S(1)}, f32[32,128]{1,0:T(8,128)S(1)}, u32[]{:S(2)}, u32[]{:S(2)}) collective-permute-start(f32[32,128]{1,0:T(8,128)S(1)} %pad_maximum_fusion), channel_id=1, source_target_pairs={{0,4},{1,5},{2,6},{3,7},{4,0},{5,1},{6,2},{7,3},{8,12},{9,13},{10,... | collective-permute-start | bytes 49160 | tf_op jit(solution)/shard_map/ppermute | solution.py:394
  46.0 1.1 collective-permute-done.3
  47.2 4.2 %collective-permute-start.4 = (f32[32,128]{1,0:T(8,128)S(1)}, f32[32,128]{1,0:T(8,128)S(1)}, u32[]{:S(2)}, u32[]{:S(2)}) collective-permute-start(f32[32,128]{1,0:T(8,128)S(1)} %pad_maximum_fusion.1), channel_id=1, source_target_pairs={{0,2},{1,3},{2,4},{3,5},{4,6},{5,7},{6,0},{7,1},{8,10},{9,11},{10,... | collective-permute-start | bytes 49160 | tf_op jit(solution)/shard_map/ppermute | solution.py:394
  51.4 1.4 %copy-done.2 = f32[1,3,137,8,128]{4,3,2,1,0:T(8,128)S(1)} copy-done((f32[1,3,137,8,128]{4,3,2,1,0:T(8,128)S(1)}, f32[1,3,137,8,128]{4,3,2,1,0:T(8,128)}, u32[]{:S(2)}) %copy-start.2) | copy-done | bytes 1683480
  52.9 1.3 %copy-done.8 = f32[6,416,128]{2,1,0:T(8,128)S(1)} copy-done((f32[6,416,128]{2,1,0:T(8,128)S(1)}, f32[6,416,128]{2,1,0:T(8,128)}, u32[]{:S(2)}) %copy-start.8) | copy-done | bytes 1277976
  56.2 12.3 %shard_map.106 = (f32[8,416,128]{2,1,0:T(8,128)S(1)}, f32[16,104,128]{2,1,0:T(8,128)S(1)}, f32[16,104,128]{2,1,0:T(8,128)S(1)}) custom-call(f32[411,8,128]{2,1,0:T(8,128)S(1)} %bitcast.30, f32[4,8,128]{2,1,0:T(8,128)S(1)} %bitcast.32, f32[6,416,128]{2,1,0:T(8,128)S(1)} %copy-done.8, f32[6,416,128]{2,1,0:T(8,128)} %collective-permute-done.1.east_ref, ...), custom_call_target="tpu_custom_call" | custom-call | flops 15000000512 | bytes 10223616 | tf_op jit(solution)/shard_map/pallas_call | solution.py:43
  68.5 1.2 copy-done.18
  69.7 2.3 %collective-permute-start.5 = (f32[32,128]{1,0:T(8,128)S(1)}, f32[32,128]{1,0:T(8,128)S(1)}, u32[]{:S(2)}, u32[]{:S(2)}) collective-permute-start(f32[32,128]{1,0:T(8,128)S(1)} %pad_maximum_fusion.2), channel_id=1, source_target_pairs={{0,1},{1,2},{2,3},{3,4},{4,5},{5,6},{6,7},{7,0},{8,9},{9,10},{10,1... | collective-permute-start | bytes 49160 | tf_op jit(solution)/shard_map/ppermute | solution.py:394
  72.0 3.5 %collective-permute-start.2 = (f32[16,104,128]{2,1,0:T(8,128)S(1)}, f32[16,104,128]{2,1,0:T(8,128)S(1)}, u32[]{:S(2)}, u32[]{:S(2)}) collective-permute-start(f32[16,104,128]{2,1,0:T(8,128)S(1)} %get-tuple-element.19), channel_id=1, source_target_pairs={{0,8},{8,0},{1,9},{9,1},{2,10},{10,2},{3,11},{11,3},{4,12},{12,4},... | collective-permute-start | bytes 2555912 | tf_op jit(solution)/shard_map/ppermute | solution.py:490
  75.6 2.0 %collective-permute-done.2.partner_ref = f32[16,104,128]{2,1,0:T(8,128)S(1)} collective-permute-done((f32[16,104,128]{2,1,0:T(8,128)S(1)}, f32[16,104,128]{2,1,0:T(8,128)S(1)}, u32[]{:S(2)}, u32[]{:S(2)}) %collective-permute-start.2) | collective-permute-done | bytes 852000 | tf_op jit(solution)/shard_map/ppermute | solution.py:490
  79.5 6.8 %all-to-all-start = ((f32[16,104,128]{2,1,0:T(8,128)}), f32[16,104,128]{2,1,0:T(8,128)}, u32[]{:S(2)}, u32[]{:S(2)}) async-start(f32[16,104,128]{2,1,0:T(8,128)} %shard_map.109.order_ref), calls=%async_computation | async-start | bytes 1703936 | tf_op jit(solution)/shard_map/all_to_all | solution.py:493
  86.3 1.4 %copy-done.19 = f32[8,416,128]{2,1,0:T(8,128)S(1)} copy-done((f32[8,416,128]{2,1,0:T(8,128)S(1)}, f32[8,416,128]{2,1,0:T(8,128)}, u32[]{:S(2)}) %copy-start.19) | copy-done | bytes 1703960
  87.7 3.6 %shard_map.110.order_ref = f32[8,128]{1,0:T(8,128)S(1)} custom-call(f32[8,8,128]{2,1,0:T(8,128)S(1)} %bitcast.33, f32[8,416,128]{2,1,0:T(8,128)S(1)} %copy-done.19, f32[16,104,128]{2,1,0:T(8,128)} %shard_map.109.order_ref), custom_call_target="tpu_custom_call" | custom-call | flops 3000000000 | bytes 1703936 | tf_op jit(solution)/shard_map/pallas_call | solution.py:43
  91.6 6.6 %collective-permute-done.6 = f32[4,128]{1,0:T(4,128)S(1)} collective-permute-done((f32[4,128]{1,0:T(4,128)S(1)}, f32[4,128]{1,0:T(4,128)S(1)}, u32[]{:S(2)}, u32[]{:S(2)}) %collective-permute-start.6) | collective-permute-done | bytes 2080 | tf_op jit(solution)/shard_map/ppermute | solution.py:394
  98.2 2.3 %all-to-all-done.in_ref = f32[16,104,128]{2,1,0:T(8,128)} async-done(((f32[16,104,128]{2,1,0:T(8,128)}), f32[16,104,128]{2,1,0:T(8,128)}, u32[]{:S(2)}, u32[]{:S(2)}) %all-to-all-start) | async-done | bytes 852000 | tf_op jit(solution)/shard_map/all_to_all | solution.py:493
  100.5 1.4 %shard_map.111 = f32[16,104,128]{2,1,0:T(8,128)S(1)} custom-call(f32[16,104,128]{2,1,0:T(8,128)} %all-to-all-done.in_ref, f32[8,128]{1,0:T(8,128)S(1)} %shard_map.110.order_ref), custom_call_target="tpu_custom_call" | custom-call | flops 10000000 | bytes 1703936 | tf_op jit(solution)/shard_map/pallas_call | solution.py:43
  102.8 3.9 %all-to-all-start.1 = ((f32[16,104,128]{2,1,0:T(8,128)}), f32[16,104,128]{2,1,0:T(8,128)S(1)}, u32[]{:S(2)}, u32[]{:S(2)}) async-start(f32[16,104,128]{2,1,0:T(8,128)} %copy-done.5), calls=%async_computation.1 | async-start | bytes 1703936 | tf_op jit(solution)/shard_map/all_to_all | solution.py:507
  106.8 3.3 %collective-permute-done.7 = f32[4,128]{1,0:T(4,128)S(1)} collective-permute-done((f32[4,128]{1,0:T(4,128)S(1)}, f32[4,128]{1,0:T(4,128)S(1)}, u32[]{:S(2)}, u32[]{:S(2)}) %collective-permute-start.7) | collective-permute-done | bytes 2080 | tf_op jit(solution)/shard_map/ppermute | solution.py:394
  110.1 1.3 %collective-permute-start.8 = (f32[4,128]{1,0:T(4,128)S(1)}, f32[4,128]{1,0:T(4,128)S(1)}, u32[]{:S(2)}, u32[]{:S(2)}) collective-permute-start(f32[4,128]{1,0:T(4,128)S(1)} %pad_maximum_fusion.4), channel_id=1, source_target_pairs={{0,7},{1,0},{2,1},{3,2},{4,3},{5,4},{6,5},{7,6},{8,15},{9,8},{10,9... | collective-permute-start | bytes 6152 | tf_op jit(solution)/shard_map/ppermute | solution.py:394
  114.8 4.8 %all-to-all-done.1.before_ref = f32[16,104,128]{2,1,0:T(8,128)S(1)} async-done(((f32[16,104,128]{2,1,0:T(8,128)}), f32[16,104,128]{2,1,0:T(8,128)S(1)}, u32[]{:S(2)}, u32[]{:S(2)}) %all-to-all-start.1) | async-done | bytes 852000 | tf_op jit(solution)/shard_map/all_to_all | solution.py:507
  120.4 3.3 %collective-permute-start.9 = (f32[16,104,128]{2,1,0:T(8,128)S(1)}, f32[16,104,128]{2,1,0:T(8,128)S(1)}, u32[]{:S(2)}, u32[]{:S(2)}) collective-permute-start(f32[16,104,128]{2,1,0:T(8,128)S(1)} %shard_map.113), channel_id=1, source_target_pairs={{0,8},{8,0},{1,9},{9,1},{2,10},{10,2},{3,11},{11,3},{4,12},{12,4},... | collective-permute-start | bytes 2555912 | tf_op jit(solution)/shard_map/ppermute | solution.py:523
  123.7 2.0 %collective-permute-done.9.other_ref = f32[16,104,128]{2,1,0:T(8,128)S(1)} collective-permute-done((f32[16,104,128]{2,1,0:T(8,128)S(1)}, f32[16,104,128]{2,1,0:T(8,128)S(1)}, u32[]{:S(2)}, u32[]{:S(2)}) %collective-permute-start.9) | collective-permute-done | bytes 852000 | tf_op jit(solution)/shard_map/ppermute | solution.py:523
  125.7 1.8 %shard_map.114 = f32[411,8,128]{2,1,0:T(8,128)} custom-call(s32[1]{0:T(128)} %bitcast.core_ref, f32[8,416,128]{2,1,0:T(8,128)S(1)} %copy-done.1, f32[16,104,128]{2,1,0:T(8,128)S(1)} %all-to-all-done.1.before_ref, f32[16,104,128]{2,1,0:T(8,128)S(1)} %copy-done.4, f32[16,104,128]{2,1,0:T(8,128)S(1)} %collective-permute-done.9.other_ref), custom_call_target="tpu_custom_call" | custom-call | flops 10000000 | bytes 6815744 | tf_op jit(solution)/shard_map/pallas_call | solution.py:43
  (71 shorter events, 11.4 us)
Async XLA Ops:
  0.6 8.5 %copy-start.20 = (f32[1,411,411]{2,0,1:T(1,128)S(1)}, f32[1,411,411]{2,0,1:T(1,128)}, u32[]{:S(2)}) copy-start(f32[1,411,411]{2,0,1:T(1,128)} %param.12) | copy-start | bytes 2027056
  3.4 31.4 %collective-permute-start = (f32[6,416,128]{2,1,0:T(8,128)}, f32[6,416,128]{2,1,0:T(8,128)S(1)}, u32[]{:S(2)}, u32[]{:S(2)}) collective-permute-start(f32[6,416,128]{2,1,0:T(8,128)} %get-tuple-element.15), channel_id=1, source_target_pairs={{0,1},{1,2},{2,3},{3,4},{4,5},{5,6},{6,7},{8,9},{9,10},{10,11},{11... | collective-permute-start | bytes 3833864 | tf_op jit(solution)/shard_map/ppermute | solution.py:416
  7.9 31.1 %collective-permute-start.1 = (f32[6,416,128]{2,1,0:T(8,128)}, f32[6,416,128]{2,1,0:T(8,128)}, u32[]{:S(2)}, u32[]{:S(2)}) collective-permute-start(f32[6,416,128]{2,1,0:T(8,128)} %get-tuple-element.13.order_ref), channel_id=1, source_target_pairs={{1,0},{2,1},{3,2},{4,3},{5,4},{6,5},{7,6},{9,8},{10,9},{11,10},{12... | collective-permute-start | bytes 3833864 | tf_op jit(solution)/shard_map/ppermute | solution.py:417
  10.2 6.5 %copy-start.13 = (s32[3,1,512]{2,1,0:T(1,128)S(1)}, s32[3,1,512]{2,1,0:T(1,128)}, u32[]{:S(2)}) copy-start(s32[3,1,512]{2,1,0:T(1,128)} %index_ref.1) | copy-start | bytes 18436
  10.2 6.5 %copy-start.14 = (f32[2,1,512]{2,1,0:T(1,128)S(1)}, f32[2,1,512]{2,1,0:T(1,128)}, u32[]{:S(2)}) copy-start(f32[2,1,512]{2,1,0:T(1,128)} %frac_ref.1) | copy-start | bytes 12292
  16.7 1.5 %copy-start = (f32[8,416,128]{2,1,0:T(8,128)S(1)}, f32[8,416,128]{2,1,0:T(8,128)}, u32[]{:S(2)}) copy-start(f32[8,416,128]{2,1,0:T(8,128)} %get-tuple-element.14.base_ref.order_ref) | copy-start | bytes 5111812
  18.2 33.2 %copy-start.11 = (f32[1,4,8,128]{3,2,1,0:T(8,128)S(1)}, f32[1,4,8,128]{3,2,1,0:T(8,128)}, u32[]{:S(2)}) copy-start(f32[1,4,8,128]{3,2,1,0:T(8,128)} %param.13) | copy-start | bytes 49156
  20.1 0.7 copy-start.9
  20.8 30.6 %copy-start.1 = (f32[8,416,128]{2,1,0:T(8,128)S(1)}, f32[8,416,128]{2,1,0:T(8,128)}, u32[]{:S(2)}) copy-start(f32[8,416,128]{2,1,0:T(8,128)} %get-tuple-element.14.base_ref.order_ref) | copy-start | bytes 5111812
  34.8 1.1 copy-start.6
  38.9 1.3 %copy-start.7 = (f32[6,416,128]{2,1,0:T(8,128)S(1)}, f32[6,416,128]{2,1,0:T(8,128)}, u32[]{:S(2)}) copy-start(f32[6,416,128]{2,1,0:T(8,128)} %copy-done.6) | copy-start | bytes 3833860
  40.3 6.9 %collective-permute-start.3 = (f32[32,128]{1,0:T(8,128)S(1)}, f32[32,128]{1,0:T(8,128)S(1)}, u32[]{:S(2)}, u32[]{:S(2)}) collective-permute-start(f32[32,128]{1,0:T(8,128)S(1)} %pad_maximum_fusion), channel_id=1, source_target_pairs={{0,4},{1,5},{2,6},{3,7},{4,0},{5,1},{6,2},{7,3},{8,12},{9,13},{10,... | collective-permute-start | bytes 49160 | tf_op jit(solution)/shard_map/ppermute | solution.py:394
  47.2 22.5 %collective-permute-start.4 = (f32[32,128]{1,0:T(8,128)S(1)}, f32[32,128]{1,0:T(8,128)S(1)}, u32[]{:S(2)}, u32[]{:S(2)}) collective-permute-start(f32[32,128]{1,0:T(8,128)S(1)} %pad_maximum_fusion.1), channel_id=1, source_target_pairs={{0,2},{1,3},{2,4},{3,5},{4,6},{5,7},{6,0},{7,1},{8,10},{9,11},{10,... | collective-permute-start | bytes 49160 | tf_op jit(solution)/shard_map/ppermute | solution.py:394
  51.4 1.4 %copy-start.2 = (f32[1,3,137,8,128]{4,3,2,1,0:T(8,128)S(1)}, f32[1,3,137,8,128]{4,3,2,1,0:T(8,128)}, u32[]{:S(2)}) copy-start(f32[1,3,137,8,128]{4,3,2,1,0:T(8,128)} %param.9) | copy-start | bytes 5050372
  52.9 1.3 %copy-start.8 = (f32[6,416,128]{2,1,0:T(8,128)S(1)}, f32[6,416,128]{2,1,0:T(8,128)}, u32[]{:S(2)}) copy-start(f32[6,416,128]{2,1,0:T(8,128)} %copy-done.6) | copy-start | bytes 3833860
  54.2 1.0 copy-start.16
  55.2 1.0 copy-start.17
  68.5 1.2 copy-start.18
  69.7 5.8 %collective-permute-start.5 = (f32[32,128]{1,0:T(8,128)S(1)}, f32[32,128]{1,0:T(8,128)S(1)}, u32[]{:S(2)}, u32[]{:S(2)}) collective-permute-start(f32[32,128]{1,0:T(8,128)S(1)} %pad_maximum_fusion.2), channel_id=1, source_target_pairs={{0,1},{1,2},{2,3},{3,4},{4,5},{5,6},{6,7},{7,0},{8,9},{9,10},{10,1... | collective-permute-start | bytes 49160 | tf_op jit(solution)/shard_map/ppermute | solution.py:394
  72.0 5.5 %collective-permute-start.2 = (f32[16,104,128]{2,1,0:T(8,128)S(1)}, f32[16,104,128]{2,1,0:T(8,128)S(1)}, u32[]{:S(2)}, u32[]{:S(2)}) collective-permute-start(f32[16,104,128]{2,1,0:T(8,128)S(1)} %get-tuple-element.19), channel_id=1, source_target_pairs={{0,8},{8,0},{1,9},{9,1},{2,10},{10,2},{3,11},{11,3},{4,12},{12,4},... | collective-permute-start | bytes 2555912 | tf_op jit(solution)/shard_map/ppermute | solution.py:490
  78.5 0.9 copy-start.3
  79.5 21.1 %all-to-all-start = ((f32[16,104,128]{2,1,0:T(8,128)}), f32[16,104,128]{2,1,0:T(8,128)}, u32[]{:S(2)}, u32[]{:S(2)}) async-start(f32[16,104,128]{2,1,0:T(8,128)} %shard_map.109.order_ref), calls=%async_computation | async-start | bytes 1703936 | tf_op jit(solution)/shard_map/all_to_all | solution.py:493
  86.3 1.5 %copy-start.19 = (f32[8,416,128]{2,1,0:T(8,128)S(1)}, f32[8,416,128]{2,1,0:T(8,128)}, u32[]{:S(2)}) copy-start(f32[8,416,128]{2,1,0:T(8,128)} %copy-done.18) | copy-start | bytes 5111812
  91.4 6.8 %collective-permute-start.6 = (f32[4,128]{1,0:T(4,128)S(1)}, f32[4,128]{1,0:T(4,128)S(1)}, u32[]{:S(2)}, u32[]{:S(2)}) collective-permute-start(f32[4,128]{1,0:T(4,128)S(1)} %slice.134), channel_id=1, source_target_pairs={{0,4},{1,5},{2,6},{3,7},{4,0},{5,1},{6,2},{7,3},{8,12},{9,13},{10,... | collective-permute-start | bytes 6152 | tf_op jit(solution)/shard_map/ppermute | solution.py:394
  98.2 14.8 %copy-start.15 = (f32[1,512]{1,0:T(1,128)S(1)}, f32[1,512]{1,0:T(1,128)}, u32[]{:S(2)}) copy-start(f32[1,512]{1,0:T(1,128)} %value_ref.1) | copy-start | bytes 6148
  101.9 0.9 copy-start.5
  102.8 16.8 %all-to-all-start.1 = ((f32[16,104,128]{2,1,0:T(8,128)}), f32[16,104,128]{2,1,0:T(8,128)S(1)}, u32[]{:S(2)}, u32[]{:S(2)}) async-start(f32[16,104,128]{2,1,0:T(8,128)} %copy-done.5), calls=%async_computation.1 | async-start | bytes 1703936 | tf_op jit(solution)/shard_map/all_to_all | solution.py:507
  106.7 3.4 %collective-permute-start.7 = (f32[4,128]{1,0:T(4,128)S(1)}, f32[4,128]{1,0:T(4,128)S(1)}, u32[]{:S(2)}, u32[]{:S(2)}) collective-permute-start(f32[4,128]{1,0:T(4,128)S(1)} %pad_maximum_fusion.3), channel_id=1, source_target_pairs={{0,6},{1,7},{2,0},{3,1},{4,2},{5,3},{6,4},{7,5},{8,14},{9,15},{10,... | collective-permute-start | bytes 6152 | tf_op jit(solution)/shard_map/ppermute | solution.py:394
  110.1 2.8 %collective-permute-start.8 = (f32[4,128]{1,0:T(4,128)S(1)}, f32[4,128]{1,0:T(4,128)S(1)}, u32[]{:S(2)}, u32[]{:S(2)}) collective-permute-start(f32[4,128]{1,0:T(4,128)S(1)} %pad_maximum_fusion.4), channel_id=1, source_target_pairs={{0,7},{1,0},{2,1},{3,2},{4,3},{5,4},{6,5},{7,6},{8,15},{9,8},{10,9... | collective-permute-start | bytes 6152 | tf_op jit(solution)/shard_map/ppermute | solution.py:394
  113.0 1.0 copy-start.10
  120.3 5.4 %copy-start.4 = (f32[16,104,128]{2,1,0:T(8,128)S(1)}, f32[16,104,128]{2,1,0:T(8,128)}, u32[]{:S(2)}) copy-start(f32[16,104,128]{2,1,0:T(8,128)} %copy-done.3) | copy-start | bytes 2555908
  120.4 5.3 %collective-permute-start.9 = (f32[16,104,128]{2,1,0:T(8,128)S(1)}, f32[16,104,128]{2,1,0:T(8,128)S(1)}, u32[]{:S(2)}, u32[]{:S(2)}) collective-permute-start(f32[16,104,128]{2,1,0:T(8,128)S(1)} %shard_map.113), channel_id=1, source_target_pairs={{0,8},{8,0},{1,9},{9,1},{2,10},{10,2},{3,11},{11,3},{4,12},{12,4},... | collective-permute-start | bytes 2555912 | tf_op jit(solution)/shard_map/ppermute | solution.py:523
  (1 other events, 0.7 us)

commit v5 on v4

--- a/solution.py
+++ b/solution.py
@@ -28,16 +28,14 @@
 WIDE = 56
 
 
-def call(body, outs, ins, mib, scratch=(), flops=0, moved=0, smem=(), far=(), far_out=(), unread=()):
+def call(body, outs, ins, scratch=(), flops=0, moved=0, smem=(), far=(), far_out=()):
     specs = [
-        pl.BlockSpec(
-            memory_space=pltpu.SMEM if at in smem else pltpu.HBM if at in far else pl.ANY if at in unread else pltpu.VMEM
-        )
+        pl.BlockSpec(memory_space=pltpu.SMEM if at in smem else pl.ANY if at in far else pltpu.VMEM)
         for at in range(len(ins))
     ]
     many = isinstance(outs, (list, tuple))
     out_specs = [
-        pl.BlockSpec(memory_space=pltpu.HBM if at in far_out else pltpu.VMEM)
+        pl.BlockSpec(memory_space=pl.ANY if at in far_out else pltpu.VMEM)
         for at in range(len(outs) if many else 1)
     ]
     return pl.pallas_call(
@@ -46,7 +44,7 @@
         in_specs=specs,
         out_specs=out_specs if many else out_specs[0],
         scratch_shapes=list(scratch),
-        compiler_params=pltpu.CompilerParams(vmem_limit_bytes=mib * MIB),
+        compiler_params=pltpu.CompilerParams(vmem_limit_bytes=WIDE * MIB),
         cost_estimate=pl.CostEstimate(flops=flops, bytes_accessed=moved, transcendentals=0),
     )(*ins)
 
@@ -68,7 +66,7 @@
     return total + jnp.dot(left_low, high, preferred_element_type=F32)
 
 
-def pack_kernel(inc_ref, rate_ref, west_ref, east_ref, held, rates, west, east, in_sems, out_sems):
+def pack_kernel(inc_ref, rate_ref, west_ref, east_ref, sent_ref, held, rates, west, east, in_sems, out_sems):
     count = PAD // PART
     incoming = [pltpu.make_async_copy(rate_ref, rates, in_sems.at[count])]
     for b in range(count):
@@ -76,6 +74,7 @@
         incoming.append(pltpu.make_async_copy(inc_ref.at[rows], held.at[rows], in_sems.at[b]))
     for copy in incoming:
         copy.start()
+    sent_ref[...] = jnp.zeros((8, LANES), F32)
     flat = held.reshape(PAD * COLS, LANES)
     outgoing = []
     incoming[0].wait()
@@ -104,9 +103,8 @@
     halo = shape(STEPS, PAD, LANES)
     return call(
         pack_kernel,
-        [halo, halo],
+        [halo, halo, shape(8, LANES)],
         (state, rates),
-        WIDE,
         scratch=[
             pltpu.VMEM((PAD, COLS, LANES), F32),
             pltpu.VMEM((4, COLS, LANES), F32),
@@ -122,7 +120,7 @@
 
 
 def prepare_kernel(
-    inc_ref, forcing_ref, root_ref, physics_ref, order_ref, base_ref, high_ref, low_ref,
+    inc_ref, forcing_ref, root_ref, physics_ref, order_ref, base_ref, high_ref, low_ref, ready_ref,
     start, force, root, square, drive, base, high, low, sems
 ):
     incoming = [
@@ -132,6 +130,7 @@
     ]
     for copy in incoming:
         copy.start()
+    ready_ref[...] = jnp.zeros((8, LANES), F32)
     square[...] = jnp.zeros((PAD, PAD), F32)
     square[:ROWS, :ROWS] = 0.2 * physics_ref[...]
     once = square[...]
@@ -169,7 +168,7 @@
 
 
 def advance_kernel(
-    inc_ref, rate_ref, west_ref, east_ref, core_ref, high_ref, low_ref, base_ref,
+    inc_ref, rate_ref, west_ref, east_ref, core_ref, high_ref, low_ref, base_ref, order_ref,
     end_ref, keep_ref, send_ref,
     rate, west_rate, east_rate, table, band, own, west, east, odd, even, state, base, high, low, sems
 ):
@@ -278,8 +277,9 @@
         copy.wait()
 
 
-def pair_kernel(keep_ref, partner_ref, order_ref, pair_ref):
+def pair_kernel(keep_ref, partner_ref, pair_ref, ready_ref):
     pair_ref[...] = keep_ref[...] + partner_ref[...]
+    ready_ref[...] = jnp.zeros((8, LANES), F32)
 
 
 def scan_kernel(in_ref, order_ref, out_ref):
@@ -299,34 +299,55 @@
     out_ref[...] = before_ref[...] + first * keep_ref[...]
 
 
-def finish_kernel(core_ref, base_ref, before_ref, partner_ref, other_ref, out_ref):
+def finish_kernel(core_ref, base_ref, before_ref, partner_ref, other_ref, out_ref, base, before, partner, other, out, sems, out_sems):
     core = core_ref[0]
-    flat = out_ref.reshape(ROWS * COLS, LANES)
+    incoming = []
+    for q in range(4):
+        rows = pl.ds(q * PART, PART)
+        incoming.append(
+            [
+                pltpu.make_async_copy(base_ref.at[:, rows], base.at[:, rows], sems.at[0, q]),
+                pltpu.make_async_copy(before_ref.at[:, q], before.at[:, q], sems.at[1, q]),
+                pltpu.make_async_copy(partner_ref.at[:, q], partner.at[:, q], sems.at[2, q]),
+                pltpu.make_async_copy(other_ref.at[:, q], other.at[:, q], sems.at[3, q]),
+            ]
+        )
+        for copy in incoming[q]:
+            copy.start()
+    flat = out.reshape(PAD * COLS, LANES)
     second = (core == 1).astype(F32)
-    for c in range(COLS):
-        mine = core == c // 4
-        i = c % 4
-        for q in range(4):
-            size = min(PART, ROWS - q * PART)
-            own = before_ref[4 * i + q, :size] + second * partner_ref[4 * i + q, :size]
-            earlier = jnp.where(mine, own, other_ref[4 * i + q, :size])
-            flat[pl.ds(q * PART * COLS + c, size, stride=COLS), :] = (
-                base_ref[c, q * PART : q * PART + size, :] + earlier
+    outgoing = []
+    for q in range(4):
+        for copy in incoming[q]:
+            copy.wait()
+        for c in range(COLS):
+            i = c % 4
+            own = before[i, q] + second * partner[i, q]
+            earlier = jnp.where(core == c // 4, own, other[i, q])
+            flat[pl.ds(q * PART * COLS + c, PART, stride=COLS), :] = (
+                base[c, q * PART : (q + 1) * PART, :] + earlier
             )
-
-
-def sort_kernel(me_ref, index_ref, frac_ref, order_ref, out_ref, chosen_ref, spread_ref):
+        rows = pl.ds(q * PART, min(PART, ROWS - q * PART))
+        outgoing.append(pltpu.make_async_copy(out.at[rows], out_ref.at[rows], out_sems.at[q]))
+        outgoing[-1].start()
+    for copy in outgoing:
+        copy.wait()
+
+
+def spread_of(place):
+    return (lax.broadcasted_iota(jnp.int32, (CAP, SLOTS), 0) == place.astype(jnp.int32)).astype(F32)
+
+
+def sort_kernel(index_ref, frac_ref, order_ref, out_ref, place_ref):
     column_x = index_ref[0]
     bucket = lax.broadcasted_iota(jnp.int32, (TILES, SLOTS), 0)
-    further = ((column_x >> 3) - me_ref[0] + TILES) & (TILES - 1)
-    chosen = (bucket == further).astype(F32)
+    chosen = (bucket == (column_x >> 3)).astype(F32)
     before = lax.broadcasted_iota(jnp.int32, (SLOTS, SLOTS), 0) < lax.broadcasted_iota(jnp.int32, (SLOTS, SLOTS), 1)
     rank = jnp.dot(chosen.astype(BF16), before.astype(F32).astype(BF16), preferred_element_type=F32)
     place = jnp.sum(chosen * rank, axis=0, keepdims=True)
-    spread = lax.broadcasted_iota(jnp.int32, (CAP, SLOTS), 0) == place.astype(jnp.int32)
-    spread = spread.astype(F32)
-    chosen_ref[...] = chosen
-    spread_ref[...] = spread
+    spread = spread_of(place)
+    place_ref[:TILES] = chosen
+    place_ref[TILES:] = jnp.broadcast_to(place, (TILES, SLOTS))
     values = jnp.concatenate(
         [
             (column_x & (COLS - 1)).astype(F32),
@@ -345,18 +366,19 @@
         )
 
 
-def hand_on_kernel(in_ref, west_ref, east_ref, out_ref):
-    out_ref[...] = in_ref[...]
-
-
-def observe_kernel(obs_ref, end_ref, order_ref, out_ref, end_high, end_low):
+def observe_kernel(me_ref, obs_ref, end_ref, order_ref, out_ref, end_high, end_low, end, sems):
+    copies = [pltpu.make_async_copy(end_ref.at[c], end.at[c], sems.at[c]) for c in range(COLS)]
+    for copy in copies:
+        copy.start()
     for c in range(COLS):
-        high, low = two_parts(end_ref[c])
+        copies[c].wait()
+        high, low = two_parts(end[c])
         end_high[:, c * LANES : (c + 1) * LANES] = high
         end_low[:, c * LANES : (c + 1) * LANES] = low
     lanes = 2 * CAP
     for j in range(0, TILES, 2):
-        fields = [jnp.concatenate([obs_ref[j, i : i + 1], obs_ref[j + 1, i : i + 1]], 1) for i in range(5)]
+        tiles = [(me_ref[0] - j - k + TILES) & (TILES - 1) for k in range(2)]
+        fields = [jnp.concatenate([obs_ref[t, i : i + 1] for t in tiles], 1) for i in range(5)]
         column, line, row = [(f + 0.5).astype(jnp.int32) for f in fields[:3]]
         across, upward = fields[3:]
         y = lax.broadcasted_iota(jnp.int32, (LANES, lanes), 0)
@@ -381,22 +403,31 @@
         out_ref[j + 1 : j + 2, :] = value[:, CAP:]
 
 
-def depart_kernel(count_ref, back_ref, chosen_ref, spread_ref, value_ref, out_ref):
-    spread = jnp.dot(back_ref[...], spread_ref[...], precision=HIGHEST, preferred_element_type=F32)
-    evolved = jnp.sum(spread * chosen_ref[...], axis=0, keepdims=True)
+def depart_kernel(count_ref, me_ref, back_ref, place_ref, value_ref, out_ref):
+    spread = jnp.dot(
+        back_ref[...], spread_of(place_ref[TILES : TILES + 1]), precision=HIGHEST, preferred_element_type=F32
+    )
+    evolved = jnp.zeros((1, SLOTS), F32)
+    for j in range(TILES):
+        tile = (me_ref[0] + j) & (TILES - 1)
+        evolved = evolved + spread[j : j + 1] * place_ref[pl.ds(tile, 1)]
     live = lax.broadcasted_iota(jnp.int32, (1, SLOTS), 1) < count_ref[0, 0]
     out_ref[...] = jnp.where(live, value_ref[...] - evolved, 0.0)
 
 
-def hop(blocks, bit, sign):
-    moving = [j for j in range(TILES) if j & bit]
-    parcel = jnp.concatenate([blocks[j] for j in moving], 0)
-    parcel = lax.ppermute(parcel, "tile", [(i, (i + sign * bit) % TILES) for i in range(TILES)])
+def ring_step(blocks, by, offsets):
     size = blocks[0].shape[0]
-    result = list(blocks)
-    for at, j in enumerate(moving):
-        result[j] = parcel[at * size : (at + 1) * size]
-    return result
+    parcel = jnp.concatenate([blocks[o] for o in offsets], 0)
+    parcel = lax.ppermute(parcel, "tile", [(i, (i + by) % TILES) for i in range(TILES)])
+    return {o: parcel[at * size : (at + 1) * size] for at, o in enumerate(offsets)}
+
+
+def give_back(found):
+    blocks = {o: found[-o % TILES : -o % TILES + 1] for o in range(-4, 4)}
+    for width, forward, backward in ((3, (2, 3), (-4, -3, -2)), (1, (-2, 1), (-4, -1, 2))):
+        arrived = {**ring_step(blocks, width, forward), **ring_step(blocks, -width, backward)}
+        blocks = {**blocks, **arrived}
+    return jnp.concatenate([blocks[-j if j <= 4 else TILES - j] for j in range(TILES)], 0)
 
 
 def per_device(
@@ -412,14 +443,13 @@
     to_west = [(i + 1, i) for i in range(TILES - 1)]
     to_east = [(i, i + 1) for i in range(TILES - 1)]
 
-    west, east = pack(state, rates)
+    west, east, sent = pack(state, rates)
     from_west = lax.ppermute(east, "tile", to_east)
     from_east = lax.ppermute(west, "tile", to_west)
-    base, high, low = call(
+    base, high, low, ready = call(
         prepare_kernel,
-        [shape(COLS, PAD, LANES), shape(PAD, PAD, dtype=BF16), shape(PAD, PAD, dtype=BF16)],
-        (state, drive, error_root, physics.reshape(ROWS, ROWS), west),
-        WIDE,
+        [shape(COLS, PAD, LANES), shape(PAD, PAD, dtype=BF16), shape(PAD, PAD, dtype=BF16), shape(8, LANES)],
+        (state, drive, error_root, physics.reshape(ROWS, ROWS), sent),
         scratch=[
             pltpu.VMEM((ROWS, COLS, LANES), F32),
             pltpu.VMEM((ROWS, COLS, LANES), F32),
@@ -435,34 +465,21 @@
         moved=10**6,
         far=(0, 1, 2),
         far_out=(0, 1, 2),
-        unread=(4,),
-    )
-    queries, chosen, spread = call(
+    )
+    queries, places = call(
         sort_kernel,
-        [shape(TILES, FIELDS, CAP), shape(TILES, SLOTS), shape(CAP, SLOTS)],
-        (me, obs_index, obs_frac, base),
-        8,
+        [shape(TILES, FIELDS, CAP), shape(2 * TILES, SLOTS)],
+        (obs_index, obs_frac, ready),
         flops=10**7,
         moved=10**5,
-        smem=(0,),
-        unread=(3,),
-    )
-    queries = call(
-        hand_on_kernel,
-        shape(TILES, FIELDS, CAP),
-        (queries, from_west, from_east),
-        4,
-        moved=10**5,
-        unread=(1, 2),
-    )
-    blocks = hop([queries[j] for j in range(TILES)], 4, 1)
+    )
+    arrived = lax.all_to_all(queries, "tile", 0, 0, tiled=True)
     parts = shape(PARTS, PART, LANES)
     wide = COLS + 2 * STEPS
     end, keep, send = call(
         advance_kernel,
         [shape(COLS, PAD, LANES), parts, parts],
-        (state, rates, from_west, from_east, core, high, low, base),
-        30,
+        (state, rates, from_west, from_east, core, high, low, base, arrived),
         scratch=[
             pltpu.VMEM((4, COLS, LANES), F32),
             pltpu.VMEM((STEPS, 8, LANES), F32),
@@ -483,52 +500,55 @@
         flops=15 * 10**9,
         moved=6 * field,
         smem=(4,),
-        far=(0, 1, 2, 3, 5, 6, 7),
+        far=(0, 1, 2, 3, 5, 6, 7, 8),
         far_out=(0,),
     )
     swap = [(0, 1), (1, 0)]
     partner = lax.ppermute(send, "core", swap)
-    blocks = hop(blocks, 2, 1)
-    pair = call(pair_kernel, parts, (keep, partner, blocks[7]), 6, flops=10**6, moved=2 * field, unread=(2,))
+    pair, paired = call(pair_kernel, [parts, shape(8, LANES)], (keep, partner), flops=10**6, moved=2 * field)
     gathered = lax.all_to_all(pair, ("y", "x"), 0, 0, tiled=True)
-    blocks = hop(blocks, 1, 1)
-    arrived = jnp.concatenate(blocks, 0).reshape(TILES, FIELDS, CAP)
     found = call(
         observe_kernel,
         shape(TILES, CAP),
-        (arrived, end, pair),
-        10,
-        scratch=[pltpu.VMEM((PAD, COLS * LANES), BF16), pltpu.VMEM((PAD, COLS * LANES), BF16)],
+        (me, arrived, end, paired),
+        scratch=[
+            pltpu.VMEM((PAD, COLS * LANES), BF16),
+            pltpu.VMEM((PAD, COLS * LANES), BF16),
+            pltpu.VMEM((COLS, PAD, LANES), F32),
+            pltpu.SemaphoreType.DMA((COLS,)),
+        ],
         flops=3 * 10**9,
         moved=field,
-        unread=(2,),
-    )
-    totals = call(scan_kernel, parts, (gathered, found), 6, flops=10**7, moved=field, unread=(1,))
+        smem=(0,),
+        far=(2,),
+    )
+    totals = call(scan_kernel, parts, (gathered, found), flops=10**7, moved=field)
     before = lax.all_to_all(totals, ("y", "x"), 0, 0, tiled=True)
-    back = [found[j : j + 1] for j in range(TILES)]
-    for bit in (4, 2, 1):
-        back = hop(back, bit, -1)
     departure = call(
         depart_kernel,
         shape(1, SLOTS),
-        (obs_count, jnp.concatenate(back, 0), chosen, spread, obs_value),
-        4,
+        (obs_count, me, give_back(found), places, obs_value),
         flops=10**7,
         moved=10**6,
-        smem=(0,),
+        smem=(0, 1),
     )
     for_partner = call(
-        share_kernel, parts, (core, before, keep, departure), 6, flops=10**7, moved=2 * field, smem=(0,), unread=(3,)
+        share_kernel, parts, (core, before, keep, departure), flops=10**7, moved=2 * field, smem=(0,), far=(3,)
     )
     other = lax.ppermute(for_partner, "core", swap)
+    fours = (4, 4, PART, LANES)
     summed = call(
         finish_kernel,
         shape(ROWS, COLS, LANES),
-        (core, base, before, partner, other),
-        10,
+        (core, base, before.reshape(fours), partner.reshape(fours), other.reshape(fours)),
+        scratch=[pltpu.VMEM((COLS, PAD, LANES), F32)]
+        + [pltpu.VMEM(fours, F32)] * 3
+        + [pltpu.VMEM((PAD, COLS, LANES), F32), pltpu.SemaphoreType.DMA((4, 4)), pltpu.SemaphoreType.DMA((4,))],
         flops=10**7,
         moved=4 * field,
         smem=(0,),
+        far=(1, 2, 3, 4),
+        far_out=(0,),
     )
     return summed.reshape(increment.shape), departure
 

time: 128 us -> 122 us (0.953)
  waiting for transfers between devices: 40.1 us -> 26.1 us
  Pallas kernels: 32.2 us -> 44.7 us
  local copies, waits for them, and re-layouts: 16.5 us -> 7.65 us
  starting transfers between devices: 37.2 us -> 40.5 us
    ppermute x1, waiting for transfers between devices: 14 us -> 0.01 us  [per_device(): from_west = lax.ppermute(east, 'tile', to_east)]
    all_to_all x0 -> x1, waiting for transfers between devices: none -> 12.8 us  [per_device(): arrived = lax.all_to_all(queries, 'tile', 0, 0, tiled=True)]
    pallas_call x11 -> x10, Pallas kernels: 32.2 us -> 44.7 us  [call(): pl.pallas_call(body, out_shape=outs, in_specs=specs, out_specs=out_specs...]
    unnamed x50 -> x17, local copies, waits for them, and re-layouts: 16.4 us -> 6.05 us
    all_to_all x0 -> x1, starting transfers between devices: none -> 9.77 us  [per_device(): arrived = lax.all_to_all(queries, 'tile', 0, 0, tiled=True)]
    ppermute x6 -> x4, waiting for transfers between devices: 11.9 us -> 3.29 us  [ring_step(): lax.ppermute(parcel, 'tile', [(i, (i + by) % TILES) for i in range(TILES)])]
    ppermute x6 -> x4, starting transfers between devices: 13.9 us -> 7.8 us  [ring_step(): lax.ppermute(parcel, 'tile', [(i, (i + by) % TILES) for i in range(TILES)])]
    ppermute x1, waiting for transfers between devices: 3.05 us -> 0.01 us  [per_device(): from_east = lax.ppermute(west, 'tile', to_west)]
  transfers between devices with their start and end apart: 12 -> 11, of which waited for: 10 -> 8; matrix products, arithmetic and copies ran while one was open for 1% -> 2% of each run, Pallas kernels for 20% -> 17%
where the time goes in v5:
time: 122 us; the launch traced here: 121 us
  Pallas kernels  44.7 us (37%)
  starting transfers between devices  40.5 us (33%)
  waiting for transfers between devices  26.1 us (21%)
  local copies, waits for them, and re-layouts  7.65 us (6%)
  between operations  1.58 us (1%)
    pallas_call x10, Pallas kernels, call(): pl.pallas_call(body, out_shape=outs, in_specs=specs, out_specs=out_specs...  44.7 us
    all_to_all x1, waiting for transfers between devices, per_device(): arrived = lax.all_to_all(queries, 'tile', 0, 0, tiled=True)  12.8 us
    all_to_all x1, starting transfers between devices, per_device(): arrived = lax.all_to_all(queries, 'tile', 0, 0, tiled=True)  9.77 us
    ppermute x4, starting transfers between devices, ring_step(): lax.ppermute(parcel, 'tile', [(i, (i + by) % TILES) for i in range(TILES)])  7.8 us
    all_to_all x1, starting transfers between devices, per_device(): gathered = lax.all_to_all(pair, ('y', 'x'), 0, 0, tiled=True)  6.77 us
    unnamed x17, local copies, waits for them, and re-layouts  6.05 us
    all_to_all x1, starting transfers between devices, per_device(): before = lax.all_to_all(totals, ('y', 'x'), 0, 0, tiled=True)  5.4 us
    all_to_all x1, waiting for transfers between devices, per_device(): before = lax.all_to_all(totals, ('y', 'x'), 0, 0, tiled=True)  5.04 us
  transfers between devices with their start and end apart: 11, of which 8 were waited for; matrix products, arithmetic and copies ran while one was open for 2% of the time, Pallas kernels for 17%

profile of v5, /device:TPU:1, one launch (start us, length us, event | category | flops | bytes accessed | tf_op | source)
XLA Modules:
  0.0 120.7 jit_solution(1754487863280967335)
XLA Ops:
  0.6 3.3 %shard_map.104 = (f32[6,416,128]{2,1,0:T(8,128)}, f32[6,416,128]{2,1,0:T(8,128)}, f32[8,128]{1,0:T(8,128)}) custom-call(f32[411,8,128]{2,1,0:T(8,128)} %bitcast.13, f32[4,8,128]{2,1,0:T(8,128)} %bitcast.21), custom_call_target="tpu_custom_call" | custom-call | bytes 5111808 | tf_op jit(solution)/shard_map/pallas_call | solution.py:41
  4.0 4.5 %collective-permute-start = (f32[6,416,128]{2,1,0:T(8,128)}, f32[6,416,128]{2,1,0:T(8,128)S(1)}, u32[]{:S(2)}, u32[]{:S(2)}) collective-permute-start(f32[6,416,128]{2,1,0:T(8,128)} %get-tuple-element.18), channel_id=1, source_target_pairs={{0,1},{1,2},{2,3},{3,4},{4,5},{5,6},{6,7},{8,9},{9,10},{10,11},{11... | collective-permute-start | bytes 3833864 | tf_op jit(solution)/shard_map/ppermute | solution.py:447
  8.4 1.3 %collective-permute-start.1 = (f32[6,416,128]{2,1,0:T(8,128)}, f32[6,416,128]{2,1,0:T(8,128)S(1)}, u32[]{:S(2)}, u32[]{:S(2)}) collective-permute-start(f32[6,416,128]{2,1,0:T(8,128)} %get-tuple-element.19), channel_id=1, source_target_pairs={{1,0},{2,1},{3,2},{4,3},{5,4},{6,5},{7,6},{9,8},{10,9},{11,10},{12... | collective-permute-start | bytes 3833864 | tf_op jit(solution)/shard_map/ppermute | solution.py:448
  9.8 1.0 copy.13
  10.7 7.1 %shard_map.105 = (f32[8,416,128]{2,1,0:T(8,128)}, bf16[416,416]{1,0:T(8,128)(2,1)}, bf16[416,416]{1,0:T(8,128)(2,1)}, f32[8,128]{1,0:T(8,128)}) custom-call(f32[411,8,128]{2,1,0:T(8,128)} %bitcast.14, f32[411,8,128]{2,1,0:T(8,128)} %bitcast.18, f32[411,411]{1,0:T(8,128)} %root_ref.1, f32[411,411]{1,0:T(8,128)} %bitcast.16, f32[8,128]{1,0:T(8,128)} %get-tuple-element.16.order_ref), custom_call_target="tpu_custom_call" | custom-call | flops 100000000 | bytes 1000000 | tf_op jit(solution)/shard_map/pallas_call | solution.py:41
  17.9 3.2 %shard_map.106 = (f32[8,8,128]{2,1,0:T(8,128)}, f32[16,512]{1,0:T(8,128)}) custom-call(s32[3,1,512]{2,1,0:T(1,128)} %index_ref.1, f32[2,1,512]{2,1,0:T(1,128)} %frac_ref.1, f32[8,128]{1,0:T(8,128)} %get-tuple-element.22.order_ref), custom_call_target="tpu_custom_call" | custom-call | flops 10000000 | bytes 100000 | tf_op jit(solution)/shard_map/pallas_call | solution.py:41
  21.1 9.8 %all-to-all-start = ((f32[8,8,128]{2,1,0:T(8,128)}), f32[8,8,128]{2,1,0:T(8,128)S(1)}, u32[]{:S(2)}, u32[]{:S(2)}) async-start(f32[8,8,128]{2,1,0:T(8,128)} %get-tuple-element.23), calls=%async_computation | async-start | bytes 65536 | tf_op jit(solution)/shard_map/all_to_all | solution.py:476
  30.9 12.8 %all-to-all-done.order_ref.obs_ref = f32[8,8,128]{2,1,0:T(8,128)S(1)} async-done(((f32[8,8,128]{2,1,0:T(8,128)}), f32[8,8,128]{2,1,0:T(8,128)S(1)}, u32[]{:S(2)}, u32[]{:S(2)}) %all-to-all-start) | async-done | bytes 32800 | tf_op jit(solution)/shard_map/all_to_all | solution.py:476
  45.1 12.6 %shard_map.107 = (f32[8,416,128]{2,1,0:T(8,128)}, f32[16,104,128]{2,1,0:T(8,128)}, f32[16,104,128]{2,1,0:T(8,128)}) custom-call(f32[411,8,128]{2,1,0:T(8,128)} %bitcast.15, f32[4,8,128]{2,1,0:T(8,128)} %bitcast.22, f32[6,416,128]{2,1,0:T(8,128)} %copy-done.6, f32[6,416,128]{2,1,0:T(8,128)} %copy-done.7, s32[1]{0:T(128)} %bitcast.core_ref, ...), custom_call_target="tpu_custom_call" | custom-call | flops 15000000512 | bytes 10223616 | tf_op jit(solution)/shard_map/pallas_call | solution.py:41
  57.7 1.8 %collective-permute-start.2 = (f32[16,104,128]{2,1,0:T(8,128)}, f32[16,104,128]{2,1,0:T(8,128)S(1)}, u32[]{:S(2)}, u32[]{:S(2)}) collective-permute-start(f32[16,104,128]{2,1,0:T(8,128)} %get-tuple-element.25), channel_id=1, source_target_pairs={{0,8},{8,0},{1,9},{9,1},{2,10},{10,2},{3,11},{11,3},{4,12},{12,4},... | collective-permute-start | bytes 2555912 | tf_op jit(solution)/shard_map/ppermute | solution.py:507
  60.2 1.6 %collective-permute-done.2.partner_ref = f32[16,104,128]{2,1,0:T(8,128)S(1)} collective-permute-done((f32[16,104,128]{2,1,0:T(8,128)}, f32[16,104,128]{2,1,0:T(8,128)S(1)}, u32[]{:S(2)}, u32[]{:S(2)}) %collective-permute-start.2) | collective-permute-done | bytes 852000 | tf_op jit(solution)/shard_map/ppermute | solution.py:507
  61.8 0.9 copy-done.1
  62.7 2.4 %shard_map.108 = (f32[16,104,128]{2,1,0:T(8,128)}, f32[8,128]{1,0:T(8,128)}) custom-call(f32[16,104,128]{2,1,0:T(8,128)} %get-tuple-element.24.keep_ref, f32[16,104,128]{2,1,0:T(8,128)} %copy-done.1), custom_call_target="tpu_custom_call" | custom-call | flops 1000000 | bytes 3407872 | tf_op jit(solution)/shard_map/pallas_call | solution.py:41
  65.1 6.8 %all-to-all-start.1 = ((f32[16,104,128]{2,1,0:T(8,128)}), f32[16,104,128]{2,1,0:T(8,128)S(1)}, u32[]{:S(2)}, u32[]{:S(2)}) async-start(f32[16,104,128]{2,1,0:T(8,128)} %get-tuple-element.26), calls=%async_computation.1 | async-start | bytes 1703936 | tf_op jit(solution)/shard_map/all_to_all | solution.py:509
  71.9 6.5 %shard_map.109.order_ref = f32[8,128]{1,0:T(8,128)} custom-call(s32[1]{0:T(128)} %bitcast.4.me_ref, f32[8,8,128]{2,1,0:T(8,128)} %copy-done.5, f32[8,416,128]{2,1,0:T(8,128)} %get-tuple-element.27.end_ref, f32[8,128]{1,0:T(8,128)} %get-tuple-element.28.order_ref), custom_call_target="tpu_custom_call" | custom-call | flops 3000000000 | bytes 1703936 | tf_op jit(solution)/shard_map/pallas_call | solution.py:41
  78.3 1.0 fusion
  79.3 3.3 %collective-permute-start.4 = (f32[2,128]{1,0:T(2,128)S(1)}, f32[2,128]{1,0:T(2,128)S(1)}, u32[]{:S(2)}, u32[]{:S(2)}) collective-permute-start(f32[2,128]{1,0:T(2,128)S(1)} %pad_maximum_fusion.2), channel_id=1, source_target_pairs={{0,3},{1,4},{2,5},{3,6},{4,7},{5,0},{6,1},{7,2},{8,11},{9,12},{10,... | collective-permute-start | bytes 3080 | tf_op jit(solution)/shard_map/ppermute | solution.py:421
  82.6 1.3 %collective-permute-start.3 = (f32[3,128]{1,0:T(4,128)S(1)}, f32[3,128]{1,0:T(4,128)S(1)}, u32[]{:S(2)}, u32[]{:S(2)}) collective-permute-start(f32[3,128]{1,0:T(4,128)S(1)} %pad_maximum_fusion), channel_id=1, source_target_pairs={{0,5},{1,6},{2,7},{3,0},{4,1},{5,2},{6,3},{7,4},{8,13},{9,14},{10,... | collective-permute-start | bytes 4616 | tf_op jit(solution)/shard_map/ppermute | solution.py:421
  84.8 1.2 %all-to-all-done.1.in_ref = f32[16,104,128]{2,1,0:T(8,128)S(1)} async-done(((f32[16,104,128]{2,1,0:T(8,128)}), f32[16,104,128]{2,1,0:T(8,128)S(1)}, u32[]{:S(2)}, u32[]{:S(2)}) %all-to-all-start.1) | async-done | bytes 852000 | tf_op jit(solution)/shard_map/all_to_all | solution.py:509
  86.1 0.9 copy-done.2
  87.0 2.3 %shard_map.110 = f32[16,104,128]{2,1,0:T(8,128)} custom-call(f32[16,104,128]{2,1,0:T(8,128)} %copy-done.2, f32[8,128]{1,0:T(8,128)} %shard_map.109.order_ref), custom_call_target="tpu_custom_call" | custom-call | flops 10000000 | bytes 1703936 | tf_op jit(solution)/shard_map/pallas_call | solution.py:41
  89.2 5.4 %all-to-all-start.2 = ((f32[16,104,128]{2,1,0:T(8,128)}), f32[16,104,128]{2,1,0:T(8,128)S(1)}, u32[]{:S(2)}, u32[]{:S(2)}) async-start(f32[16,104,128]{2,1,0:T(8,128)} %shard_map.110), calls=%async_computation.2 | async-start | bytes 1703936 | tf_op jit(solution)/shard_map/all_to_all | solution.py:526
  94.7 3.1 %collective-permute-start.6 = (f32[2,128]{1,0:T(2,128)S(1)}, f32[2,128]{1,0:T(2,128)S(1)}, u32[]{:S(2)}, u32[]{:S(2)}) collective-permute-start(f32[2,128]{1,0:T(2,128)S(1)} %pad_maximum_fusion.3), channel_id=1, source_target_pairs={{0,1},{1,2},{2,3},{3,4},{4,5},{5,6},{6,7},{7,0},{8,9},{9,10},{10,1... | collective-permute-start | bytes 3080 | tf_op jit(solution)/shard_map/ppermute | solution.py:421
  98.5 1.8 %collective-permute-done.5 = f32[3,128]{1,0:T(4,128)S(1)} collective-permute-done((f32[3,128]{1,0:T(4,128)S(1)}, f32[3,128]{1,0:T(4,128)S(1)}, u32[]{:S(2)}, u32[]{:S(2)}) %collective-permute-start.5) | collective-permute-done | bytes 1568 | tf_op jit(solution)/shard_map/ppermute | solution.py:421
  100.9 1.6 %shard_map.111.order_ref = f32[1,512]{1,0:T(1,128)} custom-call(s32[1,1]{1,0:T(1,128)S(6)} %copy.14.count_ref, s32[1]{0:T(128)} %bitcast.4.me_ref, f32[8,128]{1,0:T(8,128)} %concatenate.19.back_ref, f32[16,512]{1,0:T(8,128)} %get-tuple-element.29.place_ref, f32[1,512]{1,0:T(1,128)} %value_ref.1), custom_call_target="tpu_custom_call" | custom-call | flops 10000000 | bytes 1000000 | tf_op jit(solution)/shard_map/pallas_call | solution.py:41
  102.5 5.0 %all-to-all-done.2.before_ref = f32[16,104,128]{2,1,0:T(8,128)S(1)} async-done(((f32[16,104,128]{2,1,0:T(8,128)}), f32[16,104,128]{2,1,0:T(8,128)S(1)}, u32[]{:S(2)}, u32[]{:S(2)}) %all-to-all-start.2) | async-done | bytes 852000 | tf_op jit(solution)/shard_map/all_to_all | solution.py:526
  107.6 0.9 copy-done
  108.5 2.4 %shard_map.112 = f32[16,104,128]{2,1,0:T(8,128)} custom-call(s32[1]{0:T(128)} %bitcast.core_ref, f32[16,104,128]{2,1,0:T(8,128)} %copy-done, f32[16,104,128]{2,1,0:T(8,128)} %get-tuple-element.24.keep_ref, f32[1,512]{1,0:T(1,128)} %shard_map.111.order_ref), custom_call_target="tpu_custom_call" | custom-call | flops 10000000 | bytes 3407872 | tf_op jit(solution)/shard_map/pallas_call | solution.py:41
  110.9 3.2 %collective-permute-start.7 = (f32[16,104,128]{2,1,0:T(8,128)}, f32[16,104,128]{2,1,0:T(8,128)S(1)}, u32[]{:S(2)}, u32[]{:S(2)}) collective-permute-start(f32[16,104,128]{2,1,0:T(8,128)} %shard_map.112), channel_id=1, source_target_pairs={{0,8},{8,0},{1,9},{9,1},{2,10},{10,2},{3,11},{11,3},{4,12},{12,4},... | collective-permute-start | bytes 2555912 | tf_op jit(solution)/shard_map/ppermute | solution.py:538
  114.1 2.2 %collective-permute-done.7 = f32[16,104,128]{2,1,0:T(8,128)S(1)} collective-permute-done((f32[16,104,128]{2,1,0:T(8,128)}, f32[16,104,128]{2,1,0:T(8,128)S(1)}, u32[]{:S(2)}, u32[]{:S(2)}) %collective-permute-start.7) | collective-permute-done | bytes 852000 | tf_op jit(solution)/shard_map/ppermute | solution.py:538
  116.4 0.9 copy-done.3
  117.3 3.2 %shard_map.113 = f32[411,8,128]{2,1,0:T(8,128)} custom-call(s32[1]{0:T(128)} %bitcast.core_ref, f32[8,416,128]{2,1,0:T(8,128)} %get-tuple-element.17.base_ref, f32[4,4,104,128]{3,2,1,0:T(8,128)} %bitcast.12, f32[4,4,104,128]{3,2,1,0:T(8,128)} %bitcast.17, f32[4,4,104,128]{3,2,1,0:T(8,128)} %bitcast.20), custom_call_target="tpu_custom_call" | custom-call | flops 10000000 | bytes 6815744 | tf_op jit(solution)/shard_map/pallas_call | solution.py:41
  (27 shorter events, 3.7 us)
Async XLA Ops:
  0.6 9.1 %copy-start.4 = (f32[1,411,411]{2,0,1:T(1,128)S(1)}, f32[1,411,411]{2,0,1:T(1,128)}, u32[]{:S(2)}) copy-start(f32[1,411,411]{2,0,1:T(1,128)} %param.12) | copy-start | bytes 2027056
  4.0 39.7 %collective-permute-start = (f32[6,416,128]{2,1,0:T(8,128)}, f32[6,416,128]{2,1,0:T(8,128)S(1)}, u32[]{:S(2)}, u32[]{:S(2)}) collective-permute-start(f32[6,416,128]{2,1,0:T(8,128)} %get-tuple-element.18), channel_id=1, source_target_pairs={{0,1},{1,2},{2,3},{3,4},{4,5},{5,6},{6,7},{8,9},{9,10},{10,11},{11... | collective-permute-start | bytes 3833864 | tf_op jit(solution)/shard_map/ppermute | solution.py:447
  8.4 35.2 %collective-permute-start.1 = (f32[6,416,128]{2,1,0:T(8,128)}, f32[6,416,128]{2,1,0:T(8,128)S(1)}, u32[]{:S(2)}, u32[]{:S(2)}) collective-permute-start(f32[6,416,128]{2,1,0:T(8,128)} %get-tuple-element.19), channel_id=1, source_target_pairs={{1,0},{2,1},{3,2},{4,3},{5,4},{6,5},{7,6},{9,8},{10,9},{11,10},{12... | collective-permute-start | bytes 3833864 | tf_op jit(solution)/shard_map/ppermute | solution.py:448
  21.1 22.5 %all-to-all-start = ((f32[8,8,128]{2,1,0:T(8,128)}), f32[8,8,128]{2,1,0:T(8,128)S(1)}, u32[]{:S(2)}, u32[]{:S(2)}) async-start(f32[8,8,128]{2,1,0:T(8,128)} %get-tuple-element.23), calls=%async_computation | async-start | bytes 65536 | tf_op jit(solution)/shard_map/all_to_all | solution.py:476
  43.6 0.6 copy-start.5
  43.6 1.1 copy-start.6
  43.6 1.5 %copy-start.7 = (f32[6,416,128]{2,1,0:T(8,128)}, f32[6,416,128]{2,1,0:T(8,128)S(1)}, u32[]{:S(2)}) copy-start(f32[6,416,128]{2,1,0:T(8,128)S(1)} %collective-permute-done.1.east_ref) | copy-start | bytes 3833860
  57.7 4.0 %collective-permute-start.2 = (f32[16,104,128]{2,1,0:T(8,128)}, f32[16,104,128]{2,1,0:T(8,128)S(1)}, u32[]{:S(2)}, u32[]{:S(2)}) collective-permute-start(f32[16,104,128]{2,1,0:T(8,128)} %get-tuple-element.25), channel_id=1, source_target_pairs={{0,8},{8,0},{1,9},{9,1},{2,10},{10,2},{3,11},{11,3},{4,12},{12,4},... | collective-permute-start | bytes 2555912 | tf_op jit(solution)/shard_map/ppermute | solution.py:507
  61.8 0.9 copy-start.1
  65.1 21.0 %all-to-all-start.1 = ((f32[16,104,128]{2,1,0:T(8,128)}), f32[16,104,128]{2,1,0:T(8,128)S(1)}, u32[]{:S(2)}, u32[]{:S(2)}) async-start(f32[16,104,128]{2,1,0:T(8,128)} %get-tuple-element.26), calls=%async_computation.1 | async-start | bytes 1703936 | tf_op jit(solution)/shard_map/all_to_all | solution.py:509
  79.3 5.5 %collective-permute-start.4 = (f32[2,128]{1,0:T(2,128)S(1)}, f32[2,128]{1,0:T(2,128)S(1)}, u32[]{:S(2)}, u32[]{:S(2)}) collective-permute-start(f32[2,128]{1,0:T(2,128)S(1)} %pad_maximum_fusion.2), channel_id=1, source_target_pairs={{0,3},{1,4},{2,5},{3,6},{4,7},{5,0},{6,1},{7,2},{8,11},{9,12},{10,... | collective-permute-start | bytes 3080 | tf_op jit(solution)/shard_map/ppermute | solution.py:421
  82.6 12.1 %collective-permute-start.3 = (f32[3,128]{1,0:T(4,128)S(1)}, f32[3,128]{1,0:T(4,128)S(1)}, u32[]{:S(2)}, u32[]{:S(2)}) collective-permute-start(f32[3,128]{1,0:T(4,128)S(1)} %pad_maximum_fusion), channel_id=1, source_target_pairs={{0,5},{1,6},{2,7},{3,0},{4,1},{5,2},{6,3},{7,4},{8,13},{9,14},{10,... | collective-permute-start | bytes 4616 | tf_op jit(solution)/shard_map/ppermute | solution.py:421
  86.1 0.9 copy-start.2
  89.2 18.3 %all-to-all-start.2 = ((f32[16,104,128]{2,1,0:T(8,128)}), f32[16,104,128]{2,1,0:T(8,128)S(1)}, u32[]{:S(2)}, u32[]{:S(2)}) async-start(f32[16,104,128]{2,1,0:T(8,128)} %shard_map.110), calls=%async_computation.2 | async-start | bytes 1703936 | tf_op jit(solution)/shard_map/all_to_all | solution.py:526
  94.7 3.8 %collective-permute-start.6 = (f32[2,128]{1,0:T(2,128)S(1)}, f32[2,128]{1,0:T(2,128)S(1)}, u32[]{:S(2)}, u32[]{:S(2)}) collective-permute-start(f32[2,128]{1,0:T(2,128)S(1)} %pad_maximum_fusion.3), channel_id=1, source_target_pairs={{0,1},{1,2},{2,3},{3,4},{4,5},{5,6},{6,7},{7,0},{8,9},{9,10},{10,1... | collective-permute-start | bytes 3080 | tf_op jit(solution)/shard_map/ppermute | solution.py:421
  97.8 2.5 %collective-permute-start.5 = (f32[3,128]{1,0:T(4,128)S(1)}, f32[3,128]{1,0:T(4,128)S(1)}, u32[]{:S(2)}, u32[]{:S(2)}) collective-permute-start(f32[3,128]{1,0:T(4,128)S(1)} %pad_maximum_fusion.1), channel_id=1, source_target_pairs={{0,7},{1,0},{2,1},{3,2},{4,3},{5,4},{6,5},{7,6},{8,15},{9,8},{10,9... | collective-permute-start | bytes 4616 | tf_op jit(solution)/shard_map/ppermute | solution.py:421
  107.6 0.9 copy-start
  110.9 5.5 %collective-permute-start.7 = (f32[16,104,128]{2,1,0:T(8,128)}, f32[16,104,128]{2,1,0:T(8,128)S(1)}, u32[]{:S(2)}, u32[]{:S(2)}) collective-permute-start(f32[16,104,128]{2,1,0:T(8,128)} %shard_map.112), channel_id=1, source_target_pairs={{0,8},{8,0},{1,9},{9,1},{2,10},{10,2},{3,11},{11,3},{4,12},{12,4},... | collective-permute-start | bytes 2555912 | tf_op jit(solution)/shard_map/ppermute | solution.py:538
  116.3 0.9 copy-start.3

commit v6 on v5

--- a/solution.py
+++ b/solution.py
@@ -28,7 +28,7 @@
 WIDE = 56
 
 
-def call(body, outs, ins, scratch=(), flops=0, moved=0, smem=(), far=(), far_out=()):
+def call(body, outs, ins, scratch=(), flops=0, moved=0, smem=(), far=(), far_out=(), mib=WIDE):
     specs = [
         pl.BlockSpec(memory_space=pltpu.SMEM if at in smem else pl.ANY if at in far else pltpu.VMEM)
         for at in range(len(ins))
@@ -44,7 +44,7 @@
         in_specs=specs,
         out_specs=out_specs if many else out_specs[0],
         scratch_shapes=list(scratch),
-        compiler_params=pltpu.CompilerParams(vmem_limit_bytes=WIDE * MIB),
+        compiler_params=pltpu.CompilerParams(vmem_limit_bytes=mib * MIB),
         cost_estimate=pl.CostEstimate(flops=flops, bytes_accessed=moved, transcendentals=0),
     )(*ins)
 
@@ -167,10 +167,14 @@
         copy.wait()
 
 
+def rotated(j):
+    return j % 5 in (0, 2)
+
+
 def advance_kernel(
     inc_ref, rate_ref, west_ref, east_ref, core_ref, high_ref, low_ref, base_ref, order_ref,
     end_ref, keep_ref, send_ref,
-    rate, west_rate, east_rate, table, band, own, west, east, odd, even, state, base, high, low, sems
+    rate, west_rate, east_rate, table, band, own, west, east, odd, even, state, base, high, low, split, sems
 ):
     at = PAD - 8
     weights = [
@@ -208,8 +212,13 @@
         else:
             rates = [east_rate[j - STEPS - COLS, first + i : first + i + 1, :] for i in range(4)]
         center = 1.0 - (rates[0] + rates[1] + rates[2] + rates[3])
-        table[2 * j] = jnp.broadcast_to(rates[0], (8, LANES))
-        table[2 * j + 1] = jnp.broadcast_to(rates[1], (8, LANES))
+        table[5 * j] = jnp.broadcast_to(rates[0], (8, LANES))
+        table[5 * j + 1] = jnp.broadcast_to(rates[1], (8, LANES))
+        if rotated(j):
+            table[5 * j + 2] = jnp.broadcast_to(center, (8, LANES))
+            table[5 * j + 3] = jnp.broadcast_to(jnp.where(lane[:1] == LANES - 1, 0.0, rates[2]), (8, LANES))
+            table[5 * j + 4] = jnp.broadcast_to(jnp.where(lane[:1] == 0, 0.0, rates[3]), (8, LANES))
+            continue
         along = jnp.where(row == lane, center, 0.0)
         along = jnp.where(row == lane + 1, rates[2], along)
         along = jnp.where(row == lane - 1, rates[3], along)
@@ -220,11 +229,16 @@
         band[j, LANES:, LANES:] = jnp.zeros((LANES, LANES), BF16)
     flat = own.reshape(PAD * COLS, LANES)
 
-    for copy in fields:
+    for copy in fields[:3]:
         copy.wait()
 
     def block(b, carry):
         rows = pl.ds(pl.multiple_of(b * HALF, 16), HALF)
+
+        @pl.when(b == 1)
+        def _():
+            for copy in fields[3:]:
+                copy.wait()
 
         def load(step, j):
             if step > 0:
@@ -240,11 +254,18 @@
 
         for step in range(1, STEPS + 1):
             for j in range(step, wide - step):
-                parts = jnp.concatenate(two_parts(load(step - 1, j)), 1)
-                along = jnp.dot(parts, band[j], preferred_element_type=F32)
-                total = tiles(along[:, :LANES] + along[:, LANES:])
-                total = total + table[2 * j] * tiles(load(step - 1, j + 1))
-                total = total + table[2 * j + 1] * tiles(load(step - 1, j - 1))
+                value = load(step - 1, j)
+                if rotated(j):
+                    value = tiles(value)
+                    total = table[5 * j + 2] * value
+                    total = total + table[5 * j + 3] * pltpu.roll(value, LANES - 1, 2)
+                    total = total + table[5 * j + 4] * pltpu.roll(value, 1, 2)
+                else:
+                    parts = jnp.concatenate(two_parts(value), 1)
+                    along = jnp.dot(parts, band[j], preferred_element_type=F32)
+                    total = tiles(along[:, :LANES] + along[:, LANES:])
+                total = total + table[5 * j] * tiles(load(step - 1, j + 1))
+                total = total + table[5 * j + 1] * tiles(load(step - 1, j - 1))
                 total = total.reshape(HALF, LANES)
                 if step == STEPS:
                     state[j - STEPS, rows, :] = total
@@ -269,8 +290,10 @@
                 state[c + k] = column
                 rest = base[c + k] - column
                 for q in range(4):
-                    out_ref[4 * (i + k) + q] = rest[q * PART : (q + 1) * PART]
-            pair = pl.ds(c, 2)
+                    split[kind, 4 * (i + k) + q] = rest[q * PART : (q + 1) * PART]
+            pair, some = pl.ds(c, 2), pl.ds(4 * i, 8)
+            outgoing.append(pltpu.make_async_copy(split.at[kind, some], out_ref.at[some], sems.at[16 + kind * 2 + i // 2]))
+            outgoing[-1].start()
             outgoing.append(pltpu.make_async_copy(state.at[pair], end_ref.at[pair], sems.at[12 + kind * 2 + i // 2]))
             outgoing[-1].start()
     for copy in outgoing:
@@ -299,36 +322,21 @@
     out_ref[...] = before_ref[...] + first * keep_ref[...]
 
 
-def finish_kernel(core_ref, base_ref, before_ref, partner_ref, other_ref, out_ref, base, before, partner, other, out, sems, out_sems):
+def finish_kernel(core_ref, base_ref, before_ref, partner_ref, other_ref, out_ref, out, sems):
     core = core_ref[0]
-    incoming = []
-    for q in range(4):
-        rows = pl.ds(q * PART, PART)
-        incoming.append(
-            [
-                pltpu.make_async_copy(base_ref.at[:, rows], base.at[:, rows], sems.at[0, q]),
-                pltpu.make_async_copy(before_ref.at[:, q], before.at[:, q], sems.at[1, q]),
-                pltpu.make_async_copy(partner_ref.at[:, q], partner.at[:, q], sems.at[2, q]),
-                pltpu.make_async_copy(other_ref.at[:, q], other.at[:, q], sems.at[3, q]),
-            ]
-        )
-        for copy in incoming[q]:
-            copy.start()
     flat = out.reshape(PAD * COLS, LANES)
     second = (core == 1).astype(F32)
     outgoing = []
     for q in range(4):
-        for copy in incoming[q]:
-            copy.wait()
         for c in range(COLS):
-            i = c % 4
-            own = before[i, q] + second * partner[i, q]
-            earlier = jnp.where(core == c // 4, own, other[i, q])
+            at = 4 * (c % 4) + q
+            own = before_ref[at] + second * partner_ref[at]
+            earlier = jnp.where(core == c // 4, own, other_ref[at])
             flat[pl.ds(q * PART * COLS + c, PART, stride=COLS), :] = (
-                base[c, q * PART : (q + 1) * PART, :] + earlier
+                base_ref[c, q * PART : (q + 1) * PART, :] + earlier
             )
         rows = pl.ds(q * PART, min(PART, ROWS - q * PART))
-        outgoing.append(pltpu.make_async_copy(out.at[rows], out_ref.at[rows], out_sems.at[q]))
+        outgoing.append(pltpu.make_async_copy(out.at[rows], out_ref.at[rows], sems.at[q]))
         outgoing[-1].start()
     for copy in outgoing:
         copy.wait()
@@ -366,13 +374,9 @@
         )
 
 
-def observe_kernel(me_ref, obs_ref, end_ref, order_ref, out_ref, end_high, end_low, end, sems):
-    copies = [pltpu.make_async_copy(end_ref.at[c], end.at[c], sems.at[c]) for c in range(COLS)]
-    for copy in copies:
-        copy.start()
+def observe_kernel(me_ref, obs_ref, end_ref, order_ref, out_ref, end_high, end_low):
     for c in range(COLS):
-        copies[c].wait()
-        high, low = two_parts(end[c])
+        high, low = two_parts(end_ref[c])
         end_high[:, c * LANES : (c + 1) * LANES] = high
         end_low[:, c * LANES : (c + 1) * LANES] = low
     lanes = 2 * CAP
@@ -403,7 +407,8 @@
         out_ref[j + 1 : j + 2, :] = value[:, CAP:]
 
 
-def depart_kernel(count_ref, me_ref, back_ref, place_ref, value_ref, out_ref):
+def depart_kernel(count_ref, me_ref, back_ref, place_ref, value_ref, out_ref, ready_ref):
+    ready_ref[...] = jnp.zeros((8, LANES), F32)
     spread = jnp.dot(
         back_ref[...], spread_of(place_ref[TILES : TILES + 1]), precision=HIGHEST, preferred_element_type=F32
     )
@@ -472,6 +477,7 @@
         (obs_index, obs_frac, ready),
         flops=10**7,
         moved=10**5,
+        mib=8,
     )
     arrived = lax.all_to_all(queries, "tile", 0, 0, tiled=True)
     parts = shape(PARTS, PART, LANES)
@@ -484,7 +490,7 @@
             pltpu.VMEM((4, COLS, LANES), F32),
             pltpu.VMEM((STEPS, 8, LANES), F32),
             pltpu.VMEM((STEPS, 8, LANES), F32),
-            pltpu.VMEM((2 * wide, 8, LANES), F32),
+            pltpu.VMEM((5 * wide, 8, LANES), F32),
             pltpu.VMEM((wide, 2 * LANES, 2 * LANES), BF16),
             pltpu.VMEM((PAD, COLS, LANES), F32),
             pltpu.VMEM((STEPS, PAD, LANES), F32),
@@ -495,17 +501,18 @@
             pltpu.VMEM((COLS, PAD, LANES), F32),
             pltpu.VMEM((PAD, PAD), BF16),
             pltpu.VMEM((PAD, PAD), BF16),
-            pltpu.SemaphoreType.DMA((16,)),
+            pltpu.VMEM((2, PARTS, PART, LANES), F32),
+            pltpu.SemaphoreType.DMA((20,)),
         ],
         flops=15 * 10**9,
         moved=6 * field,
         smem=(4,),
         far=(0, 1, 2, 3, 5, 6, 7, 8),
-        far_out=(0,),
+        far_out=range(3),
     )
     swap = [(0, 1), (1, 0)]
     partner = lax.ppermute(send, "core", swap)
-    pair, paired = call(pair_kernel, [parts, shape(8, LANES)], (keep, partner), flops=10**6, moved=2 * field)
+    pair, paired = call(pair_kernel, [parts, shape(8, LANES)], (keep, partner), flops=10**6, moved=2 * field, mib=6)
     gathered = lax.all_to_all(pair, ("y", "x"), 0, 0, tiled=True)
     found = call(
         observe_kernel,
@@ -514,41 +521,37 @@
         scratch=[
             pltpu.VMEM((PAD, COLS * LANES), BF16),
             pltpu.VMEM((PAD, COLS * LANES), BF16),
-            pltpu.VMEM((COLS, PAD, LANES), F32),
-            pltpu.SemaphoreType.DMA((COLS,)),
         ],
         flops=3 * 10**9,
         moved=field,
         smem=(0,),
-        far=(2,),
-    )
-    totals = call(scan_kernel, parts, (gathered, found), flops=10**7, moved=field)
+        mib=10,
+    )
+    totals = call(scan_kernel, parts, (gathered, found), flops=10**7, moved=field, mib=6)
     before = lax.all_to_all(totals, ("y", "x"), 0, 0, tiled=True)
-    departure = call(
+    departure, departed = call(
         depart_kernel,
-        shape(1, SLOTS),
+        [shape(1, SLOTS), shape(8, LANES)],
         (obs_count, me, give_back(found), places, obs_value),
         flops=10**7,
         moved=10**6,
         smem=(0, 1),
+        mib=4,
     )
     for_partner = call(
-        share_kernel, parts, (core, before, keep, departure), flops=10**7, moved=2 * field, smem=(0,), far=(3,)
+        share_kernel, parts, (core, before, keep, departed), flops=10**7, moved=2 * field, smem=(0,), mib=6
     )
     other = lax.ppermute(for_partner, "core", swap)
-    fours = (4, 4, PART, LANES)
     summed = call(
         finish_kernel,
         shape(ROWS, COLS, LANES),
-        (core, base, before.reshape(fours), partner.reshape(fours), other.reshape(fours)),
-        scratch=[pltpu.VMEM((COLS, PAD, LANES), F32)]
-        + [pltpu.VMEM(fours, F32)] * 3
-        + [pltpu.VMEM((PAD, COLS, LANES), F32), pltpu.SemaphoreType.DMA((4, 4)), pltpu.SemaphoreType.DMA((4,))],
+        (core, base, before, partner, other),
+        scratch=[pltpu.VMEM((PAD, COLS, LANES), F32), pltpu.SemaphoreType.DMA((4,))],
         flops=10**7,
         moved=4 * field,
         smem=(0,),
-        far=(1, 2, 3, 4),
         far_out=(0,),
+        mib=10,
     )
     return summed.reshape(increment.shape), departure
 

time: 122 us -> 110 us (0.902)
  Pallas kernels: 44.7 us -> 33.5 us
  waiting for transfers between devices: 26.1 us -> 30 us
  local copies, waits for them, and re-layouts: 7.65 us -> 5.44 us
  starting transfers between devices: 40.5 us -> 38.5 us
    pallas_call x10, Pallas kernels: 44.7 us -> 33.5 us  [call(): pl.pallas_call(body, out_shape=outs, in_specs=specs, out_specs=out_specs...]
    all_to_all x1, waiting for transfers between devices: 1.25 us -> 3.27 us  [per_device(): gathered = lax.all_to_all(pair, ('y', 'x'), 0, 0, tiled=True)]
    all_to_all x1, starting transfers between devices: 5.4 us -> 3.79 us  [per_device(): before = lax.all_to_all(totals, ('y', 'x'), 0, 0, tiled=True)]
    all_to_all x1, waiting for transfers between devices: 5.04 us -> 6.46 us  [per_device(): before = lax.all_to_all(totals, ('y', 'x'), 0, 0, tiled=True)]
    unnamed x17 -> x25, local copies, waits for them, and re-layouts: 6.05 us -> 5.38 us
  transfers between devices with their start and end apart: 11 -> 11, of which waited for: 8 -> 8; matrix products, arithmetic and copies ran while one was open for 2% -> 1% of each run, Pallas kernels for 17% -> 14%
where the time goes in v6:
time: 110 us; the launch traced here: 109 us
  starting transfers between devices  38.5 us (35%)
  Pallas kernels  33.5 us (30%)
  waiting for transfers between devices  30 us (27%)
  local copies, waits for them, and re-layouts  5.44 us (5%)
  between operations  1.64 us (1%)
    pallas_call x10, Pallas kernels, call(): pl.pallas_call(body, out_shape=outs, in_specs=specs, out_specs=out_specs...  33.5 us
    all_to_all x1, waiting for transfers between devices, per_device(): arrived = lax.all_to_all(queries, 'tile', 0, 0, tiled=True)  12.8 us
    all_to_all x1, starting transfers between devices, per_device(): arrived = lax.all_to_all(queries, 'tile', 0, 0, tiled=True)  9.77 us
    ppermute x4, starting transfers between devices, ring_step(): lax.ppermute(parcel, 'tile', [(i, (i + by) % TILES) for i in range(TILES)])  7.79 us
    all_to_all x1, starting transfers between devices, per_device(): gathered = lax.all_to_all(pair, ('y', 'x'), 0, 0, tiled=True)  6.76 us
    all_to_all x1, waiting for transfers between devices, per_device(): before = lax.all_to_all(totals, ('y', 'x'), 0, 0, tiled=True)  6.46 us
    unnamed x25, local copies, waits for them, and re-layouts  5.38 us
    ppermute x1, starting transfers between devices, per_device(): from_west = lax.ppermute(east, 'tile', to_east)  4.45 us
  transfers between devices with their start and end apart: 11, of which 8 were waited for; matrix products, arithmetic and copies ran while one was open for 1% of the time, Pallas kernels for 14%

profile of v6, /device:TPU:1, one launch (start us, length us, event | category | flops | bytes accessed | tf_op | source)
XLA Modules:
  0.0 109.1 jit_solution(18236788316153748246)
XLA Ops:
  0.6 3.3 %shard_map.104 = (f32[6,416,128]{2,1,0:T(8,128)}, f32[6,416,128]{2,1,0:T(8,128)}, f32[8,128]{1,0:T(8,128)}) custom-call(f32[411,8,128]{2,1,0:T(8,128)} %bitcast.9, f32[4,8,128]{2,1,0:T(8,128)} %bitcast.15), custom_call_target="tpu_custom_call" | custom-call | bytes 5111808 | tf_op jit(solution)/shard_map/pallas_call | solution.py:41
  4.0 4.5 %collective-permute-start = (f32[6,416,128]{2,1,0:T(8,128)}, f32[6,416,128]{2,1,0:T(8,128)S(1)}, u32[]{:S(2)}, u32[]{:S(2)}) collective-permute-start(f32[6,416,128]{2,1,0:T(8,128)} %get-tuple-element.20), channel_id=1, source_target_pairs={{0,1},{1,2},{2,3},{3,4},{4,5},{5,6},{6,7},{8,9},{9,10},{10,11},{11... | collective-permute-start | bytes 3833864 | tf_op jit(solution)/shard_map/ppermute | solution.py:452
  8.4 1.3 %collective-permute-start.1 = (f32[6,416,128]{2,1,0:T(8,128)}, f32[6,416,128]{2,1,0:T(8,128)}, u32[]{:S(2)}, u32[]{:S(2)}) collective-permute-start(f32[6,416,128]{2,1,0:T(8,128)} %get-tuple-element.21), channel_id=1, source_target_pairs={{1,0},{2,1},{3,2},{4,3},{5,4},{6,5},{7,6},{9,8},{10,9},{11,10},{12... | collective-permute-start | bytes 3833864 | tf_op jit(solution)/shard_map/ppermute | solution.py:453
  9.7 1.0 copy.13
  10.7 7.1 %shard_map.105 = (f32[8,416,128]{2,1,0:T(8,128)}, bf16[416,416]{1,0:T(8,128)(2,1)}, bf16[416,416]{1,0:T(8,128)(2,1)}, f32[8,128]{1,0:T(8,128)}) custom-call(f32[411,8,128]{2,1,0:T(8,128)} %bitcast.10, f32[411,8,128]{2,1,0:T(8,128)} %bitcast.13, f32[411,411]{1,0:T(8,128)} %root_ref.1, f32[411,411]{1,0:T(8,128)} %bitcast.12, f32[8,128]{1,0:T(8,128)} %get-tuple-element.18.order_ref), custom_call_target="tpu_custom_call" | custom-call | flops 100000000 | bytes 1000000 | tf_op jit(solution)/shard_map/pallas_call | solution.py:41
  17.9 0.7 copy-done.8
  18.5 2.5 %shard_map.106 = (f32[8,8,128]{2,1,0:T(8,128)}, f32[16,512]{1,0:T(8,128)S(1)}) custom-call(s32[3,1,512]{2,1,0:T(1,128)S(1)} %copy-done.6, f32[2,1,512]{2,1,0:T(1,128)S(1)} %copy-done.7, f32[8,128]{1,0:T(8,128)S(1)} %copy-done.8), custom_call_target="tpu_custom_call" | custom-call | flops 10000000 | bytes 100000 | tf_op jit(solution)/shard_map/pallas_call | solution.py:41
  21.1 9.8 %all-to-all-start = ((f32[8,8,128]{2,1,0:T(8,128)}), f32[8,8,128]{2,1,0:T(8,128)S(1)}, u32[]{:S(2)}, u32[]{:S(2)}) async-start(f32[8,8,128]{2,1,0:T(8,128)} %get-tuple-element.25), calls=%async_computation | async-start | bytes 65536 | tf_op jit(solution)/shard_map/all_to_all | solution.py:482
  30.8 12.8 %all-to-all-done.order_ref.obs_ref = f32[8,8,128]{2,1,0:T(8,128)S(1)} async-done(((f32[8,8,128]{2,1,0:T(8,128)}), f32[8,8,128]{2,1,0:T(8,128)S(1)}, u32[]{:S(2)}, u32[]{:S(2)}) %all-to-all-start) | async-done | bytes 32800 | tf_op jit(solution)/shard_map/all_to_all | solution.py:482
  43.6 0.6 copy-done.3
  44.7 12.4 %shard_map.107 = (f32[8,416,128]{2,1,0:T(8,128)}, f32[16,104,128]{2,1,0:T(8,128)}, f32[16,104,128]{2,1,0:T(8,128)}) custom-call(f32[411,8,128]{2,1,0:T(8,128)} %bitcast.11, f32[4,8,128]{2,1,0:T(8,128)} %bitcast.16, f32[6,416,128]{2,1,0:T(8,128)} %copy-done.11, f32[6,416,128]{2,1,0:T(8,128)} %collective-permute-done.1.east_ref, s32[1]{0:T(128)} %bitcast.core_ref, ...), custom_call_target="tpu_custom_call" | custom-call | flops 15000000512 | bytes 10223616 | tf_op jit(solution)/shard_map/pallas_call | solution.py:41
  57.1 1.9 %collective-permute-start.2 = (f32[16,104,128]{2,1,0:T(8,128)}, f32[16,104,128]{2,1,0:T(8,128)S(1)}, u32[]{:S(2)}, u32[]{:S(2)}) collective-permute-start(f32[16,104,128]{2,1,0:T(8,128)} %get-tuple-element.27), channel_id=1, source_target_pairs={{0,8},{8,0},{1,9},{9,1},{2,10},{10,2},{3,11},{11,3},{4,12},{12,4},... | collective-permute-start | bytes 2555912 | tf_op jit(solution)/shard_map/ppermute | solution.py:514
  59.7 1.6 %collective-permute-done.2.partner_ref = f32[16,104,128]{2,1,0:T(8,128)S(1)} collective-permute-done((f32[16,104,128]{2,1,0:T(8,128)}, f32[16,104,128]{2,1,0:T(8,128)S(1)}, u32[]{:S(2)}, u32[]{:S(2)}) %collective-permute-start.2) | collective-permute-done | bytes 852000 | tf_op jit(solution)/shard_map/ppermute | solution.py:514
  61.2 1.2 %copy-done = f32[16,104,128]{2,1,0:T(8,128)S(1)} copy-done((f32[16,104,128]{2,1,0:T(8,128)S(1)}, f32[16,104,128]{2,1,0:T(8,128)}, u32[]{:S(2)}) %copy-start) | copy-done | bytes 851992
  62.4 1.0 shard_map.108
  63.4 6.8 %all-to-all-start.1 = ((f32[16,104,128]{2,1,0:T(8,128)}), f32[16,104,128]{2,1,0:T(8,128)S(1)}, u32[]{:S(2)}, u32[]{:S(2)}) async-start(f32[16,104,128]{2,1,0:T(8,128)} %get-tuple-element.28), calls=%async_computation.1 | async-start | bytes 1703936 | tf_op jit(solution)/shard_map/all_to_all | solution.py:516
  70.2 1.4 %copy-done.9 = f32[8,416,128]{2,1,0:T(8,128)S(1)} copy-done((f32[8,416,128]{2,1,0:T(8,128)S(1)}, f32[8,416,128]{2,1,0:T(8,128)}, u32[]{:S(2)}) %copy-start.9) | copy-done | bytes 1703960
  71.6 3.6 %shard_map.109.order_ref = f32[8,128]{1,0:T(8,128)S(1)} custom-call(s32[1]{0:T(128)} %bitcast.4.me_ref, f32[8,8,128]{2,1,0:T(8,128)S(1)} %copy-done.4, f32[8,416,128]{2,1,0:T(8,128)S(1)} %copy-done.9, f32[8,128]{1,0:T(8,128)S(1)} %get-tuple-element.30.order_ref), custom_call_target="tpu_custom_call" | custom-call | flops 3000000000 | bytes 1703936 | tf_op jit(solution)/shard_map/pallas_call | solution.py:41
  75.3 3.3 %collective-permute-start.4 = (f32[2,128]{1,0:T(2,128)S(1)}, f32[2,128]{1,0:T(2,128)S(1)}, u32[]{:S(2)}, u32[]{:S(2)}) collective-permute-start(f32[2,128]{1,0:T(2,128)S(1)} %pad_maximum_fusion.2), channel_id=1, source_target_pairs={{0,3},{1,4},{2,5},{3,6},{4,7},{5,0},{6,1},{7,2},{8,11},{9,12},{10,... | collective-permute-start | bytes 3080 | tf_op jit(solution)/shard_map/ppermute | solution.py:426
  78.6 1.3 %collective-permute-start.3 = (f32[3,128]{1,0:T(4,128)S(1)}, f32[3,128]{1,0:T(4,128)S(1)}, u32[]{:S(2)}, u32[]{:S(2)}) collective-permute-start(f32[3,128]{1,0:T(4,128)S(1)} %pad_maximum_fusion), channel_id=1, source_target_pairs={{0,5},{1,6},{2,7},{3,0},{4,1},{5,2},{6,3},{7,4},{8,13},{9,14},{10,... | collective-permute-start | bytes 4616 | tf_op jit(solution)/shard_map/ppermute | solution.py:426
  79.9 1.2 %collective-permute-done.4 = f32[2,128]{1,0:T(2,128)S(1)} collective-permute-done((f32[2,128]{1,0:T(2,128)S(1)}, f32[2,128]{1,0:T(2,128)S(1)}, u32[]{:S(2)}, u32[]{:S(2)}) %collective-permute-start.4) | collective-permute-done | bytes 1056 | tf_op jit(solution)/shard_map/ppermute | solution.py:426
  81.1 3.3 %all-to-all-done.1.in_ref = f32[16,104,128]{2,1,0:T(8,128)S(1)} async-done(((f32[16,104,128]{2,1,0:T(8,128)}), f32[16,104,128]{2,1,0:T(8,128)S(1)}, u32[]{:S(2)}, u32[]{:S(2)}) %all-to-all-start.1) | async-done | bytes 852000 | tf_op jit(solution)/shard_map/all_to_all | solution.py:516
  84.4 1.1 %shard_map.110 = f32[16,104,128]{2,1,0:T(8,128)} custom-call(f32[16,104,128]{2,1,0:T(8,128)S(1)} %all-to-all-done.1.in_ref, f32[8,128]{1,0:T(8,128)S(1)} %shard_map.109.order_ref), custom_call_target="tpu_custom_call" | custom-call | flops 10000000 | bytes 1703936 | tf_op jit(solution)/shard_map/pallas_call | solution.py:41
  85.5 3.8 %all-to-all-start.2 = ((f32[16,104,128]{2,1,0:T(8,128)}), f32[16,104,128]{2,1,0:T(8,128)S(1)}, u32[]{:S(2)}, u32[]{:S(2)}) async-start(f32[16,104,128]{2,1,0:T(8,128)} %shard_map.110), calls=%async_computation.2 | async-start | bytes 1703936 | tf_op jit(solution)/shard_map/all_to_all | solution.py:531
  89.4 3.1 %collective-permute-start.6 = (f32[2,128]{1,0:T(2,128)S(1)}, f32[2,128]{1,0:T(2,128)S(1)}, u32[]{:S(2)}, u32[]{:S(2)}) collective-permute-start(f32[2,128]{1,0:T(2,128)S(1)} %pad_maximum_fusion.3), channel_id=1, source_target_pairs={{0,1},{1,2},{2,3},{3,4},{4,5},{5,6},{6,7},{7,0},{8,9},{9,10},{10,1... | collective-permute-start | bytes 3080 | tf_op jit(solution)/shard_map/ppermute | solution.py:426
  92.5 0.6 collective-permute-done.6
  93.2 2.1 %collective-permute-done.5 = f32[3,128]{1,0:T(4,128)S(1)} collective-permute-done((f32[3,128]{1,0:T(4,128)S(1)}, f32[3,128]{1,0:T(4,128)S(1)}, u32[]{:S(2)}, u32[]{:S(2)}) %collective-permute-start.5) | collective-permute-done | bytes 1568 | tf_op jit(solution)/shard_map/ppermute | solution.py:426
  95.3 0.9 shard_map.111
  96.2 6.5 %all-to-all-done.2.before_ref = f32[16,104,128]{2,1,0:T(8,128)S(1)} async-done(((f32[16,104,128]{2,1,0:T(8,128)}), f32[16,104,128]{2,1,0:T(8,128)S(1)}, u32[]{:S(2)}, u32[]{:S(2)}) %all-to-all-start.2) | async-done | bytes 852000 | tf_op jit(solution)/shard_map/all_to_all | solution.py:531
  102.7 2.8 %collective-permute-start.7 = (f32[16,104,128]{2,1,0:T(8,128)S(1)}, f32[16,104,128]{2,1,0:T(8,128)S(1)}, u32[]{:S(2)}, u32[]{:S(2)}) collective-permute-start(f32[16,104,128]{2,1,0:T(8,128)S(1)} %shard_map.112), channel_id=1, source_target_pairs={{0,8},{8,0},{1,9},{9,1},{2,10},{10,2},{3,11},{11,3},{4,12},{12,4},... | collective-permute-start | bytes 2555912 | tf_op jit(solution)/shard_map/ppermute | solution.py:544
  105.5 2.0 %collective-permute-done.7.other_ref = f32[16,104,128]{2,1,0:T(8,128)S(1)} collective-permute-done((f32[16,104,128]{2,1,0:T(8,128)S(1)}, f32[16,104,128]{2,1,0:T(8,128)S(1)}, u32[]{:S(2)}, u32[]{:S(2)}) %collective-permute-start.7) | collective-permute-done | bytes 852000 | tf_op jit(solution)/shard_map/ppermute | solution.py:544
  107.5 1.4 %shard_map.113 = f32[411,8,128]{2,1,0:T(8,128)} custom-call(s32[1]{0:T(128)} %bitcast.core_ref, f32[8,416,128]{2,1,0:T(8,128)S(1)} %copy-done.2, f32[16,104,128]{2,1,0:T(8,128)S(1)} %all-to-all-done.2.before_ref, f32[16,104,128]{2,1,0:T(8,128)S(1)} %collective-permute-done.2.partner_ref, f32[16,104,128]{2,1,0:T(8,128)S(1)} %collective-permute-done.7.other_ref), custom_call_target="tpu_custom_call" | custom-call | flops 10000000 | bytes 6815744 | tf_op jit(solution)/shard_map/pallas_call | solution.py:41
  (35 shorter events, 0.8 us)
Async XLA Ops:
  0.6 9.1 %copy-start.10 = (f32[1,411,411]{2,0,1:T(1,128)S(1)}, f32[1,411,411]{2,0,1:T(1,128)}, u32[]{:S(2)}) copy-start(f32[1,411,411]{2,0,1:T(1,128)} %param.12) | copy-start | bytes 2027056
  4.0 39.7 %collective-permute-start = (f32[6,416,128]{2,1,0:T(8,128)}, f32[6,416,128]{2,1,0:T(8,128)S(1)}, u32[]{:S(2)}, u32[]{:S(2)}) collective-permute-start(f32[6,416,128]{2,1,0:T(8,128)} %get-tuple-element.20), channel_id=1, source_target_pairs={{0,1},{1,2},{2,3},{3,4},{4,5},{5,6},{6,7},{8,9},{9,10},{10,11},{11... | collective-permute-start | bytes 3833864 | tf_op jit(solution)/shard_map/ppermute | solution.py:452
  8.4 35.2 %collective-permute-start.1 = (f32[6,416,128]{2,1,0:T(8,128)}, f32[6,416,128]{2,1,0:T(8,128)}, u32[]{:S(2)}, u32[]{:S(2)}) collective-permute-start(f32[6,416,128]{2,1,0:T(8,128)} %get-tuple-element.21), channel_id=1, source_target_pairs={{1,0},{2,1},{3,2},{4,3},{5,4},{6,5},{7,6},{9,8},{10,9},{11,10},{12... | collective-permute-start | bytes 3833864 | tf_op jit(solution)/shard_map/ppermute | solution.py:453
  10.7 7.1 %copy-start.6 = (s32[3,1,512]{2,1,0:T(1,128)S(1)}, s32[3,1,512]{2,1,0:T(1,128)}, u32[]{:S(2)}) copy-start(s32[3,1,512]{2,1,0:T(1,128)} %index_ref.1) | copy-start | bytes 18436
  10.7 7.1 %copy-start.7 = (f32[2,1,512]{2,1,0:T(1,128)S(1)}, f32[2,1,512]{2,1,0:T(1,128)}, u32[]{:S(2)}) copy-start(f32[2,1,512]{2,1,0:T(1,128)} %frac_ref.1) | copy-start | bytes 12292
  17.9 0.7 copy-start.8
  21.1 22.6 %all-to-all-start = ((f32[8,8,128]{2,1,0:T(8,128)}), f32[8,8,128]{2,1,0:T(8,128)S(1)}, u32[]{:S(2)}, u32[]{:S(2)}) async-start(f32[8,8,128]{2,1,0:T(8,128)} %get-tuple-element.25), calls=%async_computation | async-start | bytes 65536 | tf_op jit(solution)/shard_map/all_to_all | solution.py:482
  43.6 0.6 copy-start.3
  43.6 1.1 %copy-start.11 = (f32[6,416,128]{2,1,0:T(8,128)}, f32[6,416,128]{2,1,0:T(8,128)S(1)}, u32[]{:S(2)}) copy-start(f32[6,416,128]{2,1,0:T(8,128)S(1)} %collective-permute-done.west_ref) | copy-start | bytes 3833860
  57.1 4.1 %collective-permute-start.2 = (f32[16,104,128]{2,1,0:T(8,128)}, f32[16,104,128]{2,1,0:T(8,128)S(1)}, u32[]{:S(2)}, u32[]{:S(2)}) collective-permute-start(f32[16,104,128]{2,1,0:T(8,128)} %get-tuple-element.27), channel_id=1, source_target_pairs={{0,8},{8,0},{1,9},{9,1},{2,10},{10,2},{3,11},{11,3},{4,12},{12,4},... | collective-permute-start | bytes 2555912 | tf_op jit(solution)/shard_map/ppermute | solution.py:514
  61.2 1.2 %copy-start = (f32[16,104,128]{2,1,0:T(8,128)S(1)}, f32[16,104,128]{2,1,0:T(8,128)}, u32[]{:S(2)}) copy-start(f32[16,104,128]{2,1,0:T(8,128)} %get-tuple-element.26.keep_ref) | copy-start | bytes 2555908
  62.4 7.8 %copy-start.4 = (f32[8,8,128]{2,1,0:T(8,128)S(1)}, f32[8,8,128]{2,1,0:T(8,128)}, u32[]{:S(2)}) copy-start(f32[8,8,128]{2,1,0:T(8,128)} %copy-done.3) | copy-start | bytes 98308
  63.4 21.0 %all-to-all-start.1 = ((f32[16,104,128]{2,1,0:T(8,128)}), f32[16,104,128]{2,1,0:T(8,128)S(1)}, u32[]{:S(2)}, u32[]{:S(2)}) async-start(f32[16,104,128]{2,1,0:T(8,128)} %get-tuple-element.28), calls=%async_computation.1 | async-start | bytes 1703936 | tf_op jit(solution)/shard_map/all_to_all | solution.py:516
  70.2 1.5 %copy-start.9 = (f32[8,416,128]{2,1,0:T(8,128)S(1)}, f32[8,416,128]{2,1,0:T(8,128)}, u32[]{:S(2)}) copy-start(f32[8,416,128]{2,1,0:T(8,128)} %get-tuple-element.29.end_ref) | copy-start | bytes 5111812
  75.3 5.8 %collective-permute-start.4 = (f32[2,128]{1,0:T(2,128)S(1)}, f32[2,128]{1,0:T(2,128)S(1)}, u32[]{:S(2)}, u32[]{:S(2)}) collective-permute-start(f32[2,128]{1,0:T(2,128)S(1)} %pad_maximum_fusion.2), channel_id=1, source_target_pairs={{0,3},{1,4},{2,5},{3,6},{4,7},{5,0},{6,1},{7,2},{8,11},{9,12},{10,... | collective-permute-start | bytes 3080 | tf_op jit(solution)/shard_map/ppermute | solution.py:426
  78.6 10.7 %collective-permute-start.3 = (f32[3,128]{1,0:T(4,128)S(1)}, f32[3,128]{1,0:T(4,128)S(1)}, u32[]{:S(2)}, u32[]{:S(2)}) collective-permute-start(f32[3,128]{1,0:T(4,128)S(1)} %pad_maximum_fusion), channel_id=1, source_target_pairs={{0,5},{1,6},{2,7},{3,0},{4,1},{5,2},{6,3},{7,4},{8,13},{9,14},{10,... | collective-permute-start | bytes 4616 | tf_op jit(solution)/shard_map/ppermute | solution.py:426
  81.1 14.2 %copy-start.5 = (f32[1,512]{1,0:T(1,128)S(1)}, f32[1,512]{1,0:T(1,128)}, u32[]{:S(2)}) copy-start(f32[1,512]{1,0:T(1,128)} %value_ref.1) | copy-start | bytes 6148
  81.1 21.5 %copy-start.1 = (f32[16,104,128]{2,1,0:T(8,128)S(1)}, f32[16,104,128]{2,1,0:T(8,128)}, u32[]{:S(2)}) copy-start(f32[16,104,128]{2,1,0:T(8,128)} %get-tuple-element.26.keep_ref) | copy-start | bytes 2555908
  85.5 17.1 %all-to-all-start.2 = ((f32[16,104,128]{2,1,0:T(8,128)}), f32[16,104,128]{2,1,0:T(8,128)S(1)}, u32[]{:S(2)}, u32[]{:S(2)}) async-start(f32[16,104,128]{2,1,0:T(8,128)} %shard_map.110), calls=%async_computation.2 | async-start | bytes 1703936 | tf_op jit(solution)/shard_map/all_to_all | solution.py:531
  89.4 3.8 %collective-permute-start.6 = (f32[2,128]{1,0:T(2,128)S(1)}, f32[2,128]{1,0:T(2,128)S(1)}, u32[]{:S(2)}, u32[]{:S(2)}) collective-permute-start(f32[2,128]{1,0:T(2,128)S(1)} %pad_maximum_fusion.3), channel_id=1, source_target_pairs={{0,1},{1,2},{2,3},{3,4},{4,5},{5,6},{6,7},{7,0},{8,9},{9,10},{10,1... | collective-permute-start | bytes 3080 | tf_op jit(solution)/shard_map/ppermute | solution.py:426
  92.5 2.8 %collective-permute-start.5 = (f32[3,128]{1,0:T(4,128)S(1)}, f32[3,128]{1,0:T(4,128)S(1)}, u32[]{:S(2)}, u32[]{:S(2)}) collective-permute-start(f32[3,128]{1,0:T(4,128)S(1)} %pad_maximum_fusion.1), channel_id=1, source_target_pairs={{0,7},{1,0},{2,1},{3,2},{4,3},{5,4},{6,5},{7,6},{8,15},{9,8},{10,9... | collective-permute-start | bytes 4616 | tf_op jit(solution)/shard_map/ppermute | solution.py:426
  102.6 4.9 %copy-start.2 = (f32[8,416,128]{2,1,0:T(8,128)S(1)}, f32[8,416,128]{2,1,0:T(8,128)}, u32[]{:S(2)}) copy-start(f32[8,416,128]{2,1,0:T(8,128)} %get-tuple-element.19.base_ref) | copy-start | bytes 5111812
  102.7 4.8 %collective-permute-start.7 = (f32[16,104,128]{2,1,0:T(8,128)S(1)}, f32[16,104,128]{2,1,0:T(8,128)S(1)}, u32[]{:S(2)}, u32[]{:S(2)}) collective-permute-start(f32[16,104,128]{2,1,0:T(8,128)S(1)} %shard_map.112), channel_id=1, source_target_pairs={{0,8},{8,0},{1,9},{9,1},{2,10},{10,2},{3,11},{11,3},{4,12},{12,4},... | collective-permute-start | bytes 2555912 | tf_op jit(solution)/shard_map/ppermute | solution.py:544

commit v7 on v6

--- a/solution.py
+++ b/solution.py
@@ -66,7 +66,7 @@
     return total + jnp.dot(left_low, high, preferred_element_type=F32)
 
 
-def pack_kernel(inc_ref, rate_ref, west_ref, east_ref, sent_ref, held, rates, west, east, in_sems, out_sems):
+def pack_kernel(inc_ref, rate_ref, west0_ref, east0_ref, west1_ref, east1_ref, sent_ref, held, rates, west, east, in_sems, out_sems):
     count = PAD // PART
     incoming = [pltpu.make_async_copy(rate_ref, rates, in_sems.at[count])]
     for b in range(count):
@@ -76,46 +76,61 @@
         copy.start()
     sent_ref[...] = jnp.zeros((8, LANES), F32)
     flat = held.reshape(PAD * COLS, LANES)
+    held[ROWS:] = jnp.zeros((PAD - ROWS, COLS, LANES), F32)
     outgoing = []
     incoming[0].wait()
-    for b in range(count):
-        incoming[b + 1].wait()
-        size = min(PART, ROWS - b * PART)
-        for c in range(COLS):
-            column = flat[pl.ds(b * PART * COLS + c, size, stride=COLS), :]
-            if size < PART:
+    for half, (west_ref, east_ref) in enumerate(((west0_ref, east0_ref), (west1_ref, east1_ref))):
+        for b in (2 * half, 2 * half + 1):
+            incoming[b + 1].wait()
+            rows = slice(b * PART, (b + 1) * PART)
+            for c in range(COLS):
+                column = flat[pl.ds(b * PART * COLS + c, PART, stride=COLS), :]
+                if c < STEPS:
+                    west[c, rows, :] = column
+                if c >= COLS - STEPS:
+                    east[c - COLS + STEPS, rows, :] = column
+        if half == 0:
+            for c in range(COLS):
                 weights = [rates[i, c : c + 1, :] for i in range(4)]
-                column = jnp.concatenate([column] + weights + [jnp.zeros((1, LANES), F32)], 0)
-            if c < STEPS:
-                west[c, b * PART : (b + 1) * PART, :] = column
-            if c >= COLS - STEPS:
-                east[c - COLS + STEPS, b * PART : (b + 1) * PART, :] = column
-        rows = pl.ds(b * PART, PART)
-        outgoing.append(pltpu.make_async_copy(west.at[:, rows], west_ref.at[:, rows], out_sems.at[2 * b]))
-        outgoing.append(pltpu.make_async_copy(east.at[:, rows], east_ref.at[:, rows], out_sems.at[2 * b + 1]))
-        outgoing[-2].start()
-        outgoing[-1].start()
+                weights = jnp.concatenate(weights + [jnp.zeros((4, LANES), F32)], 0)
+                if c < STEPS:
+                    west[c, PAD:, :] = weights
+                if c >= COLS - STEPS:
+                    east[c - COLS + STEPS, PAD:, :] = weights
+        for at, (held_side, side_ref) in enumerate(((west, west_ref), (east, east_ref))):
+            mine = pl.ds(half * HALF, HALF)
+            outgoing.append(
+                pltpu.make_async_copy(held_side.at[:, mine], side_ref.at[:, pl.ds(0, HALF)], out_sems.at[4 * half + at])
+            )
+            outgoing[-1].start()
+            if half == 0:
+                outgoing.append(
+                    pltpu.make_async_copy(
+                        held_side.at[:, pl.ds(PAD, 8)], side_ref.at[:, pl.ds(HALF, 8)], out_sems.at[2 + at]
+                    )
+                )
+                outgoing[-1].start()
     for copy in outgoing:
         copy.wait()
 
 
 def pack(state, rates):
-    halo = shape(STEPS, PAD, LANES)
+    first, second = shape(STEPS, HALF + 8, LANES), shape(STEPS, HALF, LANES)
     return call(
         pack_kernel,
-        [halo, halo, shape(8, LANES)],
+        [first, first, second, second, shape(8, LANES)],
         (state, rates),
         scratch=[
             pltpu.VMEM((PAD, COLS, LANES), F32),
             pltpu.VMEM((4, COLS, LANES), F32),
-            pltpu.VMEM((STEPS, PAD, LANES), F32),
-            pltpu.VMEM((STEPS, PAD, LANES), F32),
+            pltpu.VMEM((STEPS, PAD + 8, LANES), F32),
+            pltpu.VMEM((STEPS, PAD + 8, LANES), F32),
             pltpu.SemaphoreType.DMA((PAD // PART + 1,)),
-            pltpu.SemaphoreType.DMA((2 * PAD // PART,)),
+            pltpu.SemaphoreType.DMA((6,)),
         ],
         moved=3 * PAD * COLS * LANES * 4,
         far=(0, 1),
-        far_out=(0, 1),
+        far_out=range(4),
     )
 
 
@@ -171,46 +186,37 @@
     return j % 5 in (0, 2)
 
 
-def advance_kernel(
-    inc_ref, rate_ref, west_ref, east_ref, core_ref, high_ref, low_ref, base_ref, order_ref,
-    end_ref, keep_ref, send_ref,
-    rate, west_rate, east_rate, table, band, own, west, east, odd, even, state, base, high, low, split, sems
-):
-    at = PAD - 8
+def transport(half, refs, scratch, out, later=()):
+    inc_ref, rate_ref, west_ref, east_ref, west_rate_ref, east_rate_ref = refs
+    rate, west_rate, east_rate, table, band, own, west, east, odd, even, sems = scratch
+    valid = min(HALF, ROWS - half * HALF)
     weights = [
         pltpu.make_async_copy(rate_ref, rate, sems.at[0]),
-        pltpu.make_async_copy(west_ref.at[:, pl.ds(at, 8)], west_rate, sems.at[1]),
-        pltpu.make_async_copy(east_ref.at[:, pl.ds(at, 8)], east_rate, sems.at[2]),
-    ]
-    fields = []
-    for b in range(2):
-        valid = min(HALF, ROWS - b * HALF)
-        rows = pl.ds(b * HALF, HALF)
-        mine = pl.ds(b * HALF, valid)
-        fields.append(pltpu.make_async_copy(inc_ref.at[mine], own.at[mine], sems.at[3 + 3 * b]))
-        fields.append(pltpu.make_async_copy(west_ref.at[:, rows], west.at[:, rows], sems.at[4 + 3 * b]))
-        fields.append(pltpu.make_async_copy(east_ref.at[:, rows], east.at[:, rows], sems.at[5 + 3 * b]))
-    later = [
-        pltpu.make_async_copy(high_ref, high, sems.at[9]),
-        pltpu.make_async_copy(low_ref, low, sems.at[10]),
-        pltpu.make_async_copy(base_ref, base, sems.at[11]),
-    ]
-    for copy in weights + fields + later:
+        pltpu.make_async_copy(west_rate_ref.at[:, pl.ds(HALF, 8)], west_rate, sems.at[1]),
+        pltpu.make_async_copy(east_rate_ref.at[:, pl.ds(HALF, 8)], east_rate, sems.at[2]),
+    ]
+    rows = pl.ds(0, HALF)
+    fields = [
+        pltpu.make_async_copy(inc_ref.at[pl.ds(half * HALF, valid)], own.at[pl.ds(0, valid)], sems.at[3]),
+        pltpu.make_async_copy(west_ref.at[:, rows], west, sems.at[4]),
+        pltpu.make_async_copy(east_ref.at[:, rows], east, sems.at[5]),
+    ]
+    for copy in weights + fields + list(later):
         copy.start()
-    own[ROWS:] = jnp.zeros((PAD - ROWS, COLS, LANES), F32)
+    if valid < HALF:
+        own[valid:] = jnp.zeros((HALF - valid, COLS, LANES), F32)
     for copy in weights:
         copy.wait()
     row = lax.broadcasted_iota(jnp.int32, (LANES, LANES), 0)
     lane = lax.broadcasted_iota(jnp.int32, (LANES, LANES), 1)
     wide = COLS + 2 * STEPS
-    first = ROWS - at
     for j in range(1, wide - 1):
         if j < STEPS:
-            rates = [west_rate[j, first + i : first + i + 1, :] for i in range(4)]
+            rates = [west_rate[j, i : i + 1, :] for i in range(4)]
         elif j < STEPS + COLS:
             rates = [rate[i, j - STEPS : j - STEPS + 1, :] for i in range(4)]
         else:
-            rates = [east_rate[j - STEPS - COLS, first + i : first + i + 1, :] for i in range(4)]
+            rates = [east_rate[j - STEPS - COLS, i : i + 1, :] for i in range(4)]
         center = 1.0 - (rates[0] + rates[1] + rates[2] + rates[3])
         table[5 * j] = jnp.broadcast_to(rates[0], (8, LANES))
         table[5 * j + 1] = jnp.broadcast_to(rates[1], (8, LANES))
@@ -227,54 +233,79 @@
         band[j, LANES:, :LANES] = along_high
         band[j, :LANES, LANES:] = along_low
         band[j, LANES:, LANES:] = jnp.zeros((LANES, LANES), BF16)
-    flat = own.reshape(PAD * COLS, LANES)
-
-    for copy in fields[:3]:
-        copy.wait()
-
-    def block(b, carry):
-        rows = pl.ds(pl.multiple_of(b * HALF, 16), HALF)
-
-        @pl.when(b == 1)
-        def _():
-            for copy in fields[3:]:
-                copy.wait()
-
-        def load(step, j):
-            if step > 0:
-                return (odd if step % 2 else even)[j]
-            if j < STEPS:
-                return west[j, rows, :]
-            if j < STEPS + COLS:
-                return flat[pl.ds(b * (HALF * COLS) + j - STEPS, HALF, stride=COLS), :]
-            return east[j - STEPS - COLS, rows, :]
-
-        def tiles(value):
-            return value.reshape(HALF // 8, 8, LANES)
-
-        for step in range(1, STEPS + 1):
-            for j in range(step, wide - step):
-                value = load(step - 1, j)
-                if rotated(j):
-                    value = tiles(value)
-                    total = table[5 * j + 2] * value
-                    total = total + table[5 * j + 3] * pltpu.roll(value, LANES - 1, 2)
-                    total = total + table[5 * j + 4] * pltpu.roll(value, 1, 2)
-                else:
-                    parts = jnp.concatenate(two_parts(value), 1)
-                    along = jnp.dot(parts, band[j], preferred_element_type=F32)
-                    total = tiles(along[:, :LANES] + along[:, LANES:])
-                total = total + table[5 * j] * tiles(load(step - 1, j + 1))
-                total = total + table[5 * j + 1] * tiles(load(step - 1, j - 1))
-                total = total.reshape(HALF, LANES)
-                if step == STEPS:
-                    state[j - STEPS, rows, :] = total
-                else:
-                    (odd if step % 2 else even)[j] = total
-        return carry
-
-    lax.fori_loop(0, 2, block, 0)
-
+    flat = own.reshape(HALF * COLS, LANES)
+    for copy in fields:
+        copy.wait()
+
+    def load(step, j):
+        if step > 0:
+            return (odd if step % 2 else even)[j]
+        if j < STEPS:
+            return west[j]
+        if j < STEPS + COLS:
+            return flat[pl.ds(j - STEPS, HALF, stride=COLS), :]
+        return east[j - STEPS - COLS]
+
+    def tiles(value):
+        return value.reshape(HALF // 8, 8, LANES)
+
+    for step in range(1, STEPS + 1):
+        for j in range(step, wide - step):
+            value = load(step - 1, j)
+            if rotated(j):
+                value = tiles(value)
+                total = table[5 * j + 2] * value
+                total = total + table[5 * j + 3] * pltpu.roll(value, LANES - 1, 2)
+                total = total + table[5 * j + 4] * pltpu.roll(value, 1, 2)
+            else:
+                parts = jnp.concatenate(two_parts(value), 1)
+                along = jnp.dot(parts, band[j], preferred_element_type=F32)
+                total = tiles(along[:, :LANES] + along[:, LANES:])
+            total = total + table[5 * j] * tiles(load(step - 1, j + 1))
+            total = total + table[5 * j + 1] * tiles(load(step - 1, j - 1))
+            total = total.reshape(HALF, LANES)
+            if step == STEPS:
+                out[j - STEPS] = total
+            else:
+                (odd if step % 2 else even)[j] = total
+
+
+def transport_scratch():
+    wide = COLS + 2 * STEPS
+    return [
+        pltpu.VMEM((4, COLS, LANES), F32),
+        pltpu.VMEM((STEPS, 8, LANES), F32),
+        pltpu.VMEM((STEPS, 8, LANES), F32),
+        pltpu.VMEM((5 * wide, 8, LANES), F32),
+        pltpu.VMEM((wide, 2 * LANES, 2 * LANES), BF16),
+        pltpu.VMEM((HALF, COLS, LANES), F32),
+        pltpu.VMEM((STEPS, HALF, LANES), F32),
+        pltpu.VMEM((STEPS, HALF, LANES), F32),
+        pltpu.VMEM((wide, HALF, LANES), F32),
+        pltpu.VMEM((wide, HALF, LANES), F32),
+        pltpu.SemaphoreType.DMA((6,)),
+    ]
+
+
+def upper_kernel(*refs):
+    ins, (order_ref, out_ref, ready_ref, out, sem), scratch = refs[:6], refs[6:11], refs[11:]
+    ready_ref[...] = jnp.zeros((8, LANES), F32)
+    transport(0, ins, scratch, out)
+    copy = pltpu.make_async_copy(out, out_ref, sem)
+    copy.start()
+    copy.wait()
+
+
+def advance_kernel(*refs):
+    ins, (core_ref, upper_ref, high_ref, low_ref, base_ref, order_ref) = refs[:6], refs[6:12]
+    end_ref, keep_ref, send_ref, upper, lower, base, high, low, split, sems = refs[12:22]
+    later = [
+        pltpu.make_async_copy(high_ref, high, sems.at[0]),
+        pltpu.make_async_copy(low_ref, low, sems.at[1]),
+        pltpu.make_async_copy(upper_ref, upper, sems.at[2]),
+        pltpu.make_async_copy(base_ref, base, sems.at[3]),
+    ]
+    transport(1, ins, refs[22:], lower, later)
     for copy in later:
         copy.wait()
     core = core_ref[0]
@@ -283,26 +314,21 @@
         start = 4 * (core ^ kind)
         for i in (0, 2):
             c = start + i
-            column = jnp.concatenate([state[c], state[c + 1]], 1)
+            column = jnp.concatenate([jnp.concatenate([upper[c + k], lower[c + k]], 0) for k in range(2)], 1)
             end = column + product(high[...], low[...], column)
             for k in range(2):
                 column = end[:, k * LANES : (k + 1) * LANES]
-                state[c + k] = column
                 rest = base[c + k] - column
+                base[c + k] = column
                 for q in range(4):
                     split[kind, 4 * (i + k) + q] = rest[q * PART : (q + 1) * PART]
             pair, some = pl.ds(c, 2), pl.ds(4 * i, 8)
-            outgoing.append(pltpu.make_async_copy(split.at[kind, some], out_ref.at[some], sems.at[16 + kind * 2 + i // 2]))
-            outgoing[-1].start()
-            outgoing.append(pltpu.make_async_copy(state.at[pair], end_ref.at[pair], sems.at[12 + kind * 2 + i // 2]))
+            outgoing.append(pltpu.make_async_copy(split.at[kind, some], out_ref.at[some], sems.at[4 + kind * 2 + i // 2]))
+            outgoing.append(pltpu.make_async_copy(base.at[pair], end_ref.at[pair], sems.at[8 + kind * 2 + i // 2]))
+            outgoing[-2].start()
             outgoing[-1].start()
     for copy in outgoing:
         copy.wait()
-
-
-def pair_kernel(keep_ref, partner_ref, pair_ref, ready_ref):
-    pair_ref[...] = keep_ref[...] + partner_ref[...]
-    ready_ref[...] = jnp.zeros((8, LANES), F32)
 
 
 def scan_kernel(in_ref, order_ref, out_ref):
@@ -448,9 +474,9 @@
     to_west = [(i + 1, i) for i in range(TILES - 1)]
     to_east = [(i, i + 1) for i in range(TILES - 1)]
 
-    west, east, sent = pack(state, rates)
-    from_west = lax.ppermute(east, "tile", to_east)
-    from_east = lax.ppermute(west, "tile", to_west)
+    west0, east0, west1, east1, sent = pack(state, rates)
+    halo0 = lax.ppermute(east0, "tile", to_east), lax.ppermute(west0, "tile", to_west)
+    halo1 = lax.ppermute(east1, "tile", to_east), lax.ppermute(west1, "tile", to_west)
     base, high, low, ready = call(
         prepare_kernel,
         [shape(COLS, PAD, LANES), shape(PAD, PAD, dtype=BF16), shape(PAD, PAD, dtype=BF16), shape(8, LANES)],
@@ -471,48 +497,50 @@
         far=(0, 1, 2),
         far_out=(0, 1, 2),
     )
+    upper, uppered = call(
+        upper_kernel,
+        [shape(COLS, HALF, LANES), shape(8, LANES)],
+        (state, rates, *halo0, *halo0, ready),
+        scratch=[pltpu.VMEM((COLS, HALF, LANES), F32), pltpu.SemaphoreType.DMA] + transport_scratch(),
+        flops=10**8,
+        moved=10**6,
+        far=range(6),
+        far_out=(0,),
+    )
     queries, places = call(
         sort_kernel,
         [shape(TILES, FIELDS, CAP), shape(2 * TILES, SLOTS)],
-        (obs_index, obs_frac, ready),
+        (obs_index, obs_frac, uppered),
         flops=10**7,
         moved=10**5,
         mib=8,
     )
     arrived = lax.all_to_all(queries, "tile", 0, 0, tiled=True)
     parts = shape(PARTS, PART, LANES)
-    wide = COLS + 2 * STEPS
     end, keep, send = call(
         advance_kernel,
         [shape(COLS, PAD, LANES), parts, parts],
-        (state, rates, from_west, from_east, core, high, low, base, arrived),
+        (state, rates, *halo1, *halo0, core, upper, high, low, base, arrived),
         scratch=[
-            pltpu.VMEM((4, COLS, LANES), F32),
-            pltpu.VMEM((STEPS, 8, LANES), F32),
-            pltpu.VMEM((STEPS, 8, LANES), F32),
-            pltpu.VMEM((5 * wide, 8, LANES), F32),
-            pltpu.VMEM((wide, 2 * LANES, 2 * LANES), BF16),
-            pltpu.VMEM((PAD, COLS, LANES), F32),
-            pltpu.VMEM((STEPS, PAD, LANES), F32),
-            pltpu.VMEM((STEPS, PAD, LANES), F32),
-            pltpu.VMEM((wide, HALF, LANES), F32),
-            pltpu.VMEM((wide, HALF, LANES), F32),
-            pltpu.VMEM((COLS, PAD, LANES), F32),
+            pltpu.VMEM((COLS, HALF, LANES), F32),
+            pltpu.VMEM((COLS, HALF, LANES), F32),
             pltpu.VMEM((COLS, PAD, LANES), F32),
             pltpu.VMEM((PAD, PAD), BF16),
             pltpu.VMEM((PAD, PAD), BF16),
             pltpu.VMEM((2, PARTS, PART, LANES), F32),
-            pltpu.SemaphoreType.DMA((20,)),
-        ],
+            pltpu.SemaphoreType.DMA((12,)),
+        ]
+        + transport_scratch(),
         flops=15 * 10**9,
         moved=6 * field,
-        smem=(4,),
-        far=(0, 1, 2, 3, 5, 6, 7, 8),
+        smem=(6,),
+        far=(0, 1, 2, 3, 4, 5, 7, 8, 9, 10, 11),
         far_out=range(3),
     )
     swap = [(0, 1), (1, 0)]
     partner = lax.ppermute(send, "core", swap)
-    pair, paired = call(pair_kernel, [parts, shape(8, LANES)], (keep, partner), flops=10**6, moved=2 * field, mib=6)
+    pair = keep + partner
+    paired = pair[0, :8]
     gathered = lax.all_to_all(pair, ("y", "x"), 0, 0, tiled=True)
     found = call(
         observe_kernel,

time: 110 us -> 117 us (1.064)
  starting transfers between devices: 38.5 us -> 44.5 us
  waiting for transfers between devices: 30 us -> 27.4 us
  other arithmetic: 0.04 us -> 2.19 us
  Pallas kernels: 33.5 us -> 35.4 us
    all_to_all x1, waiting for transfers between devices: 12.8 us -> 6.85 us  [per_device(): arrived = lax.all_to_all(queries, 'tile', 0, 0, tiled=True)]
    ppermute x2 -> x4, starting transfers between devices: 5.74 us -> 11.2 us  [the longest x1 4.41 us: per_device(): lax.ppermute(east0, 'tile', to_east)]
    ppermute x2 -> x4, waiting for transfers between devices: 0.01 us -> 3.02 us  [the longest x1 3.01 us: per_device(): lax.ppermute(west0, 'tile', to_west)]
    ppermute x1, starting transfers between devices: 1.86 us -> 4.53 us  [per_device(): partner = lax.ppermute(send, 'core', swap)]
    all_to_all x1, waiting for transfers between devices: 6.46 us -> 8.64 us  [per_device(): before = lax.all_to_all(totals, ('y', 'x'), 0, 0, tiled=True)]
    add x0 -> x1, other arithmetic: none -> 2.15 us  [per_device(): pair = keep + partner]
    pallas_call x10, Pallas kernels: 33.5 us -> 35.4 us  [call(): pl.pallas_call(body, out_shape=outs, in_specs=specs, out_specs=out_specs...]
    ppermute x4, waiting for transfers between devices: 3.88 us -> 2.05 us  [ring_step(): lax.ppermute(parcel, 'tile', [(i, (i + by) % TILES) for i in range(TILES)])]
  transfers between devices with their start and end apart: 11 -> 13, of which waited for: 8 -> 8; matrix products, arithmetic and copies ran while one was open for 1% -> 1% of each run, Pallas kernels for 14% -> 19%
where the time goes in v7:
time: 117 us
  starting transfers between devices  44.5 us (38%)
  Pallas kernels  35.4 us (30%)
  waiting for transfers between devices  27.4 us (23%)
  local copies, waits for them, and re-layouts  5.29 us (5%)
  other arithmetic  2.19 us (2%)
  between operations  1.69 us (1%)
    pallas_call x10, Pallas kernels, call(): pl.pallas_call(body, out_shape=outs, in_specs=specs, out_specs=out_specs...  35.4 us
    all_to_all x1, waiting for transfers between devices, per_device(): before = lax.all_to_all(totals, ('y', 'x'), 0, 0, tiled=True)  8.64 us
    all_to_all x1, starting transfers between devices, per_device(): arrived = lax.all_to_all(queries, 'tile', 0, 0, tiled=True)  8.03 us
    ppermute x4, starting transfers between devices, ring_step(): lax.ppermute(parcel, 'tile', [(i, (i + by) % TILES) for i in range(TILES)])  7.45 us
    all_to_all x1, waiting for transfers between devices, per_device(): arrived = lax.all_to_all(queries, 'tile', 0, 0, tiled=True)  6.85 us
    all_to_all x1, starting transfers between devices, per_device(): gathered = lax.all_to_all(pair, ('y', 'x'), 0, 0, tiled=True)  6.75 us
    unnamed x27, local copies, waits for them, and re-layouts  4.55 us
    ppermute x1, starting transfers between devices, per_device(): partner = lax.ppermute(send, 'core', swap)  4.53 us
  transfers between devices with their start and end apart: 13, of which 8 were waited for; matrix products, arithmetic and copies ran while one was open for 1% of the time, Pallas kernels for 19%

profile of v7, /device:TPU:1, one launch (start us, length us, event | category | flops | bytes accessed | tf_op | source)
XLA Modules:
  0.0 116.6 jit_solution(11836085480031276753)
XLA Ops:
  0.6 3.5 %shard_map.104 = (f32[6,216,128]{2,1,0:T(8,128)}, f32[6,216,128]{2,1,0:T(8,128)}, f32[6,208,128]{2,1,0:T(8,128)}, f32[6,208,128]{2,1,0:T(8,128)}, f32[8,128]{1,0:T(8,128)}) custom-call(f32[411,8,128]{2,1,0:T(8,128)} %bitcast.11, f32[4,8,128]{2,1,0:T(8,128)} %bitcast.18), custom_call_target="tpu_custom_call" | custom-call | bytes 5111808 | tf_op jit(solution)/shard_map/pallas_call | solution.py:41
  4.1 4.4 %collective-permute-start.2 = (f32[6,216,128]{2,1,0:T(8,128)}, f32[6,216,128]{2,1,0:T(8,128)S(1)}, u32[]{:S(2)}, u32[]{:S(2)}) collective-permute-start(f32[6,216,128]{2,1,0:T(8,128)} %get-tuple-element.24), channel_id=1, source_target_pairs={{0,1},{1,2},{2,3},{3,4},{4,5},{5,6},{6,7},{8,9},{9,10},{10,11},{11... | collective-permute-start | bytes 1990664 | tf_op jit(solution)/shard_map/ppermute | solution.py:478
  8.5 1.3 %collective-permute-start.3 = (f32[6,216,128]{2,1,0:T(8,128)}, f32[6,216,128]{2,1,0:T(8,128)S(1)}, u32[]{:S(2)}, u32[]{:S(2)}) collective-permute-start(f32[6,216,128]{2,1,0:T(8,128)} %get-tuple-element.25), channel_id=1, source_target_pairs={{1,0},{2,1},{3,2},{4,3},{5,4},{6,5},{7,6},{9,8},{10,9},{11,10},{12... | collective-permute-start | bytes 1990664 | tf_op jit(solution)/shard_map/ppermute | solution.py:478
  9.8 4.2 %collective-permute-start = (f32[6,208,128]{2,1,0:T(8,128)}, f32[6,208,128]{2,1,0:T(8,128)S(1)}, u32[]{:S(2)}, u32[]{:S(2)}) collective-permute-start(f32[6,208,128]{2,1,0:T(8,128)} %get-tuple-element.22), channel_id=1, source_target_pairs={{0,1},{1,2},{2,3},{3,4},{4,5},{5,6},{6,7},{8,9},{9,10},{10,11},{11... | collective-permute-start | bytes 1916936 | tf_op jit(solution)/shard_map/ppermute | solution.py:479
  14.0 1.3 %collective-permute-start.1 = (f32[6,208,128]{2,1,0:T(8,128)}, f32[6,208,128]{2,1,0:T(8,128)}, u32[]{:S(2)}, u32[]{:S(2)}) collective-permute-start(f32[6,208,128]{2,1,0:T(8,128)} %get-tuple-element.23), channel_id=1, source_target_pairs={{1,0},{2,1},{3,2},{4,3},{5,4},{6,5},{7,6},{9,8},{10,9},{11,10},{12... | collective-permute-start | bytes 1916936 | tf_op jit(solution)/shard_map/ppermute | solution.py:479
  15.3 1.0 copy.13
  16.3 7.1 %shard_map.105 = (f32[8,416,128]{2,1,0:T(8,128)}, bf16[416,416]{1,0:T(8,128)(2,1)}, bf16[416,416]{1,0:T(8,128)(2,1)}, f32[8,128]{1,0:T(8,128)}) custom-call(f32[411,8,128]{2,1,0:T(8,128)} %bitcast.12, f32[411,8,128]{2,1,0:T(8,128)} %bitcast.16, f32[411,411]{1,0:T(8,128)} %root_ref.1, f32[411,411]{1,0:T(8,128)} %bitcast.15, f32[8,128]{1,0:T(8,128)} %get-tuple-element.20.order_ref), custom_call_target="tpu_custom_call" | custom-call | flops 100000000 | bytes 1000000 | tf_op jit(solution)/shard_map/pallas_call | solution.py:41
  23.4 3.0 %collective-permute-done.3.refs_3_.refs_5_ = f32[6,216,128]{2,1,0:T(8,128)S(1)} collective-permute-done((f32[6,216,128]{2,1,0:T(8,128)}, f32[6,216,128]{2,1,0:T(8,128)S(1)}, u32[]{:S(2)}, u32[]{:S(2)}) %collective-permute-start.3) | collective-permute-done | bytes 663584 | tf_op jit(solution)/shard_map/ppermute | solution.py:478
  26.4 0.8 copy-done.10
  27.3 7.0 %shard_map.106 = (f32[8,208,128]{2,1,0:T(8,128)}, f32[8,128]{1,0:T(8,128)}) custom-call(f32[411,8,128]{2,1,0:T(8,128)} %bitcast.13, f32[4,8,128]{2,1,0:T(8,128)} %bitcast.19, f32[6,216,128]{2,1,0:T(8,128)} %copy-done.9, f32[6,216,128]{2,1,0:T(8,128)} %copy-done.10, f32[6,216,128]{2,1,0:T(8,128)} %copy-done.9, f32[6,216,128]{2,1,0:T(8,128)} %copy-done.10, ...), custom_call_target="tpu_custom_call" | custom-call | flops 100000000 | bytes 1000000 | tf_op jit(solution)/shard_map/pallas_call | solution.py:41
  35.0 2.5 %shard_map.107 = (f32[8,8,128]{2,1,0:T(8,128)}, f32[16,512]{1,0:T(8,128)S(1)}) custom-call(s32[3,1,512]{2,1,0:T(1,128)S(1)} %copy-done.5, f32[2,1,512]{2,1,0:T(1,128)S(1)} %copy-done.6, f32[8,128]{1,0:T(8,128)S(1)} %copy-done.7), custom_call_target="tpu_custom_call" | custom-call | flops 10000000 | bytes 100000 | tf_op jit(solution)/shard_map/pallas_call | solution.py:41
  37.5 8.0 %all-to-all-start = ((f32[8,8,128]{2,1,0:T(8,128)}), f32[8,8,128]{2,1,0:T(8,128)S(1)}, u32[]{:S(2)}, u32[]{:S(2)}) async-start(f32[8,8,128]{2,1,0:T(8,128)} %get-tuple-element.31), calls=%async_computation | async-start | bytes 65536 | tf_op jit(solution)/shard_map/all_to_all | solution.py:518
  45.6 6.9 %all-to-all-done.refs_11_.obs_ref = f32[8,8,128]{2,1,0:T(8,128)S(1)} async-done(((f32[8,8,128]{2,1,0:T(8,128)}), f32[8,8,128]{2,1,0:T(8,128)S(1)}, u32[]{:S(2)}, u32[]{:S(2)}) %all-to-all-start) | async-done | bytes 32800 | tf_op jit(solution)/shard_map/all_to_all | solution.py:518
  53.0 8.3 %shard_map.108 = (f32[8,416,128]{2,1,0:T(8,128)}, f32[16,104,128]{2,1,0:T(8,128)}, f32[16,104,128]{2,1,0:T(8,128)}) custom-call(f32[411,8,128]{2,1,0:T(8,128)} %bitcast.14, f32[4,8,128]{2,1,0:T(8,128)} %bitcast.20, f32[6,208,128]{2,1,0:T(8,128)} %copy-done.12, f32[6,208,128]{2,1,0:T(8,128)} %collective-permute-done.1.refs_3_, f32[6,216,128]{2,1,0:T(8,128)} %copy-done.9, ...), custom_call_target="tpu_custom_call" | custom-call | flops 15000000512 | bytes 10223616 | tf_op jit(solution)/shard_map/pallas_call | solution.py:41
  61.3 4.5 %collective-permute-start.4 = (f32[16,104,128]{2,1,0:T(8,128)}, f32[16,104,128]{2,1,0:T(8,128)S(1)}, u32[]{:S(2)}, u32[]{:S(2)}) collective-permute-start(f32[16,104,128]{2,1,0:T(8,128)} %get-tuple-element.33), channel_id=1, source_target_pairs={{0,8},{8,0},{1,9},{9,1},{2,10},{10,2},{3,11},{11,3},{4,12},{12,4},... | collective-permute-start | bytes 2555912 | tf_op jit(solution)/shard_map/ppermute | solution.py:541
  66.5 1.6 %collective-permute-done.4.partner_ref = f32[16,104,128]{2,1,0:T(8,128)S(1)} collective-permute-done((f32[16,104,128]{2,1,0:T(8,128)}, f32[16,104,128]{2,1,0:T(8,128)S(1)}, u32[]{:S(2)}, u32[]{:S(2)}) %collective-permute-start.4) | collective-permute-done | bytes 852000 | tf_op jit(solution)/shard_map/ppermute | solution.py:541
  68.1 2.1 %add.3 = f32[16,104,128]{2,1,0:T(8,128)} add(f32[16,104,128]{2,1,0:T(8,128)} %get-tuple-element.32.keep_ref, f32[16,104,128]{2,1,0:T(8,128)S(1)} %collective-permute-done.4.partner_ref) | non-fusion elementwise | flops 212992 | bytes 2555904 | tf_op jit(solution)/shard_map/add | solution.py:542
  70.9 6.8 %all-to-all-start.1 = ((f32[16,104,128]{2,1,0:T(8,128)}), f32[16,104,128]{2,1,0:T(8,128)S(1)}, u32[]{:S(2)}, u32[]{:S(2)}) async-start(f32[16,104,128]{2,1,0:T(8,128)} %add.3), calls=%async_computation.1 | async-start | bytes 1703936 | tf_op jit(solution)/shard_map/all_to_all | solution.py:544
  77.7 1.4 %copy-done.8 = f32[8,416,128]{2,1,0:T(8,128)S(1)} copy-done((f32[8,416,128]{2,1,0:T(8,128)S(1)}, f32[8,416,128]{2,1,0:T(8,128)}, u32[]{:S(2)}) %copy-start.8) | copy-done | bytes 1703960
  79.1 3.6 %shard_map.109.order_ref = f32[8,128]{1,0:T(8,128)S(1)} custom-call(s32[1]{0:T(128)} %bitcast.4.me_ref, f32[8,8,128]{2,1,0:T(8,128)S(1)} %copy-done.3, f32[8,416,128]{2,1,0:T(8,128)S(1)} %copy-done.8, f32[8,128]{1,0:T(8,128)S(1)} %slice_bitcast_fusion.order_ref), custom_call_target="tpu_custom_call" | custom-call | flops 3000000000 | bytes 1703936 | tf_op jit(solution)/shard_map/pallas_call | solution.py:41
  83.1 4.3 %collective-permute-start.5 = (f32[3,128]{1,0:T(4,128)S(1)}, f32[3,128]{1,0:T(4,128)S(1)}, u32[]{:S(2)}, u32[]{:S(2)}) collective-permute-start(f32[3,128]{1,0:T(4,128)S(1)} %pad_maximum_fusion), channel_id=1, source_target_pairs={{0,5},{1,6},{2,7},{3,0},{4,1},{5,2},{6,3},{7,4},{8,13},{9,14},{10,... | collective-permute-start | bytes 4616 | tf_op jit(solution)/shard_map/ppermute | solution.py:452
  87.4 1.2 %collective-permute-done.6 = f32[2,128]{1,0:T(2,128)S(1)} collective-permute-done((f32[2,128]{1,0:T(2,128)S(1)}, f32[2,128]{1,0:T(2,128)S(1)}, u32[]{:S(2)}, u32[]{:S(2)}) %collective-permute-start.6) | collective-permute-done | bytes 1056 | tf_op jit(solution)/shard_map/ppermute | solution.py:452
  88.6 3.3 %all-to-all-done.1.in_ref = f32[16,104,128]{2,1,0:T(8,128)S(1)} async-done(((f32[16,104,128]{2,1,0:T(8,128)}), f32[16,104,128]{2,1,0:T(8,128)S(1)}, u32[]{:S(2)}, u32[]{:S(2)}) %all-to-all-start.1) | async-done | bytes 852000 | tf_op jit(solution)/shard_map/all_to_all | solution.py:544
  91.9 1.1 shard_map.110
  93.0 3.8 %all-to-all-start.2 = ((f32[16,104,128]{2,1,0:T(8,128)}), f32[16,104,128]{2,1,0:T(8,128)S(1)}, u32[]{:S(2)}, u32[]{:S(2)}) async-start(f32[16,104,128]{2,1,0:T(8,128)} %shard_map.110), calls=%async_computation.2 | async-start | bytes 1703936 | tf_op jit(solution)/shard_map/all_to_all | solution.py:559
  97.2 2.5 %collective-permute-start.7 = (f32[3,128]{1,0:T(4,128)S(1)}, f32[3,128]{1,0:T(4,128)S(1)}, u32[]{:S(2)}, u32[]{:S(2)}) collective-permute-start(f32[3,128]{1,0:T(4,128)S(1)} %pad_maximum_fusion.1), channel_id=1, source_target_pairs={{0,7},{1,0},{2,1},{3,2},{4,3},{5,4},{6,5},{7,6},{8,15},{9,8},{10,9... | collective-permute-start | bytes 4616 | tf_op jit(solution)/shard_map/ppermute | solution.py:452
  99.7 0.9 collective-permute-done.8
  100.6 0.9 shard_map.111
  101.5 8.6 %all-to-all-done.2.before_ref = f32[16,104,128]{2,1,0:T(8,128)S(1)} async-done(((f32[16,104,128]{2,1,0:T(8,128)}), f32[16,104,128]{2,1,0:T(8,128)S(1)}, u32[]{:S(2)}, u32[]{:S(2)}) %all-to-all-start.2) | async-done | bytes 852000 | tf_op jit(solution)/shard_map/all_to_all | solution.py:559
  110.2 2.8 %collective-permute-start.9 = (f32[16,104,128]{2,1,0:T(8,128)S(1)}, f32[16,104,128]{2,1,0:T(8,128)S(1)}, u32[]{:S(2)}, u32[]{:S(2)}) collective-permute-start(f32[16,104,128]{2,1,0:T(8,128)S(1)} %shard_map.112), channel_id=1, source_target_pairs={{0,8},{8,0},{1,9},{9,1},{2,10},{10,2},{3,11},{11,3},{4,12},{12,4},... | collective-permute-start | bytes 2555912 | tf_op jit(solution)/shard_map/ppermute | solution.py:572
  113.0 2.0 %collective-permute-done.9.other_ref = f32[16,104,128]{2,1,0:T(8,128)S(1)} collective-permute-done((f32[16,104,128]{2,1,0:T(8,128)S(1)}, f32[16,104,128]{2,1,0:T(8,128)S(1)}, u32[]{:S(2)}, u32[]{:S(2)}) %collective-permute-start.9) | collective-permute-done | bytes 852000 | tf_op jit(solution)/shard_map/ppermute | solution.py:572
  115.0 1.4 %shard_map.113 = f32[411,8,128]{2,1,0:T(8,128)} custom-call(s32[1]{0:T(128)} %bitcast.refs_6_.core_ref, f32[8,416,128]{2,1,0:T(8,128)S(1)} %copy-done.1, f32[16,104,128]{2,1,0:T(8,128)S(1)} %all-to-all-done.2.before_ref, f32[16,104,128]{2,1,0:T(8,128)S(1)} %collective-permute-done.4.partner_ref, f32[16,104,128]{2,1,0:T(8,128)S(1)} %collective-permute-done.9.other_ref), custom_call_target="tpu_custom_call" | custom-call | flops 10000000 | bytes 6815744 | tf_op jit(solution)/shard_map/pallas_call | solution.py:41
  (43 shorter events, 2.9 us)
Async XLA Ops:
  0.6 14.7 %copy-start.11 = (f32[1,411,411]{2,0,1:T(1,128)S(1)}, f32[1,411,411]{2,0,1:T(1,128)}, u32[]{:S(2)}) copy-start(f32[1,411,411]{2,0,1:T(1,128)} %param.12) | copy-start | bytes 2027056
  4.1 19.3 %collective-permute-start.2 = (f32[6,216,128]{2,1,0:T(8,128)}, f32[6,216,128]{2,1,0:T(8,128)S(1)}, u32[]{:S(2)}, u32[]{:S(2)}) collective-permute-start(f32[6,216,128]{2,1,0:T(8,128)} %get-tuple-element.24), channel_id=1, source_target_pairs={{0,1},{1,2},{2,3},{3,4},{4,5},{5,6},{6,7},{8,9},{9,10},{10,11},{11... | collective-permute-start | bytes 1990664 | tf_op jit(solution)/shard_map/ppermute | solution.py:478
  8.5 17.9 %collective-permute-start.3 = (f32[6,216,128]{2,1,0:T(8,128)}, f32[6,216,128]{2,1,0:T(8,128)S(1)}, u32[]{:S(2)}, u32[]{:S(2)}) collective-permute-start(f32[6,216,128]{2,1,0:T(8,128)} %get-tuple-element.25), channel_id=1, source_target_pairs={{1,0},{2,1},{3,2},{4,3},{5,4},{6,5},{7,6},{9,8},{10,9},{11,10},{12... | collective-permute-start | bytes 1990664 | tf_op jit(solution)/shard_map/ppermute | solution.py:478
  9.8 35.7 %collective-permute-start = (f32[6,208,128]{2,1,0:T(8,128)}, f32[6,208,128]{2,1,0:T(8,128)S(1)}, u32[]{:S(2)}, u32[]{:S(2)}) collective-permute-start(f32[6,208,128]{2,1,0:T(8,128)} %get-tuple-element.22), channel_id=1, source_target_pairs={{0,1},{1,2},{2,3},{3,4},{4,5},{5,6},{6,7},{8,9},{9,10},{10,11},{11... | collective-permute-start | bytes 1916936 | tf_op jit(solution)/shard_map/ppermute | solution.py:479
  14.0 31.5 %collective-permute-start.1 = (f32[6,208,128]{2,1,0:T(8,128)}, f32[6,208,128]{2,1,0:T(8,128)}, u32[]{:S(2)}, u32[]{:S(2)}) collective-permute-start(f32[6,208,128]{2,1,0:T(8,128)} %get-tuple-element.23), channel_id=1, source_target_pairs={{1,0},{2,1},{3,2},{4,3},{5,4},{6,5},{7,6},{9,8},{10,9},{11,10},{12... | collective-permute-start | bytes 1916936 | tf_op jit(solution)/shard_map/ppermute | solution.py:479
  23.4 3.0 %copy-start.9 = (f32[6,216,128]{2,1,0:T(8,128)}, f32[6,216,128]{2,1,0:T(8,128)S(1)}, u32[]{:S(2)}) copy-start(f32[6,216,128]{2,1,0:T(8,128)S(1)} %collective-permute-done.2.refs_2_.refs_4_) | copy-start | bytes 1990660
  26.4 0.8 copy-start.10
  27.3 7.0 %copy-start.5 = (s32[3,1,512]{2,1,0:T(1,128)S(1)}, s32[3,1,512]{2,1,0:T(1,128)}, u32[]{:S(2)}) copy-start(s32[3,1,512]{2,1,0:T(1,128)} %index_ref.1) | copy-start | bytes 18436
  27.3 7.1 %copy-start.6 = (f32[2,1,512]{2,1,0:T(1,128)S(1)}, f32[2,1,512]{2,1,0:T(1,128)}, u32[]{:S(2)}) copy-start(f32[2,1,512]{2,1,0:T(1,128)} %frac_ref.1) | copy-start | bytes 12292
  34.3 0.7 copy-start.7
  37.5 14.9 %all-to-all-start = ((f32[8,8,128]{2,1,0:T(8,128)}), f32[8,8,128]{2,1,0:T(8,128)S(1)}, u32[]{:S(2)}, u32[]{:S(2)}) async-start(f32[8,8,128]{2,1,0:T(8,128)} %get-tuple-element.31), calls=%async_computation | async-start | bytes 65536 | tf_op jit(solution)/shard_map/all_to_all | solution.py:518
  45.5 6.9 %copy-start.12 = (f32[6,208,128]{2,1,0:T(8,128)}, f32[6,208,128]{2,1,0:T(8,128)S(1)}, u32[]{:S(2)}) copy-start(f32[6,208,128]{2,1,0:T(8,128)S(1)} %collective-permute-done.refs_2_) | copy-start | bytes 1916932
  52.4 0.6 copy-start.2
  61.3 6.7 %collective-permute-start.4 = (f32[16,104,128]{2,1,0:T(8,128)}, f32[16,104,128]{2,1,0:T(8,128)S(1)}, u32[]{:S(2)}, u32[]{:S(2)}) collective-permute-start(f32[16,104,128]{2,1,0:T(8,128)} %get-tuple-element.33), channel_id=1, source_target_pairs={{0,8},{8,0},{1,9},{9,1},{2,10},{10,2},{3,11},{11,3},{4,12},{12,4},... | collective-permute-start | bytes 2555912 | tf_op jit(solution)/shard_map/ppermute | solution.py:541
  68.1 9.6 %copy-start.3 = (f32[8,8,128]{2,1,0:T(8,128)S(1)}, f32[8,8,128]{2,1,0:T(8,128)}, u32[]{:S(2)}) copy-start(f32[8,8,128]{2,1,0:T(8,128)} %copy-done.2) | copy-start | bytes 98308
  70.9 21.0 %all-to-all-start.1 = ((f32[16,104,128]{2,1,0:T(8,128)}), f32[16,104,128]{2,1,0:T(8,128)S(1)}, u32[]{:S(2)}, u32[]{:S(2)}) async-start(f32[16,104,128]{2,1,0:T(8,128)} %add.3), calls=%async_computation.1 | async-start | bytes 1703936 | tf_op jit(solution)/shard_map/all_to_all | solution.py:544
  77.7 1.5 %copy-start.8 = (f32[8,416,128]{2,1,0:T(8,128)S(1)}, f32[8,416,128]{2,1,0:T(8,128)}, u32[]{:S(2)}) copy-start(f32[8,416,128]{2,1,0:T(8,128)} %get-tuple-element.34.end_ref) | copy-start | bytes 5111812
  82.8 5.8 %collective-permute-start.6 = (f32[2,128]{1,0:T(2,128)S(1)}, f32[2,128]{1,0:T(2,128)S(1)}, u32[]{:S(2)}, u32[]{:S(2)}) collective-permute-start(f32[2,128]{1,0:T(2,128)S(1)} %pad_maximum_fusion.2), channel_id=1, source_target_pairs={{0,3},{1,4},{2,5},{3,6},{4,7},{5,0},{6,1},{7,2},{8,11},{9,12},{10,... | collective-permute-start | bytes 3080 | tf_op jit(solution)/shard_map/ppermute | solution.py:452
  83.1 13.6 %collective-permute-start.5 = (f32[3,128]{1,0:T(4,128)S(1)}, f32[3,128]{1,0:T(4,128)S(1)}, u32[]{:S(2)}, u32[]{:S(2)}) collective-permute-start(f32[3,128]{1,0:T(4,128)S(1)} %pad_maximum_fusion), channel_id=1, source_target_pairs={{0,5},{1,6},{2,7},{3,0},{4,1},{5,2},{6,3},{7,4},{8,13},{9,14},{10,... | collective-permute-start | bytes 4616 | tf_op jit(solution)/shard_map/ppermute | solution.py:452
  88.6 12.0 %copy-start.4 = (f32[1,512]{1,0:T(1,128)S(1)}, f32[1,512]{1,0:T(1,128)}, u32[]{:S(2)}) copy-start(f32[1,512]{1,0:T(1,128)} %value_ref.1) | copy-start | bytes 6148
  88.6 21.5 %copy-start = (f32[16,104,128]{2,1,0:T(8,128)S(1)}, f32[16,104,128]{2,1,0:T(8,128)}, u32[]{:S(2)}) copy-start(f32[16,104,128]{2,1,0:T(8,128)} %get-tuple-element.32.keep_ref) | copy-start | bytes 2555908
  93.0 17.1 %all-to-all-start.2 = ((f32[16,104,128]{2,1,0:T(8,128)}), f32[16,104,128]{2,1,0:T(8,128)S(1)}, u32[]{:S(2)}, u32[]{:S(2)}) async-start(f32[16,104,128]{2,1,0:T(8,128)} %shard_map.110), calls=%async_computation.2 | async-start | bytes 1703936 | tf_op jit(solution)/shard_map/all_to_all | solution.py:559
  96.8 3.7 %collective-permute-start.8 = (f32[2,128]{1,0:T(2,128)S(1)}, f32[2,128]{1,0:T(2,128)S(1)}, u32[]{:S(2)}, u32[]{:S(2)}) collective-permute-start(f32[2,128]{1,0:T(2,128)S(1)} %pad_maximum_fusion.3), channel_id=1, source_target_pairs={{0,1},{1,2},{2,3},{3,4},{4,5},{5,6},{6,7},{7,0},{8,9},{9,10},{10,1... | collective-permute-start | bytes 3080 | tf_op jit(solution)/shard_map/ppermute | solution.py:452
  97.2 3.3 %collective-permute-start.7 = (f32[3,128]{1,0:T(4,128)S(1)}, f32[3,128]{1,0:T(4,128)S(1)}, u32[]{:S(2)}, u32[]{:S(2)}) collective-permute-start(f32[3,128]{1,0:T(4,128)S(1)} %pad_maximum_fusion.1), channel_id=1, source_target_pairs={{0,7},{1,0},{2,1},{3,2},{4,3},{5,4},{6,5},{7,6},{8,15},{9,8},{10,9... | collective-permute-start | bytes 4616 | tf_op jit(solution)/shard_map/ppermute | solution.py:452
  110.1 4.9 %copy-start.1 = (f32[8,416,128]{2,1,0:T(8,128)S(1)}, f32[8,416,128]{2,1,0:T(8,128)}, u32[]{:S(2)}) copy-start(f32[8,416,128]{2,1,0:T(8,128)} %get-tuple-element.21.refs_10_.base_ref) | copy-start | bytes 5111812
  110.2 4.8 %collective-permute-start.9 = (f32[16,104,128]{2,1,0:T(8,128)S(1)}, f32[16,104,128]{2,1,0:T(8,128)S(1)}, u32[]{:S(2)}, u32[]{:S(2)}) collective-permute-start(f32[16,104,128]{2,1,0:T(8,128)S(1)} %shard_map.112), channel_id=1, source_target_pairs={{0,8},{8,0},{1,9},{9,1},{2,10},{10,2},{3,11},{11,3},{4,12},{12,4},... | collective-permute-start | bytes 2555912 | tf_op jit(solution)/shard_map/ppermute | solution.py:572

commit v8 on v6

--- a/solution.py
+++ b/solution.py
@@ -173,44 +173,18 @@
 
 def advance_kernel(
     inc_ref, rate_ref, west_ref, east_ref, core_ref, high_ref, low_ref, base_ref, order_ref,
-    end_ref, keep_ref, send_ref,
-    rate, west_rate, east_rate, table, band, own, west, east, odd, even, state, base, high, low, split, sems
+    end_ref, keep_ref, send_ref, table, band, odd, even
 ):
-    at = PAD - 8
-    weights = [
-        pltpu.make_async_copy(rate_ref, rate, sems.at[0]),
-        pltpu.make_async_copy(west_ref.at[:, pl.ds(at, 8)], west_rate, sems.at[1]),
-        pltpu.make_async_copy(east_ref.at[:, pl.ds(at, 8)], east_rate, sems.at[2]),
-    ]
-    fields = []
-    for b in range(2):
-        valid = min(HALF, ROWS - b * HALF)
-        rows = pl.ds(b * HALF, HALF)
-        mine = pl.ds(b * HALF, valid)
-        fields.append(pltpu.make_async_copy(inc_ref.at[mine], own.at[mine], sems.at[3 + 3 * b]))
-        fields.append(pltpu.make_async_copy(west_ref.at[:, rows], west.at[:, rows], sems.at[4 + 3 * b]))
-        fields.append(pltpu.make_async_copy(east_ref.at[:, rows], east.at[:, rows], sems.at[5 + 3 * b]))
-    later = [
-        pltpu.make_async_copy(high_ref, high, sems.at[9]),
-        pltpu.make_async_copy(low_ref, low, sems.at[10]),
-        pltpu.make_async_copy(base_ref, base, sems.at[11]),
-    ]
-    for copy in weights + fields + later:
-        copy.start()
-    own[ROWS:] = jnp.zeros((PAD - ROWS, COLS, LANES), F32)
-    for copy in weights:
-        copy.wait()
     row = lax.broadcasted_iota(jnp.int32, (LANES, LANES), 0)
     lane = lax.broadcasted_iota(jnp.int32, (LANES, LANES), 1)
     wide = COLS + 2 * STEPS
-    first = ROWS - at
     for j in range(1, wide - 1):
         if j < STEPS:
-            rates = [west_rate[j, first + i : first + i + 1, :] for i in range(4)]
+            rates = [west_ref[j, ROWS + i : ROWS + i + 1, :] for i in range(4)]
         elif j < STEPS + COLS:
-            rates = [rate[i, j - STEPS : j - STEPS + 1, :] for i in range(4)]
+            rates = [rate_ref[i, j - STEPS : j - STEPS + 1, :] for i in range(4)]
         else:
-            rates = [east_rate[j - STEPS - COLS, first + i : first + i + 1, :] for i in range(4)]
+            rates = [east_ref[j - STEPS - COLS, ROWS + i : ROWS + i + 1, :] for i in range(4)]
         center = 1.0 - (rates[0] + rates[1] + rates[2] + rates[3])
         table[5 * j] = jnp.broadcast_to(rates[0], (8, LANES))
         table[5 * j + 1] = jnp.broadcast_to(rates[1], (8, LANES))
@@ -227,77 +201,59 @@
         band[j, LANES:, :LANES] = along_high
         band[j, :LANES, LANES:] = along_low
         band[j, LANES:, LANES:] = jnp.zeros((LANES, LANES), BF16)
-    flat = own.reshape(PAD * COLS, LANES)
-
-    for copy in fields[:3]:
-        copy.wait()
-
-    def block(b, carry):
-        rows = pl.ds(pl.multiple_of(b * HALF, 16), HALF)
-
-        @pl.when(b == 1)
-        def _():
-            for copy in fields[3:]:
-                copy.wait()
-
-        def load(step, j):
-            if step > 0:
-                return (odd if step % 2 else even)[j]
-            if j < STEPS:
-                return west[j, rows, :]
-            if j < STEPS + COLS:
-                return flat[pl.ds(b * (HALF * COLS) + j - STEPS, HALF, stride=COLS), :]
-            return east[j - STEPS - COLS, rows, :]
-
-        def tiles(value):
-            return value.reshape(HALF // 8, 8, LANES)
-
-        for step in range(1, STEPS + 1):
-            for j in range(step, wide - step):
-                value = load(step - 1, j)
-                if rotated(j):
-                    value = tiles(value)
+    flat = inc_ref.reshape(ROWS * COLS, LANES)
+    for c in range(COLS):
+        even[STEPS + c, :ROWS, :] = flat[pl.ds(c, ROWS, stride=COLS), :]
+        even[STEPS + c, ROWS:, :] = jnp.zeros((PAD - ROWS, LANES), F32)
+
+    def load(step, j, rows):
+        if step == 0 and j < STEPS:
+            return west_ref[j, rows, :]
+        if step == 0 and j >= STEPS + COLS:
+            return east_ref[j - STEPS - COLS, rows, :]
+        return (odd if step % 2 else even)[j, rows, :]
+
+    def tiles(value):
+        return value.reshape(value.shape[0] // 8, 8, LANES)
+
+    def finish(step, j, rows, total):
+        total = total + table[5 * j] * tiles(load(step - 1, j + 1, rows))
+        total = total + table[5 * j + 1] * tiles(load(step - 1, j - 1, rows))
+        total = total.reshape(total.shape[0] * 8, LANES)
+        if step == STEPS:
+            end_ref[j - STEPS, rows, :] = total
+        else:
+            (odd if step % 2 else even)[j, rows, :] = total
+
+    quarters = [slice(q * PART, (q + 1) * PART) for q in range(4)]
+    for step in range(1, STEPS + 1):
+        for j in range(step, wide - step):
+            if rotated(j):
+                for rows in quarters:
+                    value = tiles(load(step - 1, j, rows))
                     total = table[5 * j + 2] * value
                     total = total + table[5 * j + 3] * pltpu.roll(value, LANES - 1, 2)
                     total = total + table[5 * j + 4] * pltpu.roll(value, 1, 2)
-                else:
-                    parts = jnp.concatenate(two_parts(value), 1)
-                    along = jnp.dot(parts, band[j], preferred_element_type=F32)
-                    total = tiles(along[:, :LANES] + along[:, LANES:])
-                total = total + table[5 * j] * tiles(load(step - 1, j + 1))
-                total = total + table[5 * j + 1] * tiles(load(step - 1, j - 1))
-                total = total.reshape(HALF, LANES)
-                if step == STEPS:
-                    state[j - STEPS, rows, :] = total
-                else:
-                    (odd if step % 2 else even)[j] = total
-        return carry
-
-    lax.fori_loop(0, 2, block, 0)
-
-    for copy in later:
-        copy.wait()
+                    finish(step, j, rows, total)
+            else:
+                parts = jnp.concatenate(two_parts(load(step - 1, j, slice(None))), 1)
+                along = jnp.dot(parts, band[j], preferred_element_type=F32)
+                for rows in quarters:
+                    finish(step, j, rows, tiles(along[rows, :LANES] + along[rows, LANES:]))
+
     core = core_ref[0]
-    outgoing = []
     for kind, out_ref in ((1, send_ref), (0, keep_ref)):
         start = 4 * (core ^ kind)
         for i in (0, 2):
             c = start + i
-            column = jnp.concatenate([state[c], state[c + 1]], 1)
-            end = column + product(high[...], low[...], column)
+            column = jnp.concatenate([end_ref[c], end_ref[c + 1]], 1)
+            end = column + product(high_ref[...], low_ref[...], column)
             for k in range(2):
                 column = end[:, k * LANES : (k + 1) * LANES]
-                state[c + k] = column
-                rest = base[c + k] - column
+                end_ref[c + k] = column
+                rest = base_ref[c + k] - column
                 for q in range(4):
-                    split[kind, 4 * (i + k) + q] = rest[q * PART : (q + 1) * PART]
-            pair, some = pl.ds(c, 2), pl.ds(4 * i, 8)
-            outgoing.append(pltpu.make_async_copy(split.at[kind, some], out_ref.at[some], sems.at[16 + kind * 2 + i // 2]))
-            outgoing[-1].start()
-            outgoing.append(pltpu.make_async_copy(state.at[pair], end_ref.at[pair], sems.at[12 + kind * 2 + i // 2]))
-            outgoing[-1].start()
-    for copy in outgoing:
-        copy.wait()
+                    out_ref[4 * (i + k) + q] = rest[q * PART : (q + 1) * PART]
 
 
 def pair_kernel(keep_ref, partner_ref, pair_ref, ready_ref):
@@ -470,6 +426,7 @@
         moved=10**6,
         far=(0, 1, 2),
         far_out=(0, 1, 2),
+        mib=24,
     )
     queries, places = call(
         sort_kernel,
@@ -487,28 +444,16 @@
         [shape(COLS, PAD, LANES), parts, parts],
         (state, rates, from_west, from_east, core, high, low, base, arrived),
         scratch=[
-            pltpu.VMEM((4, COLS, LANES), F32),
-            pltpu.VMEM((STEPS, 8, LANES), F32),
-            pltpu.VMEM((STEPS, 8, LANES), F32),
             pltpu.VMEM((5 * wide, 8, LANES), F32),
             pltpu.VMEM((wide, 2 * LANES, 2 * LANES), BF16),
-            pltpu.VMEM((PAD, COLS, LANES), F32),
-            pltpu.VMEM((STEPS, PAD, LANES), F32),
-            pltpu.VMEM((STEPS, PAD, LANES), F32),
-            pltpu.VMEM((wide, HALF, LANES), F32),
-            pltpu.VMEM((wide, HALF, LANES), F32),
-            pltpu.VMEM((COLS, PAD, LANES), F32),
-            pltpu.VMEM((COLS, PAD, LANES), F32),
-            pltpu.VMEM((PAD, PAD), BF16),
-            pltpu.VMEM((PAD, PAD), BF16),
-            pltpu.VMEM((2, PARTS, PART, LANES), F32),
-            pltpu.SemaphoreType.DMA((20,)),
+            pltpu.VMEM((wide, PAD, LANES), F32),
+            pltpu.VMEM((wide, PAD, LANES), F32),
         ],
         flops=15 * 10**9,
         moved=6 * field,
         smem=(4,),
-        far=(0, 1, 2, 3, 5, 6, 7, 8),
-        far_out=range(3),
+        far=(8,),
+        mib=36,
     )
     swap = [(0, 1), (1, 0)]
     partner = lax.ppermute(send, "core", swap)

time: 110 us -> 110 us (level)
  local copies, waits for them, and re-layouts: 5.44 us -> 11.3 us
  waiting for transfers between devices: 30 us -> 25.4 us
  Pallas kernels: 33.5 us -> 31.6 us
    unnamed x25 -> x35, local copies, waits for them, and re-layouts: 5.38 us -> 11.2 us
    all_to_all x1, waiting for transfers between devices: 12.8 us -> 8.65 us  [per_device(): arrived = lax.all_to_all(queries, 'tile', 0, 0, tiled=True)]
    pallas_call x10, Pallas kernels: 33.5 us -> 31.6 us  [call(): pl.pallas_call(body, out_shape=outs, in_specs=specs, out_specs=out_specs...]
  transfers between devices with their start and end apart: 11 -> 11, of which waited for: 8 -> 8; matrix products, arithmetic and copies ran while one was open for 1% -> 1% of each run, Pallas kernels for 14% -> 15%
where the time goes in v8:
time: 110 us; the launch traced here: 109 us
  starting transfers between devices  38.6 us (35%)
  Pallas kernels  31.6 us (29%)
  waiting for transfers between devices  25.4 us (23%)
  local copies, waits for them, and re-layouts  11.3 us (10%)
  between operations  1.69 us (2%)
    pallas_call x10, Pallas kernels, call(): pl.pallas_call(body, out_shape=outs, in_specs=specs, out_specs=out_specs...  31.6 us
    unnamed x35, local copies, waits for them, and re-layouts  11.2 us
    all_to_all x1, starting transfers between devices, per_device(): arrived = lax.all_to_all(queries, 'tile', 0, 0, tiled=True)  8.8 us
    all_to_all x1, waiting for transfers between devices, per_device(): arrived = lax.all_to_all(queries, 'tile', 0, 0, tiled=True)  8.65 us
    ppermute x4, starting transfers between devices, ring_step(): lax.ppermute(parcel, 'tile', [(i, (i + by) % TILES) for i in range(TILES)])  8.01 us
    all_to_all x1, starting transfers between devices, per_device(): gathered = lax.all_to_all(pair, ('y', 'x'), 0, 0, tiled=True)  6.76 us
    all_to_all x1, waiting for transfers between devices, per_device(): before = lax.all_to_all(totals, ('y', 'x'), 0, 0, tiled=True)  6.4 us
    ppermute x1, starting transfers between devices, per_device(): from_west = lax.ppermute(east, 'tile', to_east)  5.44 us
  transfers between devices with their start and end apart: 11, of which 8 were waited for; matrix products, arithmetic and copies ran while one was open for 1% of the time, Pallas kernels for 15%

profile of v8, /device:TPU:1, one launch (start us, length us, event | category | flops | bytes accessed | tf_op | source)
XLA Modules:
  0.0 108.6 jit_solution(12967847960391740680)
XLA Ops:
  0.6 3.4 %shard_map.104 = (f32[6,416,128]{2,1,0:T(8,128)}, f32[6,416,128]{2,1,0:T(8,128)}, f32[8,128]{1,0:T(8,128)}) custom-call(f32[411,8,128]{2,1,0:T(8,128)} %bitcast.9, f32[4,8,128]{2,1,0:T(8,128)} %bitcast.14), custom_call_target="tpu_custom_call" | custom-call | bytes 5111808 | tf_op jit(solution)/shard_map/pallas_call | solution.py:41
  4.1 5.4 %collective-permute-start = (f32[6,416,128]{2,1,0:T(8,128)}, f32[6,416,128]{2,1,0:T(8,128)}, u32[]{:S(2)}, u32[]{:S(2)}) collective-permute-start(f32[6,416,128]{2,1,0:T(8,128)} %get-tuple-element.20), channel_id=1, source_target_pairs={{0,1},{1,2},{2,3},{3,4},{4,5},{5,6},{6,7},{8,9},{9,10},{10,11},{11... | collective-permute-start | bytes 3833864 | tf_op jit(solution)/shard_map/ppermute | solution.py:408
  9.5 1.3 %collective-permute-start.1 = (f32[6,416,128]{2,1,0:T(8,128)}, f32[6,416,128]{2,1,0:T(8,128)}, u32[]{:S(2)}, u32[]{:S(2)}) collective-permute-start(f32[6,416,128]{2,1,0:T(8,128)} %get-tuple-element.21), channel_id=1, source_target_pairs={{1,0},{2,1},{3,2},{4,3},{5,4},{6,5},{7,6},{9,8},{10,9},{11,10},{12... | collective-permute-start | bytes 3833864 | tf_op jit(solution)/shard_map/ppermute | solution.py:409
  10.8 1.2 %copy.13 = f32[1,411,411]{2,1,0:T(8,128)S(1)} copy(f32[1,411,411]{2,0,1:T(1,128)} %param.12) | data formatting | bytes 1351368
  12.1 1.1 %copy-done.5 = f32[411,411]{1,0:T(8,128)S(1)} copy-done((f32[411,411]{1,0:T(8,128)S(1)}, f32[411,411]{1,0:T(8,128)}, u32[]{:S(2)}) %copy-start.5) | copy-done | bytes 675708
  13.2 7.9 %shard_map.105 = (f32[8,416,128]{2,1,0:T(8,128)S(1)}, bf16[416,416]{1,0:T(8,128)(2,1)S(1)}, bf16[416,416]{1,0:T(8,128)(2,1)S(1)}, f32[8,128]{1,0:T(8,128)S(1)}) custom-call(f32[411,8,128]{2,1,0:T(8,128)S(1)} %bitcast.10, f32[411,8,128]{2,1,0:T(8,128)S(1)} %bitcast.13, f32[411,411]{1,0:T(8,128)S(1)} %copy-done.5, f32[411,411]{1,0:T(8,128)S(1)} %bitcast.12, ...), custom_call_target="tpu_custom_call" | custom-call | flops 100000000 | bytes 1000000 | tf_op jit(solution)/shard_map/pallas_call | solution.py:41
  21.1 1.2 %copy-done.1 = f32[8,416,128]{2,1,0:T(8,128)} copy-done((f32[8,416,128]{2,1,0:T(8,128)}, f32[8,416,128]{2,1,0:T(8,128)S(1)}, u32[]{:S(2)}) %copy-start.1) | copy-done | bytes 1703960
  23.9 2.5 %shard_map.106 = (f32[8,8,128]{2,1,0:T(8,128)}, f32[16,512]{1,0:T(8,128)S(1)}) custom-call(s32[3,1,512]{2,1,0:T(1,128)S(1)} %copy-done.13, f32[2,1,512]{2,1,0:T(1,128)S(1)} %copy-done.14, f32[8,128]{1,0:T(8,128)S(1)} %get-tuple-element.24.order_ref), custom_call_target="tpu_custom_call" | custom-call | flops 10000000 | bytes 100000 | tf_op jit(solution)/shard_map/pallas_call | solution.py:41
  26.4 8.8 %all-to-all-start = ((f32[8,8,128]{2,1,0:T(8,128)}), f32[8,8,128]{2,1,0:T(8,128)S(1)}, u32[]{:S(2)}, u32[]{:S(2)}) async-start(f32[8,8,128]{2,1,0:T(8,128)} %get-tuple-element.25), calls=%async_computation | async-start | bytes 65536 | tf_op jit(solution)/shard_map/all_to_all | solution.py:439
  35.2 8.6 %all-to-all-done.order_ref.obs_ref = f32[8,8,128]{2,1,0:T(8,128)S(1)} async-done(((f32[8,8,128]{2,1,0:T(8,128)}), f32[8,8,128]{2,1,0:T(8,128)S(1)}, u32[]{:S(2)}, u32[]{:S(2)}) %all-to-all-start) | async-done | bytes 32800 | tf_op jit(solution)/shard_map/all_to_all | solution.py:439
  43.9 1.4 %copy-done.2 = f32[8,416,128]{2,1,0:T(8,128)S(1)} copy-done((f32[8,416,128]{2,1,0:T(8,128)S(1)}, f32[8,416,128]{2,1,0:T(8,128)}, u32[]{:S(2)}) %copy-start.2) | copy-done | bytes 1703960
  45.3 1.0 copy-done.10
  46.3 1.0 copy-done.12
  47.4 9.7 %shard_map.107 = (f32[8,416,128]{2,1,0:T(8,128)S(1)}, f32[16,104,128]{2,1,0:T(8,128)S(1)}, f32[16,104,128]{2,1,0:T(8,128)S(1)}) custom-call(f32[411,8,128]{2,1,0:T(8,128)S(1)} %bitcast.11, f32[4,8,128]{2,1,0:T(8,128)S(1)} %bitcast.15, f32[6,416,128]{2,1,0:T(8,128)} %collective-permute-done.west_ref, f32[6,416,128]{2,1,0:T(8,128)} %collective-permute-done.1.east_ref, ...), custom_call_target="tpu_custom_call" | custom-call | flops 15000000512 | bytes 10223616 | tf_op jit(solution)/shard_map/pallas_call | solution.py:41
  57.1 1.2 %copy-done.15 = f32[8,416,128]{2,1,0:T(8,128)} copy-done((f32[8,416,128]{2,1,0:T(8,128)}, f32[8,416,128]{2,1,0:T(8,128)S(1)}, u32[]{:S(2)}) %copy-start.15) | copy-done | bytes 1703960
  58.3 1.6 %collective-permute-start.2 = (f32[16,104,128]{2,1,0:T(8,128)S(1)}, f32[16,104,128]{2,1,0:T(8,128)S(1)}, u32[]{:S(2)}, u32[]{:S(2)}) collective-permute-start(f32[16,104,128]{2,1,0:T(8,128)S(1)} %get-tuple-element.27), channel_id=1, source_target_pairs={{0,8},{8,0},{1,9},{9,1},{2,10},{10,2},{3,11},{11,3},{4,12},{12,4},... | collective-permute-start | bytes 2555912 | tf_op jit(solution)/shard_map/ppermute | solution.py:459
  60.5 1.4 %collective-permute-done.2.partner_ref = f32[16,104,128]{2,1,0:T(8,128)S(1)} collective-permute-done((f32[16,104,128]{2,1,0:T(8,128)S(1)}, f32[16,104,128]{2,1,0:T(8,128)S(1)}, u32[]{:S(2)}, u32[]{:S(2)}) %collective-permute-start.2) | collective-permute-done | bytes 852000 | tf_op jit(solution)/shard_map/ppermute | solution.py:459
  62.9 6.8 %all-to-all-start.1 = ((f32[16,104,128]{2,1,0:T(8,128)}), f32[16,104,128]{2,1,0:T(8,128)S(1)}, u32[]{:S(2)}, u32[]{:S(2)}) async-start(f32[16,104,128]{2,1,0:T(8,128)} %get-tuple-element.28), calls=%async_computation.1 | async-start | bytes 1703936 | tf_op jit(solution)/shard_map/all_to_all | solution.py:461
  69.6 1.4 %copy-done.16 = f32[8,416,128]{2,1,0:T(8,128)S(1)} copy-done((f32[8,416,128]{2,1,0:T(8,128)S(1)}, f32[8,416,128]{2,1,0:T(8,128)}, u32[]{:S(2)}) %copy-start.16) | copy-done | bytes 1703960
  71.1 3.6 %shard_map.109.order_ref = f32[8,128]{1,0:T(8,128)S(1)} custom-call(s32[1]{0:T(128)} %bitcast.4.me_ref, f32[8,8,128]{2,1,0:T(8,128)S(1)} %all-to-all-done.order_ref.obs_ref, f32[8,416,128]{2,1,0:T(8,128)S(1)} %copy-done.16, f32[8,128]{1,0:T(8,128)S(1)} %get-tuple-element.30.order_ref), custom_call_target="tpu_custom_call" | custom-call | flops 3000000000 | bytes 1703936 | tf_op jit(solution)/shard_map/pallas_call | solution.py:41
  74.7 3.5 %collective-permute-start.4 = (f32[2,128]{1,0:T(2,128)S(1)}, f32[2,128]{1,0:T(2,128)S(1)}, u32[]{:S(2)}, u32[]{:S(2)}) collective-permute-start(f32[2,128]{1,0:T(2,128)S(1)} %pad_maximum_fusion.2), channel_id=1, source_target_pairs={{0,3},{1,4},{2,5},{3,6},{4,7},{5,0},{6,1},{7,2},{8,11},{9,12},{10,... | collective-permute-start | bytes 3080 | tf_op jit(solution)/shard_map/ppermute | solution.py:382
  78.3 1.3 %collective-permute-start.3 = (f32[3,128]{1,0:T(4,128)S(1)}, f32[3,128]{1,0:T(4,128)S(1)}, u32[]{:S(2)}, u32[]{:S(2)}) collective-permute-start(f32[3,128]{1,0:T(4,128)S(1)} %pad_maximum_fusion), channel_id=1, source_target_pairs={{0,5},{1,6},{2,7},{3,0},{4,1},{5,2},{6,3},{7,4},{8,13},{9,14},{10,... | collective-permute-start | bytes 4616 | tf_op jit(solution)/shard_map/ppermute | solution.py:382
  79.6 1.2 %collective-permute-done.4 = f32[2,128]{1,0:T(2,128)S(1)} collective-permute-done((f32[2,128]{1,0:T(2,128)S(1)}, f32[2,128]{1,0:T(2,128)S(1)}, u32[]{:S(2)}, u32[]{:S(2)}) %collective-permute-start.4) | collective-permute-done | bytes 1056 | tf_op jit(solution)/shard_map/ppermute | solution.py:382
  80.8 3.1 %all-to-all-done.1.in_ref = f32[16,104,128]{2,1,0:T(8,128)S(1)} async-done(((f32[16,104,128]{2,1,0:T(8,128)}), f32[16,104,128]{2,1,0:T(8,128)S(1)}, u32[]{:S(2)}, u32[]{:S(2)}) %all-to-all-start.1) | async-done | bytes 852000 | tf_op jit(solution)/shard_map/all_to_all | solution.py:461
  83.8 1.1 %shard_map.110 = f32[16,104,128]{2,1,0:T(8,128)} custom-call(f32[16,104,128]{2,1,0:T(8,128)S(1)} %all-to-all-done.1.in_ref, f32[8,128]{1,0:T(8,128)S(1)} %shard_map.109.order_ref), custom_call_target="tpu_custom_call" | custom-call | flops 10000000 | bytes 1703936 | tf_op jit(solution)/shard_map/pallas_call | solution.py:41
  85.0 3.8 %all-to-all-start.2 = ((f32[16,104,128]{2,1,0:T(8,128)}), f32[16,104,128]{2,1,0:T(8,128)S(1)}, u32[]{:S(2)}, u32[]{:S(2)}) async-start(f32[16,104,128]{2,1,0:T(8,128)} %shard_map.110), calls=%async_computation.2 | async-start | bytes 1703936 | tf_op jit(solution)/shard_map/all_to_all | solution.py:476
  88.8 3.1 %collective-permute-start.6 = (f32[2,128]{1,0:T(2,128)S(1)}, f32[2,128]{1,0:T(2,128)S(1)}, u32[]{:S(2)}, u32[]{:S(2)}) collective-permute-start(f32[2,128]{1,0:T(2,128)S(1)} %pad_maximum_fusion.3), channel_id=1, source_target_pairs={{0,1},{1,2},{2,3},{3,4},{4,5},{5,6},{6,7},{7,0},{8,9},{9,10},{10,1... | collective-permute-start | bytes 3080 | tf_op jit(solution)/shard_map/ppermute | solution.py:382
  92.6 2.1 %collective-permute-done.5 = f32[3,128]{1,0:T(4,128)S(1)} collective-permute-done((f32[3,128]{1,0:T(4,128)S(1)}, f32[3,128]{1,0:T(4,128)S(1)}, u32[]{:S(2)}, u32[]{:S(2)}) %collective-permute-start.5) | collective-permute-done | bytes 1568 | tf_op jit(solution)/shard_map/ppermute | solution.py:382
  95.6 6.4 %all-to-all-done.2.before_ref = f32[16,104,128]{2,1,0:T(8,128)S(1)} async-done(((f32[16,104,128]{2,1,0:T(8,128)}), f32[16,104,128]{2,1,0:T(8,128)S(1)}, u32[]{:S(2)}, u32[]{:S(2)}) %all-to-all-start.2) | async-done | bytes 852000 | tf_op jit(solution)/shard_map/all_to_all | solution.py:476
  102.1 3.0 %collective-permute-start.7 = (f32[16,104,128]{2,1,0:T(8,128)S(1)}, f32[16,104,128]{2,1,0:T(8,128)S(1)}, u32[]{:S(2)}, u32[]{:S(2)}) collective-permute-start(f32[16,104,128]{2,1,0:T(8,128)S(1)} %shard_map.112), channel_id=1, source_target_pairs={{0,8},{8,0},{1,9},{9,1},{2,10},{10,2},{3,11},{11,3},{4,12},{12,4},... | collective-permute-start | bytes 2555912 | tf_op jit(solution)/shard_map/ppermute | solution.py:489
  105.1 2.0 %collective-permute-done.7.other_ref = f32[16,104,128]{2,1,0:T(8,128)S(1)} collective-permute-done((f32[16,104,128]{2,1,0:T(8,128)S(1)}, f32[16,104,128]{2,1,0:T(8,128)S(1)}, u32[]{:S(2)}, u32[]{:S(2)}) %collective-permute-start.7) | collective-permute-done | bytes 852000 | tf_op jit(solution)/shard_map/ppermute | solution.py:489
  107.1 1.4 %shard_map.113 = f32[411,8,128]{2,1,0:T(8,128)} custom-call(s32[1]{0:T(128)} %bitcast.core_ref, f32[8,416,128]{2,1,0:T(8,128)S(1)} %copy-done.3, f32[16,104,128]{2,1,0:T(8,128)S(1)} %all-to-all-done.2.before_ref, f32[16,104,128]{2,1,0:T(8,128)S(1)} %collective-permute-done.2.partner_ref, f32[16,104,128]{2,1,0:T(8,128)S(1)} %collective-permute-done.7.other_ref), custom_call_target="tpu_custom_call" | custom-call | flops 10000000 | bytes 6815744 | tf_op jit(solution)/shard_map/pallas_call | solution.py:41
  (45 shorter events, 4.3 us)
Async XLA Ops:
  0.6 11.4 %copy-start = (f32[1,3,137,8,128]{4,3,2,1,0:T(8,128)S(1)}, f32[1,3,137,8,128]{4,3,2,1,0:T(8,128)}, u32[]{:S(2)}) copy-start(f32[1,3,137,8,128]{4,3,2,1,0:T(8,128)} %param.9) | copy-start | bytes 5050372
  0.6 11.4 %copy-start.4 = (f32[1,3,137,8,128]{4,3,2,1,0:T(8,128)S(1)}, f32[1,3,137,8,128]{4,3,2,1,0:T(8,128)}, u32[]{:S(2)}) copy-start(f32[1,3,137,8,128]{4,3,2,1,0:T(8,128)} %param.10) | copy-start | bytes 5050372
  4.1 8.0 %copy-start.7 = (f32[8,128]{1,0:T(8,128)S(1)}, f32[8,128]{1,0:T(8,128)}, u32[]{:S(2)}) copy-start(f32[8,128]{1,0:T(8,128)} %get-tuple-element.18.order_ref) | copy-start | bytes 12292
  4.1 39.8 %collective-permute-start = (f32[6,416,128]{2,1,0:T(8,128)}, f32[6,416,128]{2,1,0:T(8,128)}, u32[]{:S(2)}, u32[]{:S(2)}) collective-permute-start(f32[6,416,128]{2,1,0:T(8,128)} %get-tuple-element.20), channel_id=1, source_target_pairs={{0,1},{1,2},{2,3},{3,4},{4,5},{5,6},{6,7},{8,9},{9,10},{10,11},{11... | collective-permute-start | bytes 3833864 | tf_op jit(solution)/shard_map/ppermute | solution.py:408
  9.5 34.4 %collective-permute-start.1 = (f32[6,416,128]{2,1,0:T(8,128)}, f32[6,416,128]{2,1,0:T(8,128)}, u32[]{:S(2)}, u32[]{:S(2)}) collective-permute-start(f32[6,416,128]{2,1,0:T(8,128)} %get-tuple-element.21), channel_id=1, source_target_pairs={{1,0},{2,1},{3,2},{4,3},{5,4},{6,5},{7,6},{9,8},{10,9},{11,10},{12... | collective-permute-start | bytes 3833864 | tf_op jit(solution)/shard_map/ppermute | solution.py:409
  12.0 1.2 %copy-start.5 = (f32[411,411]{1,0:T(8,128)S(1)}, f32[411,411]{1,0:T(8,128)}, u32[]{:S(2)}) copy-start(f32[411,411]{1,0:T(8,128)} %root_ref.1) | copy-start | bytes 2027056
  13.2 10.7 %copy-start.13 = (s32[3,1,512]{2,1,0:T(1,128)S(1)}, s32[3,1,512]{2,1,0:T(1,128)}, u32[]{:S(2)}) copy-start(s32[3,1,512]{2,1,0:T(1,128)} %index_ref.1) | copy-start | bytes 18436
  13.2 10.7 %copy-start.14 = (f32[2,1,512]{2,1,0:T(1,128)S(1)}, f32[2,1,512]{2,1,0:T(1,128)}, u32[]{:S(2)}) copy-start(f32[2,1,512]{2,1,0:T(1,128)} %frac_ref.1) | copy-start | bytes 12292
  13.2 30.7 %copy-start.6 = (f32[1,4,8,128]{3,2,1,0:T(8,128)S(1)}, f32[1,4,8,128]{3,2,1,0:T(8,128)}, u32[]{:S(2)}) copy-start(f32[1,4,8,128]{3,2,1,0:T(8,128)} %param.13) | copy-start | bytes 49156
  21.1 1.2 %copy-start.1 = (f32[8,416,128]{2,1,0:T(8,128)}, f32[8,416,128]{2,1,0:T(8,128)S(1)}, u32[]{:S(2)}) copy-start(f32[8,416,128]{2,1,0:T(8,128)S(1)} %get-tuple-element.19.base_ref) | copy-start | bytes 5111812
  22.4 0.8 copy-start.9
  23.1 0.8 copy-start.11
  26.4 17.4 %all-to-all-start = ((f32[8,8,128]{2,1,0:T(8,128)}), f32[8,8,128]{2,1,0:T(8,128)S(1)}, u32[]{:S(2)}, u32[]{:S(2)}) async-start(f32[8,8,128]{2,1,0:T(8,128)} %get-tuple-element.25), calls=%async_computation | async-start | bytes 65536 | tf_op jit(solution)/shard_map/all_to_all | solution.py:439
  43.9 1.5 %copy-start.2 = (f32[8,416,128]{2,1,0:T(8,128)S(1)}, f32[8,416,128]{2,1,0:T(8,128)}, u32[]{:S(2)}) copy-start(f32[8,416,128]{2,1,0:T(8,128)} %copy-done.1) | copy-start | bytes 5111812
  45.3 1.0 copy-start.10
  46.3 1.0 copy-start.12
  57.1 1.2 %copy-start.15 = (f32[8,416,128]{2,1,0:T(8,128)}, f32[8,416,128]{2,1,0:T(8,128)S(1)}, u32[]{:S(2)}) copy-start(f32[8,416,128]{2,1,0:T(8,128)S(1)} %get-tuple-element.29.end_ref) | copy-start | bytes 5111812
  58.3 3.6 %collective-permute-start.2 = (f32[16,104,128]{2,1,0:T(8,128)S(1)}, f32[16,104,128]{2,1,0:T(8,128)S(1)}, u32[]{:S(2)}, u32[]{:S(2)}) collective-permute-start(f32[16,104,128]{2,1,0:T(8,128)S(1)} %get-tuple-element.27), channel_id=1, source_target_pairs={{0,8},{8,0},{1,9},{9,1},{2,10},{10,2},{3,11},{11,3},{4,12},{12,4},... | collective-permute-start | bytes 2555912 | tf_op jit(solution)/shard_map/ppermute | solution.py:459
  62.9 21.0 %all-to-all-start.1 = ((f32[16,104,128]{2,1,0:T(8,128)}), f32[16,104,128]{2,1,0:T(8,128)S(1)}, u32[]{:S(2)}, u32[]{:S(2)}) async-start(f32[16,104,128]{2,1,0:T(8,128)} %get-tuple-element.28), calls=%async_computation.1 | async-start | bytes 1703936 | tf_op jit(solution)/shard_map/all_to_all | solution.py:461
  69.6 1.5 %copy-start.16 = (f32[8,416,128]{2,1,0:T(8,128)S(1)}, f32[8,416,128]{2,1,0:T(8,128)}, u32[]{:S(2)}) copy-start(f32[8,416,128]{2,1,0:T(8,128)} %copy-done.15) | copy-start | bytes 5111812
  74.7 6.0 %collective-permute-start.4 = (f32[2,128]{1,0:T(2,128)S(1)}, f32[2,128]{1,0:T(2,128)S(1)}, u32[]{:S(2)}, u32[]{:S(2)}) collective-permute-start(f32[2,128]{1,0:T(2,128)S(1)} %pad_maximum_fusion.2), channel_id=1, source_target_pairs={{0,3},{1,4},{2,5},{3,6},{4,7},{5,0},{6,1},{7,2},{8,11},{9,12},{10,... | collective-permute-start | bytes 3080 | tf_op jit(solution)/shard_map/ppermute | solution.py:382
  78.3 10.5 %collective-permute-start.3 = (f32[3,128]{1,0:T(4,128)S(1)}, f32[3,128]{1,0:T(4,128)S(1)}, u32[]{:S(2)}, u32[]{:S(2)}) collective-permute-start(f32[3,128]{1,0:T(4,128)S(1)} %pad_maximum_fusion), channel_id=1, source_target_pairs={{0,5},{1,6},{2,7},{3,0},{4,1},{5,2},{6,3},{7,4},{8,13},{9,14},{10,... | collective-permute-start | bytes 4616 | tf_op jit(solution)/shard_map/ppermute | solution.py:382
  80.8 14.0 %copy-start.8 = (f32[1,512]{1,0:T(1,128)S(1)}, f32[1,512]{1,0:T(1,128)}, u32[]{:S(2)}) copy-start(f32[1,512]{1,0:T(1,128)} %value_ref.1) | copy-start | bytes 6148
  85.0 17.0 %all-to-all-start.2 = ((f32[16,104,128]{2,1,0:T(8,128)}), f32[16,104,128]{2,1,0:T(8,128)S(1)}, u32[]{:S(2)}, u32[]{:S(2)}) async-start(f32[16,104,128]{2,1,0:T(8,128)} %shard_map.110), calls=%async_computation.2 | async-start | bytes 1703936 | tf_op jit(solution)/shard_map/all_to_all | solution.py:476
  88.8 3.8 %collective-permute-start.6 = (f32[2,128]{1,0:T(2,128)S(1)}, f32[2,128]{1,0:T(2,128)S(1)}, u32[]{:S(2)}, u32[]{:S(2)}) collective-permute-start(f32[2,128]{1,0:T(2,128)S(1)} %pad_maximum_fusion.3), channel_id=1, source_target_pairs={{0,1},{1,2},{2,3},{3,4},{4,5},{5,6},{6,7},{7,0},{8,9},{9,10},{10,1... | collective-permute-start | bytes 3080 | tf_op jit(solution)/shard_map/ppermute | solution.py:382
  91.9 2.8 %collective-permute-start.5 = (f32[3,128]{1,0:T(4,128)S(1)}, f32[3,128]{1,0:T(4,128)S(1)}, u32[]{:S(2)}, u32[]{:S(2)}) collective-permute-start(f32[3,128]{1,0:T(4,128)S(1)} %pad_maximum_fusion.1), channel_id=1, source_target_pairs={{0,7},{1,0},{2,1},{3,2},{4,3},{5,4},{6,5},{7,6},{8,15},{9,8},{10,9... | collective-permute-start | bytes 4616 | tf_op jit(solution)/shard_map/ppermute | solution.py:382
  102.0 5.1 %copy-start.3 = (f32[8,416,128]{2,1,0:T(8,128)S(1)}, f32[8,416,128]{2,1,0:T(8,128)}, u32[]{:S(2)}) copy-start(f32[8,416,128]{2,1,0:T(8,128)} %copy-done.1) | copy-start | bytes 5111812
  102.1 5.0 %collective-permute-start.7 = (f32[16,104,128]{2,1,0:T(8,128)S(1)}, f32[16,104,128]{2,1,0:T(8,128)S(1)}, u32[]{:S(2)}, u32[]{:S(2)}) collective-permute-start(f32[16,104,128]{2,1,0:T(8,128)S(1)} %shard_map.112), channel_id=1, source_target_pairs={{0,8},{8,0},{1,9},{9,1},{2,10},{10,2},{3,11},{11,3},{4,12},{12,4},... | collective-permute-start | bytes 2555912 | tf_op jit(solution)/shard_map/ppermute | solution.py:489

commit v9 on v8

--- a/solution.py
+++ b/solution.py
@@ -17,6 +17,7 @@
 PART = 104
 TILES = 8
 HALF = 208
+STORE = 160
 SLOTS = 512
 CAP = 128
 FIELDS = 8
@@ -120,8 +121,8 @@
 
 
 def prepare_kernel(
-    inc_ref, forcing_ref, root_ref, physics_ref, order_ref, base_ref, high_ref, low_ref, ready_ref,
-    start, force, root, square, drive, base, high, low, sems
+    inc_ref, forcing_ref, root_ref, physics_ref, order_ref, base_ref, store_ref, ready_ref,
+    start, force, root, square, drive, base, columns, powers, sems
 ):
     incoming = [
         pltpu.make_async_copy(root_ref, root, sems.at[0]),
@@ -138,13 +139,12 @@
     twice_parts = two_parts(twice)
     four = 2.0 * twice + product(*twice_parts, twice)
     six = twice + four + product(*twice_parts, four)
-    high[...], low[...] = two_parts(six)
-    outgoing = [
-        pltpu.make_async_copy(high, high_ref, sems.at[3]),
-        pltpu.make_async_copy(low, low_ref, sems.at[4]),
-    ]
-    for copy in outgoing:
-        copy.start()
+    powers[3] = jnp.zeros((PAD, LANES), F32)
+    for p in range(4):
+        width = min(LANES, PAD - p * LANES)
+        powers[p, :, :width] = six[:, p * LANES : p * LANES + width]
+    outgoing = [pltpu.make_async_copy(powers, store_ref.at[pl.ds(2 * COLS, 4)], sems.at[3])]
+    outgoing[0].start()
     for copy in incoming:
         copy.wait()
     square[:ROWS, :ROWS] = root[...]
@@ -157,12 +157,18 @@
         drive[:ROWS, LANES:] = force_flat[pl.ds(c + 1, ROWS, stride=COLS), :]
         forced = product(root_high, root_low, drive[...])
         for k in range(2):
-            column = forced[:, k * LANES : (k + 1) * LANES]
-            base[c + k, :ROWS, :] = start_flat[pl.ds(c + k, ROWS, stride=COLS), :] - column[:ROWS]
-            base[c + k, ROWS:, :] = column[ROWS:]
-        pair = pl.ds(c, 2)
-        outgoing.append(pltpu.make_async_copy(base.at[pair], base_ref.at[pair], sems.at[5 + c // 2]))
-        outgoing[-1].start()
+            column = start_flat[pl.ds(c + k, ROWS, stride=COLS), :]
+            taken = forced[:, k * LANES : (k + 1) * LANES]
+            columns[c + k, :ROWS, :] = column
+            columns[c + k, ROWS:, :] = jnp.zeros((PAD - ROWS, LANES), F32)
+            base[c + k, :ROWS, :] = column - taken[:ROWS]
+            base[c + k, ROWS:, :] = taken[ROWS:]
+        pair, beyond = pl.ds(c, 2), pl.ds(COLS + c, 2)
+        outgoing.append(pltpu.make_async_copy(base.at[pair], base_ref.at[pair], sems.at[4 + c // 2]))
+        outgoing.append(pltpu.make_async_copy(base.at[pair], store_ref.at[pair], sems.at[8 + c // 2]))
+        outgoing.append(pltpu.make_async_copy(columns.at[pair], store_ref.at[beyond], sems.at[12 + c // 2]))
+        for copy in outgoing[-3:]:
+            copy.start()
     for copy in outgoing:
         copy.wait()
 
@@ -172,9 +178,17 @@
 
 
 def advance_kernel(
-    inc_ref, rate_ref, west_ref, east_ref, core_ref, high_ref, low_ref, base_ref, order_ref,
-    end_ref, keep_ref, send_ref, table, band, odd, even
+    rate_ref, west_ref, east_ref, core_ref, store_ref, order_ref,
+    end_ref, keep_ref, send_ref, table, band, odd, even, end_held, base, powers, sems
 ):
+    own = pltpu.make_async_copy(store_ref.at[pl.ds(COLS, COLS)], even.at[pl.ds(STEPS, COLS)], sems.at[0])
+    own.start()
+    later = [
+        pltpu.make_async_copy(store_ref.at[pl.ds(2 * COLS, 4)], powers, sems.at[1]),
+        pltpu.make_async_copy(store_ref.at[pl.ds(0, COLS)], base, sems.at[2]),
+    ]
+    for copy in later:
+        copy.start()
     row = lax.broadcasted_iota(jnp.int32, (LANES, LANES), 0)
     lane = lax.broadcasted_iota(jnp.int32, (LANES, LANES), 1)
     wide = COLS + 2 * STEPS
@@ -201,10 +215,7 @@
         band[j, LANES:, :LANES] = along_high
         band[j, :LANES, LANES:] = along_low
         band[j, LANES:, LANES:] = jnp.zeros((LANES, LANES), BF16)
-    flat = inc_ref.reshape(ROWS * COLS, LANES)
-    for c in range(COLS):
-        even[STEPS + c, :ROWS, :] = flat[pl.ds(c, ROWS, stride=COLS), :]
-        even[STEPS + c, ROWS:, :] = jnp.zeros((PAD - ROWS, LANES), F32)
+    own.wait()
 
     def load(step, j, rows):
         if step == 0 and j < STEPS:
@@ -221,7 +232,7 @@
         total = total + table[5 * j + 1] * tiles(load(step - 1, j - 1, rows))
         total = total.reshape(total.shape[0] * 8, LANES)
         if step == STEPS:
-            end_ref[j - STEPS, rows, :] = total
+            end_held[j - STEPS, rows, :] = total
         else:
             (odd if step % 2 else even)[j, rows, :] = total
 
@@ -241,19 +252,28 @@
                 for rows in quarters:
                     finish(step, j, rows, tiles(along[rows, :LANES] + along[rows, LANES:]))
 
+    for copy in later:
+        copy.wait()
+    high, low = two_parts(jnp.concatenate([powers[p] for p in range(4)], 1)[:, :PAD])
     core = core_ref[0]
+    outgoing = []
     for kind, out_ref in ((1, send_ref), (0, keep_ref)):
         start = 4 * (core ^ kind)
         for i in (0, 2):
             c = start + i
-            column = jnp.concatenate([end_ref[c], end_ref[c + 1]], 1)
-            end = column + product(high_ref[...], low_ref[...], column)
+            column = jnp.concatenate([end_held[c], end_held[c + 1]], 1)
+            end = column + product(high, low, column)
             for k in range(2):
                 column = end[:, k * LANES : (k + 1) * LANES]
-                end_ref[c + k] = column
-                rest = base_ref[c + k] - column
+                end_held[c + k] = column
+                rest = base[c + k] - column
                 for q in range(4):
                     out_ref[4 * (i + k) + q] = rest[q * PART : (q + 1) * PART]
+            pair = pl.ds(c, 2)
+            outgoing.append(pltpu.make_async_copy(end_held.at[pair], end_ref.at[pair], sems.at[3 + 2 * kind + i // 2]))
+            outgoing[-1].start()
+    for copy in outgoing:
+        copy.wait()
 
 
 def pair_kernel(keep_ref, partner_ref, pair_ref, ready_ref):
@@ -330,9 +350,13 @@
         )
 
 
-def observe_kernel(me_ref, obs_ref, end_ref, order_ref, out_ref, end_high, end_low):
+def observe_kernel(me_ref, obs_ref, end_ref, order_ref, out_ref, end_high, end_low, end, sems):
+    copies = [pltpu.make_async_copy(end_ref.at[c], end.at[c], sems.at[c]) for c in range(COLS)]
+    for copy in copies:
+        copy.start()
     for c in range(COLS):
-        high, low = two_parts(end_ref[c])
+        copies[c].wait()
+        high, low = two_parts(end[c])
         end_high[:, c * LANES : (c + 1) * LANES] = high
         end_low[:, c * LANES : (c + 1) * LANES] = low
     lanes = 2 * CAP
@@ -407,9 +431,10 @@
     west, east, sent = pack(state, rates)
     from_west = lax.ppermute(east, "tile", to_east)
     from_east = lax.ppermute(west, "tile", to_west)
-    base, high, low, ready = call(
+    store = shape(STORE, PAD, LANES)
+    base, planes, ready = call(
         prepare_kernel,
-        [shape(COLS, PAD, LANES), shape(PAD, PAD, dtype=BF16), shape(PAD, PAD, dtype=BF16), shape(8, LANES)],
+        [shape(COLS, PAD, LANES), store, shape(8, LANES)],
         (state, drive, error_root, physics.reshape(ROWS, ROWS), sent),
         scratch=[
             pltpu.VMEM((ROWS, COLS, LANES), F32),
@@ -418,14 +443,14 @@
             pltpu.VMEM((PAD, PAD), F32),
             pltpu.VMEM((PAD, 2 * LANES), F32),
             pltpu.VMEM((COLS, PAD, LANES), F32),
-            pltpu.VMEM((PAD, PAD), BF16),
-            pltpu.VMEM((PAD, PAD), BF16),
-            pltpu.SemaphoreType.DMA((9,)),
+            pltpu.VMEM((COLS, PAD, LANES), F32),
+            pltpu.VMEM((4, PAD, LANES), F32),
+            pltpu.SemaphoreType.DMA((16,)),
         ],
         flops=10**8,
         moved=10**6,
         far=(0, 1, 2),
-        far_out=(0, 1, 2),
+        far_out=(0, 1),
         mib=24,
     )
     queries, places = call(
@@ -441,18 +466,23 @@
     wide = COLS + 2 * STEPS
     end, keep, send = call(
         advance_kernel,
-        [shape(COLS, PAD, LANES), parts, parts],
-        (state, rates, from_west, from_east, core, high, low, base, arrived),
+        [store, parts, parts],
+        (rates, from_west, from_east, core, planes, arrived),
         scratch=[
             pltpu.VMEM((5 * wide, 8, LANES), F32),
             pltpu.VMEM((wide, 2 * LANES, 2 * LANES), BF16),
             pltpu.VMEM((wide, PAD, LANES), F32),
             pltpu.VMEM((wide, PAD, LANES), F32),
+            pltpu.VMEM((COLS, PAD, LANES), F32),
+            pltpu.VMEM((COLS, PAD, LANES), F32),
+            pltpu.VMEM((4, PAD, LANES), F32),
+            pltpu.SemaphoreType.DMA((7,)),
         ],
         flops=15 * 10**9,
         moved=6 * field,
-        smem=(4,),
-        far=(8,),
+        smem=(3,),
+        far=(4, 5),
+        far_out=(0,),
         mib=36,
     )
     swap = [(0, 1), (1, 0)]
@@ -466,10 +496,13 @@
         scratch=[
             pltpu.VMEM((PAD, COLS * LANES), BF16),
             pltpu.VMEM((PAD, COLS * LANES), BF16),
+            pltpu.VMEM((COLS, PAD, LANES), F32),
+            pltpu.SemaphoreType.DMA((COLS,)),
         ],
         flops=3 * 10**9,
         moved=field,
         smem=(0,),
+        far=(2,),
         mib=10,
     )
     totals = call(scan_kernel, parts, (gathered, found), flops=10**7, moved=field, mib=6)

time: 110 us -> 118 us (1.073)
  Pallas kernels: 31.6 us -> 36.2 us
  starting transfers between devices: 38.6 us -> 42.1 us
  local copies, waits for them, and re-layouts: 11.3 us -> 14.3 us
  waiting for transfers between devices: 25.4 us -> 22.6 us
    pallas_call x10, Pallas kernels: 31.6 us -> 36.2 us  [call(): pl.pallas_call(body, out_shape=outs, in_specs=specs, out_specs=out_specs...]
    all_to_all x1, waiting for transfers between devices: 3.08 us -> 0.01 us  [per_device(): gathered = lax.all_to_all(pair, ('y', 'x'), 0, 0, tiled=True)]
    unnamed x35 -> x23, local copies, waits for them, and re-layouts: 11.2 us -> 14.3 us
    all_to_all x1, starting transfers between devices: 3.79 us -> 6.66 us  [per_device(): before = lax.all_to_all(totals, ('y', 'x'), 0, 0, tiled=True)]
  transfers between devices with their start and end apart: 11 -> 11, of which waited for: 8 -> 7; matrix products, arithmetic and copies ran while one was open for 1% -> 1% of each run, Pallas kernels for 15% -> 16%
where the time goes in v9:
time: 118 us; the launch traced here: 117 us
  starting transfers between devices  42.1 us (36%)
  Pallas kernels  36.2 us (31%)
  waiting for transfers between devices  22.6 us (19%)
  local copies, waits for them, and re-layouts  14.3 us (12%)
  between operations  1.68 us (1%)
    pallas_call x10, Pallas kernels, call(): pl.pallas_call(body, out_shape=outs, in_specs=specs, out_specs=out_specs...  36.2 us
    unnamed x23, local copies, waits for them, and re-layouts  14.3 us
    all_to_all x1, starting transfers between devices, per_device(): arrived = lax.all_to_all(queries, 'tile', 0, 0, tiled=True)  9.77 us
    all_to_all x1, waiting for transfers between devices, per_device(): arrived = lax.all_to_all(queries, 'tile', 0, 0, tiled=True)  9.53 us
    ppermute x4, starting transfers between devices, ring_step(): lax.ppermute(parcel, 'tile', [(i, (i + by) % TILES) for i in range(TILES)])  8.02 us
    all_to_all x1, starting transfers between devices, per_device(): gathered = lax.all_to_all(pair, ('y', 'x'), 0, 0, tiled=True)  6.76 us
    all_to_all x1, starting transfers between devices, per_device(): before = lax.all_to_all(totals, ('y', 'x'), 0, 0, tiled=True)  6.66 us
    all_to_all x1, waiting for transfers between devices, per_device(): before = lax.all_to_all(totals, ('y', 'x'), 0, 0, tiled=True)  6.38 us
  transfers between devices with their start and end apart: 11, of which 7 were waited for; matrix products, arithmetic and copies ran while one was open for 1% of the time, Pallas kernels for 16%

profile of v9, /device:TPU:1, one launch (start us, length us, event | category | flops | bytes accessed | tf_op | source)
XLA Modules:
  0.0 116.9 jit_solution(14987881558522077609)
XLA Ops:
  0.6 3.4 %shard_map.104 = (f32[6,416,128]{2,1,0:T(8,128)}, f32[6,416,128]{2,1,0:T(8,128)}, f32[8,128]{1,0:T(8,128)}) custom-call(f32[411,8,128]{2,1,0:T(8,128)} %bitcast.9, f32[4,8,128]{2,1,0:T(8,128)} %bitcast.13), custom_call_target="tpu_custom_call" | custom-call | bytes 5111808 | tf_op jit(solution)/shard_map/pallas_call | solution.py:42
  4.1 4.5 %collective-permute-start = (f32[6,416,128]{2,1,0:T(8,128)}, f32[6,416,128]{2,1,0:T(8,128)S(1)}, u32[]{:S(2)}, u32[]{:S(2)}) collective-permute-start(f32[6,416,128]{2,1,0:T(8,128)} %get-tuple-element.19), channel_id=1, source_target_pairs={{0,1},{1,2},{2,3},{3,4},{4,5},{5,6},{6,7},{8,9},{9,10},{10,11},{11... | collective-permute-start | bytes 3833864 | tf_op jit(solution)/shard_map/ppermute | solution.py:432
  8.5 1.3 %collective-permute-start.1 = (f32[6,416,128]{2,1,0:T(8,128)}, f32[6,416,128]{2,1,0:T(8,128)}, u32[]{:S(2)}, u32[]{:S(2)}) collective-permute-start(f32[6,416,128]{2,1,0:T(8,128)} %get-tuple-element.20), channel_id=1, source_target_pairs={{1,0},{2,1},{3,2},{4,3},{5,4},{6,5},{7,6},{9,8},{10,9},{11,10},{12... | collective-permute-start | bytes 3833864 | tf_op jit(solution)/shard_map/ppermute | solution.py:433
  9.8 1.2 %copy.13 = f32[1,411,411]{2,1,0:T(8,128)S(1)} copy(f32[1,411,411]{2,0,1:T(1,128)} %param.12) | data formatting | bytes 1351368
  11.1 1.1 copy-done.5
  12.3 8.4 %shard_map.105 = (f32[8,416,128]{2,1,0:T(8,128)S(1)}, f32[160,416,128]{2,1,0:T(8,128)}, f32[8,128]{1,0:T(8,128)S(1)}) custom-call(f32[411,8,128]{2,1,0:T(8,128)S(1)} %bitcast.10, f32[411,8,128]{2,1,0:T(8,128)S(1)} %bitcast.12, f32[411,411]{1,0:T(8,128)S(1)} %copy-done.5, f32[411,411]{1,0:T(8,128)S(1)} %bitcast.11, f32[8,128]{1,0:T(8,128)S(1)} %copy-done.7), custom_call_target="tpu_custom_call" | custom-call | flops 100000000 | bytes 1000000 | tf_op jit(solution)/shard_map/pallas_call | solution.py:42
  20.7 1.2 %copy-done.2 = f32[8,416,128]{2,1,0:T(8,128)} copy-done((f32[8,416,128]{2,1,0:T(8,128)}, f32[8,416,128]{2,1,0:T(8,128)S(1)}, u32[]{:S(2)}) %copy-start.2) | copy-done | bytes 1703960
  21.9 2.5 %shard_map.106 = (f32[8,8,128]{2,1,0:T(8,128)}, f32[16,512]{1,0:T(8,128)S(1)}) custom-call(s32[3,1,512]{2,1,0:T(1,128)S(1)} %copy-done.9, f32[2,1,512]{2,1,0:T(1,128)S(1)} %copy-done.10, f32[8,128]{1,0:T(8,128)S(1)} %get-tuple-element.22.order_ref), custom_call_target="tpu_custom_call" | custom-call | flops 10000000 | bytes 100000 | tf_op jit(solution)/shard_map/pallas_call | solution.py:42
  24.4 9.8 %all-to-all-start = ((f32[8,8,128]{2,1,0:T(8,128)}), f32[8,8,128]{2,1,0:T(8,128)S(1)}, u32[]{:S(2)}, u32[]{:S(2)}) async-start(f32[8,8,128]{2,1,0:T(8,128)} %get-tuple-element.23), calls=%async_computation | async-start | bytes 65536 | tf_op jit(solution)/shard_map/all_to_all | solution.py:464
  34.2 9.5 %all-to-all-done.order_ref.obs_ref = f32[8,8,128]{2,1,0:T(8,128)S(1)} async-done(((f32[8,8,128]{2,1,0:T(8,128)}), f32[8,8,128]{2,1,0:T(8,128)S(1)}, u32[]{:S(2)}, u32[]{:S(2)}) %all-to-all-start) | async-done | bytes 32800 | tf_op jit(solution)/shard_map/all_to_all | solution.py:464
  43.7 11.1 %shard_map.107 = (f32[160,416,128]{2,1,0:T(8,128)}, f32[16,104,128]{2,1,0:T(8,128)S(1)}, f32[16,104,128]{2,1,0:T(8,128)S(1)}) custom-call(f32[4,8,128]{2,1,0:T(8,128)S(1)} %bitcast.14, f32[6,416,128]{2,1,0:T(8,128)S(1)} %collective-permute-done.west_ref, f32[6,416,128]{2,1,0:T(8,128)} %collective-permute-done.1.east_ref, s32[1]{0:T(128)} %bitcast.core_ref, ...), custom_call_target="tpu_custom_call" | custom-call | flops 15000000512 | bytes 10223616 | tf_op jit(solution)/shard_map/pallas_call | solution.py:42
  54.9 1.8 %collective-permute-start.2 = (f32[16,104,128]{2,1,0:T(8,128)S(1)}, f32[16,104,128]{2,1,0:T(8,128)S(1)}, u32[]{:S(2)}, u32[]{:S(2)}) collective-permute-start(f32[16,104,128]{2,1,0:T(8,128)S(1)} %get-tuple-element.25), channel_id=1, source_target_pairs={{0,8},{8,0},{1,9},{9,1},{2,10},{10,2},{3,11},{11,3},{4,12},{12,4},... | collective-permute-start | bytes 2555912 | tf_op jit(solution)/shard_map/ppermute | solution.py:489
  57.3 1.4 %collective-permute-done.2.partner_ref = f32[16,104,128]{2,1,0:T(8,128)S(1)} collective-permute-done((f32[16,104,128]{2,1,0:T(8,128)S(1)}, f32[16,104,128]{2,1,0:T(8,128)S(1)}, u32[]{:S(2)}, u32[]{:S(2)}) %collective-permute-start.2) | collective-permute-done | bytes 852000 | tf_op jit(solution)/shard_map/ppermute | solution.py:489
  58.7 1.0 shard_map.108
  59.7 6.8 %all-to-all-start.1 = ((f32[16,104,128]{2,1,0:T(8,128)}), f32[16,104,128]{2,1,0:T(8,128)S(1)}, u32[]{:S(2)}, u32[]{:S(2)}) async-start(f32[16,104,128]{2,1,0:T(8,128)} %get-tuple-element.26), calls=%async_computation.1 | async-start | bytes 1703936 | tf_op jit(solution)/shard_map/all_to_all | solution.py:491
  66.5 10.7 %copy-done = f32[160,416,128]{2,1,0:T(8,128)S(1)} copy-done((f32[160,416,128]{2,1,0:T(8,128)S(1)}, f32[160,416,128]{2,1,0:T(8,128)}, u32[]{:S(2)}) %copy-start) | copy-done | bytes 34078744
  77.2 6.3 %shard_map.109.order_ref = f32[8,128]{1,0:T(8,128)S(1)} custom-call(s32[1]{0:T(128)} %bitcast.4.me_ref, f32[8,8,128]{2,1,0:T(8,128)S(1)} %all-to-all-done.order_ref.obs_ref, f32[160,416,128]{2,1,0:T(8,128)S(1)} %copy-done, f32[8,128]{1,0:T(8,128)S(1)} %get-tuple-element.28.order_ref), custom_call_target="tpu_custom_call" | custom-call | flops 3000000000 | bytes 1703936 | tf_op jit(solution)/shard_map/pallas_call | solution.py:42
  83.4 3.5 %collective-permute-start.4 = (f32[2,128]{1,0:T(2,128)S(1)}, f32[2,128]{1,0:T(2,128)S(1)}, u32[]{:S(2)}, u32[]{:S(2)}) collective-permute-start(f32[2,128]{1,0:T(2,128)S(1)} %pad_maximum_fusion.2), channel_id=1, source_target_pairs={{0,3},{1,4},{2,5},{3,6},{4,7},{5,0},{6,1},{7,2},{8,11},{9,12},{10,... | collective-permute-start | bytes 3080 | tf_op jit(solution)/shard_map/ppermute | solution.py:406
  86.9 1.3 %collective-permute-start.3 = (f32[3,128]{1,0:T(4,128)S(1)}, f32[3,128]{1,0:T(4,128)S(1)}, u32[]{:S(2)}, u32[]{:S(2)}) collective-permute-start(f32[3,128]{1,0:T(4,128)S(1)} %pad_maximum_fusion), channel_id=1, source_target_pairs={{0,5},{1,6},{2,7},{3,0},{4,1},{5,2},{6,3},{7,4},{8,13},{9,14},{10,... | collective-permute-start | bytes 4616 | tf_op jit(solution)/shard_map/ppermute | solution.py:406
  88.3 0.9 collective-permute-done.4
  89.2 1.1 shard_map.110
  90.3 6.7 %all-to-all-start.2 = ((f32[16,104,128]{2,1,0:T(8,128)}), f32[16,104,128]{2,1,0:T(8,128)S(1)}, u32[]{:S(2)}, u32[]{:S(2)}) async-start(f32[16,104,128]{2,1,0:T(8,128)} %shard_map.110), calls=%async_computation.2 | async-start | bytes 1703936 | tf_op jit(solution)/shard_map/all_to_all | solution.py:509
  97.0 3.1 %collective-permute-start.6 = (f32[2,128]{1,0:T(2,128)S(1)}, f32[2,128]{1,0:T(2,128)S(1)}, u32[]{:S(2)}, u32[]{:S(2)}) collective-permute-start(f32[2,128]{1,0:T(2,128)S(1)} %pad_maximum_fusion.3), channel_id=1, source_target_pairs={{0,1},{1,2},{2,3},{3,4},{4,5},{5,6},{6,7},{7,0},{8,9},{9,10},{10,1... | collective-permute-start | bytes 3080 | tf_op jit(solution)/shard_map/ppermute | solution.py:406
  100.1 0.1 collective-permute-start.5
  100.2 0.6 collective-permute-done.6
  100.8 1.8 %collective-permute-done.5 = f32[3,128]{1,0:T(4,128)S(1)} collective-permute-done((f32[3,128]{1,0:T(4,128)S(1)}, f32[3,128]{1,0:T(4,128)S(1)}, u32[]{:S(2)}, u32[]{:S(2)}) %collective-permute-start.5) | collective-permute-done | bytes 1568 | tf_op jit(solution)/shard_map/ppermute | solution.py:406
  102.7 0.9 shard_map.111
  103.5 6.4 %all-to-all-done.2.before_ref = f32[16,104,128]{2,1,0:T(8,128)S(1)} async-done(((f32[16,104,128]{2,1,0:T(8,128)}), f32[16,104,128]{2,1,0:T(8,128)S(1)}, u32[]{:S(2)}, u32[]{:S(2)}) %all-to-all-start.2) | async-done | bytes 852000 | tf_op jit(solution)/shard_map/all_to_all | solution.py:509
  109.9 0.1 shard_map.112
  110.0 3.3 %collective-permute-start.7 = (f32[16,104,128]{2,1,0:T(8,128)S(1)}, f32[16,104,128]{2,1,0:T(8,128)S(1)}, u32[]{:S(2)}, u32[]{:S(2)}) collective-permute-start(f32[16,104,128]{2,1,0:T(8,128)S(1)} %shard_map.112), channel_id=1, source_target_pairs={{0,8},{8,0},{1,9},{9,1},{2,10},{10,2},{3,11},{11,3},{4,12},{12,4},... | collective-permute-start | bytes 2555912 | tf_op jit(solution)/shard_map/ppermute | solution.py:522
  113.3 2.0 %collective-permute-done.7.other_ref = f32[16,104,128]{2,1,0:T(8,128)S(1)} collective-permute-done((f32[16,104,128]{2,1,0:T(8,128)S(1)}, f32[16,104,128]{2,1,0:T(8,128)S(1)}, u32[]{:S(2)}, u32[]{:S(2)}) %collective-permute-start.7) | collective-permute-done | bytes 852000 | tf_op jit(solution)/shard_map/ppermute | solution.py:522
  115.3 1.4 %shard_map.113 = f32[411,8,128]{2,1,0:T(8,128)} custom-call(s32[1]{0:T(128)} %bitcast.core_ref, f32[8,416,128]{2,1,0:T(8,128)S(1)} %copy-done.3, f32[16,104,128]{2,1,0:T(8,128)S(1)} %all-to-all-done.2.before_ref, f32[16,104,128]{2,1,0:T(8,128)S(1)} %collective-permute-done.2.partner_ref, f32[16,104,128]{2,1,0:T(8,128)S(1)} %collective-permute-done.7.other_ref), custom_call_target="tpu_custom_call" | custom-call | flops 10000000 | bytes 6815744 | tf_op jit(solution)/shard_map/pallas_call | solution.py:42
  (33 shorter events, 0.1 us)
Async XLA Ops:
  0.6 10.4 %copy-start.1 = (f32[1,3,137,8,128]{4,3,2,1,0:T(8,128)S(1)}, f32[1,3,137,8,128]{4,3,2,1,0:T(8,128)}, u32[]{:S(2)}) copy-start(f32[1,3,137,8,128]{4,3,2,1,0:T(8,128)} %param.9) | copy-start | bytes 5050372
  0.6 10.4 %copy-start.4 = (f32[1,3,137,8,128]{4,3,2,1,0:T(8,128)S(1)}, f32[1,3,137,8,128]{4,3,2,1,0:T(8,128)}, u32[]{:S(2)}) copy-start(f32[1,3,137,8,128]{4,3,2,1,0:T(8,128)} %param.10) | copy-start | bytes 5050372
  4.1 7.0 %copy-start.7 = (f32[8,128]{1,0:T(8,128)S(1)}, f32[8,128]{1,0:T(8,128)}, u32[]{:S(2)}) copy-start(f32[8,128]{1,0:T(8,128)} %get-tuple-element.17.order_ref) | copy-start | bytes 12292
  4.1 39.7 %collective-permute-start = (f32[6,416,128]{2,1,0:T(8,128)}, f32[6,416,128]{2,1,0:T(8,128)S(1)}, u32[]{:S(2)}, u32[]{:S(2)}) collective-permute-start(f32[6,416,128]{2,1,0:T(8,128)} %get-tuple-element.19), channel_id=1, source_target_pairs={{0,1},{1,2},{2,3},{3,4},{4,5},{5,6},{6,7},{8,9},{9,10},{10,11},{11... | collective-permute-start | bytes 3833864 | tf_op jit(solution)/shard_map/ppermute | solution.py:432
  8.5 35.2 %collective-permute-start.1 = (f32[6,416,128]{2,1,0:T(8,128)}, f32[6,416,128]{2,1,0:T(8,128)}, u32[]{:S(2)}, u32[]{:S(2)}) collective-permute-start(f32[6,416,128]{2,1,0:T(8,128)} %get-tuple-element.20), channel_id=1, source_target_pairs={{1,0},{2,1},{3,2},{4,3},{5,4},{6,5},{7,6},{9,8},{10,9},{11,10},{12... | collective-permute-start | bytes 3833864 | tf_op jit(solution)/shard_map/ppermute | solution.py:433
  11.1 1.2 copy-start.5
  12.3 9.7 %copy-start.9 = (s32[3,1,512]{2,1,0:T(1,128)S(1)}, s32[3,1,512]{2,1,0:T(1,128)}, u32[]{:S(2)}) copy-start(s32[3,1,512]{2,1,0:T(1,128)} %index_ref.1) | copy-start | bytes 18436
  12.3 9.7 %copy-start.10 = (f32[2,1,512]{2,1,0:T(1,128)S(1)}, f32[2,1,512]{2,1,0:T(1,128)}, u32[]{:S(2)}) copy-start(f32[2,1,512]{2,1,0:T(1,128)} %frac_ref.1) | copy-start | bytes 12292
  12.3 31.5 %copy-start.6 = (f32[1,4,8,128]{3,2,1,0:T(8,128)S(1)}, f32[1,4,8,128]{3,2,1,0:T(8,128)}, u32[]{:S(2)}) copy-start(f32[1,4,8,128]{3,2,1,0:T(8,128)} %param.13) | copy-start | bytes 49156
  20.7 1.2 %copy-start.2 = (f32[8,416,128]{2,1,0:T(8,128)}, f32[8,416,128]{2,1,0:T(8,128)S(1)}, u32[]{:S(2)}) copy-start(f32[8,416,128]{2,1,0:T(8,128)S(1)} %get-tuple-element.18.base_ref) | copy-start | bytes 5111812
  24.4 19.3 %all-to-all-start = ((f32[8,8,128]{2,1,0:T(8,128)}), f32[8,8,128]{2,1,0:T(8,128)S(1)}, u32[]{:S(2)}, u32[]{:S(2)}) async-start(f32[8,8,128]{2,1,0:T(8,128)} %get-tuple-element.23), calls=%async_computation | async-start | bytes 65536 | tf_op jit(solution)/shard_map/all_to_all | solution.py:464
  54.9 3.8 %collective-permute-start.2 = (f32[16,104,128]{2,1,0:T(8,128)S(1)}, f32[16,104,128]{2,1,0:T(8,128)S(1)}, u32[]{:S(2)}, u32[]{:S(2)}) collective-permute-start(f32[16,104,128]{2,1,0:T(8,128)S(1)} %get-tuple-element.25), channel_id=1, source_target_pairs={{0,8},{8,0},{1,9},{9,1},{2,10},{10,2},{3,11},{11,3},{4,12},{12,4},... | collective-permute-start | bytes 2555912 | tf_op jit(solution)/shard_map/ppermute | solution.py:489
  59.7 29.5 %all-to-all-start.1 = ((f32[16,104,128]{2,1,0:T(8,128)}), f32[16,104,128]{2,1,0:T(8,128)S(1)}, u32[]{:S(2)}, u32[]{:S(2)}) async-start(f32[16,104,128]{2,1,0:T(8,128)} %get-tuple-element.26), calls=%async_computation.1 | async-start | bytes 1703936 | tf_op jit(solution)/shard_map/all_to_all | solution.py:491
  66.5 10.7 %copy-start = (f32[160,416,128]{2,1,0:T(8,128)S(1)}, f32[160,416,128]{2,1,0:T(8,128)}, u32[]{:S(2)}) copy-start(f32[160,416,128]{2,1,0:T(8,128)} %get-tuple-element.27.end_ref) | copy-start | bytes 102236160
  83.4 5.7 %collective-permute-start.4 = (f32[2,128]{1,0:T(2,128)S(1)}, f32[2,128]{1,0:T(2,128)S(1)}, u32[]{:S(2)}, u32[]{:S(2)}) collective-permute-start(f32[2,128]{1,0:T(2,128)S(1)} %pad_maximum_fusion.2), channel_id=1, source_target_pairs={{0,3},{1,4},{2,5},{3,6},{4,7},{5,0},{6,1},{7,2},{8,11},{9,12},{10,... | collective-permute-start | bytes 3080 | tf_op jit(solution)/shard_map/ppermute | solution.py:406
  86.9 10.0 %collective-permute-start.3 = (f32[3,128]{1,0:T(4,128)S(1)}, f32[3,128]{1,0:T(4,128)S(1)}, u32[]{:S(2)}, u32[]{:S(2)}) collective-permute-start(f32[3,128]{1,0:T(4,128)S(1)} %pad_maximum_fusion), channel_id=1, source_target_pairs={{0,5},{1,6},{2,7},{3,0},{4,1},{5,2},{6,3},{7,4},{8,13},{9,14},{10,... | collective-permute-start | bytes 4616 | tf_op jit(solution)/shard_map/ppermute | solution.py:406
  89.2 13.5 %copy-start.8 = (f32[1,512]{1,0:T(1,128)S(1)}, f32[1,512]{1,0:T(1,128)}, u32[]{:S(2)}) copy-start(f32[1,512]{1,0:T(1,128)} %value_ref.1) | copy-start | bytes 6148
  90.3 19.6 %all-to-all-start.2 = ((f32[16,104,128]{2,1,0:T(8,128)}), f32[16,104,128]{2,1,0:T(8,128)S(1)}, u32[]{:S(2)}, u32[]{:S(2)}) async-start(f32[16,104,128]{2,1,0:T(8,128)} %shard_map.110), calls=%async_computation.2 | async-start | bytes 1703936 | tf_op jit(solution)/shard_map/all_to_all | solution.py:509
  97.0 3.8 %collective-permute-start.6 = (f32[2,128]{1,0:T(2,128)S(1)}, f32[2,128]{1,0:T(2,128)S(1)}, u32[]{:S(2)}, u32[]{:S(2)}) collective-permute-start(f32[2,128]{1,0:T(2,128)S(1)} %pad_maximum_fusion.3), channel_id=1, source_target_pairs={{0,1},{1,2},{2,3},{3,4},{4,5},{5,6},{6,7},{7,0},{8,9},{9,10},{10,1... | collective-permute-start | bytes 3080 | tf_op jit(solution)/shard_map/ppermute | solution.py:406
  100.1 2.5 %collective-permute-start.5 = (f32[3,128]{1,0:T(4,128)S(1)}, f32[3,128]{1,0:T(4,128)S(1)}, u32[]{:S(2)}, u32[]{:S(2)}) collective-permute-start(f32[3,128]{1,0:T(4,128)S(1)} %pad_maximum_fusion.1), channel_id=1, source_target_pairs={{0,7},{1,0},{2,1},{3,2},{4,3},{5,4},{6,5},{7,6},{8,15},{9,8},{10,9... | collective-permute-start | bytes 4616 | tf_op jit(solution)/shard_map/ppermute | solution.py:406
  109.9 5.4 %copy-start.3 = (f32[8,416,128]{2,1,0:T(8,128)S(1)}, f32[8,416,128]{2,1,0:T(8,128)}, u32[]{:S(2)}) copy-start(f32[8,416,128]{2,1,0:T(8,128)} %copy-done.2) | copy-start | bytes 5111812
  110.0 5.3 %collective-permute-start.7 = (f32[16,104,128]{2,1,0:T(8,128)S(1)}, f32[16,104,128]{2,1,0:T(8,128)S(1)}, u32[]{:S(2)}, u32[]{:S(2)}) collective-permute-start(f32[16,104,128]{2,1,0:T(8,128)S(1)} %shard_map.112), channel_id=1, source_target_pairs={{0,8},{8,0},{1,9},{9,1},{2,10},{10,2},{3,11},{11,3},{4,12},{12,4},... | collective-permute-start | bytes 2555912 | tf_op jit(solution)/shard_map/ppermute | solution.py:522

commit v10 on v9

--- a/solution.py
+++ b/solution.py
@@ -18,6 +18,7 @@
 TILES = 8
 HALF = 208
 STORE = 160
+END_STORE = 320
 SLOTS = 512
 CAP = 128
 FIELDS = 8
@@ -215,8 +216,6 @@
         band[j, LANES:, :LANES] = along_high
         band[j, :LANES, LANES:] = along_low
         band[j, LANES:, LANES:] = jnp.zeros((LANES, LANES), BF16)
-    own.wait()
-
     def load(step, j, rows):
         if step == 0 and j < STEPS:
             return west_ref[j, rows, :]
@@ -238,7 +237,13 @@
 
     quarters = [slice(q * PART, (q + 1) * PART) for q in range(4)]
     for step in range(1, STEPS + 1):
-        for j in range(step, wide - step):
+        order = list(range(step, wide - step))
+        if step == 1:
+            apart = [j for j in order if j < STEPS - 1 or j > STEPS + COLS]
+            order = apart + [j for j in order if j not in apart]
+        for j in order:
+            if step == 1 and j == STEPS - 1:
+                own.wait()
             if rotated(j):
                 for rows in quarters:
                     value = tiles(load(step - 1, j, rows))
@@ -466,7 +471,7 @@
     wide = COLS + 2 * STEPS
     end, keep, send = call(
         advance_kernel,
-        [store, parts, parts],
+        [shape(END_STORE, PAD, LANES), parts, parts],
         (rates, from_west, from_east, core, planes, arrived),
         scratch=[
             pltpu.VMEM((5 * wide, 8, LANES), F32),

time: 118 us -> 106 us (0.90)
  local copies, waits for them, and re-layouts: 14.3 us -> 3.6 us
  waiting for transfers between devices: 22.6 us -> 26.2 us
  starting transfers between devices: 42.1 us -> 38.9 us
  Pallas kernels: 36.2 us -> 34.5 us
    unnamed x23 -> x21, local copies, waits for them, and re-layouts: 14.3 us -> 3.55 us
    all_to_all x1, waiting for transfers between devices: 0.01 us -> 3.06 us  [per_device(): gathered = lax.all_to_all(pair, ('y', 'x'), 0, 0, tiled=True)]
    all_to_all x1, starting transfers between devices: 6.66 us -> 3.79 us  [per_device(): before = lax.all_to_all(totals, ('y', 'x'), 0, 0, tiled=True)]
    pallas_call x10, Pallas kernels: 36.2 us -> 34.5 us  [call(): pl.pallas_call(body, out_shape=outs, in_specs=specs, out_specs=out_specs...]
  transfers between devices with their start and end apart: 11 -> 11, of which waited for: 7 -> 8; matrix products, arithmetic and copies ran while one was open for 1% -> 1% of each run, Pallas kernels for 16% -> 17%
where the time goes in v10:
time: 106 us; the launch traced here: 105 us
  starting transfers between devices  38.9 us (37%)
  Pallas kernels  34.5 us (33%)
  waiting for transfers between devices  26.2 us (25%)
  local copies, waits for them, and re-layouts  3.6 us (3%)
  between operations  1.66 us (2%)
    pallas_call x10, Pallas kernels, call(): pl.pallas_call(body, out_shape=outs, in_specs=specs, out_specs=out_specs...  34.5 us
    all_to_all x1, starting transfers between devices, per_device(): arrived = lax.all_to_all(queries, 'tile', 0, 0, tiled=True)  9.77 us
    all_to_all x1, waiting for transfers between devices, per_device(): arrived = lax.all_to_all(queries, 'tile', 0, 0, tiled=True)  9.53 us
    ppermute x4, starting transfers between devices, ring_step(): lax.ppermute(parcel, 'tile', [(i, (i + by) % TILES) for i in range(TILES)])  8.01 us
    all_to_all x1, starting transfers between devices, per_device(): gathered = lax.all_to_all(pair, ('y', 'x'), 0, 0, tiled=True)  6.76 us
    all_to_all x1, waiting for transfers between devices, per_device(): before = lax.all_to_all(totals, ('y', 'x'), 0, 0, tiled=True)  6.39 us
    ppermute x1, starting transfers between devices, per_device(): from_west = lax.ppermute(east, 'tile', to_east)  4.45 us
    ppermute x4, waiting for transfers between devices, ring_step(): lax.ppermute(parcel, 'tile', [(i, (i + by) % TILES) for i in range(TILES)])  3.88 us
  transfers between devices with their start and end apart: 11, of which 8 were waited for; matrix products, arithmetic and copies ran while one was open for 1% of the time, Pallas kernels for 17%

profile of v10, /device:TPU:1, one launch (start us, length us, event | category | flops | bytes accessed | tf_op | source)
XLA Modules:
  0.0 104.9 jit_solution(8214036345406282851)
XLA Ops:
  0.6 3.4 %shard_map.104 = (f32[6,416,128]{2,1,0:T(8,128)}, f32[6,416,128]{2,1,0:T(8,128)}, f32[8,128]{1,0:T(8,128)}) custom-call(f32[411,8,128]{2,1,0:T(8,128)} %bitcast.9, f32[4,8,128]{2,1,0:T(8,128)} %bitcast.13), custom_call_target="tpu_custom_call" | custom-call | bytes 5111808 | tf_op jit(solution)/shard_map/pallas_call | solution.py:43
  4.1 4.5 %collective-permute-start = (f32[6,416,128]{2,1,0:T(8,128)}, f32[6,416,128]{2,1,0:T(8,128)S(1)}, u32[]{:S(2)}, u32[]{:S(2)}) collective-permute-start(f32[6,416,128]{2,1,0:T(8,128)} %get-tuple-element.19), channel_id=1, source_target_pairs={{0,1},{1,2},{2,3},{3,4},{4,5},{5,6},{6,7},{8,9},{9,10},{10,11},{11... | collective-permute-start | bytes 3833864 | tf_op jit(solution)/shard_map/ppermute | solution.py:437
  8.5 1.3 %collective-permute-start.1 = (f32[6,416,128]{2,1,0:T(8,128)}, f32[6,416,128]{2,1,0:T(8,128)}, u32[]{:S(2)}, u32[]{:S(2)}) collective-permute-start(f32[6,416,128]{2,1,0:T(8,128)} %get-tuple-element.20), channel_id=1, source_target_pairs={{1,0},{2,1},{3,2},{4,3},{5,4},{6,5},{7,6},{9,8},{10,9},{11,10},{12... | collective-permute-start | bytes 3833864 | tf_op jit(solution)/shard_map/ppermute | solution.py:438
  9.8 1.2 %copy.13 = f32[1,411,411]{2,1,0:T(8,128)S(1)} copy(f32[1,411,411]{2,0,1:T(1,128)} %param.12) | data formatting | bytes 1351368
  11.1 1.1 %copy-done.4 = f32[411,411]{1,0:T(8,128)S(1)} copy-done((f32[411,411]{1,0:T(8,128)S(1)}, f32[411,411]{1,0:T(8,128)}, u32[]{:S(2)}) %copy-start.4) | copy-done | bytes 675708
  12.3 8.5 %shard_map.105 = (f32[8,416,128]{2,1,0:T(8,128)S(1)}, f32[160,416,128]{2,1,0:T(8,128)}, f32[8,128]{1,0:T(8,128)S(1)}) custom-call(f32[411,8,128]{2,1,0:T(8,128)S(1)} %bitcast.10, f32[411,8,128]{2,1,0:T(8,128)S(1)} %bitcast.12, f32[411,411]{1,0:T(8,128)S(1)} %copy-done.4, f32[411,411]{1,0:T(8,128)S(1)} %bitcast.11, f32[8,128]{1,0:T(8,128)S(1)} %copy-done.6), custom_call_target="tpu_custom_call" | custom-call | flops 100000000 | bytes 1000000 | tf_op jit(solution)/shard_map/pallas_call | solution.py:43
  20.8 1.2 %copy-done.1 = f32[8,416,128]{2,1,0:T(8,128)} copy-done((f32[8,416,128]{2,1,0:T(8,128)}, f32[8,416,128]{2,1,0:T(8,128)S(1)}, u32[]{:S(2)}) %copy-start.1) | copy-done | bytes 1703960
  21.9 2.5 %shard_map.106 = (f32[8,8,128]{2,1,0:T(8,128)}, f32[16,512]{1,0:T(8,128)S(1)}) custom-call(s32[3,1,512]{2,1,0:T(1,128)S(1)} %copy-done.8, f32[2,1,512]{2,1,0:T(1,128)S(1)} %copy-done.9, f32[8,128]{1,0:T(8,128)S(1)} %get-tuple-element.22.order_ref), custom_call_target="tpu_custom_call" | custom-call | flops 10000000 | bytes 100000 | tf_op jit(solution)/shard_map/pallas_call | solution.py:43
  24.4 9.8 %all-to-all-start = ((f32[8,8,128]{2,1,0:T(8,128)}), f32[8,8,128]{2,1,0:T(8,128)S(1)}, u32[]{:S(2)}, u32[]{:S(2)}) async-start(f32[8,8,128]{2,1,0:T(8,128)} %get-tuple-element.23), calls=%async_computation | async-start | bytes 65536 | tf_op jit(solution)/shard_map/all_to_all | solution.py:469
  34.2 9.5 %all-to-all-done.order_ref.obs_ref = f32[8,8,128]{2,1,0:T(8,128)S(1)} async-done(((f32[8,8,128]{2,1,0:T(8,128)}), f32[8,8,128]{2,1,0:T(8,128)S(1)}, u32[]{:S(2)}, u32[]{:S(2)}) %all-to-all-start) | async-done | bytes 32800 | tf_op jit(solution)/shard_map/all_to_all | solution.py:469
  43.7 10.6 %shard_map.107 = (f32[320,416,128]{2,1,0:T(8,128)}, f32[16,104,128]{2,1,0:T(8,128)S(1)}, f32[16,104,128]{2,1,0:T(8,128)S(1)}) custom-call(f32[4,8,128]{2,1,0:T(8,128)S(1)} %bitcast.14, f32[6,416,128]{2,1,0:T(8,128)S(1)} %collective-permute-done.west_ref, f32[6,416,128]{2,1,0:T(8,128)} %collective-permute-done.1.east_ref, s32[1]{0:T(128)} %bitcast.core_ref, ...), custom_call_target="tpu_custom_call" | custom-call | flops 15000000512 | bytes 10223616 | tf_op jit(solution)/shard_map/pallas_call | solution.py:43
  54.4 1.8 %collective-permute-start.2 = (f32[16,104,128]{2,1,0:T(8,128)S(1)}, f32[16,104,128]{2,1,0:T(8,128)S(1)}, u32[]{:S(2)}, u32[]{:S(2)}) collective-permute-start(f32[16,104,128]{2,1,0:T(8,128)S(1)} %get-tuple-element.25), channel_id=1, source_target_pairs={{0,8},{8,0},{1,9},{9,1},{2,10},{10,2},{3,11},{11,3},{4,12},{12,4},... | collective-permute-start | bytes 2555912 | tf_op jit(solution)/shard_map/ppermute | solution.py:494
  56.8 1.4 %collective-permute-done.2.partner_ref = f32[16,104,128]{2,1,0:T(8,128)S(1)} collective-permute-done((f32[16,104,128]{2,1,0:T(8,128)S(1)}, f32[16,104,128]{2,1,0:T(8,128)S(1)}, u32[]{:S(2)}, u32[]{:S(2)}) %collective-permute-start.2) | collective-permute-done | bytes 852000 | tf_op jit(solution)/shard_map/ppermute | solution.py:494
  58.2 1.0 shard_map.108
  59.2 6.8 %all-to-all-start.1 = ((f32[16,104,128]{2,1,0:T(8,128)}), f32[16,104,128]{2,1,0:T(8,128)S(1)}, u32[]{:S(2)}, u32[]{:S(2)}) async-start(f32[16,104,128]{2,1,0:T(8,128)} %get-tuple-element.26), calls=%async_computation.1 | async-start | bytes 1703936 | tf_op jit(solution)/shard_map/all_to_all | solution.py:496
  65.9 5.1 %shard_map.109.order_ref = f32[8,128]{1,0:T(8,128)S(1)} custom-call(s32[1]{0:T(128)} %bitcast.4.me_ref, f32[8,8,128]{2,1,0:T(8,128)S(1)} %all-to-all-done.order_ref.obs_ref, f32[320,416,128]{2,1,0:T(8,128)} %get-tuple-element.27.end_ref, f32[8,128]{1,0:T(8,128)S(1)} %get-tuple-element.28.order_ref), custom_call_target="tpu_custom_call" | custom-call | flops 3000000000 | bytes 1703936 | tf_op jit(solution)/shard_map/pallas_call | solution.py:43
  71.1 3.5 %collective-permute-start.4 = (f32[2,128]{1,0:T(2,128)S(1)}, f32[2,128]{1,0:T(2,128)S(1)}, u32[]{:S(2)}, u32[]{:S(2)}) collective-permute-start(f32[2,128]{1,0:T(2,128)S(1)} %pad_maximum_fusion.2), channel_id=1, source_target_pairs={{0,3},{1,4},{2,5},{3,6},{4,7},{5,0},{6,1},{7,2},{8,11},{9,12},{10,... | collective-permute-start | bytes 3080 | tf_op jit(solution)/shard_map/ppermute | solution.py:411
  74.6 1.3 %collective-permute-start.3 = (f32[3,128]{1,0:T(4,128)S(1)}, f32[3,128]{1,0:T(4,128)S(1)}, u32[]{:S(2)}, u32[]{:S(2)}) collective-permute-start(f32[3,128]{1,0:T(4,128)S(1)} %pad_maximum_fusion), channel_id=1, source_target_pairs={{0,5},{1,6},{2,7},{3,0},{4,1},{5,2},{6,3},{7,4},{8,13},{9,14},{10,... | collective-permute-start | bytes 4616 | tf_op jit(solution)/shard_map/ppermute | solution.py:411
  75.9 1.2 %collective-permute-done.4 = f32[2,128]{1,0:T(2,128)S(1)} collective-permute-done((f32[2,128]{1,0:T(2,128)S(1)}, f32[2,128]{1,0:T(2,128)S(1)}, u32[]{:S(2)}, u32[]{:S(2)}) %collective-permute-start.4) | collective-permute-done | bytes 1056 | tf_op jit(solution)/shard_map/ppermute | solution.py:411
  77.1 3.1 %all-to-all-done.1.in_ref = f32[16,104,128]{2,1,0:T(8,128)S(1)} async-done(((f32[16,104,128]{2,1,0:T(8,128)}), f32[16,104,128]{2,1,0:T(8,128)S(1)}, u32[]{:S(2)}, u32[]{:S(2)}) %all-to-all-start.1) | async-done | bytes 852000 | tf_op jit(solution)/shard_map/all_to_all | solution.py:496
  80.2 1.1 %shard_map.110 = f32[16,104,128]{2,1,0:T(8,128)} custom-call(f32[16,104,128]{2,1,0:T(8,128)S(1)} %all-to-all-done.1.in_ref, f32[8,128]{1,0:T(8,128)S(1)} %shard_map.109.order_ref), custom_call_target="tpu_custom_call" | custom-call | flops 10000000 | bytes 1703936 | tf_op jit(solution)/shard_map/pallas_call | solution.py:43
  81.3 3.8 %all-to-all-start.2 = ((f32[16,104,128]{2,1,0:T(8,128)}), f32[16,104,128]{2,1,0:T(8,128)S(1)}, u32[]{:S(2)}, u32[]{:S(2)}) async-start(f32[16,104,128]{2,1,0:T(8,128)} %shard_map.110), calls=%async_computation.2 | async-start | bytes 1703936 | tf_op jit(solution)/shard_map/all_to_all | solution.py:514
  85.1 3.1 %collective-permute-start.6 = (f32[2,128]{1,0:T(2,128)S(1)}, f32[2,128]{1,0:T(2,128)S(1)}, u32[]{:S(2)}, u32[]{:S(2)}) collective-permute-start(f32[2,128]{1,0:T(2,128)S(1)} %pad_maximum_fusion.3), channel_id=1, source_target_pairs={{0,1},{1,2},{2,3},{3,4},{4,5},{5,6},{6,7},{7,0},{8,9},{9,10},{10,1... | collective-permute-start | bytes 3080 | tf_op jit(solution)/shard_map/ppermute | solution.py:411
  88.2 0.1 collective-permute-start.5
  88.3 0.6 collective-permute-done.6
  88.9 2.1 %collective-permute-done.5 = f32[3,128]{1,0:T(4,128)S(1)} collective-permute-done((f32[3,128]{1,0:T(4,128)S(1)}, f32[3,128]{1,0:T(4,128)S(1)}, u32[]{:S(2)}, u32[]{:S(2)}) %collective-permute-start.5) | collective-permute-done | bytes 1568 | tf_op jit(solution)/shard_map/ppermute | solution.py:411
  91.0 0.9 shard_map.111
  91.9 6.4 %all-to-all-done.2.before_ref = f32[16,104,128]{2,1,0:T(8,128)S(1)} async-done(((f32[16,104,128]{2,1,0:T(8,128)}), f32[16,104,128]{2,1,0:T(8,128)S(1)}, u32[]{:S(2)}, u32[]{:S(2)}) %all-to-all-start.2) | async-done | bytes 852000 | tf_op jit(solution)/shard_map/all_to_all | solution.py:514
  98.3 0.1 shard_map.112
  98.4 3.0 %collective-permute-start.7 = (f32[16,104,128]{2,1,0:T(8,128)S(1)}, f32[16,104,128]{2,1,0:T(8,128)S(1)}, u32[]{:S(2)}, u32[]{:S(2)}) collective-permute-start(f32[16,104,128]{2,1,0:T(8,128)S(1)} %shard_map.112), channel_id=1, source_target_pairs={{0,8},{8,0},{1,9},{9,1},{2,10},{10,2},{3,11},{11,3},{4,12},{12,4},... | collective-permute-start | bytes 2555912 | tf_op jit(solution)/shard_map/ppermute | solution.py:527
  101.4 2.0 %collective-permute-done.7.other_ref = f32[16,104,128]{2,1,0:T(8,128)S(1)} collective-permute-done((f32[16,104,128]{2,1,0:T(8,128)S(1)}, f32[16,104,128]{2,1,0:T(8,128)S(1)}, u32[]{:S(2)}, u32[]{:S(2)}) %collective-permute-start.7) | collective-permute-done | bytes 852000 | tf_op jit(solution)/shard_map/ppermute | solution.py:527
  103.4 1.4 %shard_map.113 = f32[411,8,128]{2,1,0:T(8,128)} custom-call(s32[1]{0:T(128)} %bitcast.core_ref, f32[8,416,128]{2,1,0:T(8,128)S(1)} %copy-done.2, f32[16,104,128]{2,1,0:T(8,128)S(1)} %all-to-all-done.2.before_ref, f32[16,104,128]{2,1,0:T(8,128)S(1)} %collective-permute-done.2.partner_ref, f32[16,104,128]{2,1,0:T(8,128)S(1)} %collective-permute-done.7.other_ref), custom_call_target="tpu_custom_call" | custom-call | flops 10000000 | bytes 6815744 | tf_op jit(solution)/shard_map/pallas_call | solution.py:43
  (31 shorter events, 0.1 us)
Async XLA Ops:
  0.6 10.4 %copy-start = (f32[1,3,137,8,128]{4,3,2,1,0:T(8,128)S(1)}, f32[1,3,137,8,128]{4,3,2,1,0:T(8,128)}, u32[]{:S(2)}) copy-start(f32[1,3,137,8,128]{4,3,2,1,0:T(8,128)} %param.9) | copy-start | bytes 5050372
  0.6 10.4 %copy-start.3 = (f32[1,3,137,8,128]{4,3,2,1,0:T(8,128)S(1)}, f32[1,3,137,8,128]{4,3,2,1,0:T(8,128)}, u32[]{:S(2)}) copy-start(f32[1,3,137,8,128]{4,3,2,1,0:T(8,128)} %param.10) | copy-start | bytes 5050372
  4.1 7.0 %copy-start.6 = (f32[8,128]{1,0:T(8,128)S(1)}, f32[8,128]{1,0:T(8,128)}, u32[]{:S(2)}) copy-start(f32[8,128]{1,0:T(8,128)} %get-tuple-element.17.order_ref) | copy-start | bytes 12292
  4.1 39.7 %collective-permute-start = (f32[6,416,128]{2,1,0:T(8,128)}, f32[6,416,128]{2,1,0:T(8,128)S(1)}, u32[]{:S(2)}, u32[]{:S(2)}) collective-permute-start(f32[6,416,128]{2,1,0:T(8,128)} %get-tuple-element.19), channel_id=1, source_target_pairs={{0,1},{1,2},{2,3},{3,4},{4,5},{5,6},{6,7},{8,9},{9,10},{10,11},{11... | collective-permute-start | bytes 3833864 | tf_op jit(solution)/shard_map/ppermute | solution.py:437
  8.5 35.2 %collective-permute-start.1 = (f32[6,416,128]{2,1,0:T(8,128)}, f32[6,416,128]{2,1,0:T(8,128)}, u32[]{:S(2)}, u32[]{:S(2)}) collective-permute-start(f32[6,416,128]{2,1,0:T(8,128)} %get-tuple-element.20), channel_id=1, source_target_pairs={{1,0},{2,1},{3,2},{4,3},{5,4},{6,5},{7,6},{9,8},{10,9},{11,10},{12... | collective-permute-start | bytes 3833864 | tf_op jit(solution)/shard_map/ppermute | solution.py:438
  11.1 1.2 %copy-start.4 = (f32[411,411]{1,0:T(8,128)S(1)}, f32[411,411]{1,0:T(8,128)}, u32[]{:S(2)}) copy-start(f32[411,411]{1,0:T(8,128)} %root_ref.1) | copy-start | bytes 2027056
  12.2 9.7 %copy-start.8 = (s32[3,1,512]{2,1,0:T(1,128)S(1)}, s32[3,1,512]{2,1,0:T(1,128)}, u32[]{:S(2)}) copy-start(s32[3,1,512]{2,1,0:T(1,128)} %index_ref.1) | copy-start | bytes 18436
  12.2 9.7 %copy-start.9 = (f32[2,1,512]{2,1,0:T(1,128)S(1)}, f32[2,1,512]{2,1,0:T(1,128)}, u32[]{:S(2)}) copy-start(f32[2,1,512]{2,1,0:T(1,128)} %frac_ref.1) | copy-start | bytes 12292
  12.2 31.5 %copy-start.5 = (f32[1,4,8,128]{3,2,1,0:T(8,128)S(1)}, f32[1,4,8,128]{3,2,1,0:T(8,128)}, u32[]{:S(2)}) copy-start(f32[1,4,8,128]{3,2,1,0:T(8,128)} %param.13) | copy-start | bytes 49156
  20.7 1.2 %copy-start.1 = (f32[8,416,128]{2,1,0:T(8,128)}, f32[8,416,128]{2,1,0:T(8,128)S(1)}, u32[]{:S(2)}) copy-start(f32[8,416,128]{2,1,0:T(8,128)S(1)} %get-tuple-element.18.base_ref) | copy-start | bytes 5111812
  24.4 19.3 %all-to-all-start = ((f32[8,8,128]{2,1,0:T(8,128)}), f32[8,8,128]{2,1,0:T(8,128)S(1)}, u32[]{:S(2)}, u32[]{:S(2)}) async-start(f32[8,8,128]{2,1,0:T(8,128)} %get-tuple-element.23), calls=%async_computation | async-start | bytes 65536 | tf_op jit(solution)/shard_map/all_to_all | solution.py:469
  54.4 3.8 %collective-permute-start.2 = (f32[16,104,128]{2,1,0:T(8,128)S(1)}, f32[16,104,128]{2,1,0:T(8,128)S(1)}, u32[]{:S(2)}, u32[]{:S(2)}) collective-permute-start(f32[16,104,128]{2,1,0:T(8,128)S(1)} %get-tuple-element.25), channel_id=1, source_target_pairs={{0,8},{8,0},{1,9},{9,1},{2,10},{10,2},{3,11},{11,3},{4,12},{12,4},... | collective-permute-start | bytes 2555912 | tf_op jit(solution)/shard_map/ppermute | solution.py:494
  59.2 21.0 %all-to-all-start.1 = ((f32[16,104,128]{2,1,0:T(8,128)}), f32[16,104,128]{2,1,0:T(8,128)S(1)}, u32[]{:S(2)}, u32[]{:S(2)}) async-start(f32[16,104,128]{2,1,0:T(8,128)} %get-tuple-element.26), calls=%async_computation.1 | async-start | bytes 1703936 | tf_op jit(solution)/shard_map/all_to_all | solution.py:496
  71.1 6.0 %collective-permute-start.4 = (f32[2,128]{1,0:T(2,128)S(1)}, f32[2,128]{1,0:T(2,128)S(1)}, u32[]{:S(2)}, u32[]{:S(2)}) collective-permute-start(f32[2,128]{1,0:T(2,128)S(1)} %pad_maximum_fusion.2), channel_id=1, source_target_pairs={{0,3},{1,4},{2,5},{3,6},{4,7},{5,0},{6,1},{7,2},{8,11},{9,12},{10,... | collective-permute-start | bytes 3080 | tf_op jit(solution)/shard_map/ppermute | solution.py:411
  74.6 10.5 %collective-permute-start.3 = (f32[3,128]{1,0:T(4,128)S(1)}, f32[3,128]{1,0:T(4,128)S(1)}, u32[]{:S(2)}, u32[]{:S(2)}) collective-permute-start(f32[3,128]{1,0:T(4,128)S(1)} %pad_maximum_fusion), channel_id=1, source_target_pairs={{0,5},{1,6},{2,7},{3,0},{4,1},{5,2},{6,3},{7,4},{8,13},{9,14},{10,... | collective-permute-start | bytes 4616 | tf_op jit(solution)/shard_map/ppermute | solution.py:411
  77.1 13.9 %copy-start.7 = (f32[1,512]{1,0:T(1,128)S(1)}, f32[1,512]{1,0:T(1,128)}, u32[]{:S(2)}) copy-start(f32[1,512]{1,0:T(1,128)} %value_ref.1) | copy-start | bytes 6148
  81.3 17.0 %all-to-all-start.2 = ((f32[16,104,128]{2,1,0:T(8,128)}), f32[16,104,128]{2,1,0:T(8,128)S(1)}, u32[]{:S(2)}, u32[]{:S(2)}) async-start(f32[16,104,128]{2,1,0:T(8,128)} %shard_map.110), calls=%async_computation.2 | async-start | bytes 1703936 | tf_op jit(solution)/shard_map/all_to_all | solution.py:514
  85.1 3.8 %collective-permute-start.6 = (f32[2,128]{1,0:T(2,128)S(1)}, f32[2,128]{1,0:T(2,128)S(1)}, u32[]{:S(2)}, u32[]{:S(2)}) collective-permute-start(f32[2,128]{1,0:T(2,128)S(1)} %pad_maximum_fusion.3), channel_id=1, source_target_pairs={{0,1},{1,2},{2,3},{3,4},{4,5},{5,6},{6,7},{7,0},{8,9},{9,10},{10,1... | collective-permute-start | bytes 3080 | tf_op jit(solution)/shard_map/ppermute | solution.py:411
  88.2 2.8 %collective-permute-start.5 = (f32[3,128]{1,0:T(4,128)S(1)}, f32[3,128]{1,0:T(4,128)S(1)}, u32[]{:S(2)}, u32[]{:S(2)}) collective-permute-start(f32[3,128]{1,0:T(4,128)S(1)} %pad_maximum_fusion.1), channel_id=1, source_target_pairs={{0,7},{1,0},{2,1},{3,2},{4,3},{5,4},{6,5},{7,6},{8,15},{9,8},{10,9... | collective-permute-start | bytes 4616 | tf_op jit(solution)/shard_map/ppermute | solution.py:411
  98.3 5.1 %copy-start.2 = (f32[8,416,128]{2,1,0:T(8,128)S(1)}, f32[8,416,128]{2,1,0:T(8,128)}, u32[]{:S(2)}) copy-start(f32[8,416,128]{2,1,0:T(8,128)} %copy-done.1) | copy-start | bytes 5111812
  98.4 5.0 %collective-permute-start.7 = (f32[16,104,128]{2,1,0:T(8,128)S(1)}, f32[16,104,128]{2,1,0:T(8,128)S(1)}, u32[]{:S(2)}, u32[]{:S(2)}) collective-permute-start(f32[16,104,128]{2,1,0:T(8,128)S(1)} %shard_map.112), channel_id=1, source_target_pairs={{0,8},{8,0},{1,9},{9,1},{2,10},{10,2},{3,11},{11,3},{4,12},{12,4},... | collective-permute-start | bytes 2555912 | tf_op jit(solution)/shard_map/ppermute | solution.py:527

commit v11 on v10

--- a/solution.py
+++ b/solution.py
@@ -174,10 +174,6 @@
         copy.wait()
 
 
-def rotated(j):
-    return j % 5 in (0, 2)
-
-
 def advance_kernel(
     rate_ref, west_ref, east_ref, core_ref, store_ref, order_ref,
     end_ref, keep_ref, send_ref, table, band, odd, even, end_held, base, powers, sems
@@ -201,13 +197,8 @@
         else:
             rates = [east_ref[j - STEPS - COLS, ROWS + i : ROWS + i + 1, :] for i in range(4)]
         center = 1.0 - (rates[0] + rates[1] + rates[2] + rates[3])
-        table[5 * j] = jnp.broadcast_to(rates[0], (8, LANES))
-        table[5 * j + 1] = jnp.broadcast_to(rates[1], (8, LANES))
-        if rotated(j):
-            table[5 * j + 2] = jnp.broadcast_to(center, (8, LANES))
-            table[5 * j + 3] = jnp.broadcast_to(jnp.where(lane[:1] == LANES - 1, 0.0, rates[2]), (8, LANES))
-            table[5 * j + 4] = jnp.broadcast_to(jnp.where(lane[:1] == 0, 0.0, rates[3]), (8, LANES))
-            continue
+        table[2 * j] = jnp.broadcast_to(rates[0], (8, LANES))
+        table[2 * j + 1] = jnp.broadcast_to(rates[1], (8, LANES))
         along = jnp.where(row == lane, center, 0.0)
         along = jnp.where(row == lane + 1, rates[2], along)
         along = jnp.where(row == lane - 1, rates[3], along)
@@ -227,8 +218,8 @@
         return value.reshape(value.shape[0] // 8, 8, LANES)
 
     def finish(step, j, rows, total):
-        total = total + table[5 * j] * tiles(load(step - 1, j + 1, rows))
-        total = total + table[5 * j + 1] * tiles(load(step - 1, j - 1, rows))
+        total = total + table[2 * j] * tiles(load(step - 1, j + 1, rows))
+        total = total + table[2 * j + 1] * tiles(load(step - 1, j - 1, rows))
         total = total.reshape(total.shape[0] * 8, LANES)
         if step == STEPS:
             end_held[j - STEPS, rows, :] = total
@@ -244,18 +235,10 @@
         for j in order:
             if step == 1 and j == STEPS - 1:
                 own.wait()
-            if rotated(j):
-                for rows in quarters:
-                    value = tiles(load(step - 1, j, rows))
-                    total = table[5 * j + 2] * value
-                    total = total + table[5 * j + 3] * pltpu.roll(value, LANES - 1, 2)
-                    total = total + table[5 * j + 4] * pltpu.roll(value, 1, 2)
-                    finish(step, j, rows, total)
-            else:
-                parts = jnp.concatenate(two_parts(load(step - 1, j, slice(None))), 1)
-                along = jnp.dot(parts, band[j], preferred_element_type=F32)
-                for rows in quarters:
-                    finish(step, j, rows, tiles(along[rows, :LANES] + along[rows, LANES:]))
+            parts = jnp.concatenate(two_parts(load(step - 1, j, slice(None))), 1)
+            along = jnp.dot(parts, band[j], preferred_element_type=F32)
+            for rows in quarters:
+                finish(step, j, rows, tiles(along[rows, :LANES] + along[rows, LANES:]))
 
     for copy in later:
         copy.wait()
@@ -474,7 +457,7 @@
         [shape(END_STORE, PAD, LANES), parts, parts],
         (rates, from_west, from_east, core, planes, arrived),
         scratch=[
-            pltpu.VMEM((5 * wide, 8, LANES), F32),
+            pltpu.VMEM((2 * wide, 8, LANES), F32),
             pltpu.VMEM((wide, 2 * LANES, 2 * LANES), BF16),
             pltpu.VMEM((wide, PAD, LANES), F32),
             pltpu.VMEM((wide, PAD, LANES), F32),

time: 106 us -> 106 us (level)
  no operation moved by 1% of the time
where the time goes in v11:
time: 106 us; the launch traced here: 104 us
  starting transfers between devices  38.9 us (37%)
  Pallas kernels  34 us (32%)
  waiting for transfers between devices  26.2 us (25%)
  local copies, waits for them, and re-layouts  3.6 us (3%)
  between operations  1.66 us (2%)
    pallas_call x10, Pallas kernels, call(): pl.pallas_call(body, out_shape=outs, in_specs=specs, out_specs=out_specs...  34 us
    all_to_all x1, starting transfers between devices, per_device(): arrived = lax.all_to_all(queries, 'tile', 0, 0, tiled=True)  9.77 us
    all_to_all x1, waiting for transfers between devices, per_device(): arrived = lax.all_to_all(queries, 'tile', 0, 0, tiled=True)  9.53 us
    ppermute x4, starting transfers between devices, ring_step(): lax.ppermute(parcel, 'tile', [(i, (i + by) % TILES) for i in range(TILES)])  8.01 us
    all_to_all x1, starting transfers between devices, per_device(): gathered = lax.all_to_all(pair, ('y', 'x'), 0, 0, tiled=True)  6.75 us
    all_to_all x1, waiting for transfers between devices, per_device(): before = lax.all_to_all(totals, ('y', 'x'), 0, 0, tiled=True)  6.38 us
    ppermute x1, starting transfers between devices, per_device(): from_west = lax.ppermute(east, 'tile', to_east)  4.45 us
    ppermute x4, waiting for transfers between devices, ring_step(): lax.ppermute(parcel, 'tile', [(i, (i + by) % TILES) for i in range(TILES)])  3.88 us
  transfers between devices with their start and end apart: 11, of which 8 were waited for; matrix products, arithmetic and copies ran while one was open for 1% of the time, Pallas kernels for 17%

profile of v11, /device:TPU:1, one launch (start us, length us, event | category | flops | bytes accessed | tf_op | source)
XLA Modules:
  0.0 104.4 jit_solution(13052396318526862087)
XLA Ops:
  0.6 3.4 %shard_map.104 = (f32[6,416,128]{2,1,0:T(8,128)}, f32[6,416,128]{2,1,0:T(8,128)}, f32[8,128]{1,0:T(8,128)}) custom-call(f32[411,8,128]{2,1,0:T(8,128)} %bitcast.9, f32[4,8,128]{2,1,0:T(8,128)} %bitcast.13), custom_call_target="tpu_custom_call" | custom-call | bytes 5111808 | tf_op jit(solution)/shard_map/pallas_call | solution.py:43
  4.1 4.5 %collective-permute-start = (f32[6,416,128]{2,1,0:T(8,128)}, f32[6,416,128]{2,1,0:T(8,128)S(1)}, u32[]{:S(2)}, u32[]{:S(2)}) collective-permute-start(f32[6,416,128]{2,1,0:T(8,128)} %get-tuple-element.19), channel_id=1, source_target_pairs={{0,1},{1,2},{2,3},{3,4},{4,5},{5,6},{6,7},{8,9},{9,10},{10,11},{11... | collective-permute-start | bytes 3833864 | tf_op jit(solution)/shard_map/ppermute | solution.py:420
  8.5 1.3 %collective-permute-start.1 = (f32[6,416,128]{2,1,0:T(8,128)}, f32[6,416,128]{2,1,0:T(8,128)}, u32[]{:S(2)}, u32[]{:S(2)}) collective-permute-start(f32[6,416,128]{2,1,0:T(8,128)} %get-tuple-element.20), channel_id=1, source_target_pairs={{1,0},{2,1},{3,2},{4,3},{5,4},{6,5},{7,6},{9,8},{10,9},{11,10},{12... | collective-permute-start | bytes 3833864 | tf_op jit(solution)/shard_map/ppermute | solution.py:421
  9.8 1.2 %copy.13 = f32[1,411,411]{2,1,0:T(8,128)S(1)} copy(f32[1,411,411]{2,0,1:T(1,128)} %param.12) | data formatting | bytes 1351368
  11.1 1.1 %copy-done.4 = f32[411,411]{1,0:T(8,128)S(1)} copy-done((f32[411,411]{1,0:T(8,128)S(1)}, f32[411,411]{1,0:T(8,128)}, u32[]{:S(2)}) %copy-start.4) | copy-done | bytes 675708
  12.3 8.5 %shard_map.105 = (f32[8,416,128]{2,1,0:T(8,128)S(1)}, f32[160,416,128]{2,1,0:T(8,128)}, f32[8,128]{1,0:T(8,128)S(1)}) custom-call(f32[411,8,128]{2,1,0:T(8,128)S(1)} %bitcast.10, f32[411,8,128]{2,1,0:T(8,128)S(1)} %bitcast.12, f32[411,411]{1,0:T(8,128)S(1)} %copy-done.4, f32[411,411]{1,0:T(8,128)S(1)} %bitcast.11, f32[8,128]{1,0:T(8,128)S(1)} %copy-done.6), custom_call_target="tpu_custom_call" | custom-call | flops 100000000 | bytes 1000000 | tf_op jit(solution)/shard_map/pallas_call | solution.py:43
  20.8 1.2 %copy-done.1 = f32[8,416,128]{2,1,0:T(8,128)} copy-done((f32[8,416,128]{2,1,0:T(8,128)}, f32[8,416,128]{2,1,0:T(8,128)S(1)}, u32[]{:S(2)}) %copy-start.1) | copy-done | bytes 1703960
  21.9 2.5 %shard_map.106 = (f32[8,8,128]{2,1,0:T(8,128)}, f32[16,512]{1,0:T(8,128)S(1)}) custom-call(s32[3,1,512]{2,1,0:T(1,128)S(1)} %copy-done.8, f32[2,1,512]{2,1,0:T(1,128)S(1)} %copy-done.9, f32[8,128]{1,0:T(8,128)S(1)} %get-tuple-element.22.order_ref), custom_call_target="tpu_custom_call" | custom-call | flops 10000000 | bytes 100000 | tf_op jit(solution)/shard_map/pallas_call | solution.py:43
  24.4 9.8 %all-to-all-start = ((f32[8,8,128]{2,1,0:T(8,128)}), f32[8,8,128]{2,1,0:T(8,128)S(1)}, u32[]{:S(2)}, u32[]{:S(2)}) async-start(f32[8,8,128]{2,1,0:T(8,128)} %get-tuple-element.23), calls=%async_computation | async-start | bytes 65536 | tf_op jit(solution)/shard_map/all_to_all | solution.py:452
  34.2 9.5 %all-to-all-done.order_ref.obs_ref = f32[8,8,128]{2,1,0:T(8,128)S(1)} async-done(((f32[8,8,128]{2,1,0:T(8,128)}), f32[8,8,128]{2,1,0:T(8,128)S(1)}, u32[]{:S(2)}, u32[]{:S(2)}) %all-to-all-start) | async-done | bytes 32800 | tf_op jit(solution)/shard_map/all_to_all | solution.py:452
  43.7 10.1 %shard_map.107 = (f32[320,416,128]{2,1,0:T(8,128)}, f32[16,104,128]{2,1,0:T(8,128)S(1)}, f32[16,104,128]{2,1,0:T(8,128)S(1)}) custom-call(f32[4,8,128]{2,1,0:T(8,128)S(1)} %bitcast.14, f32[6,416,128]{2,1,0:T(8,128)S(1)} %collective-permute-done.west_ref, f32[6,416,128]{2,1,0:T(8,128)} %collective-permute-done.1.east_ref, s32[1]{0:T(128)} %bitcast.core_ref, ...), custom_call_target="tpu_custom_call" | custom-call | flops 15000000512 | bytes 10223616 | tf_op jit(solution)/shard_map/pallas_call | solution.py:43
  53.8 1.8 %collective-permute-start.2 = (f32[16,104,128]{2,1,0:T(8,128)S(1)}, f32[16,104,128]{2,1,0:T(8,128)S(1)}, u32[]{:S(2)}, u32[]{:S(2)}) collective-permute-start(f32[16,104,128]{2,1,0:T(8,128)S(1)} %get-tuple-element.25), channel_id=1, source_target_pairs={{0,8},{8,0},{1,9},{9,1},{2,10},{10,2},{3,11},{11,3},{4,12},{12,4},... | collective-permute-start | bytes 2555912 | tf_op jit(solution)/shard_map/ppermute | solution.py:477
  56.3 1.4 %collective-permute-done.2.partner_ref = f32[16,104,128]{2,1,0:T(8,128)S(1)} collective-permute-done((f32[16,104,128]{2,1,0:T(8,128)S(1)}, f32[16,104,128]{2,1,0:T(8,128)S(1)}, u32[]{:S(2)}, u32[]{:S(2)}) %collective-permute-start.2) | collective-permute-done | bytes 852000 | tf_op jit(solution)/shard_map/ppermute | solution.py:477
  57.7 1.0 shard_map.108
  58.6 6.8 %all-to-all-start.1 = ((f32[16,104,128]{2,1,0:T(8,128)}), f32[16,104,128]{2,1,0:T(8,128)S(1)}, u32[]{:S(2)}, u32[]{:S(2)}) async-start(f32[16,104,128]{2,1,0:T(8,128)} %get-tuple-element.26), calls=%async_computation.1 | async-start | bytes 1703936 | tf_op jit(solution)/shard_map/all_to_all | solution.py:479
  65.4 5.1 %shard_map.109.order_ref = f32[8,128]{1,0:T(8,128)S(1)} custom-call(s32[1]{0:T(128)} %bitcast.4.me_ref, f32[8,8,128]{2,1,0:T(8,128)S(1)} %all-to-all-done.order_ref.obs_ref, f32[320,416,128]{2,1,0:T(8,128)} %get-tuple-element.27.end_ref, f32[8,128]{1,0:T(8,128)S(1)} %get-tuple-element.28.order_ref), custom_call_target="tpu_custom_call" | custom-call | flops 3000000000 | bytes 1703936 | tf_op jit(solution)/shard_map/pallas_call | solution.py:43
  70.6 3.5 %collective-permute-start.4 = (f32[2,128]{1,0:T(2,128)S(1)}, f32[2,128]{1,0:T(2,128)S(1)}, u32[]{:S(2)}, u32[]{:S(2)}) collective-permute-start(f32[2,128]{1,0:T(2,128)S(1)} %pad_maximum_fusion.2), channel_id=1, source_target_pairs={{0,3},{1,4},{2,5},{3,6},{4,7},{5,0},{6,1},{7,2},{8,11},{9,12},{10,... | collective-permute-start | bytes 3080 | tf_op jit(solution)/shard_map/ppermute | solution.py:394
  74.1 1.3 %collective-permute-start.3 = (f32[3,128]{1,0:T(4,128)S(1)}, f32[3,128]{1,0:T(4,128)S(1)}, u32[]{:S(2)}, u32[]{:S(2)}) collective-permute-start(f32[3,128]{1,0:T(4,128)S(1)} %pad_maximum_fusion), channel_id=1, source_target_pairs={{0,5},{1,6},{2,7},{3,0},{4,1},{5,2},{6,3},{7,4},{8,13},{9,14},{10,... | collective-permute-start | bytes 4616 | tf_op jit(solution)/shard_map/ppermute | solution.py:394
  75.4 1.2 %collective-permute-done.4 = f32[2,128]{1,0:T(2,128)S(1)} collective-permute-done((f32[2,128]{1,0:T(2,128)S(1)}, f32[2,128]{1,0:T(2,128)S(1)}, u32[]{:S(2)}, u32[]{:S(2)}) %collective-permute-start.4) | collective-permute-done | bytes 1056 | tf_op jit(solution)/shard_map/ppermute | solution.py:394
  76.6 3.0 %all-to-all-done.1.in_ref = f32[16,104,128]{2,1,0:T(8,128)S(1)} async-done(((f32[16,104,128]{2,1,0:T(8,128)}), f32[16,104,128]{2,1,0:T(8,128)S(1)}, u32[]{:S(2)}, u32[]{:S(2)}) %all-to-all-start.1) | async-done | bytes 852000 | tf_op jit(solution)/shard_map/all_to_all | solution.py:479
  79.6 1.1 %shard_map.110 = f32[16,104,128]{2,1,0:T(8,128)} custom-call(f32[16,104,128]{2,1,0:T(8,128)S(1)} %all-to-all-done.1.in_ref, f32[8,128]{1,0:T(8,128)S(1)} %shard_map.109.order_ref), custom_call_target="tpu_custom_call" | custom-call | flops 10000000 | bytes 1703936 | tf_op jit(solution)/shard_map/pallas_call | solution.py:43
  80.7 3.8 %all-to-all-start.2 = ((f32[16,104,128]{2,1,0:T(8,128)}), f32[16,104,128]{2,1,0:T(8,128)S(1)}, u32[]{:S(2)}, u32[]{:S(2)}) async-start(f32[16,104,128]{2,1,0:T(8,128)} %shard_map.110), calls=%async_computation.2 | async-start | bytes 1703936 | tf_op jit(solution)/shard_map/all_to_all | solution.py:497
  84.6 3.1 %collective-permute-start.6 = (f32[2,128]{1,0:T(2,128)S(1)}, f32[2,128]{1,0:T(2,128)S(1)}, u32[]{:S(2)}, u32[]{:S(2)}) collective-permute-start(f32[2,128]{1,0:T(2,128)S(1)} %pad_maximum_fusion.3), channel_id=1, source_target_pairs={{0,1},{1,2},{2,3},{3,4},{4,5},{5,6},{6,7},{7,0},{8,9},{9,10},{10,1... | collective-permute-start | bytes 3080 | tf_op jit(solution)/shard_map/ppermute | solution.py:394
  87.7 0.1 collective-permute-start.5
  87.8 0.6 collective-permute-done.6
  88.4 2.1 %collective-permute-done.5 = f32[3,128]{1,0:T(4,128)S(1)} collective-permute-done((f32[3,128]{1,0:T(4,128)S(1)}, f32[3,128]{1,0:T(4,128)S(1)}, u32[]{:S(2)}, u32[]{:S(2)}) %collective-permute-start.5) | collective-permute-done | bytes 1568 | tf_op jit(solution)/shard_map/ppermute | solution.py:394
  90.5 0.9 shard_map.111
  91.4 6.4 %all-to-all-done.2.before_ref = f32[16,104,128]{2,1,0:T(8,128)S(1)} async-done(((f32[16,104,128]{2,1,0:T(8,128)}), f32[16,104,128]{2,1,0:T(8,128)S(1)}, u32[]{:S(2)}, u32[]{:S(2)}) %all-to-all-start.2) | async-done | bytes 852000 | tf_op jit(solution)/shard_map/all_to_all | solution.py:497
  97.8 0.1 shard_map.112
  97.9 3.0 %collective-permute-start.7 = (f32[16,104,128]{2,1,0:T(8,128)S(1)}, f32[16,104,128]{2,1,0:T(8,128)S(1)}, u32[]{:S(2)}, u32[]{:S(2)}) collective-permute-start(f32[16,104,128]{2,1,0:T(8,128)S(1)} %shard_map.112), channel_id=1, source_target_pairs={{0,8},{8,0},{1,9},{9,1},{2,10},{10,2},{3,11},{11,3},{4,12},{12,4},... | collective-permute-start | bytes 2555912 | tf_op jit(solution)/shard_map/ppermute | solution.py:510
  100.8 2.0 %collective-permute-done.7.other_ref = f32[16,104,128]{2,1,0:T(8,128)S(1)} collective-permute-done((f32[16,104,128]{2,1,0:T(8,128)S(1)}, f32[16,104,128]{2,1,0:T(8,128)S(1)}, u32[]{:S(2)}, u32[]{:S(2)}) %collective-permute-start.7) | collective-permute-done | bytes 852000 | tf_op jit(solution)/shard_map/ppermute | solution.py:510
  102.9 1.4 %shard_map.113 = f32[411,8,128]{2,1,0:T(8,128)} custom-call(s32[1]{0:T(128)} %bitcast.core_ref, f32[8,416,128]{2,1,0:T(8,128)S(1)} %copy-done.2, f32[16,104,128]{2,1,0:T(8,128)S(1)} %all-to-all-done.2.before_ref, f32[16,104,128]{2,1,0:T(8,128)S(1)} %collective-permute-done.2.partner_ref, f32[16,104,128]{2,1,0:T(8,128)S(1)} %collective-permute-done.7.other_ref), custom_call_target="tpu_custom_call" | custom-call | flops 10000000 | bytes 6815744 | tf_op jit(solution)/shard_map/pallas_call | solution.py:43
  (31 shorter events, 0.1 us)
Async XLA Ops:
  0.6 10.4 %copy-start = (f32[1,3,137,8,128]{4,3,2,1,0:T(8,128)S(1)}, f32[1,3,137,8,128]{4,3,2,1,0:T(8,128)}, u32[]{:S(2)}) copy-start(f32[1,3,137,8,128]{4,3,2,1,0:T(8,128)} %param.9) | copy-start | bytes 5050372
  0.6 10.4 %copy-start.3 = (f32[1,3,137,8,128]{4,3,2,1,0:T(8,128)S(1)}, f32[1,3,137,8,128]{4,3,2,1,0:T(8,128)}, u32[]{:S(2)}) copy-start(f32[1,3,137,8,128]{4,3,2,1,0:T(8,128)} %param.10) | copy-start | bytes 5050372
  4.1 7.0 %copy-start.6 = (f32[8,128]{1,0:T(8,128)S(1)}, f32[8,128]{1,0:T(8,128)}, u32[]{:S(2)}) copy-start(f32[8,128]{1,0:T(8,128)} %get-tuple-element.17.order_ref) | copy-start | bytes 12292
  4.1 39.7 %collective-permute-start = (f32[6,416,128]{2,1,0:T(8,128)}, f32[6,416,128]{2,1,0:T(8,128)S(1)}, u32[]{:S(2)}, u32[]{:S(2)}) collective-permute-start(f32[6,416,128]{2,1,0:T(8,128)} %get-tuple-element.19), channel_id=1, source_target_pairs={{0,1},{1,2},{2,3},{3,4},{4,5},{5,6},{6,7},{8,9},{9,10},{10,11},{11... | collective-permute-start | bytes 3833864 | tf_op jit(solution)/shard_map/ppermute | solution.py:420
  8.5 35.2 %collective-permute-start.1 = (f32[6,416,128]{2,1,0:T(8,128)}, f32[6,416,128]{2,1,0:T(8,128)}, u32[]{:S(2)}, u32[]{:S(2)}) collective-permute-start(f32[6,416,128]{2,1,0:T(8,128)} %get-tuple-element.20), channel_id=1, source_target_pairs={{1,0},{2,1},{3,2},{4,3},{5,4},{6,5},{7,6},{9,8},{10,9},{11,10},{12... | collective-permute-start | bytes 3833864 | tf_op jit(solution)/shard_map/ppermute | solution.py:421
  11.1 1.2 %copy-start.4 = (f32[411,411]{1,0:T(8,128)S(1)}, f32[411,411]{1,0:T(8,128)}, u32[]{:S(2)}) copy-start(f32[411,411]{1,0:T(8,128)} %root_ref.1) | copy-start | bytes 2027056
  12.2 9.7 %copy-start.8 = (s32[3,1,512]{2,1,0:T(1,128)S(1)}, s32[3,1,512]{2,1,0:T(1,128)}, u32[]{:S(2)}) copy-start(s32[3,1,512]{2,1,0:T(1,128)} %index_ref.1) | copy-start | bytes 18436
  12.2 9.7 %copy-start.9 = (f32[2,1,512]{2,1,0:T(1,128)S(1)}, f32[2,1,512]{2,1,0:T(1,128)}, u32[]{:S(2)}) copy-start(f32[2,1,512]{2,1,0:T(1,128)} %frac_ref.1) | copy-start | bytes 12292
  12.2 31.5 %copy-start.5 = (f32[1,4,8,128]{3,2,1,0:T(8,128)S(1)}, f32[1,4,8,128]{3,2,1,0:T(8,128)}, u32[]{:S(2)}) copy-start(f32[1,4,8,128]{3,2,1,0:T(8,128)} %param.13) | copy-start | bytes 49156
  20.7 1.2 %copy-start.1 = (f32[8,416,128]{2,1,0:T(8,128)}, f32[8,416,128]{2,1,0:T(8,128)S(1)}, u32[]{:S(2)}) copy-start(f32[8,416,128]{2,1,0:T(8,128)S(1)} %get-tuple-element.18.base_ref) | copy-start | bytes 5111812
  24.4 19.3 %all-to-all-start = ((f32[8,8,128]{2,1,0:T(8,128)}), f32[8,8,128]{2,1,0:T(8,128)S(1)}, u32[]{:S(2)}, u32[]{:S(2)}) async-start(f32[8,8,128]{2,1,0:T(8,128)} %get-tuple-element.23), calls=%async_computation | async-start | bytes 65536 | tf_op jit(solution)/shard_map/all_to_all | solution.py:452
  53.8 3.8 %collective-permute-start.2 = (f32[16,104,128]{2,1,0:T(8,128)S(1)}, f32[16,104,128]{2,1,0:T(8,128)S(1)}, u32[]{:S(2)}, u32[]{:S(2)}) collective-permute-start(f32[16,104,128]{2,1,0:T(8,128)S(1)} %get-tuple-element.25), channel_id=1, source_target_pairs={{0,8},{8,0},{1,9},{9,1},{2,10},{10,2},{3,11},{11,3},{4,12},{12,4},... | collective-permute-start | bytes 2555912 | tf_op jit(solution)/shard_map/ppermute | solution.py:477
  58.6 21.0 %all-to-all-start.1 = ((f32[16,104,128]{2,1,0:T(8,128)}), f32[16,104,128]{2,1,0:T(8,128)S(1)}, u32[]{:S(2)}, u32[]{:S(2)}) async-start(f32[16,104,128]{2,1,0:T(8,128)} %get-tuple-element.26), calls=%async_computation.1 | async-start | bytes 1703936 | tf_op jit(solution)/shard_map/all_to_all | solution.py:479
  70.6 6.0 %collective-permute-start.4 = (f32[2,128]{1,0:T(2,128)S(1)}, f32[2,128]{1,0:T(2,128)S(1)}, u32[]{:S(2)}, u32[]{:S(2)}) collective-permute-start(f32[2,128]{1,0:T(2,128)S(1)} %pad_maximum_fusion.2), channel_id=1, source_target_pairs={{0,3},{1,4},{2,5},{3,6},{4,7},{5,0},{6,1},{7,2},{8,11},{9,12},{10,... | collective-permute-start | bytes 3080 | tf_op jit(solution)/shard_map/ppermute | solution.py:394
  74.1 10.5 %collective-permute-start.3 = (f32[3,128]{1,0:T(4,128)S(1)}, f32[3,128]{1,0:T(4,128)S(1)}, u32[]{:S(2)}, u32[]{:S(2)}) collective-permute-start(f32[3,128]{1,0:T(4,128)S(1)} %pad_maximum_fusion), channel_id=1, source_target_pairs={{0,5},{1,6},{2,7},{3,0},{4,1},{5,2},{6,3},{7,4},{8,13},{9,14},{10,... | collective-permute-start | bytes 4616 | tf_op jit(solution)/shard_map/ppermute | solution.py:394
  76.6 13.9 %copy-start.7 = (f32[1,512]{1,0:T(1,128)S(1)}, f32[1,512]{1,0:T(1,128)}, u32[]{:S(2)}) copy-start(f32[1,512]{1,0:T(1,128)} %value_ref.1) | copy-start | bytes 6148
  80.7 17.0 %all-to-all-start.2 = ((f32[16,104,128]{2,1,0:T(8,128)}), f32[16,104,128]{2,1,0:T(8,128)S(1)}, u32[]{:S(2)}, u32[]{:S(2)}) async-start(f32[16,104,128]{2,1,0:T(8,128)} %shard_map.110), calls=%async_computation.2 | async-start | bytes 1703936 | tf_op jit(solution)/shard_map/all_to_all | solution.py:497
  84.6 3.8 %collective-permute-start.6 = (f32[2,128]{1,0:T(2,128)S(1)}, f32[2,128]{1,0:T(2,128)S(1)}, u32[]{:S(2)}, u32[]{:S(2)}) collective-permute-start(f32[2,128]{1,0:T(2,128)S(1)} %pad_maximum_fusion.3), channel_id=1, source_target_pairs={{0,1},{1,2},{2,3},{3,4},{4,5},{5,6},{6,7},{7,0},{8,9},{9,10},{10,1... | collective-permute-start | bytes 3080 | tf_op jit(solution)/shard_map/ppermute | solution.py:394
  87.7 2.8 %collective-permute-start.5 = (f32[3,128]{1,0:T(4,128)S(1)}, f32[3,128]{1,0:T(4,128)S(1)}, u32[]{:S(2)}, u32[]{:S(2)}) collective-permute-start(f32[3,128]{1,0:T(4,128)S(1)} %pad_maximum_fusion.1), channel_id=1, source_target_pairs={{0,7},{1,0},{2,1},{3,2},{4,3},{5,4},{6,5},{7,6},{8,15},{9,8},{10,9... | collective-permute-start | bytes 4616 | tf_op jit(solution)/shard_map/ppermute | solution.py:394
  97.8 5.1 %copy-start.2 = (f32[8,416,128]{2,1,0:T(8,128)S(1)}, f32[8,416,128]{2,1,0:T(8,128)}, u32[]{:S(2)}) copy-start(f32[8,416,128]{2,1,0:T(8,128)} %copy-done.1) | copy-start | bytes 5111812
  97.9 5.0 %collective-permute-start.7 = (f32[16,104,128]{2,1,0:T(8,128)S(1)}, f32[16,104,128]{2,1,0:T(8,128)S(1)}, u32[]{:S(2)}, u32[]{:S(2)}) collective-permute-start(f32[16,104,128]{2,1,0:T(8,128)S(1)} %shard_map.112), channel_id=1, source_target_pairs={{0,8},{8,0},{1,9},{9,1},{2,10},{10,2},{3,11},{11,3},{4,12},{12,4},... | collective-permute-start | bytes 2555912 | tf_op jit(solution)/shard_map/ppermute | solution.py:510
